TPU v7x, 256 devices: a whole 4x4x8 slice. The times are simulated.
256 devices in a mesh: slab: 8 (over x, core), panel: 32 (over y, z).
Axes of the slice: x: 4, y: 4, z: 8, core: 2. Of those that a mesh axis runs over, the one named last changes fastest.
Arguments:
- ranges: float32 [8, 4, 1024, 1024], P('slab', None, 'panel'), may hold values from -1.5 to 1.5
- pattern: int32 [8, 4, 16, 16], P('slab'), may hold values 0 or 1
Outputs:
- combined: float32 [8, 4, 1024, 1024], P('slab', None, 'panel')
All inputs are finite; a program needn't handle non-finite values. No bound on the sum of `pattern` on one device may be relied on, other than what follows from the above.
Results may differ from a plain program's by a relative error of at most 0.01.
Values may be sent and summed in bfloat16 or wider, within the bound.
No kernel may reach another device: no remote copies, remote signals or barrier semaphores. Data moves between devices by JAX's collectives and lax.ppermute only.
A program may use at most 64 MiB of HBM per device.

v0:
```python
import jax
import jax.numpy as jnp
from jax import lax
from jax.sharding import PartitionSpec as P

M = 1024
BLK = 64
LEVELS = 2


def partner_2(block, axis, distance):
    count = lax.axis_size(axis)
    route = []
    for low in range(count):
        high = low | 1 << distance
        if high != low and high < count:
            route += [(low, high), (high, low)]
    return lax.ppermute(block, axis, route)


def to_half(values):
    return values.astype(jnp.bfloat16)


def star(head, tail, row_start):
    head_top, head_up, head_down, head_bottom = (head[0], head[1], head[2], head[3])
    tail_top, tail_up, tail_down, tail_bottom = (tail[0], tail[1], tail[2], tail[3])
    local_rows = head.shape[1]
    right_bottom, right_up, right_down = (
        lax.all_gather(to_half(head_bottom), "panel", axis=0, tiled=True),
        lax.all_gather(to_half(tail_up), "panel", axis=0, tiled=True),
        lax.all_gather(to_half(head_down), "panel", axis=0, tiled=True),
    )

    def spread(values):
        return lax.all_gather(to_half(values), "panel", axis=0, tiled=True)

    def multiply(left, right):
        return jnp.dot(to_half(left), right, preferred_element_type=jnp.float32)

    col_ids = jnp.arange(M, dtype=jnp.int32)
    all_ids = jnp.arange(M, dtype=jnp.int32)
    eye_right = (all_ids[:, None] == col_ids[None, :]).astype(jnp.float32)
    row_ids = row_start + jnp.arange(local_rows, dtype=jnp.int32)
    eye_rows = (row_ids[:, None] == all_ids[None, :]).astype(jnp.float32)
    loop_term = multiply(tail_top, right_bottom)
    loop_kept = lax.optimization_barrier(to_half(loop_term)).astype(jnp.float32)
    right_loop = spread(loop_term)
    right_defect = to_half(eye_right - right_loop.astype(jnp.float32))
    right_guess = to_half(eye_right + right_loop.astype(jnp.float32))
    guess = eye_rows + loop_kept
    guess = 2.0 * guess - multiply(multiply(guess, right_defect), right_guess)
    right_inverse = spread(guess)
    lifted = multiply(head_up, right_inverse)
    joint_up = multiply(lifted, right_up)
    bounce = multiply(tail_top, right_down)
    right_bounce = spread(bounce)
    joint_top = head_top + multiply(lifted, right_bounce)
    reach = multiply(tail_down, right_bottom)
    through = multiply(reach, right_inverse)
    joint_down = multiply(tail_down, right_down) + multiply(through, right_bounce)
    joint_bottom = (
        tail_bottom + multiply(reach, right_up) + multiply(multiply(through, right_loop), right_up)
    )
    return jnp.stack([joint_top, joint_up, joint_down, joint_bottom])


def body(ranges, pattern):
    group_blocks = ranges[0]
    local_rows = group_blocks.shape[1]
    block_count = pattern.shape[2]
    row_start = lax.axis_index("panel") * local_rows
    row_ids = row_start + jnp.arange(local_rows, dtype=jnp.int32)
    col_ids = jnp.arange(M, dtype=jnp.int32)
    block_ids = jnp.arange(block_count, dtype=jnp.int32)
    row_pick = (row_ids[:, None] // BLK == block_ids[None, :]).astype(jnp.float32)
    col_pick = (block_ids[:, None] == col_ids[None, :] // BLK).astype(jnp.float32)
    block_mask = jnp.einsum("mi,gij,jc->gmc", row_pick, pattern[0].astype(jnp.float32), col_pick)
    merged = group_blocks * block_mask
    for tree_level in range(LEVELS):
        partner = partner_2(merged, "slab", tree_level)
        is_lower = lax.axis_index("slab") >> tree_level & 1 == 0
        head_blocks = jnp.where(is_lower, merged, partner)
        tail_blocks = jnp.where(is_lower, partner, merged)
        merged = star(head_blocks, tail_blocks, row_start)
    return merged[None]


def solution(mesh):
    return jax.shard_map(
        body,
        mesh=mesh,
        in_specs=(P("slab", None, "panel", None), P("slab", None, None, None)),
        out_specs=P("slab", None, "panel", None),
        check_vma=False,
    )
```

profile of v0, /device:TPU:1, one launch (start us, length us, event | category | flops | bytes accessed | tf_op | source)
XLA Modules:
  0.0 979.0 jit_solution(15303100877699659643)
XLA Ops:
  6.6 1.5 convolution_multiply_fusion
  8.1 3.3 collective-permute-start
  11.4 1.5 collective-permute-done
  14.6 75.1 %all-gather.31.cloned.1.call-done = bf16[1,1024,1024]{2,1,0:T(8,128)(2,1)} async-done(((bf16[1,32,1024]{2,1,0:T(8,128)(2,1)}), bf16[1,1024,1024]{2,1,0:T(8,128)(2,1)}) %all-gather.31.cloned.1.call-update) | async-done | bytes 2097168 | tf_op jit(solution)/shard_map/all_gather | solution.py:30
  89.7 2.7 fusion.70
  93.9 73.8 %all-gather.19.cloned.1.call-done = bf16[1024,1024]{1,0:T(8,128)(2,1)} async-done(((bf16[32,1024]{1,0:T(8,128)(2,1)}), bf16[1024,1024]{1,0:T(8,128)(2,1)}) %all-gather.19.cloned.1.call-update) | async-done | bytes 2097168 | tf_op jit(solution)/shard_map/all_gather | solution.py:36
  167.7 3.9 fusion.67
  171.6 73.8 %all-gather.33.cloned.1.call-done = bf16[1,1024,1024]{2,1,0:T(8,128)(2,1)} async-done(((bf16[1,32,1024]{2,1,0:T(8,128)(2,1)}), bf16[1,1024,1024]{2,1,0:T(8,128)(2,1)}) %all-gather.33.cloned.1.call-update) | async-done | bytes 2097168 | tf_op jit(solution)/shard_map/all_gather | solution.py:32
  245.5 2.7 fusion.76
  248.7 74.4 %all-gather.35.cloned.1.call-done = bf16[1,1024,1024]{2,1,0:T(8,128)(2,1)} async-done(((bf16[1,32,1024]{2,1,0:T(8,128)(2,1)}), bf16[1,1024,1024]{2,1,0:T(8,128)(2,1)}) %all-gather.35.cloned.1.call-update) | async-done | bytes 2097168 | tf_op jit(solution)/shard_map/all_gather | solution.py:31
  323.1 2.7 fusion.28
  325.8 74.9 %all-gather.21.cloned.1.call-done = bf16[1024,1024]{1,0:T(8,128)(2,1)} async-done(((bf16[32,1024]{1,0:T(8,128)(2,1)}), bf16[1024,1024]{1,0:T(8,128)(2,1)}) %all-gather.21.cloned.1.call-update) | async-done | bytes 2097168 | tf_op jit(solution)/shard_map/all_gather | solution.py:36
  400.7 2.2 convolution_convert_fusion.4
  403.4 74.9 %all-gather.23.cloned.1.call-done = bf16[1024,1024]{1,0:T(8,128)(2,1)} async-done(((bf16[32,1024]{1,0:T(8,128)(2,1)}), bf16[1024,1024]{1,0:T(8,128)(2,1)}) %all-gather.23.cloned.1.call-update) | async-done | bytes 2097168 | tf_op jit(solution)/shard_map/all_gather | solution.py:36
  478.3 2.1 fusion.143
  480.4 2.2 fusion.49
  484.5 2.4 fusion.105
  488.2 7.7 collective-permute-done.1
  498.3 75.7 %all-gather.37.cloned.1.call-done = bf16[1,1024,1024]{2,1,0:T(8,128)(2,1)} async-done(((bf16[1,32,1024]{2,1,0:T(8,128)(2,1)}), bf16[1,1024,1024]{2,1,0:T(8,128)(2,1)}) %all-gather.37.cloned.1.call-update) | async-done | bytes 2097168 | tf_op jit(solution)/shard_map/all_gather | solution.py:30
  574.0 2.7 fusion.79
  578.2 73.8 %all-gather.25.cloned.1.call-done = bf16[1024,1024]{1,0:T(8,128)(2,1)} async-done(((bf16[32,1024]{1,0:T(8,128)(2,1)}), bf16[1024,1024]{1,0:T(8,128)(2,1)}) %all-gather.25.cloned.1.call-update) | async-done | bytes 2097168 | tf_op jit(solution)/shard_map/all_gather | solution.py:36
  652.0 3.8 fusion.64
  655.9 73.8 %all-gather.39.cloned.1.call-done = bf16[1,1024,1024]{2,1,0:T(8,128)(2,1)} async-done(((bf16[1,32,1024]{2,1,0:T(8,128)(2,1)}), bf16[1,1024,1024]{2,1,0:T(8,128)(2,1)}) %all-gather.39.cloned.1.call-update) | async-done | bytes 2097168 | tf_op jit(solution)/shard_map/all_gather | solution.py:32
  729.8 2.7 fusion.85
  733.0 74.4 %all-gather.41.cloned.1.call-done = bf16[1,1024,1024]{2,1,0:T(8,128)(2,1)} async-done(((bf16[1,32,1024]{2,1,0:T(8,128)(2,1)}), bf16[1,1024,1024]{2,1,0:T(8,128)(2,1)}) %all-gather.41.cloned.1.call-update) | async-done | bytes 2097168 | tf_op jit(solution)/shard_map/all_gather | solution.py:31
  807.4 2.1 fusion.14
  809.4 75.7 %all-gather.27.cloned.1.call-done = bf16[1024,1024]{1,0:T(8,128)(2,1)} async-done(((bf16[32,1024]{1,0:T(8,128)(2,1)}), bf16[1024,1024]{1,0:T(8,128)(2,1)}) %all-gather.27.cloned.1.call-update) | async-done | bytes 2097168 | tf_op jit(solution)/shard_map/all_gather | solution.py:36
  885.2 2.2 convolution_convert_fusion.1
  888.7 74.1 %all-gather.29.cloned.1.call-done = bf16[1024,1024]{1,0:T(8,128)(2,1)} async-done(((bf16[32,1024]{1,0:T(8,128)(2,1)}), bf16[1024,1024]{1,0:T(8,128)(2,1)}) %all-gather.29.cloned.1.call-update) | async-done | bytes 2097168 | tf_op jit(solution)/shard_map/all_gather | solution.py:36
  962.8 2.1 fusion.144
  964.8 2.2 fusion.55
  968.9 2.4 fusion.100
  (64 shorter events, 15.8 us)
Async XLA Ops:
  6.5 83.1 %all-gather.31.cloned.1.call-start = ((), (), s32[]{:S(2)}) async-start(), calls=%async_computation.6 | async-start | bytes 2162688 | tf_op jit(solution)/shard_map/all_gather | solution.py:30
  8.1 4.9 collective-permute-start
  14.6 153.1 %all-gather.19.cloned.1.call-start = ((), (), s32[]{:S(2)}) async-start(), calls=%async_computation | async-start | bytes 2162688 | tf_op jit(solution)/shard_map/all_gather | solution.py:36
  92.4 153.1 %all-gather.33.cloned.1.call-start = ((), (), s32[]{:S(2)}) async-start(), calls=%async_computation.7 | async-start | bytes 2162688 | tf_op jit(solution)/shard_map/all_gather | solution.py:32
  93.1 230.0 %all-gather.35.cloned.1.call-start = ((), (), s32[]{:S(2)}) async-start(), calls=%async_computation.8 | async-start | bytes 2162688 | tf_op jit(solution)/shard_map/all_gather | solution.py:31
  93.8 306.9 %all-gather.21.cloned.1.call-start = ((), (), s32[]{:S(2)}) async-start(), calls=%async_computation.1 | async-start | bytes 2162688 | tf_op jit(solution)/shard_map/all_gather | solution.py:36
  171.5 76.7 %copy-start.2 = (bf16[1,1024,1024]{2,1,0:T(8,128)(2,1)S(1)}, bf16[1,1024,1024]{2,1,0:T(8,128)(2,1)}, u32[]{:S(2)}) copy-start(bf16[1,1024,1024]{2,1,0:T(8,128)(2,1)} %all-gather.31.cloned.1.call-done) | copy-start | bytes 6291460
  171.6 306.7 %all-gather.23.cloned.1.call-start = ((), (), s32[]{:S(2)}) async-start(), calls=%async_computation.2 | async-start | bytes 2162688 | tf_op jit(solution)/shard_map/all_gather | solution.py:36
  248.2 325.8 %all-gather.37.cloned.1.call-start = ((), (), s32[]{:S(2)}) async-start(), calls=%async_computation.9 | async-start | bytes 2162688 | tf_op jit(solution)/shard_map/all_gather | solution.py:30
  400.7 2.2 copy-start.4
  403.4 79.2 %copy-start = (bf16[1,1024,1024]{2,1,0:T(8,128)(2,1)S(1)}, bf16[1,1024,1024]{2,1,0:T(8,128)(2,1)}, u32[]{:S(2)}) copy-start(bf16[1,1024,1024]{2,1,0:T(8,128)(2,1)} %all-gather.35.cloned.1.call-done) | copy-start | bytes 6291460
  480.4 2.7 copy-start.5
  482.6 1.9 copy-start.9
  486.9 8.9 collective-permute-start.1
  496.8 0.7 copy-start.8
  498.2 153.8 %all-gather.25.cloned.1.call-start = ((), (), s32[]{:S(2)}) async-start(), calls=%async_computation.3 | async-start | bytes 2162688 | tf_op jit(solution)/shard_map/all_gather | solution.py:36
  576.7 153.1 %all-gather.39.cloned.1.call-start = ((), (), s32[]{:S(2)}) async-start(), calls=%async_computation.10 | async-start | bytes 2162688 | tf_op jit(solution)/shard_map/all_gather | solution.py:32
  577.5 229.9 %all-gather.41.cloned.1.call-start = ((), (), s32[]{:S(2)}) async-start(), calls=%async_computation.11 | async-start | bytes 2162688 | tf_op jit(solution)/shard_map/all_gather | solution.py:31
  578.1 307.0 %all-gather.27.cloned.1.call-start = ((), (), s32[]{:S(2)}) async-start(), calls=%async_computation.4 | async-start | bytes 2162688 | tf_op jit(solution)/shard_map/all_gather | solution.py:36
  655.9 76.6 %copy-start.3 = (bf16[1,1024,1024]{2,1,0:T(8,128)(2,1)S(1)}, bf16[1,1024,1024]{2,1,0:T(8,128)(2,1)}, u32[]{:S(2)}) copy-start(bf16[1,1024,1024]{2,1,0:T(8,128)(2,1)} %all-gather.37.cloned.1.call-done) | copy-start | bytes 6291460
  655.9 306.9 %all-gather.29.cloned.1.call-start = ((), (), s32[]{:S(2)}) async-start(), calls=%async_computation.5 | async-start | bytes 2162688 | tf_op jit(solution)/shard_map/all_gather | solution.py:36
  885.2 2.2 copy-start.6
  888.7 78.4 %copy-start.1 = (bf16[1,1024,1024]{2,1,0:T(8,128)(2,1)S(1)}, bf16[1,1024,1024]{2,1,0:T(8,128)(2,1)}, u32[]{:S(2)}) copy-start(bf16[1,1024,1024]{2,1,0:T(8,128)(2,1)} %all-gather.41.cloned.1.call-done) | copy-start | bytes 6291460
  964.8 2.7 copy-start.7
Sparse Core Ops, SparseCore 0:
  14.7 74.9 all-gather.30
  92.5 75.1 all-gather.18
  170.3 75.1 all-gather.32
  247.9 75.1 all-gather.34
  325.5 75.1 all-gather.20
  403.1 75.1 all-gather.22
  498.4 75.5 all-gather.36
  576.8 75.1 all-gather.24
  654.6 75.1 all-gather.38
  732.2 75.1 all-gather.40
  810.0 75.1 all-gather.26
  887.6 75.1 all-gather.28
where the time goes:
time: 983 us; the launch traced here: 979 us
  waiting for transfers between devices  905 us (92%)
  matrix products  48.9 us (5%)
  between operations  13.7 us (1%)
    all_gather x6, waiting for transfers between devices, spread(): return lax.all_gather(to_half(values), 'panel', axis=0, tiled=True)  447 us
    all_gather x2, waiting for transfers between devices, star(): lax.all_gather(to_half(head_bottom), 'panel', axis=0, tiled=True)  151 us
    all_gather x2, waiting for transfers between devices, star(): lax.all_gather(to_half(tail_up), 'panel', axis=0, tiled=True)  149 us
    all_gather x2, waiting for transfers between devices, star(): lax.all_gather(to_half(head_down), 'panel', axis=0, tiled=True)  148 us
    dot_general x24, matrix products, multiply(): return jnp.dot(to_half(left), right, preferred_element_type=jnp.float32)  47.4 us
  transfers between devices with their start and end apart: 14, of which 14 were waited for; matrix products, arithmetic and copies ran while one was open for 3% of the time, Pallas kernels for 0%

commit v1 on v0

v1 whole, which is shorter than its diff:
```python
import functools
import jax
import jax.numpy as jnp
from jax import lax
from jax.experimental import pallas as pl
from jax.experimental.pallas import tpu as pltpu
from jax.sharding import PartitionSpec as P

M = 1024
BLK = 64
LEVELS = 2
NX, NC, NY, NZ = 4, 2, 4, 8
AXES = ("slab", "panel")
TILE = 256


def device(x, c, y, z):
    return ((x % NX) * NC + c) * NY * NZ + (y % NY) * NZ + z % NZ


def route(move):
    pairs = []
    for x in range(NX):
        for c in range(NC):
            for y in range(NY):
                for z in range(NZ):
                    target = move(x, c, y, z)
                    if target is not None:
                        pairs.append((device(x, c, y, z), device(*target)))
    return pairs


def send(block, move):
    return lax.ppermute(block, AXES, route(move))


def step(sign, core0=None, core1=None):
    def move(x, c, y, z):
        axis = core0 if c == 0 else core1
        if axis is None:
            return None
        return (x, c, y + sign, z) if axis == "y" else (x, c, y, z + sign)

    return move


def gather(block):
    s1p = send(block, step(1, "y", "z"))
    s1m = send(block, step(-1, "y", "z"))
    s2p = send(s1p, step(1, "y", "z"))
    s2m = send(s1m, step(-1, None, "z"))
    wide0 = jnp.concatenate([block, s1p, s1m, s2p])
    h1p = send(wide0, step(1, "z", None))
    h1m = send(wide0, step(-1, "z", None))
    s3p = send(s2p, step(1, None, "z"))
    s3m = send(s2m, step(-1, None, "z"))
    s4p = send(s3p, step(1, None, "z"))
    wide1 = jnp.concatenate([block, s1p, s1m, s2p, s2m, s3p, s3m, s4p])
    g1p = send(wide1, step(1, None, "y"))
    g1m = send(wide1, step(-1, None, "y"))
    h2p = send(h1p, step(1, "z", None))
    h2m = send(h1m, step(-1, "z", None))
    h3p = send(h2p, step(1, "z", None))
    h3m = send(h2m, step(-1, "z", None))
    h4p = send(h3p, step(1, "z", None))
    half = g1p.shape[0] // 2
    g2p = send(g1p[:half], step(1, None, "y"))
    g2m = send(g1m[half:], step(-1, None, "y"))
    return [wide0, h1p, h1m, h2p, h2m, h3p, h3m, h4p], [wide1, g1p, g1m, g2p, g2m]


Y_FROM = (0, -1, 1, -2)
Z_FROM = (0, -1, 1, -2, 2, -3, 3, -4)


def place():
    panel = lax.axis_index("panel")
    return panel // NZ, panel % NZ


def row_of(y, z):
    return pl.multiple_of((lax.rem(y + NY, NY) * NZ + lax.rem(z + NZ, NZ)) * 32, 32)


def wide_dot(left, factor, out):
    rows = left.shape[0]

    @pl.loop(0, M // TILE)
    def _(tile):
        cols = pl.ds(pl.multiple_of(tile * TILE, TILE), TILE)
        out[pl.ds(0, rows), cols] = jnp.dot(
            left[...], factor[:, cols], preferred_element_type=jnp.float32
        )


def chain_kernel(where, rows, *refs):
    parts, (out, first, second, left, prod, sums, sem) = refs[:8], refs[8:]
    y, z = where[1], where[2]

    @pl.when(where[0] == 0)
    def _():
        copies = []
        for part, z_from in zip(parts, Z_FROM):
            for k, y_from in enumerate(Y_FROM):
                at = row_of(y + y_from, z + z_from)
                for which, full in enumerate((first, second)):
                    copies.append(
                        pltpu.make_async_copy(
                            part.at[pl.ds(k * 64 + which * 32, 32)], full.at[pl.ds(at, 32)], sem
                        )
                    )
        for copy in copies:
            copy.start()
        for copy in copies:
            copy.wait()
        half = jnp.bfloat16
        down, up = rows[0], rows[1]
        left[pl.ds(0, 32)] = down.astype(half)
        left[pl.ds(32, 32)] = up.astype(half)
        wide_dot(left, second, prod)
        reach = prod[pl.ds(0, 32)]
        left[pl.ds(0, 32)] = reach.astype(half)
        sums[0] = reach
        sums[1] = up
        sums[2] = down
        sums[3] = jnp.zeros((32, M), jnp.float32)

        @pl.loop(0, 4)
        def _(n):
            wide_dot(left, first, prod)
            sums[2] += prod[pl.ds(0, 32)]
            sums[3] += prod[pl.ds(32, 32)]
            left[...] = prod[...].astype(half)
            wide_dot(left, second, prod)
            sums[0] += prod[pl.ds(0, 32)]

            @pl.when(n < 3)
            def _():
                sums[1] += prod[pl.ds(32, 32)]

            left[...] = prod[...].astype(half)

        out[...] = sums[...].astype(half)


def chain(where, rows, parts):
    any_spec = pl.BlockSpec(memory_space=pl.ANY)
    vmem = pl.BlockSpec(memory_space=pltpu.VMEM)
    return pl.pallas_call(
        chain_kernel,
        out_shape=jax.ShapeDtypeStruct((4, 32, M), jnp.bfloat16),
        in_specs=[pl.BlockSpec(memory_space=pltpu.SMEM), vmem] + [any_spec] * 8,
        out_specs=vmem,
        scratch_shapes=[
            pltpu.VMEM((M, M), jnp.bfloat16),
            pltpu.VMEM((M, M), jnp.bfloat16),
            pltpu.VMEM((64, M), jnp.bfloat16),
            pltpu.VMEM((64, M), jnp.float32),
            pltpu.VMEM((4, 32, M), jnp.float32),
            pltpu.SemaphoreType.DMA,
        ],
        compiler_params=pltpu.CompilerParams(vmem_limit_bytes=24 << 20),
        name="chain",
    )(where, rows, *parts)


def finish_kernel(where, lefts, adds, *refs):
    wide, g1p, g1m, g2p, g2m, out, first, second, prod, sem = refs
    y, z = where[1], where[2]

    @pl.when(where[0] == 1)
    def _():
        copies = []
        for k, z_from in enumerate(Z_FROM):
            far = (g2p, k) if k < 4 else (g2m, k - 4)
            for (part, slot), y_from in zip(((wide, k), (g1p, k), (g1m, k), far), Y_FROM):
                at = row_of(y + y_from, z + z_from)
                for which, full in enumerate((first, second)):
                    copies.append(
                        pltpu.make_async_copy(
                            part.at[pl.ds(slot * 64 + which * 32, 32)], full.at[pl.ds(at, 32)], sem
                        )
                    )
        for copy in copies:
            copy.start()
        for copy in copies:
            copy.wait()
        wide_dot(lefts.at[pl.ds(0, 64)], first, prod)
        out[3] = adds[1] + prod[pl.ds(0, 32)]
        out[1] = prod[pl.ds(32, 32)]
        wide_dot(lefts.at[pl.ds(64, 64)], second, prod)
        out[2] = prod[pl.ds(0, 32)]
        out[0] = adds[0] + prod[pl.ds(32, 32)]


def finish(where, lefts, adds, parts):
    any_spec = pl.BlockSpec(memory_space=pl.ANY)
    vmem = pl.BlockSpec(memory_space=pltpu.VMEM)
    return pl.pallas_call(
        finish_kernel,
        out_shape=jax.ShapeDtypeStruct((4, 32, M), jnp.float32),
        in_specs=[pl.BlockSpec(memory_space=pltpu.SMEM), vmem, vmem] + [any_spec] * 5,
        out_specs=vmem,
        scratch_shapes=[
            pltpu.VMEM((M, M), jnp.bfloat16),
            pltpu.VMEM((M, M), jnp.bfloat16),
            pltpu.VMEM((64, M), jnp.float32),
            pltpu.SemaphoreType.DMA,
        ],
        compiler_params=pltpu.CompilerParams(vmem_limit_bytes=24 << 20),
        name="finish",
    )(where, lefts, adds, *parts)


def star(where, core, block, rows, adds):
    parts0, parts1 = gather(block)
    sums = chain(where, rows, parts0)
    lefts = send(sums.reshape(128, M), lambda x, c, y, z: (x, 1, y, z) if c == 0 else None)
    return finish(where, lefts, adds, parts1)


def body(ranges, pattern):
    half = jnp.bfloat16
    slab = lax.axis_index("slab")
    panel = lax.axis_index("panel")
    core = slab % NC
    upper = (slab // NC) % 2 == 1
    where = jnp.stack([core, panel // NZ, panel % NZ]).astype(jnp.int32)
    mask_rows = lax.dynamic_slice_in_dim(pattern[0], panel * 32 // BLK, 1, axis=1)
    mask = jnp.repeat(mask_rows.astype(jnp.float32), BLK, axis=2)
    own = ranges[0] * mask

    other = send(
        jnp.stack([own[0], own[2]]), lambda x, c, y, z: (x, 1 - c, y, z)
    )
    is0 = core == 0
    block = jnp.concatenate(
        [jnp.where(is0, other[0], own[1]), jnp.where(is0, own[3], other[1])]
    ).astype(half)
    rows = jnp.stack([other[1], own[1]])
    adds = jnp.stack([other[0], own[3]])
    joint = star(where, core, block, rows, adds)

    to0 = jnp.where(upper, jnp.stack([joint[0], joint[2]]), jnp.stack([joint[3], joint[1]]))
    to0 = to0.astype(half)
    own0 = send(to0, lambda x, c, y, z: (x, 0, y, z) if c == 1 else None)
    far0 = send(to0, lambda x, c, y, z: (x ^ 1, 0, y, z) if c == 1 else None)
    own1 = jnp.where(upper, jnp.stack([joint[1], joint[3]]), jnp.stack([joint[2], joint[0]]))
    far1 = send(own1, lambda x, c, y, z: (x ^ 1, 1, y, z) if c == 1 else None)
    tail0, head0 = jnp.where(upper, own0, far0), jnp.where(upper, far0, own0)
    tail1, head1 = jnp.where(upper, own1, far1), jnp.where(upper, far1, own1)
    block = jnp.where(
        is0,
        jnp.concatenate([tail0[0], head0[0]]),
        jnp.concatenate([tail1[0], head1[0]]).astype(half),
    )
    rows = jnp.stack([tail0[1], head0[1]]).astype(jnp.float32)
    adds = jnp.stack([head1[1], tail1[1]])
    joint = star(where, core, block, rows, adds)
    shared = send(joint, lambda x, c, y, z: (x, 0, y, z) if c == 1 else None)
    return jnp.where(is0, shared, joint)[None]


def solution(mesh):
    return jax.shard_map(
        body,
        mesh=mesh,
        in_specs=(P("slab", None, "panel", None), P("slab", None, None, None)),
        out_specs=P("slab", None, "panel", None),
        check_vma=False,
    )
```

time: 983 us -> 197 us (0.20)
  waiting for transfers between devices: 905 us -> 90.8 us
  starting transfers between devices: 5.07 us -> 78.3 us
  matrix products: 48.9 us -> 0 us
  Pallas kernels: 0 us -> 17 us
  between operations: 13.7 us -> 0.83 us
    all_gather x12 -> x0, waiting for transfers between devices: 895 us -> none  [the longest x6 447 us: spread(): return lax.all_gather(to_half(values), 'panel', axis=0, tiled=True)]
    ppermute x2 -> x43, waiting for transfers between devices: 9.2 us -> 90.8 us  [send(): return lax.ppermute(block, AXES, route(move))]
    ppermute x2 -> x43, starting transfers between devices: 4.61 us -> 78.3 us  [send(): return lax.ppermute(block, AXES, route(move))]
    dot_general x25 -> x0, matrix products: 48.9 us -> none  [the longest x24 47.4 us: multiply(): return jnp.dot(to_half(left), right, preferred_element_type=jnp.float32)]
    pallas_call x0 -> x4, Pallas kernels: none -> 17 us  [the longest x2 15.9 us: finish(): pl.pallas_call(finish_kernel, out_shape=jax.ShapeDtypeStruct((4, 32, M),...]
  transfers between devices with their start and end apart: 14 -> 43, of which waited for: 14 -> 20; matrix products, arithmetic and copies ran while one was open for 3% -> 2% of each run, Pallas kernels for 0% -> 1%
where the time goes in v1:
time: 197 us; the launch traced here: 196 us
  waiting for transfers between devices  90.8 us (46%)
  starting transfers between devices  78.3 us (40%)
  Pallas kernels  17 us (9%)
  local copies, waits for them, and re-layouts  5.43 us (3%)
  other arithmetic  4.02 us (2%)
    ppermute x43, waiting for transfers between devices, send(): return lax.ppermute(block, AXES, route(move))  90.8 us
    ppermute x43, starting transfers between devices, send(): return lax.ppermute(block, AXES, route(move))  78.3 us
    pallas_call x2, Pallas kernels, finish(): pl.pallas_call(finish_kernel, out_shape=jax.ShapeDtypeStruct((4, 32, M),...  15.9 us
  transfers between devices with their start and end apart: 43, of which 20 were waited for; matrix products, arithmetic and copies ran while one was open for 2% of the time, Pallas kernels for 1%

profile of v1, /device:TPU:1, one launch (start us, length us, event | category | flops | bytes accessed | tf_op | source)
XLA Modules:
  0.0 196.4 jit_solution(10562053833323993968)
XLA Ops:
  2.8 3.3 %collective-permute-start = (f32[2,32,1024]{2,1,0:T(8,128)S(1)}, f32[2,32,1024]{2,1,0:T(8,128)S(1)}, u32[]{:S(2)}, u32[]{:S(2)}) collective-permute-start(f32[2,32,1024]{2,1,0:T(8,128)S(1)} %pad_maximum_fusion.1), channel_id=1, source_target_pairs={{0,32},{1,33},{2,34},{3,35},{4,36},{5,37},{6,38},{7,39},{8,40},{9,... | collective-permute-start | bytes 786440 | tf_op jit(solution)/shard_map/ppermute | solution.py:34
  7.3 3.9 %collective-permute-start.2 = (bf16[64,1024]{1,0:T(8,128)(2,1)S(1)}, bf16[64,1024]{1,0:T(8,128)(2,1)S(1)}, u32[]{:S(2)}, u32[]{:S(2)}) collective-permute-start(bf16[64,1024]{1,0:T(8,128)(2,1)S(1)} %pad_maximum_fusion.5), channel_id=1, source_target_pairs={{0,24},{1,25},{2,26},{3,27},{4,28},{5,29},{6,30},{7,31},{8,0},{9,1... | collective-permute-start | bytes 393224 | tf_op jit(solution)/shard_map/ppermute | solution.py:34
  11.3 5.0 %collective-permute-done.1 = bf16[64,1024]{1,0:T(8,128)(2,1)S(1)} collective-permute-done((bf16[64,1024]{1,0:T(8,128)(2,1)S(1)}, bf16[64,1024]{1,0:T(8,128)(2,1)S(1)}, u32[]{:S(2)}, u32[]{:S(2)}) %collective-permute-start.1) | collective-permute-done | bytes 131104 | tf_op jit(solution)/shard_map/ppermute | solution.py:34
  16.4 5.0 %collective-permute-done.3 = bf16[64,1024]{1,0:T(8,128)(2,1)S(1)} collective-permute-done((bf16[64,1024]{1,0:T(8,128)(2,1)S(1)}, bf16[64,1024]{1,0:T(8,128)(2,1)S(1)}, u32[]{:S(2)}, u32[]{:S(2)}) %collective-permute-start.3) | collective-permute-done | bytes 131104 | tf_op jit(solution)/shard_map/ppermute | solution.py:34
  24.0 3.4 %collective-permute-start.13 = (bf16[64,1024]{1,0:T(8,128)(2,1)S(1)}, bf16[64,1024]{1,0:T(8,128)(2,1)S(1)}, u32[]{:S(2)}, u32[]{:S(2)}) collective-permute-start(bf16[64,1024]{1,0:T(8,128)(2,1)S(1)} %collective-permute-done.3), channel_id=1, source_target_pairs={{32,33},{33,34},{34,35},{35,36},{36,37},{37,38},{38,39},{39,32},{4... | collective-permute-start | bytes 393224 | tf_op jit(solution)/shard_map/ppermute | solution.py:34
  28.1 3.1 %collective-permute-start.14 = (bf16[64,1024]{1,0:T(8,128)(2,1)S(1)}, bf16[64,1024]{1,0:T(8,128)(2,1)S(1)}, u32[]{:S(2)}, u32[]{:S(2)}) collective-permute-start(bf16[64,1024]{1,0:T(8,128)(2,1)S(1)} %collective-permute-done.12), channel_id=1, source_target_pairs={{32,39},{33,32},{34,33},{35,34},{36,35},{37,36},{38,37},{39,38},{4... | collective-permute-start | bytes 393224 | tf_op jit(solution)/shard_map/ppermute | solution.py:34
  32.1 2.7 %collective-permute-start.15 = (bf16[64,1024]{1,0:T(8,128)(2,1)S(1)}, bf16[64,1024]{1,0:T(8,128)(2,1)S(1)}, u32[]{:S(2)}, u32[]{:S(2)}) collective-permute-start(bf16[64,1024]{1,0:T(8,128)(2,1)S(1)} %collective-permute-done.13), channel_id=1, source_target_pairs={{32,33},{33,34},{34,35},{35,36},{36,37},{37,38},{38,39},{39,32},{4... | collective-permute-start | bytes 393224 | tf_op jit(solution)/shard_map/ppermute | solution.py:34
  36.4 2.6 %collective-permute-done.15 = bf16[64,1024]{1,0:T(8,128)(2,1)S(1)} collective-permute-done((bf16[64,1024]{1,0:T(8,128)(2,1)S(1)}, bf16[64,1024]{1,0:T(8,128)(2,1)S(1)}, u32[]{:S(2)}, u32[]{:S(2)}) %collective-permute-start.15) | collective-permute-done | bytes 131104 | tf_op jit(solution)/shard_map/ppermute | solution.py:34
  39.0 5.2 %collective-permute-start.17 = (bf16[512,1024]{1,0:T(8,128)(2,1)S(1)}, bf16[512,1024]{1,0:T(8,128)(2,1)S(1)}, u32[]{:S(2)}, u32[]{:S(2)}) collective-permute-start(bf16[512,1024]{1,0:T(8,128)(2,1)S(1)} %constant_dynamic-update-slice_fusion.5.refs_0_), channel_id=1, source_target_pairs={{32,56},{33,57},{34,58},{35,59},{36,60},{37,61},{38,62},{39,63},{4... | collective-permute-start | bytes 3145736 | tf_op jit(solution)/shard_map/ppermute | solution.py:34
  53.7 2.2 %collective-permute-done.17.refs_2_ = bf16[512,1024]{1,0:T(8,128)(2,1)S(1)} collective-permute-done((bf16[512,1024]{1,0:T(8,128)(2,1)S(1)}, bf16[512,1024]{1,0:T(8,128)(2,1)S(1)}, u32[]{:S(2)}, u32[]{:S(2)}) %collective-permute-start.17) | collective-permute-done | bytes 1048608 | tf_op jit(solution)/shard_map/ppermute | solution.py:34
  56.8 5.4 %collective-permute-start.19 = (bf16[256,1024]{1,0:T(8,128)(2,1)}, bf16[256,1024]{1,0:T(8,128)(2,1)}, u32[]{:S(2)}, u32[]{:S(2)}) collective-permute-start(bf16[256,1024]{1,0:T(8,128)(2,1)} %slice.105), channel_id=1, source_target_pairs={{32,56},{33,57},{34,58},{35,59},{36,60},{37,61},{38,62},{39,63},{4... | collective-permute-start | bytes 1572872 | tf_op jit(solution)/shard_map/ppermute | solution.py:34
  63.1 2.0 %collective-permute-start.18 = (bf16[256,1024]{1,0:T(8,128)(2,1)}, bf16[256,1024]{1,0:T(8,128)(2,1)}, u32[]{:S(2)}, u32[]{:S(2)}) collective-permute-start(bf16[256,1024]{1,0:T(8,128)(2,1)} %slice.104), channel_id=1, source_target_pairs={{32,40},{33,41},{34,42},{35,43},{36,44},{37,45},{38,46},{39,47},{4... | collective-permute-start | bytes 1572872 | tf_op jit(solution)/shard_map/ppermute | solution.py:34
  68.7 6.0 %collective-permute-done.18.refs_3_ = bf16[256,1024]{1,0:T(8,128)(2,1)} collective-permute-done((bf16[256,1024]{1,0:T(8,128)(2,1)}, bf16[256,1024]{1,0:T(8,128)(2,1)}, u32[]{:S(2)}, u32[]{:S(2)}) %collective-permute-start.18) | collective-permute-done | bytes 524320 | tf_op jit(solution)/shard_map/ppermute | solution.py:34
  74.7 15.6 %collective-permute-done.11.lefts = bf16[128,1024]{1,0:T(8,128)(2,1)} collective-permute-done((bf16[128,1024]{1,0:T(8,128)(2,1)S(1)}, bf16[128,1024]{1,0:T(8,128)(2,1)}, u32[]{:S(2)}, u32[]{:S(2)}) %collective-permute-start.11) | collective-permute-done | bytes 262176 | tf_op jit(solution)/shard_map/ppermute | solution.py:34
  90.3 7.8 %finish.2 = f32[4,32,1024]{2,1,0:T(8,128)S(1)} custom-call(s32[3]{0:T(128)S(1)} %pad_add_fusion.where, bf16[128,1024]{1,0:T(8,128)(2,1)} %collective-permute-done.11.lefts, f32[2,32,1024]{2,1,0:T(8,128)S(1)} %pad_maximum_fusion.3.adds, bf16[512,1024]{1,0:T(8,128)(2,1)S(1)} %constant_dynamic-update-slice_fusion.5.refs_0_, ...), custom_call_target="tpu_custom_call" | custom-call | tf_op jit(solution)/shard_map/finish/pallas_call | solution.py:199
  100.9 3.1 %collective-permute-start.22 = (f32[2,32,1024]{2,1,0:T(8,128)S(1)}, f32[2,32,1024]{2,1,0:T(8,128)S(1)}, u32[]{:S(2)}, u32[]{:S(2)}) collective-permute-start(f32[2,32,1024]{2,1,0:T(8,128)S(1)} %maximum_select_fusion.1), channel_id=1, source_target_pairs={{32,96},{33,97},{34,98},{35,99},{36,100},{37,101},{38,102},{39,103... | collective-permute-start | bytes 786440 | tf_op jit(solution)/shard_map/ppermute | solution.py:34
  104.1 4.2 %collective-permute-done.22 = f32[2,32,1024]{2,1,0:T(8,128)S(1)} collective-permute-done((f32[2,32,1024]{2,1,0:T(8,128)S(1)}, f32[2,32,1024]{2,1,0:T(8,128)S(1)}, u32[]{:S(2)}, u32[]{:S(2)}) %collective-permute-start.22) | collective-permute-done | bytes 262176 | tf_op jit(solution)/shard_map/ppermute | solution.py:34
  108.5 2.7 %collective-permute-start.24 = (bf16[64,1024]{1,0:T(8,128)(2,1)S(1)}, bf16[64,1024]{1,0:T(8,128)(2,1)S(1)}, u32[]{:S(2)}, u32[]{:S(2)}) collective-permute-start(bf16[64,1024]{1,0:T(8,128)(2,1)S(1)} %get-tuple-element.6), channel_id=1, source_target_pairs={{0,24},{1,25},{2,26},{3,27},{4,28},{5,29},{6,30},{7,31},{8,0},{9,1... | collective-permute-start | bytes 393224 | tf_op jit(solution)/shard_map/ppermute | solution.py:34
  111.2 2.4 %collective-permute-done.23 = bf16[64,1024]{1,0:T(8,128)(2,1)S(1)} collective-permute-done((bf16[64,1024]{1,0:T(8,128)(2,1)S(1)}, bf16[64,1024]{1,0:T(8,128)(2,1)S(1)}, u32[]{:S(2)}, u32[]{:S(2)}) %collective-permute-start.23) | collective-permute-done | bytes 131104 | tf_op jit(solution)/shard_map/ppermute | solution.py:34
  113.6 5.0 %collective-permute-done.25 = bf16[64,1024]{1,0:T(8,128)(2,1)S(1)} collective-permute-done((bf16[64,1024]{1,0:T(8,128)(2,1)S(1)}, bf16[64,1024]{1,0:T(8,128)(2,1)S(1)}, u32[]{:S(2)}, u32[]{:S(2)}) %collective-permute-start.25) | collective-permute-done | bytes 131104 | tf_op jit(solution)/shard_map/ppermute | solution.py:34
  122.0 3.4 %collective-permute-start.35 = (bf16[64,1024]{1,0:T(8,128)(2,1)S(1)}, bf16[64,1024]{1,0:T(8,128)(2,1)S(1)}, u32[]{:S(2)}, u32[]{:S(2)}) collective-permute-start(bf16[64,1024]{1,0:T(8,128)(2,1)S(1)} %collective-permute-done.25), channel_id=1, source_target_pairs={{32,33},{33,34},{34,35},{35,36},{36,37},{37,38},{38,39},{39,32},{4... | collective-permute-start | bytes 393224 | tf_op jit(solution)/shard_map/ppermute | solution.py:34
  126.5 2.0 %collective-permute-start.36 = (bf16[64,1024]{1,0:T(8,128)(2,1)S(1)}, bf16[64,1024]{1,0:T(8,128)(2,1)S(1)}, u32[]{:S(2)}, u32[]{:S(2)}) collective-permute-start(bf16[64,1024]{1,0:T(8,128)(2,1)S(1)} %collective-permute-done.34), channel_id=1, source_target_pairs={{32,39},{33,32},{34,33},{35,34},{36,35},{37,36},{38,37},{39,38},{4... | collective-permute-start | bytes 393224 | tf_op jit(solution)/shard_map/ppermute | solution.py:34
  129.5 2.4 %collective-permute-start.37 = (bf16[64,1024]{1,0:T(8,128)(2,1)S(1)}, bf16[64,1024]{1,0:T(8,128)(2,1)S(1)}, u32[]{:S(2)}, u32[]{:S(2)}) collective-permute-start(bf16[64,1024]{1,0:T(8,128)(2,1)S(1)} %collective-permute-done.35), channel_id=1, source_target_pairs={{32,33},{33,34},{34,35},{35,36},{36,37},{37,38},{38,39},{39,32},{4... | collective-permute-start | bytes 393224 | tf_op jit(solution)/shard_map/ppermute | solution.py:34
  132.6 5.3 %collective-permute-done.37 = bf16[64,1024]{1,0:T(8,128)(2,1)S(1)} collective-permute-done((bf16[64,1024]{1,0:T(8,128)(2,1)S(1)}, bf16[64,1024]{1,0:T(8,128)(2,1)S(1)}, u32[]{:S(2)}, u32[]{:S(2)}) %collective-permute-start.37) | collective-permute-done | bytes 131104 | tf_op jit(solution)/shard_map/ppermute | solution.py:34
  139.8 3.4 %collective-permute-start.38 = (bf16[512,1024]{1,0:T(8,128)(2,1)S(1)}, bf16[512,1024]{1,0:T(8,128)(2,1)S(1)}, u32[]{:S(2)}, u32[]{:S(2)}) collective-permute-start(bf16[512,1024]{1,0:T(8,128)(2,1)S(1)} %constant_dynamic-update-slice_fusion.14.refs_0_), channel_id=1, source_target_pairs={{32,40},{33,41},{34,42},{35,43},{36,44},{37,45},{38,46},{39,47},{4... | collective-permute-start | bytes 3145736 | tf_op jit(solution)/shard_map/ppermute | solution.py:34
  146.0 7.7 %collective-permute-done.39.refs_2_ = bf16[512,1024]{1,0:T(8,128)(2,1)S(1)} collective-permute-done((bf16[512,1024]{1,0:T(8,128)(2,1)S(1)}, bf16[512,1024]{1,0:T(8,128)(2,1)S(1)}, u32[]{:S(2)}, u32[]{:S(2)}) %collective-permute-start.39) | collective-permute-done | bytes 1048608 | tf_op jit(solution)/shard_map/ppermute | solution.py:34
  153.7 2.8 %collective-permute-start.41 = (bf16[256,1024]{1,0:T(8,128)(2,1)S(1)}, bf16[256,1024]{1,0:T(8,128)(2,1)S(1)}, u32[]{:S(2)}, u32[]{:S(2)}) collective-permute-start(bf16[256,1024]{1,0:T(8,128)(2,1)S(1)} %slice.119), channel_id=1, source_target_pairs={{32,56},{33,57},{34,58},{35,59},{36,60},{37,61},{38,62},{39,63},{4... | collective-permute-start | bytes 1572872 | tf_op jit(solution)/shard_map/ppermute | solution.py:34
  156.6 2.4 %collective-permute-start.40 = (bf16[256,1024]{1,0:T(8,128)(2,1)S(1)}, bf16[256,1024]{1,0:T(8,128)(2,1)S(1)}, u32[]{:S(2)}, u32[]{:S(2)}) collective-permute-start(bf16[256,1024]{1,0:T(8,128)(2,1)S(1)} %slice.118), channel_id=1, source_target_pairs={{32,40},{33,41},{34,42},{35,43},{36,44},{37,45},{38,46},{39,47},{4... | collective-permute-start | bytes 1572872 | tf_op jit(solution)/shard_map/ppermute | solution.py:34
  161.1 2.9 %collective-permute-done.41.refs_4_ = bf16[256,1024]{1,0:T(8,128)(2,1)S(1)} collective-permute-done((bf16[256,1024]{1,0:T(8,128)(2,1)S(1)}, bf16[256,1024]{1,0:T(8,128)(2,1)S(1)}, u32[]{:S(2)}, u32[]{:S(2)}) %collective-permute-start.41) | collective-permute-done | bytes 524320 | tf_op jit(solution)/shard_map/ppermute | solution.py:34
  164.0 3.8 %collective-permute-done.40.refs_3_ = bf16[256,1024]{1,0:T(8,128)(2,1)S(1)} collective-permute-done((bf16[256,1024]{1,0:T(8,128)(2,1)S(1)}, bf16[256,1024]{1,0:T(8,128)(2,1)S(1)}, u32[]{:S(2)}, u32[]{:S(2)}) %collective-permute-start.40) | collective-permute-done | bytes 524320 | tf_op jit(solution)/shard_map/ppermute | solution.py:34
  167.8 16.9 %collective-permute-done.33.lefts = bf16[128,1024]{1,0:T(8,128)(2,1)S(1)} collective-permute-done((bf16[128,1024]{1,0:T(8,128)(2,1)S(1)}, bf16[128,1024]{1,0:T(8,128)(2,1)S(1)}, u32[]{:S(2)}, u32[]{:S(2)}) %collective-permute-start.33) | collective-permute-done | bytes 262176 | tf_op jit(solution)/shard_map/ppermute | solution.py:34
  184.7 8.0 %finish.3 = f32[4,32,1024]{2,1,0:T(8,128)S(1)} custom-call(s32[3]{0:T(128)S(1)} %pad_add_fusion.where, bf16[128,1024]{1,0:T(8,128)(2,1)S(1)} %collective-permute-done.33.lefts, f32[2,32,1024]{2,1,0:T(8,128)S(1)} %pad_maximum_fusion.4.adds, bf16[512,1024]{1,0:T(8,128)(2,1)S(1)} %constant_dynamic-update-slice_fusion.14.refs_0_, ...), custom_call_target="tpu_custom_call" | custom-call | tf_op jit(solution)/shard_map/finish/pallas_call | solution.py:199
  (123 shorter events, 43.8 us)
Async XLA Ops:
  7.3 9.0 %collective-permute-start.2 = (bf16[64,1024]{1,0:T(8,128)(2,1)S(1)}, bf16[64,1024]{1,0:T(8,128)(2,1)S(1)}, u32[]{:S(2)}, u32[]{:S(2)}) collective-permute-start(bf16[64,1024]{1,0:T(8,128)(2,1)S(1)} %pad_maximum_fusion.5), channel_id=1, source_target_pairs={{0,24},{1,25},{2,26},{3,27},{4,28},{5,29},{6,30},{7,31},{8,0},{9,1... | collective-permute-start | bytes 393224 | tf_op jit(solution)/shard_map/ppermute | solution.py:34
  21.4 13.5 %collective-permute-start.4 = (bf16[256,1024]{1,0:T(8,128)(2,1)S(1)}, bf16[256,1024]{1,0:T(8,128)(2,1)S(1)}, u32[]{:S(2)}, u32[]{:S(2)}) collective-permute-start(bf16[256,1024]{1,0:T(8,128)(2,1)S(1)} %get-tuple-element.30.refs_0_), channel_id=1, source_target_pairs={{0,1},{1,2},{2,3},{3,4},{4,5},{5,6},{6,7},{7,0},{8,9},{9,10},{10,1... | collective-permute-start | bytes 1572872 | tf_op jit(solution)/shard_map/ppermute | solution.py:34
  22.1 6.0 %collective-permute-start.12 = (bf16[64,1024]{1,0:T(8,128)(2,1)S(1)}, bf16[64,1024]{1,0:T(8,128)(2,1)S(1)}, u32[]{:S(2)}, u32[]{:S(2)}) collective-permute-start(bf16[64,1024]{1,0:T(8,128)(2,1)S(1)} %collective-permute-done.2), channel_id=1, source_target_pairs={{32,39},{33,32},{34,33},{35,34},{36,35},{37,36},{38,37},{39,38},{4... | collective-permute-start | bytes 393224 | tf_op jit(solution)/shard_map/ppermute | solution.py:34
  24.0 8.1 %collective-permute-start.13 = (bf16[64,1024]{1,0:T(8,128)(2,1)S(1)}, bf16[64,1024]{1,0:T(8,128)(2,1)S(1)}, u32[]{:S(2)}, u32[]{:S(2)}) collective-permute-start(bf16[64,1024]{1,0:T(8,128)(2,1)S(1)} %collective-permute-done.3), channel_id=1, source_target_pairs={{32,33},{33,34},{34,35},{35,36},{36,37},{37,38},{38,39},{39,32},{4... | collective-permute-start | bytes 393224 | tf_op jit(solution)/shard_map/ppermute | solution.py:34
  27.4 18.8 %collective-permute-start.5 = (bf16[256,1024]{1,0:T(8,128)(2,1)S(1)}, bf16[256,1024]{1,0:T(8,128)(2,1)S(1)}, u32[]{:S(2)}, u32[]{:S(2)}) collective-permute-start(bf16[256,1024]{1,0:T(8,128)(2,1)S(1)} %get-tuple-element.30.refs_0_), channel_id=1, source_target_pairs={{0,7},{1,0},{2,1},{3,2},{4,3},{5,4},{6,5},{7,6},{8,15},{9,8},{10,9... | collective-permute-start | bytes 1572872 | tf_op jit(solution)/shard_map/ppermute | solution.py:34
  28.1 8.3 %collective-permute-start.14 = (bf16[64,1024]{1,0:T(8,128)(2,1)S(1)}, bf16[64,1024]{1,0:T(8,128)(2,1)S(1)}, u32[]{:S(2)}, u32[]{:S(2)}) collective-permute-start(bf16[64,1024]{1,0:T(8,128)(2,1)S(1)} %collective-permute-done.12), channel_id=1, source_target_pairs={{32,39},{33,32},{34,33},{35,34},{36,35},{37,36},{38,37},{39,38},{4... | collective-permute-start | bytes 393224 | tf_op jit(solution)/shard_map/ppermute | solution.py:34
  32.1 6.9 %collective-permute-start.15 = (bf16[64,1024]{1,0:T(8,128)(2,1)S(1)}, bf16[64,1024]{1,0:T(8,128)(2,1)S(1)}, u32[]{:S(2)}, u32[]{:S(2)}) collective-permute-start(bf16[64,1024]{1,0:T(8,128)(2,1)S(1)} %collective-permute-done.13), channel_id=1, source_target_pairs={{32,33},{33,34},{34,35},{35,36},{36,37},{37,38},{38,39},{39,32},{4... | collective-permute-start | bytes 393224 | tf_op jit(solution)/shard_map/ppermute | solution.py:34
  34.8 13.6 %collective-permute-start.6 = (bf16[256,1024]{1,0:T(8,128)(2,1)S(1)}, bf16[256,1024]{1,0:T(8,128)(2,1)S(1)}, u32[]{:S(2)}, u32[]{:S(2)}) collective-permute-start(bf16[256,1024]{1,0:T(8,128)(2,1)S(1)} %collective-permute-done.4.refs_1_), channel_id=1, source_target_pairs={{0,1},{1,2},{2,3},{3,4},{4,5},{5,6},{6,7},{7,0},{8,9},{9,10},{10,1... | collective-permute-start | bytes 1572872 | tf_op jit(solution)/shard_map/ppermute | solution.py:34
  39.0 16.9 %collective-permute-start.17 = (bf16[512,1024]{1,0:T(8,128)(2,1)S(1)}, bf16[512,1024]{1,0:T(8,128)(2,1)S(1)}, u32[]{:S(2)}, u32[]{:S(2)}) collective-permute-start(bf16[512,1024]{1,0:T(8,128)(2,1)S(1)} %constant_dynamic-update-slice_fusion.5.refs_0_), channel_id=1, source_target_pairs={{32,56},{33,57},{34,58},{35,59},{36,60},{37,61},{38,62},{39,63},{4... | collective-permute-start | bytes 3145736 | tf_op jit(solution)/shard_map/ppermute | solution.py:34
  44.3 18.0 %collective-permute-start.16 = (bf16[512,1024]{1,0:T(8,128)(2,1)S(1)}, bf16[512,1024]{1,0:T(8,128)(2,1)S(1)}, u32[]{:S(2)}, u32[]{:S(2)}) collective-permute-start(bf16[512,1024]{1,0:T(8,128)(2,1)S(1)} %constant_dynamic-update-slice_fusion.5.refs_0_), channel_id=1, source_target_pairs={{32,40},{33,41},{34,42},{35,43},{36,44},{37,45},{38,46},{39,47},{4... | collective-permute-start | bytes 3145736 | tf_op jit(solution)/shard_map/ppermute | solution.py:34
  50.8 14.5 %collective-permute-start.9 = (bf16[256,1024]{1,0:T(8,128)(2,1)}, bf16[256,1024]{1,0:T(8,128)(2,1)}, u32[]{:S(2)}, u32[]{:S(2)}) collective-permute-start(bf16[256,1024]{1,0:T(8,128)(2,1)} %collective-permute-done.7.refs_4_), channel_id=1, source_target_pairs={{0,7},{1,0},{2,1},{3,2},{4,3},{5,4},{6,5},{7,6},{8,15},{9,8},{10,9... | collective-permute-start | bytes 1572872 | tf_op jit(solution)/shard_map/ppermute | solution.py:34
  52.2 13.0 %collective-permute-start.10 = (bf16[256,1024]{1,0:T(8,128)(2,1)}, bf16[256,1024]{1,0:T(8,128)(2,1)}, u32[]{:S(2)}, u32[]{:S(2)}) collective-permute-start(bf16[256,1024]{1,0:T(8,128)(2,1)} %collective-permute-done.8.refs_5_), channel_id=1, source_target_pairs={{0,1},{1,2},{2,3},{3,4},{4,5},{5,6},{6,7},{7,0},{8,9},{9,10},{10,1... | collective-permute-start | bytes 1572872 | tf_op jit(solution)/shard_map/ppermute | solution.py:34
  56.8 11.8 %collective-permute-start.19 = (bf16[256,1024]{1,0:T(8,128)(2,1)}, bf16[256,1024]{1,0:T(8,128)(2,1)}, u32[]{:S(2)}, u32[]{:S(2)}) collective-permute-start(bf16[256,1024]{1,0:T(8,128)(2,1)} %slice.105), channel_id=1, source_target_pairs={{32,56},{33,57},{34,58},{35,59},{36,60},{37,61},{38,62},{39,63},{4... | collective-permute-start | bytes 1572872 | tf_op jit(solution)/shard_map/ppermute | solution.py:34
  63.1 11.6 %collective-permute-start.18 = (bf16[256,1024]{1,0:T(8,128)(2,1)}, bf16[256,1024]{1,0:T(8,128)(2,1)}, u32[]{:S(2)}, u32[]{:S(2)}) collective-permute-start(bf16[256,1024]{1,0:T(8,128)(2,1)} %slice.104), channel_id=1, source_target_pairs={{32,40},{33,41},{34,42},{35,43},{36,44},{37,45},{38,46},{39,47},{4... | collective-permute-start | bytes 1572872 | tf_op jit(solution)/shard_map/ppermute | solution.py:34
  65.9 24.5 %collective-permute-start.11 = (bf16[128,1024]{1,0:T(8,128)(2,1)S(1)}, bf16[128,1024]{1,0:T(8,128)(2,1)}, u32[]{:S(2)}, u32[]{:S(2)}) collective-permute-start(bf16[128,1024]{1,0:T(8,128)(2,1)S(1)} %bitcast.24), channel_id=1, source_target_pairs={{0,32},{1,33},{2,34},{3,35},{4,36},{5,37},{6,38},{7,39},{8,40},{9,... | collective-permute-start | bytes 786440 | tf_op jit(solution)/shard_map/ppermute | solution.py:34
  98.3 5.8 %collective-permute-start.21 = (bf16[2,32,1024]{2,1,0:T(8,128)(2,1)S(1)}, bf16[2,32,1024]{2,1,0:T(8,128)(2,1)S(1)}, u32[]{:S(2)}, u32[]{:S(2)}) collective-permute-start(bf16[2,32,1024]{2,1,0:T(8,128)(2,1)S(1)} %fusion), channel_id=1, source_target_pairs={{32,64},{33,65},{34,66},{35,67},{36,68},{37,69},{38,70},{39,71},{4... | collective-permute-start | bytes 393224 | tf_op jit(solution)/shard_map/ppermute | solution.py:34
  100.9 7.4 %collective-permute-start.22 = (f32[2,32,1024]{2,1,0:T(8,128)S(1)}, f32[2,32,1024]{2,1,0:T(8,128)S(1)}, u32[]{:S(2)}, u32[]{:S(2)}) collective-permute-start(f32[2,32,1024]{2,1,0:T(8,128)S(1)} %maximum_select_fusion.1), channel_id=1, source_target_pairs={{32,96},{33,97},{34,98},{35,99},{36,100},{37,101},{38,102},{39,103... | collective-permute-start | bytes 786440 | tf_op jit(solution)/shard_map/ppermute | solution.py:34
  108.4 5.1 %collective-permute-start.23 = (bf16[64,1024]{1,0:T(8,128)(2,1)S(1)}, bf16[64,1024]{1,0:T(8,128)(2,1)S(1)}, u32[]{:S(2)}, u32[]{:S(2)}) collective-permute-start(bf16[64,1024]{1,0:T(8,128)(2,1)S(1)} %get-tuple-element.6), channel_id=1, source_target_pairs={{0,8},{1,9},{2,10},{3,11},{4,12},{5,13},{6,14},{7,15},{8,16},{9,17... | collective-permute-start | bytes 393224 | tf_op jit(solution)/shard_map/ppermute | solution.py:34
  118.6 13.2 %collective-permute-start.26 = (bf16[256,1024]{1,0:T(8,128)(2,1)S(1)}, bf16[256,1024]{1,0:T(8,128)(2,1)S(1)}, u32[]{:S(2)}, u32[]{:S(2)}) collective-permute-start(bf16[256,1024]{1,0:T(8,128)(2,1)S(1)} %pad_maximum_fusion.refs_0_), channel_id=1, source_target_pairs={{0,1},{1,2},{2,3},{3,4},{4,5},{5,6},{6,7},{7,0},{8,9},{9,10},{10,1... | collective-permute-start | bytes 1572872 | tf_op jit(solution)/shard_map/ppermute | solution.py:34
  119.3 7.2 %collective-permute-start.34 = (bf16[64,1024]{1,0:T(8,128)(2,1)S(1)}, bf16[64,1024]{1,0:T(8,128)(2,1)S(1)}, u32[]{:S(2)}, u32[]{:S(2)}) collective-permute-start(bf16[64,1024]{1,0:T(8,128)(2,1)S(1)} %collective-permute-done.24), channel_id=1, source_target_pairs={{32,39},{33,32},{34,33},{35,34},{36,35},{37,36},{38,37},{39,38},{4... | collective-permute-start | bytes 393224 | tf_op jit(solution)/shard_map/ppermute | solution.py:34
  121.3 21.9 %collective-permute-start.27 = (bf16[256,1024]{1,0:T(8,128)(2,1)S(1)}, bf16[256,1024]{1,0:T(8,128)(2,1)S(1)}, u32[]{:S(2)}, u32[]{:S(2)}) collective-permute-start(bf16[256,1024]{1,0:T(8,128)(2,1)S(1)} %pad_maximum_fusion.refs_0_), channel_id=1, source_target_pairs={{0,7},{1,0},{2,1},{3,2},{4,3},{5,4},{6,5},{7,6},{8,15},{9,8},{10,9... | collective-permute-start | bytes 1572872 | tf_op jit(solution)/shard_map/ppermute | solution.py:34
  122.0 7.5 %collective-permute-start.35 = (bf16[64,1024]{1,0:T(8,128)(2,1)S(1)}, bf16[64,1024]{1,0:T(8,128)(2,1)S(1)}, u32[]{:S(2)}, u32[]{:S(2)}) collective-permute-start(bf16[64,1024]{1,0:T(8,128)(2,1)S(1)} %collective-permute-done.25), channel_id=1, source_target_pairs={{32,33},{33,34},{34,35},{35,36},{36,37},{37,38},{38,39},{39,32},{4... | collective-permute-start | bytes 393224 | tf_op jit(solution)/shard_map/ppermute | solution.py:34
  126.5 6.1 %collective-permute-start.36 = (bf16[64,1024]{1,0:T(8,128)(2,1)S(1)}, bf16[64,1024]{1,0:T(8,128)(2,1)S(1)}, u32[]{:S(2)}, u32[]{:S(2)}) collective-permute-start(bf16[64,1024]{1,0:T(8,128)(2,1)S(1)} %collective-permute-done.34), channel_id=1, source_target_pairs={{32,39},{33,32},{34,33},{35,34},{36,35},{37,36},{38,37},{39,38},{4... | collective-permute-start | bytes 393224 | tf_op jit(solution)/shard_map/ppermute | solution.py:34
  129.5 8.4 %collective-permute-start.37 = (bf16[64,1024]{1,0:T(8,128)(2,1)S(1)}, bf16[64,1024]{1,0:T(8,128)(2,1)S(1)}, u32[]{:S(2)}, u32[]{:S(2)}) collective-permute-start(bf16[64,1024]{1,0:T(8,128)(2,1)S(1)} %collective-permute-done.35), channel_id=1, source_target_pairs={{32,33},{33,34},{34,35},{35,36},{36,37},{37,38},{38,39},{39,32},{4... | collective-permute-start | bytes 393224 | tf_op jit(solution)/shard_map/ppermute | solution.py:34
  131.8 12.0 %collective-permute-start.28 = (bf16[256,1024]{1,0:T(8,128)(2,1)S(1)}, bf16[256,1024]{1,0:T(8,128)(2,1)S(1)}, u32[]{:S(2)}, u32[]{:S(2)}) collective-permute-start(bf16[256,1024]{1,0:T(8,128)(2,1)S(1)} %collective-permute-done.26.refs_1_), channel_id=1, source_target_pairs={{0,1},{1,2},{2,3},{3,4},{4,5},{5,6},{6,7},{7,0},{8,9},{9,10},{10,1... | collective-permute-start | bytes 1572872 | tf_op jit(solution)/shard_map/ppermute | solution.py:34
  137.9 15.8 %collective-permute-start.39 = (bf16[512,1024]{1,0:T(8,128)(2,1)S(1)}, bf16[512,1024]{1,0:T(8,128)(2,1)S(1)}, u32[]{:S(2)}, u32[]{:S(2)}) collective-permute-start(bf16[512,1024]{1,0:T(8,128)(2,1)S(1)} %constant_dynamic-update-slice_fusion.14.refs_0_), channel_id=1, source_target_pairs={{32,56},{33,57},{34,58},{35,59},{36,60},{37,61},{38,62},{39,63},{4... | collective-permute-start | bytes 3145736 | tf_op jit(solution)/shard_map/ppermute | solution.py:34
  139.8 16.8 %collective-permute-start.38 = (bf16[512,1024]{1,0:T(8,128)(2,1)S(1)}, bf16[512,1024]{1,0:T(8,128)(2,1)S(1)}, u32[]{:S(2)}, u32[]{:S(2)}) collective-permute-start(bf16[512,1024]{1,0:T(8,128)(2,1)S(1)} %constant_dynamic-update-slice_fusion.14.refs_0_), channel_id=1, source_target_pairs={{32,40},{33,41},{34,42},{35,43},{36,44},{37,45},{38,46},{39,47},{4... | collective-permute-start | bytes 3145736 | tf_op jit(solution)/shard_map/ppermute | solution.py:34
  144.6 14.5 %collective-permute-start.31 = (bf16[256,1024]{1,0:T(8,128)(2,1)S(1)}, bf16[256,1024]{1,0:T(8,128)(2,1)S(1)}, u32[]{:S(2)}, u32[]{:S(2)}) collective-permute-start(bf16[256,1024]{1,0:T(8,128)(2,1)S(1)} %collective-permute-done.29.refs_4_), channel_id=1, source_target_pairs={{0,7},{1,0},{2,1},{3,2},{4,3},{5,4},{6,5},{7,6},{8,15},{9,8},{10,9... | collective-permute-start | bytes 1572872 | tf_op jit(solution)/shard_map/ppermute | solution.py:34
  145.3 13.8 %collective-permute-start.32 = (bf16[256,1024]{1,0:T(8,128)(2,1)S(1)}, bf16[256,1024]{1,0:T(8,128)(2,1)S(1)}, u32[]{:S(2)}, u32[]{:S(2)}) collective-permute-start(bf16[256,1024]{1,0:T(8,128)(2,1)S(1)} %collective-permute-done.30.refs_5_), channel_id=1, source_target_pairs={{0,1},{1,2},{2,3},{3,4},{4,5},{5,6},{6,7},{7,0},{8,9},{9,10},{10,1... | collective-permute-start | bytes 1572872 | tf_op jit(solution)/shard_map/ppermute | solution.py:34
  153.7 10.2 %collective-permute-start.41 = (bf16[256,1024]{1,0:T(8,128)(2,1)S(1)}, bf16[256,1024]{1,0:T(8,128)(2,1)S(1)}, u32[]{:S(2)}, u32[]{:S(2)}) collective-permute-start(bf16[256,1024]{1,0:T(8,128)(2,1)S(1)} %slice.119), channel_id=1, source_target_pairs={{32,56},{33,57},{34,58},{35,59},{36,60},{37,61},{38,62},{39,63},{4... | collective-permute-start | bytes 1572872 | tf_op jit(solution)/shard_map/ppermute | solution.py:34
  156.6 11.1 %collective-permute-start.40 = (bf16[256,1024]{1,0:T(8,128)(2,1)S(1)}, bf16[256,1024]{1,0:T(8,128)(2,1)S(1)}, u32[]{:S(2)}, u32[]{:S(2)}) collective-permute-start(bf16[256,1024]{1,0:T(8,128)(2,1)S(1)} %slice.118), channel_id=1, source_target_pairs={{32,40},{33,41},{34,42},{35,43},{36,44},{37,45},{38,46},{39,47},{4... | collective-permute-start | bytes 1572872 | tf_op jit(solution)/shard_map/ppermute | solution.py:34
  159.7 25.0 %collective-permute-start.33 = (bf16[128,1024]{1,0:T(8,128)(2,1)S(1)}, bf16[128,1024]{1,0:T(8,128)(2,1)S(1)}, u32[]{:S(2)}, u32[]{:S(2)}) collective-permute-start(bf16[128,1024]{1,0:T(8,128)(2,1)S(1)} %bitcast.25), channel_id=1, source_target_pairs={{0,32},{1,33},{2,34},{3,35},{4,36},{5,37},{6,38},{7,39},{8,40},{9,... | collective-permute-start | bytes 786440 | tf_op jit(solution)/shard_map/ppermute | solution.py:34
  (20 other events, 82.7 us)

commit v2 on v1

v2 whole, which is shorter than its diff:
```python
import jax
import jax.numpy as jnp
from jax import lax
from jax.experimental import pallas as pl
from jax.experimental.pallas import tpu as pltpu
from jax.sharding import PartitionSpec as P

M = 1024
BLK = 64
NX, NC, NY, NZ = 4, 2, 4, 8
AXES = ("slab", "panel")
TILE = 256
SPLIT = 384
PARTS = NZ + NY


def device(x, c, y, z):
    return ((x % NX) * NC + c) * NY * NZ + (y % NY) * NZ + z % NZ


def route(move):
    pairs = []
    for x in range(NX):
        for c in range(NC):
            for y in range(NY):
                for z in range(NZ):
                    target = move(x, c, y, z)
                    if target is not None:
                        pairs.append((device(x, c, y, z), device(*target)))
    return pairs


def send(block, move):
    return lax.ppermute(block, AXES, route(move))


def hop(axis, distance):
    def move(x, c, y, z):
        ahead = distance if c == 0 else -distance
        return (x, c, y + ahead, z) if axis == "y" else (x, c, y, z + ahead)

    return move


def gather(block):
    wide_a, wide_b = block[:, :SPLIT], block[:, SPLIT:]
    for y_distance, z_distance in ((2, 4), (1, 2)):
        more_a, more_b = lax.optimization_barrier(
            (send(wide_a, hop("y", y_distance)), send(wide_b, hop("z", z_distance)))
        )
        wide_a = jnp.concatenate([wide_a, more_a])
        wide_b = jnp.concatenate([wide_b, more_b])
    next_a, more_b = lax.optimization_barrier(
        (send(wide_a, hop("z", 1)), send(wide_b, hop("z", 1)))
    )
    wide_b = jnp.concatenate([wide_b, more_b])
    parts_a, parts_b = [wide_a, next_a], [wide_b]
    for _ in range(NZ - 2):
        parts_a.append(send(parts_a[-1], hop("z", 1)))
    for _ in range(NY - 1):
        parts_b.append(send(parts_b[-1], hop("y", 1)))
    return parts_a, parts_b


Y_BACK = (0, 2, 1, 3)
Z_BACK = (0, 4, 2, 6, 1, 5, 3, 7)


def row_of(y, z):
    return pl.multiple_of((lax.rem(y + 2 * NY, NY) * NZ + lax.rem(z + 2 * NZ, NZ)) * 32, 32)


def order(where, parts, first, second):
    parts_a, parts_b = parts[:NZ], parts[NZ:]
    way, y, z = 1 - 2 * where[0], where[1], where[2]
    for z_back, part in enumerate(parts_a):
        for k, y_back in enumerate(Y_BACK):
            at = pl.ds(row_of(y - way * y_back, z - way * z_back), 32)
            first[at, :SPLIT] = part[pl.ds(k * 64, 32)]
            second[at, :SPLIT] = part[pl.ds(k * 64 + 32, 32)]
    for y_back, part in enumerate(parts_b):
        for k, z_back in enumerate(Z_BACK):
            at = pl.ds(row_of(y - way * y_back, z - way * z_back), 32)
            first[at, SPLIT:] = part[pl.ds(k * 64, 32)]
            second[at, SPLIT:] = part[pl.ds(k * 64 + 32, 32)]


def wide_dot(left, factor, out):
    rows = left.shape[0]

    @pl.loop(0, M // TILE)
    def _(tile):
        cols = pl.ds(pl.multiple_of(tile * TILE, TILE), TILE)
        out[pl.ds(0, rows), cols] = jnp.dot(
            left[...], factor[:, cols], preferred_element_type=jnp.float32
        )


def chain_kernel(where, rows, *refs):
    parts, (out, first, second, left, prod, sums) = refs[:PARTS], refs[PARTS:]

    @pl.when(where[0] == 0)
    def _():
        order(where, parts, first, second)
        half = jnp.bfloat16
        down, up = rows[0], rows[1]
        left[pl.ds(0, 32)] = down.astype(half)
        left[pl.ds(32, 32)] = up.astype(half)
        wide_dot(left, second, prod)
        reach = prod[pl.ds(0, 32)]
        left[pl.ds(0, 32)] = reach.astype(half)
        sums[0] = reach
        sums[1] = up
        sums[2] = down
        sums[3] = jnp.zeros((32, M), jnp.float32)

        @pl.loop(0, 4)
        def _(n):
            wide_dot(left, first, prod)
            sums[2] += prod[pl.ds(0, 32)]
            sums[3] += prod[pl.ds(32, 32)]
            left[...] = prod[...].astype(half)
            wide_dot(left, second, prod)
            sums[0] += prod[pl.ds(0, 32)]

            @pl.when(n < 3)
            def _():
                sums[1] += prod[pl.ds(32, 32)]

            left[...] = prod[...].astype(half)

        out[...] = sums[...].astype(half)


def chain(where, rows, parts):
    vmem = pl.BlockSpec(memory_space=pltpu.VMEM)
    return pl.pallas_call(
        chain_kernel,
        out_shape=jax.ShapeDtypeStruct((4, 32, M), jnp.bfloat16),
        in_specs=[pl.BlockSpec(memory_space=pltpu.SMEM), vmem] + [vmem] * PARTS,
        out_specs=vmem,
        scratch_shapes=[
            pltpu.VMEM((M, M), jnp.bfloat16),
            pltpu.VMEM((M, M), jnp.bfloat16),
            pltpu.VMEM((64, M), jnp.bfloat16),
            pltpu.VMEM((64, M), jnp.float32),
            pltpu.VMEM((4, 32, M), jnp.float32),
        ],
        compiler_params=pltpu.CompilerParams(vmem_limit_bytes=24 << 20),
        name="chain",
    )(where, rows, *parts)


def order_kernel(where, *refs):
    parts, (first, second) = refs[:PARTS], refs[PARTS:]

    @pl.when(where[0] == 1)
    def _():
        order(where, parts, first, second)


def ordered(where, parts):
    vmem = pl.BlockSpec(memory_space=pltpu.VMEM)
    return pl.pallas_call(
        order_kernel,
        out_shape=[jax.ShapeDtypeStruct((M, M), jnp.bfloat16)] * 2,
        in_specs=[pl.BlockSpec(memory_space=pltpu.SMEM)] + [vmem] * PARTS,
        out_specs=[vmem, vmem],
        compiler_params=pltpu.CompilerParams(vmem_limit_bytes=24 << 20),
        name="order",
    )(where, *parts)


def finish_kernel(where, lefts, adds, first, second, out, prod):
    @pl.when(where[0] == 1)
    def _():
        wide_dot(lefts.at[pl.ds(0, 64)], first, prod)
        out[3] = adds[1] + prod[pl.ds(0, 32)]
        out[1] = prod[pl.ds(32, 32)]
        wide_dot(lefts.at[pl.ds(64, 64)], second, prod)
        out[2] = prod[pl.ds(0, 32)]
        out[0] = adds[0] + prod[pl.ds(32, 32)]


def finish(where, lefts, adds, first, second):
    vmem = pl.BlockSpec(memory_space=pltpu.VMEM)
    return pl.pallas_call(
        finish_kernel,
        out_shape=jax.ShapeDtypeStruct((4, 32, M), jnp.float32),
        in_specs=[pl.BlockSpec(memory_space=pltpu.SMEM)] + [vmem] * 4,
        out_specs=vmem,
        scratch_shapes=[pltpu.VMEM((64, M), jnp.float32)],
        compiler_params=pltpu.CompilerParams(vmem_limit_bytes=16 << 20),
        name="finish",
    )(where, lefts, adds, first, second)


def star(where, block, rows, adds):
    parts_a, parts_b = gather(block)
    parts = parts_a + parts_b
    sums = chain(where, rows, parts)
    lefts = send(sums.reshape(128, M), lambda x, c, y, z: (x, 1, y, z) if c == 0 else None)
    return finish(where, lefts, adds, *ordered(where, parts))


def body(ranges, pattern):
    half = jnp.bfloat16
    slab = lax.axis_index("slab")
    panel = lax.axis_index("panel")
    core = slab % NC
    upper = (slab // NC) % 2 == 1
    where = jnp.stack([core, panel // NZ, panel % NZ]).astype(jnp.int32)
    mask_rows = lax.dynamic_slice_in_dim(pattern[0], panel * 32 // BLK, 1, axis=1)
    mask = jnp.repeat(mask_rows.astype(jnp.float32), BLK, axis=2)
    own = ranges[0] * mask

    other = send(
        jnp.stack([own[0], own[2]]), lambda x, c, y, z: (x, 1 - c, y, z)
    )
    is0 = core == 0
    block = jnp.concatenate(
        [jnp.where(is0, other[0], own[1]), jnp.where(is0, own[3], other[1])]
    ).astype(half)
    rows = jnp.stack([other[1], own[1]])
    adds = jnp.stack([other[0], own[3]])
    joint = star(where, block, rows, adds)

    to0 = jnp.where(upper, jnp.stack([joint[0], joint[2]]), jnp.stack([joint[3], joint[1]]))
    to0 = to0.astype(half)
    own0 = send(to0, lambda x, c, y, z: (x, 0, y, z) if c == 1 else None)
    far0 = send(to0, lambda x, c, y, z: (x ^ 1, 0, y, z) if c == 1 else None)
    own1 = jnp.where(upper, jnp.stack([joint[1], joint[3]]), jnp.stack([joint[2], joint[0]]))
    far1 = send(own1.astype(half), lambda x, c, y, z: (x ^ 1, 1, y, z) if c == 1 else None)
    tail0, head0 = jnp.where(upper, own0, far0), jnp.where(upper, far0, own0)
    far1 = far1.astype(jnp.float32)
    tail1, head1 = jnp.where(upper, own1, far1), jnp.where(upper, far1, own1)
    block = jnp.where(
        is0,
        jnp.concatenate([tail0[0], head0[0]]),
        jnp.concatenate([tail1[0], head1[0]]).astype(half),
    )
    rows = jnp.stack([tail0[1], head0[1]]).astype(jnp.float32)
    adds = jnp.stack([head1[1], tail1[1]])
    joint = star(where, block, rows, adds)
    shared = send(joint, lambda x, c, y, z: (x, 0, y, z) if c == 1 else None)
    return jnp.where(is0, shared, joint)[None]


def solution(mesh):
    return jax.shard_map(
        body,
        mesh=mesh,
        in_specs=(P("slab", None, "panel", None), P("slab", None, None, None)),
        out_specs=P("slab", None, "panel", None),
        check_vma=False,
    )
```

time: 197 us -> 211 us (1.071)
  starting transfers between devices: 78.3 us -> 91.9 us
  waiting for transfers between devices: 90.8 us -> 98 us
  Pallas kernels: 17 us -> 10 us
    ppermute x43 -> x37, starting transfers between devices: 78.3 us -> 91.9 us  [send(): return lax.ppermute(block, AXES, route(move))]
    pallas_call x2, Pallas kernels: 15.9 us -> 5.08 us  [finish(): pl.pallas_call(finish_kernel, out_shape=jax.ShapeDtypeStruct((4, 32, M),...]
    ppermute x43 -> x37, waiting for transfers between devices: 90.8 us -> 98 us  [send(): return lax.ppermute(block, AXES, route(move))]
    pallas_call x0 -> x2, Pallas kernels: none -> 2.45 us  [ordered(): pl.pallas_call(order_kernel, out_shape=[jax.ShapeDtypeStruct((M, M), jnp....]
  transfers between devices with their start and end apart: 43 -> 37, of which waited for: 20 -> 27; matrix products, arithmetic and copies ran while one was open for 2% -> 1% of each run, Pallas kernels for 1% -> 1%
where the time goes in v2:
time: 211 us
  waiting for transfers between devices  98 us (46%)
  starting transfers between devices  91.9 us (44%)
  Pallas kernels  10 us (5%)
  local copies, waits for them, and re-layouts  5.52 us (3%)
  other arithmetic  5.13 us (2%)
    ppermute x37, waiting for transfers between devices, send(): return lax.ppermute(block, AXES, route(move))  98 us
    ppermute x37, starting transfers between devices, send(): return lax.ppermute(block, AXES, route(move))  91.9 us
    pallas_call x2, Pallas kernels, finish(): pl.pallas_call(finish_kernel, out_shape=jax.ShapeDtypeStruct((4, 32, M),...  5.08 us
  transfers between devices with their start and end apart: 37, of which 27 were waited for; matrix products, arithmetic and copies ran while one was open for 1% of the time, Pallas kernels for 1%

profile of v2, /device:TPU:1, one launch (start us, length us, event | category | flops | bytes accessed | tf_op | source)
XLA Modules:
  0.0 210.9 jit_solution(5662170899290139606)
XLA Ops:
  2.8 3.3 %collective-permute-start = (f32[2,32,1024]{2,1,0:T(8,128)S(1)}, f32[2,32,1024]{2,1,0:T(8,128)S(1)}, u32[]{:S(2)}, u32[]{:S(2)}) collective-permute-start(f32[2,32,1024]{2,1,0:T(8,128)S(1)} %pad_maximum_fusion.4), channel_id=1, source_target_pairs={{0,32},{1,33},{2,34},{3,35},{4,36},{5,37},{6,38},{7,39},{8,40},{9,... | collective-permute-start | bytes 786440 | tf_op jit(solution)/shard_map/ppermute | solution.py:34
  7.3 5.3 %collective-permute-start.2 = (bf16[64,640]{1,0:T(8,128)(2,1)S(1)}, bf16[64,640]{1,0:T(8,128)(2,1)S(1)}, u32[]{:S(2)}, u32[]{:S(2)}) collective-permute-start(bf16[64,640]{1,0:T(8,128)(2,1)S(1)} %pad_maximum_fusion.14), channel_id=1, source_target_pairs={{0,4},{1,5},{2,6},{3,7},{4,0},{5,1},{6,2},{7,3},{8,12},{9,13},{10,... | collective-permute-start | bytes 245768 | tf_op jit(solution)/shard_map/ppermute | solution.py:34
  12.6 2.9 %collective-permute-start.1 = (bf16[64,384]{1,0:T(8,128)(2,1)S(1)}, bf16[64,384]{1,0:T(8,128)(2,1)S(1)}, u32[]{:S(2)}, u32[]{:S(2)}) collective-permute-start(bf16[64,384]{1,0:T(8,128)(2,1)S(1)} %pad_maximum_fusion.15), channel_id=1, source_target_pairs={{0,16},{1,17},{2,18},{3,19},{4,20},{5,21},{6,22},{7,23},{8,24},{9,... | collective-permute-start | bytes 147464 | tf_op jit(solution)/shard_map/ppermute | solution.py:34
  19.3 2.8 %collective-permute-start.3 = (bf16[128,384]{1,0:T(8,128)(2,1)S(1)}, bf16[128,384]{1,0:T(8,128)(2,1)S(1)}, u32[]{:S(2)}, u32[]{:S(2)}) collective-permute-start(bf16[128,384]{1,0:T(8,128)(2,1)S(1)} %pad_maximum_fusion.12), channel_id=1, source_target_pairs={{0,8},{1,9},{2,10},{3,11},{4,12},{5,13},{6,14},{7,15},{8,16},{9,17... | collective-permute-start | bytes 294920 | tf_op jit(solution)/shard_map/ppermute | solution.py:34
  24.3 3.3 %collective-permute-start.6 = (bf16[256,640]{1,0:T(8,128)(2,1)S(1)}, bf16[256,640]{1,0:T(8,128)(2,1)S(1)}, u32[]{:S(2)}, u32[]{:S(2)}) collective-permute-start(bf16[256,640]{1,0:T(8,128)(2,1)S(1)} %pad_maximum_fusion.2), channel_id=1, source_target_pairs={{0,1},{1,2},{2,3},{3,4},{4,5},{5,6},{6,7},{7,0},{8,9},{9,10},{10,1... | collective-permute-start | bytes 983048 | tf_op jit(solution)/shard_map/ppermute | solution.py:34
  27.7 6.0 %collective-permute-done.5.refs_1_ = bf16[256,384]{1,0:T(8,128)(2,1)S(1)} collective-permute-done((bf16[256,384]{1,0:T(8,128)(2,1)S(1)}, bf16[256,384]{1,0:T(8,128)(2,1)S(1)}, u32[]{:S(2)}, u32[]{:S(2)}) %collective-permute-start.5) | collective-permute-done | bytes 196640 | tf_op jit(solution)/shard_map/ppermute | solution.py:34
  33.8 2.8 %collective-permute-start.13 = (bf16[512,640]{1,0:T(8,128)(2,1)S(1)}, bf16[512,640]{1,0:T(8,128)(2,1)S(1)}, u32[]{:S(2)}, u32[]{:S(2)}) collective-permute-start(bf16[512,640]{1,0:T(8,128)(2,1)S(1)} %pad_maximum_fusion.refs_8_), channel_id=1, source_target_pairs={{0,8},{1,9},{2,10},{3,11},{4,12},{5,13},{6,14},{7,15},{8,16},{9,17... | collective-permute-start | bytes 1966088 | tf_op jit(solution)/shard_map/ppermute | solution.py:34
  36.6 3.1 %collective-permute-start.7 = (bf16[256,384]{1,0:T(8,128)(2,1)S(1)}, bf16[256,384]{1,0:T(8,128)(2,1)S(1)}, u32[]{:S(2)}, u32[]{:S(2)}) collective-permute-start(bf16[256,384]{1,0:T(8,128)(2,1)S(1)} %collective-permute-done.5.refs_1_), channel_id=1, source_target_pairs={{0,1},{1,2},{2,3},{3,4},{4,5},{5,6},{6,7},{7,0},{8,9},{9,10},{10,1... | collective-permute-start | bytes 589832 | tf_op jit(solution)/shard_map/ppermute | solution.py:34
  39.7 4.4 %collective-permute-done.13.refs_9_ = bf16[512,640]{1,0:T(8,128)(2,1)S(1)} collective-permute-done((bf16[512,640]{1,0:T(8,128)(2,1)S(1)}, bf16[512,640]{1,0:T(8,128)(2,1)S(1)}, u32[]{:S(2)}, u32[]{:S(2)}) %collective-permute-start.13) | collective-permute-done | bytes 655392 | tf_op jit(solution)/shard_map/ppermute | solution.py:34
  44.1 3.4 %collective-permute-start.14 = (bf16[512,640]{1,0:T(8,128)(2,1)S(1)}, bf16[512,640]{1,0:T(8,128)(2,1)S(1)}, u32[]{:S(2)}, u32[]{:S(2)}) collective-permute-start(bf16[512,640]{1,0:T(8,128)(2,1)S(1)} %collective-permute-done.13.refs_9_), channel_id=1, source_target_pairs={{0,8},{1,9},{2,10},{3,11},{4,12},{5,13},{6,14},{7,15},{8,16},{9,17... | collective-permute-start | bytes 1966088 | tf_op jit(solution)/shard_map/ppermute | solution.py:34
  47.5 2.8 %collective-permute-start.8 = (bf16[256,384]{1,0:T(8,128)(2,1)S(1)}, bf16[256,384]{1,0:T(8,128)(2,1)S(1)}, u32[]{:S(2)}, u32[]{:S(2)}) collective-permute-start(bf16[256,384]{1,0:T(8,128)(2,1)S(1)} %collective-permute-done.7.refs_2_), channel_id=1, source_target_pairs={{0,1},{1,2},{2,3},{3,4},{4,5},{5,6},{6,7},{7,0},{8,9},{9,10},{10,1... | collective-permute-start | bytes 589832 | tf_op jit(solution)/shard_map/ppermute | solution.py:34
  50.3 2.6 %collective-permute-done.8.refs_3_ = bf16[256,384]{1,0:T(8,128)(2,1)S(1)} collective-permute-done((bf16[256,384]{1,0:T(8,128)(2,1)S(1)}, bf16[256,384]{1,0:T(8,128)(2,1)S(1)}, u32[]{:S(2)}, u32[]{:S(2)}) %collective-permute-start.8) | collective-permute-done | bytes 196640 | tf_op jit(solution)/shard_map/ppermute | solution.py:34
  53.0 3.4 %collective-permute-start.9 = (bf16[256,384]{1,0:T(8,128)(2,1)S(1)}, bf16[256,384]{1,0:T(8,128)(2,1)S(1)}, u32[]{:S(2)}, u32[]{:S(2)}) collective-permute-start(bf16[256,384]{1,0:T(8,128)(2,1)S(1)} %collective-permute-done.8.refs_3_), channel_id=1, source_target_pairs={{0,1},{1,2},{2,3},{3,4},{4,5},{5,6},{6,7},{7,0},{8,9},{9,10},{10,1... | collective-permute-start | bytes 589832 | tf_op jit(solution)/shard_map/ppermute | solution.py:34
  59.0 3.1 %collective-permute-start.10 = (bf16[256,384]{1,0:T(8,128)(2,1)S(1)}, bf16[256,384]{1,0:T(8,128)(2,1)}, u32[]{:S(2)}, u32[]{:S(2)}) collective-permute-start(bf16[256,384]{1,0:T(8,128)(2,1)S(1)} %collective-permute-done.9.refs_4_), channel_id=1, source_target_pairs={{0,1},{1,2},{2,3},{3,4},{4,5},{5,6},{6,7},{7,0},{8,9},{9,10},{10,1... | collective-permute-start | bytes 589832 | tf_op jit(solution)/shard_map/ppermute | solution.py:34
  64.7 3.2 %collective-permute-start.11 = (bf16[256,384]{1,0:T(8,128)(2,1)}, bf16[256,384]{1,0:T(8,128)(2,1)}, u32[]{:S(2)}, u32[]{:S(2)}) collective-permute-start(bf16[256,384]{1,0:T(8,128)(2,1)} %collective-permute-done.10.refs_5_), channel_id=1, source_target_pairs={{0,1},{1,2},{2,3},{3,4},{4,5},{5,6},{6,7},{7,0},{8,9},{9,10},{10,1... | collective-permute-start | bytes 589832 | tf_op jit(solution)/shard_map/ppermute | solution.py:34
  68.0 2.9 %collective-permute-done.11.refs_6_ = bf16[256,384]{1,0:T(8,128)(2,1)} collective-permute-done((bf16[256,384]{1,0:T(8,128)(2,1)}, bf16[256,384]{1,0:T(8,128)(2,1)}, u32[]{:S(2)}, u32[]{:S(2)}) %collective-permute-start.11) | collective-permute-done | bytes 196640 | tf_op jit(solution)/shard_map/ppermute | solution.py:34
  70.9 3.3 %collective-permute-start.12 = (bf16[256,384]{1,0:T(8,128)(2,1)}, bf16[256,384]{1,0:T(8,128)(2,1)S(1)}, u32[]{:S(2)}, u32[]{:S(2)}) collective-permute-start(bf16[256,384]{1,0:T(8,128)(2,1)} %collective-permute-done.11.refs_6_), channel_id=1, source_target_pairs={{0,1},{1,2},{2,3},{3,4},{4,5},{5,6},{6,7},{7,0},{8,9},{9,10},{10,1... | collective-permute-start | bytes 589832 | tf_op jit(solution)/shard_map/ppermute | solution.py:34
  85.6 14.3 %collective-permute-done.16.lefts = bf16[128,1024]{1,0:T(8,128)(2,1)} collective-permute-done((bf16[128,1024]{1,0:T(8,128)(2,1)}, bf16[128,1024]{1,0:T(8,128)(2,1)}, u32[]{:S(2)}, u32[]{:S(2)}) %collective-permute-start.16) | collective-permute-done | bytes 262176 | tf_op jit(solution)/shard_map/ppermute | solution.py:34
  99.9 2.7 %finish.2 = f32[4,32,1024]{2,1,0:T(8,128)S(1)} custom-call(s32[3]{0:T(128)S(1)} %pad_add_fusion.where, bf16[128,1024]{1,0:T(8,128)(2,1)} %collective-permute-done.16.lefts, f32[2,32,1024]{2,1,0:T(8,128)S(1)} %pad_maximum_fusion.6.adds, bf16[1024,1024]{1,0:T(8,128)(2,1)S(1)} %get-tuple-element.27.first, bf16[1024,1024]{1,0:T(8,128)(2,1)S(1)} %get-tuple-element.28.second), custom_call_target="tpu_custom_call" | custom-call | tf_op jit(solution)/shard_map/finish/pallas_call | solution.py:187
  102.7 3.1 %collective-permute-start.19 = (bf16[2,32,1024]{2,1,0:T(8,128)(2,1)S(1)}, bf16[2,32,1024]{2,1,0:T(8,128)(2,1)S(1)}, u32[]{:S(2)}, u32[]{:S(2)}) collective-permute-start(bf16[2,32,1024]{2,1,0:T(8,128)(2,1)S(1)} %get-tuple-element.41), channel_id=1, source_target_pairs={{32,96},{33,97},{34,98},{35,99},{36,100},{37,101},{38,102},{39,103... | collective-permute-start | bytes 393224 | tf_op jit(solution)/shard_map/ppermute | solution.py:34
  110.2 3.5 %collective-permute-start.21 = (bf16[64,640]{1,0:T(8,128)(2,1)S(1)}, bf16[64,640]{1,0:T(8,128)(2,1)S(1)}, u32[]{:S(2)}, u32[]{:S(2)}) collective-permute-start(bf16[64,640]{1,0:T(8,128)(2,1)S(1)} %slice.115), channel_id=1, source_target_pairs={{0,4},{1,5},{2,6},{3,7},{4,0},{5,1},{6,2},{7,3},{8,12},{9,13},{10,... | collective-permute-start | bytes 245768 | tf_op jit(solution)/shard_map/ppermute | solution.py:34
  113.7 2.6 %collective-permute-start.20 = (bf16[64,384]{1,0:T(8,128)(2,1)S(1)}, bf16[64,384]{1,0:T(8,128)(2,1)S(1)}, u32[]{:S(2)}, u32[]{:S(2)}) collective-permute-start(bf16[64,384]{1,0:T(8,128)(2,1)S(1)} %slice.114), channel_id=1, source_target_pairs={{0,16},{1,17},{2,18},{3,19},{4,20},{5,21},{6,22},{7,23},{8,24},{9,... | collective-permute-start | bytes 147464 | tf_op jit(solution)/shard_map/ppermute | solution.py:34
  127.0 4.7 %collective-permute-done.24.refs_1_ = bf16[256,384]{1,0:T(8,128)(2,1)S(1)} collective-permute-done((bf16[256,384]{1,0:T(8,128)(2,1)S(1)}, bf16[256,384]{1,0:T(8,128)(2,1)S(1)}, u32[]{:S(2)}, u32[]{:S(2)}) %collective-permute-start.24) | collective-permute-done | bytes 196640 | tf_op jit(solution)/shard_map/ppermute | solution.py:34
  134.2 7.5 %collective-permute-done.32.refs_9_ = bf16[512,640]{1,0:T(8,128)(2,1)S(1)} collective-permute-done((bf16[512,640]{1,0:T(8,128)(2,1)S(1)}, bf16[512,640]{1,0:T(8,128)(2,1)S(1)}, u32[]{:S(2)}, u32[]{:S(2)}) %collective-permute-start.32) | collective-permute-done | bytes 655392 | tf_op jit(solution)/shard_map/ppermute | solution.py:34
  141.7 3.1 %collective-permute-start.33 = (bf16[512,640]{1,0:T(8,128)(2,1)S(1)}, bf16[512,640]{1,0:T(8,128)(2,1)S(1)}, u32[]{:S(2)}, u32[]{:S(2)}) collective-permute-start(bf16[512,640]{1,0:T(8,128)(2,1)S(1)} %collective-permute-done.32.refs_9_), channel_id=1, source_target_pairs={{0,8},{1,9},{2,10},{3,11},{4,12},{5,13},{6,14},{7,15},{8,16},{9,17... | collective-permute-start | bytes 1966088 | tf_op jit(solution)/shard_map/ppermute | solution.py:34
  144.8 2.9 %collective-permute-start.26 = (bf16[256,384]{1,0:T(8,128)(2,1)S(1)}, bf16[256,384]{1,0:T(8,128)(2,1)S(1)}, u32[]{:S(2)}, u32[]{:S(2)}) collective-permute-start(bf16[256,384]{1,0:T(8,128)(2,1)S(1)} %collective-permute-done.24.refs_1_), channel_id=1, source_target_pairs={{0,1},{1,2},{2,3},{3,4},{4,5},{5,6},{6,7},{7,0},{8,9},{9,10},{10,1... | collective-permute-start | bytes 589832 | tf_op jit(solution)/shard_map/ppermute | solution.py:34
  150.3 3.1 %collective-permute-start.27 = (bf16[256,384]{1,0:T(8,128)(2,1)S(1)}, bf16[256,384]{1,0:T(8,128)(2,1)S(1)}, u32[]{:S(2)}, u32[]{:S(2)}) collective-permute-start(bf16[256,384]{1,0:T(8,128)(2,1)S(1)} %collective-permute-done.26.refs_2_), channel_id=1, source_target_pairs={{0,1},{1,2},{2,3},{3,4},{4,5},{5,6},{6,7},{7,0},{8,9},{9,10},{10,1... | collective-permute-start | bytes 589832 | tf_op jit(solution)/shard_map/ppermute | solution.py:34
  156.0 3.4 %collective-permute-start.28 = (bf16[256,384]{1,0:T(8,128)(2,1)S(1)}, bf16[256,384]{1,0:T(8,128)(2,1)S(1)}, u32[]{:S(2)}, u32[]{:S(2)}) collective-permute-start(bf16[256,384]{1,0:T(8,128)(2,1)S(1)} %collective-permute-done.27.refs_3_), channel_id=1, source_target_pairs={{0,1},{1,2},{2,3},{3,4},{4,5},{5,6},{6,7},{7,0},{8,9},{9,10},{10,1... | collective-permute-start | bytes 589832 | tf_op jit(solution)/shard_map/ppermute | solution.py:34
  162.1 3.1 %collective-permute-start.29 = (bf16[256,384]{1,0:T(8,128)(2,1)S(1)}, bf16[256,384]{1,0:T(8,128)(2,1)S(1)}, u32[]{:S(2)}, u32[]{:S(2)}) collective-permute-start(bf16[256,384]{1,0:T(8,128)(2,1)S(1)} %collective-permute-done.28.refs_4_), channel_id=1, source_target_pairs={{0,1},{1,2},{2,3},{3,4},{4,5},{5,6},{6,7},{7,0},{8,9},{9,10},{10,1... | collective-permute-start | bytes 589832 | tf_op jit(solution)/shard_map/ppermute | solution.py:34
  167.8 3.1 %collective-permute-start.30 = (bf16[256,384]{1,0:T(8,128)(2,1)S(1)}, bf16[256,384]{1,0:T(8,128)(2,1)S(1)}, u32[]{:S(2)}, u32[]{:S(2)}) collective-permute-start(bf16[256,384]{1,0:T(8,128)(2,1)S(1)} %collective-permute-done.29.refs_5_), channel_id=1, source_target_pairs={{0,1},{1,2},{2,3},{3,4},{4,5},{5,6},{6,7},{7,0},{8,9},{9,10},{10,1... | collective-permute-start | bytes 589832 | tf_op jit(solution)/shard_map/ppermute | solution.py:34
  173.5 3.4 %collective-permute-start.31 = (bf16[256,384]{1,0:T(8,128)(2,1)S(1)}, bf16[256,384]{1,0:T(8,128)(2,1)S(1)}, u32[]{:S(2)}, u32[]{:S(2)}) collective-permute-start(bf16[256,384]{1,0:T(8,128)(2,1)S(1)} %collective-permute-done.30.refs_6_), channel_id=1, source_target_pairs={{0,1},{1,2},{2,3},{3,4},{4,5},{5,6},{6,7},{7,0},{8,9},{9,10},{10,1... | collective-permute-start | bytes 589832 | tf_op jit(solution)/shard_map/ppermute | solution.py:34
  182.5 22.4 %collective-permute-done.35.lefts = bf16[128,1024]{1,0:T(8,128)(2,1)S(1)} collective-permute-done((bf16[128,1024]{1,0:T(8,128)(2,1)S(1)}, bf16[128,1024]{1,0:T(8,128)(2,1)S(1)}, u32[]{:S(2)}, u32[]{:S(2)}) %collective-permute-start.35) | collective-permute-done | bytes 262176 | tf_op jit(solution)/shard_map/ppermute | solution.py:34
  (97 shorter events, 68.9 us)
Async XLA Ops:
  2.8 4.5 %collective-permute-start = (f32[2,32,1024]{2,1,0:T(8,128)S(1)}, f32[2,32,1024]{2,1,0:T(8,128)S(1)}, u32[]{:S(2)}, u32[]{:S(2)}) collective-permute-start(f32[2,32,1024]{2,1,0:T(8,128)S(1)} %pad_maximum_fusion.4), channel_id=1, source_target_pairs={{0,32},{1,33},{2,34},{3,35},{4,36},{5,37},{6,38},{7,39},{8,40},{9,... | collective-permute-start | bytes 786440 | tf_op jit(solution)/shard_map/ppermute | solution.py:34
  7.3 9.7 %collective-permute-start.2 = (bf16[64,640]{1,0:T(8,128)(2,1)S(1)}, bf16[64,640]{1,0:T(8,128)(2,1)S(1)}, u32[]{:S(2)}, u32[]{:S(2)}) collective-permute-start(bf16[64,640]{1,0:T(8,128)(2,1)S(1)} %pad_maximum_fusion.14), channel_id=1, source_target_pairs={{0,4},{1,5},{2,6},{3,7},{4,0},{5,1},{6,2},{7,3},{8,12},{9,13},{10,... | collective-permute-start | bytes 245768 | tf_op jit(solution)/shard_map/ppermute | solution.py:34
  17.0 7.2 %collective-permute-start.4 = (bf16[128,640]{1,0:T(8,128)(2,1)S(1)}, bf16[128,640]{1,0:T(8,128)(2,1)S(1)}, u32[]{:S(2)}, u32[]{:S(2)}) collective-permute-start(bf16[128,640]{1,0:T(8,128)(2,1)S(1)} %pad_maximum_fusion.10), channel_id=1, source_target_pairs={{0,2},{1,3},{2,4},{3,5},{4,6},{5,7},{6,0},{7,1},{8,10},{9,11},{10,... | collective-permute-start | bytes 491528 | tf_op jit(solution)/shard_map/ppermute | solution.py:34
  19.3 4.5 %collective-permute-start.3 = (bf16[128,384]{1,0:T(8,128)(2,1)S(1)}, bf16[128,384]{1,0:T(8,128)(2,1)S(1)}, u32[]{:S(2)}, u32[]{:S(2)}) collective-permute-start(bf16[128,384]{1,0:T(8,128)(2,1)S(1)} %pad_maximum_fusion.12), channel_id=1, source_target_pairs={{0,8},{1,9},{2,10},{3,11},{4,12},{5,13},{6,14},{7,15},{8,16},{9,17... | collective-permute-start | bytes 294920 | tf_op jit(solution)/shard_map/ppermute | solution.py:34
  24.3 9.4 %collective-permute-start.6 = (bf16[256,640]{1,0:T(8,128)(2,1)S(1)}, bf16[256,640]{1,0:T(8,128)(2,1)S(1)}, u32[]{:S(2)}, u32[]{:S(2)}) collective-permute-start(bf16[256,640]{1,0:T(8,128)(2,1)S(1)} %pad_maximum_fusion.2), channel_id=1, source_target_pairs={{0,1},{1,2},{2,3},{3,4},{4,5},{5,6},{6,7},{7,0},{8,9},{9,10},{10,1... | collective-permute-start | bytes 983048 | tf_op jit(solution)/shard_map/ppermute | solution.py:34
  27.6 6.1 %collective-permute-start.5 = (bf16[256,384]{1,0:T(8,128)(2,1)S(1)}, bf16[256,384]{1,0:T(8,128)(2,1)S(1)}, u32[]{:S(2)}, u32[]{:S(2)}) collective-permute-start(bf16[256,384]{1,0:T(8,128)(2,1)S(1)} %pad_maximum_fusion.8.refs_0_), channel_id=1, source_target_pairs={{0,1},{1,2},{2,3},{3,4},{4,5},{5,6},{6,7},{7,0},{8,9},{9,10},{10,1... | collective-permute-start | bytes 589832 | tf_op jit(solution)/shard_map/ppermute | solution.py:34
  33.8 10.3 %collective-permute-start.13 = (bf16[512,640]{1,0:T(8,128)(2,1)S(1)}, bf16[512,640]{1,0:T(8,128)(2,1)S(1)}, u32[]{:S(2)}, u32[]{:S(2)}) collective-permute-start(bf16[512,640]{1,0:T(8,128)(2,1)S(1)} %pad_maximum_fusion.refs_8_), channel_id=1, source_target_pairs={{0,8},{1,9},{2,10},{3,11},{4,12},{5,13},{6,14},{7,15},{8,16},{9,17... | collective-permute-start | bytes 1966088 | tf_op jit(solution)/shard_map/ppermute | solution.py:34
  36.6 10.9 %collective-permute-start.7 = (bf16[256,384]{1,0:T(8,128)(2,1)S(1)}, bf16[256,384]{1,0:T(8,128)(2,1)S(1)}, u32[]{:S(2)}, u32[]{:S(2)}) collective-permute-start(bf16[256,384]{1,0:T(8,128)(2,1)S(1)} %collective-permute-done.5.refs_1_), channel_id=1, source_target_pairs={{0,1},{1,2},{2,3},{3,4},{4,5},{5,6},{6,7},{7,0},{8,9},{9,10},{10,1... | collective-permute-start | bytes 589832 | tf_op jit(solution)/shard_map/ppermute | solution.py:34
  44.1 18.7 %collective-permute-start.14 = (bf16[512,640]{1,0:T(8,128)(2,1)S(1)}, bf16[512,640]{1,0:T(8,128)(2,1)S(1)}, u32[]{:S(2)}, u32[]{:S(2)}) collective-permute-start(bf16[512,640]{1,0:T(8,128)(2,1)S(1)} %collective-permute-done.13.refs_9_), channel_id=1, source_target_pairs={{0,8},{1,9},{2,10},{3,11},{4,12},{5,13},{6,14},{7,15},{8,16},{9,17... | collective-permute-start | bytes 1966088 | tf_op jit(solution)/shard_map/ppermute | solution.py:34
  47.5 5.4 %collective-permute-start.8 = (bf16[256,384]{1,0:T(8,128)(2,1)S(1)}, bf16[256,384]{1,0:T(8,128)(2,1)S(1)}, u32[]{:S(2)}, u32[]{:S(2)}) collective-permute-start(bf16[256,384]{1,0:T(8,128)(2,1)S(1)} %collective-permute-done.7.refs_2_), channel_id=1, source_target_pairs={{0,1},{1,2},{2,3},{3,4},{4,5},{5,6},{6,7},{7,0},{8,9},{9,10},{10,1... | collective-permute-start | bytes 589832 | tf_op jit(solution)/shard_map/ppermute | solution.py:34
  53.0 6.0 %collective-permute-start.9 = (bf16[256,384]{1,0:T(8,128)(2,1)S(1)}, bf16[256,384]{1,0:T(8,128)(2,1)S(1)}, u32[]{:S(2)}, u32[]{:S(2)}) collective-permute-start(bf16[256,384]{1,0:T(8,128)(2,1)S(1)} %collective-permute-done.8.refs_3_), channel_id=1, source_target_pairs={{0,1},{1,2},{2,3},{3,4},{4,5},{5,6},{6,7},{7,0},{8,9},{9,10},{10,1... | collective-permute-start | bytes 589832 | tf_op jit(solution)/shard_map/ppermute | solution.py:34
  59.0 5.7 %collective-permute-start.10 = (bf16[256,384]{1,0:T(8,128)(2,1)S(1)}, bf16[256,384]{1,0:T(8,128)(2,1)}, u32[]{:S(2)}, u32[]{:S(2)}) collective-permute-start(bf16[256,384]{1,0:T(8,128)(2,1)S(1)} %collective-permute-done.9.refs_4_), channel_id=1, source_target_pairs={{0,1},{1,2},{2,3},{3,4},{4,5},{5,6},{6,7},{7,0},{8,9},{9,10},{10,1... | collective-permute-start | bytes 589832 | tf_op jit(solution)/shard_map/ppermute | solution.py:34
  62.8 14.3 %collective-permute-start.15 = (bf16[512,640]{1,0:T(8,128)(2,1)S(1)}, bf16[512,640]{1,0:T(8,128)(2,1)S(1)}, u32[]{:S(2)}, u32[]{:S(2)}) collective-permute-start(bf16[512,640]{1,0:T(8,128)(2,1)S(1)} %collective-permute-done.14.refs_10_), channel_id=1, source_target_pairs={{0,8},{1,9},{2,10},{3,11},{4,12},{5,13},{6,14},{7,15},{8,16},{9,17... | collective-permute-start | bytes 1966088 | tf_op jit(solution)/shard_map/ppermute | solution.py:34
  64.7 6.2 %collective-permute-start.11 = (bf16[256,384]{1,0:T(8,128)(2,1)}, bf16[256,384]{1,0:T(8,128)(2,1)}, u32[]{:S(2)}, u32[]{:S(2)}) collective-permute-start(bf16[256,384]{1,0:T(8,128)(2,1)} %collective-permute-done.10.refs_5_), channel_id=1, source_target_pairs={{0,1},{1,2},{2,3},{3,4},{4,5},{5,6},{6,7},{7,0},{8,9},{9,10},{10,1... | collective-permute-start | bytes 589832 | tf_op jit(solution)/shard_map/ppermute | solution.py:34
  70.9 6.2 %collective-permute-start.12 = (bf16[256,384]{1,0:T(8,128)(2,1)}, bf16[256,384]{1,0:T(8,128)(2,1)S(1)}, u32[]{:S(2)}, u32[]{:S(2)}) collective-permute-start(bf16[256,384]{1,0:T(8,128)(2,1)} %collective-permute-done.11.refs_6_), channel_id=1, source_target_pairs={{0,1},{1,2},{2,3},{3,4},{4,5},{5,6},{6,7},{7,0},{8,9},{9,10},{10,1... | collective-permute-start | bytes 589832 | tf_op jit(solution)/shard_map/ppermute | solution.py:34
  80.0 19.9 %collective-permute-start.16 = (bf16[128,1024]{1,0:T(8,128)(2,1)}, bf16[128,1024]{1,0:T(8,128)(2,1)}, u32[]{:S(2)}, u32[]{:S(2)}) collective-permute-start(bf16[128,1024]{1,0:T(8,128)(2,1)} %bitcast.7), channel_id=1, source_target_pairs={{0,32},{1,33},{2,34},{3,35},{4,36},{5,37},{6,38},{7,39},{8,40},{9,... | collective-permute-start | bytes 786440 | tf_op jit(solution)/shard_map/ppermute | solution.py:34
  102.7 6.4 %collective-permute-start.19 = (bf16[2,32,1024]{2,1,0:T(8,128)(2,1)S(1)}, bf16[2,32,1024]{2,1,0:T(8,128)(2,1)S(1)}, u32[]{:S(2)}, u32[]{:S(2)}) collective-permute-start(bf16[2,32,1024]{2,1,0:T(8,128)(2,1)S(1)} %get-tuple-element.41), channel_id=1, source_target_pairs={{32,96},{33,97},{34,98},{35,99},{36,100},{37,101},{38,102},{39,103... | collective-permute-start | bytes 393224 | tf_op jit(solution)/shard_map/ppermute | solution.py:34
  110.2 8.2 %collective-permute-start.21 = (bf16[64,640]{1,0:T(8,128)(2,1)S(1)}, bf16[64,640]{1,0:T(8,128)(2,1)S(1)}, u32[]{:S(2)}, u32[]{:S(2)}) collective-permute-start(bf16[64,640]{1,0:T(8,128)(2,1)S(1)} %slice.115), channel_id=1, source_target_pairs={{0,4},{1,5},{2,6},{3,7},{4,0},{5,1},{6,2},{7,3},{8,12},{9,13},{10,... | collective-permute-start | bytes 245768 | tf_op jit(solution)/shard_map/ppermute | solution.py:34
  113.7 4.7 %collective-permute-start.20 = (bf16[64,384]{1,0:T(8,128)(2,1)S(1)}, bf16[64,384]{1,0:T(8,128)(2,1)S(1)}, u32[]{:S(2)}, u32[]{:S(2)}) collective-permute-start(bf16[64,384]{1,0:T(8,128)(2,1)S(1)} %slice.114), channel_id=1, source_target_pairs={{0,16},{1,17},{2,18},{3,19},{4,20},{5,21},{6,22},{7,23},{8,24},{9,... | collective-permute-start | bytes 147464 | tf_op jit(solution)/shard_map/ppermute | solution.py:34
  118.5 5.1 %collective-permute-start.23 = (bf16[128,640]{1,0:T(8,128)(2,1)S(1)}, bf16[128,640]{1,0:T(8,128)(2,1)S(1)}, u32[]{:S(2)}, u32[]{:S(2)}) collective-permute-start(bf16[128,640]{1,0:T(8,128)(2,1)S(1)} %pad_maximum_fusion.11), channel_id=1, source_target_pairs={{0,2},{1,3},{2,4},{3,5},{4,6},{5,7},{6,0},{7,1},{8,10},{9,11},{10,... | collective-permute-start | bytes 491528 | tf_op jit(solution)/shard_map/ppermute | solution.py:34
  123.6 8.1 %collective-permute-start.25 = (bf16[256,640]{1,0:T(8,128)(2,1)S(1)}, bf16[256,640]{1,0:T(8,128)(2,1)S(1)}, u32[]{:S(2)}, u32[]{:S(2)}) collective-permute-start(bf16[256,640]{1,0:T(8,128)(2,1)S(1)} %pad_maximum_fusion.3), channel_id=1, source_target_pairs={{0,1},{1,2},{2,3},{3,4},{4,5},{5,6},{6,7},{7,0},{8,9},{9,10},{10,1... | collective-permute-start | bytes 983048 | tf_op jit(solution)/shard_map/ppermute | solution.py:34
  124.5 7.2 %collective-permute-start.24 = (bf16[256,384]{1,0:T(8,128)(2,1)S(1)}, bf16[256,384]{1,0:T(8,128)(2,1)S(1)}, u32[]{:S(2)}, u32[]{:S(2)}) collective-permute-start(bf16[256,384]{1,0:T(8,128)(2,1)S(1)} %pad_maximum_fusion.9.refs_0_), channel_id=1, source_target_pairs={{0,1},{1,2},{2,3},{3,4},{4,5},{5,6},{6,7},{7,0},{8,9},{9,10},{10,1... | collective-permute-start | bytes 589832 | tf_op jit(solution)/shard_map/ppermute | solution.py:34
  131.8 9.9 %collective-permute-start.32 = (bf16[512,640]{1,0:T(8,128)(2,1)S(1)}, bf16[512,640]{1,0:T(8,128)(2,1)S(1)}, u32[]{:S(2)}, u32[]{:S(2)}) collective-permute-start(bf16[512,640]{1,0:T(8,128)(2,1)S(1)} %pad_maximum_fusion.1.refs_8_), channel_id=1, source_target_pairs={{0,8},{1,9},{2,10},{3,11},{4,12},{5,13},{6,14},{7,15},{8,16},{9,17... | collective-permute-start | bytes 1966088 | tf_op jit(solution)/shard_map/ppermute | solution.py:34
  141.7 17.7 %collective-permute-start.33 = (bf16[512,640]{1,0:T(8,128)(2,1)S(1)}, bf16[512,640]{1,0:T(8,128)(2,1)S(1)}, u32[]{:S(2)}, u32[]{:S(2)}) collective-permute-start(bf16[512,640]{1,0:T(8,128)(2,1)S(1)} %collective-permute-done.32.refs_9_), channel_id=1, source_target_pairs={{0,8},{1,9},{2,10},{3,11},{4,12},{5,13},{6,14},{7,15},{8,16},{9,17... | collective-permute-start | bytes 1966088 | tf_op jit(solution)/shard_map/ppermute | solution.py:34
  144.8 5.5 %collective-permute-start.26 = (bf16[256,384]{1,0:T(8,128)(2,1)S(1)}, bf16[256,384]{1,0:T(8,128)(2,1)S(1)}, u32[]{:S(2)}, u32[]{:S(2)}) collective-permute-start(bf16[256,384]{1,0:T(8,128)(2,1)S(1)} %collective-permute-done.24.refs_1_), channel_id=1, source_target_pairs={{0,1},{1,2},{2,3},{3,4},{4,5},{5,6},{6,7},{7,0},{8,9},{9,10},{10,1... | collective-permute-start | bytes 589832 | tf_op jit(solution)/shard_map/ppermute | solution.py:34
  150.3 5.7 %collective-permute-start.27 = (bf16[256,384]{1,0:T(8,128)(2,1)S(1)}, bf16[256,384]{1,0:T(8,128)(2,1)S(1)}, u32[]{:S(2)}, u32[]{:S(2)}) collective-permute-start(bf16[256,384]{1,0:T(8,128)(2,1)S(1)} %collective-permute-done.26.refs_2_), channel_id=1, source_target_pairs={{0,1},{1,2},{2,3},{3,4},{4,5},{5,6},{6,7},{7,0},{8,9},{9,10},{10,1... | collective-permute-start | bytes 589832 | tf_op jit(solution)/shard_map/ppermute | solution.py:34
  156.0 6.0 %collective-permute-start.28 = (bf16[256,384]{1,0:T(8,128)(2,1)S(1)}, bf16[256,384]{1,0:T(8,128)(2,1)S(1)}, u32[]{:S(2)}, u32[]{:S(2)}) collective-permute-start(bf16[256,384]{1,0:T(8,128)(2,1)S(1)} %collective-permute-done.27.refs_3_), channel_id=1, source_target_pairs={{0,1},{1,2},{2,3},{3,4},{4,5},{5,6},{6,7},{7,0},{8,9},{9,10},{10,1... | collective-permute-start | bytes 589832 | tf_op jit(solution)/shard_map/ppermute | solution.py:34
  159.4 20.1 %collective-permute-start.34 = (bf16[512,640]{1,0:T(8,128)(2,1)S(1)}, bf16[512,640]{1,0:T(8,128)(2,1)S(1)}, u32[]{:S(2)}, u32[]{:S(2)}) collective-permute-start(bf16[512,640]{1,0:T(8,128)(2,1)S(1)} %collective-permute-done.33.refs_10_), channel_id=1, source_target_pairs={{0,8},{1,9},{2,10},{3,11},{4,12},{5,13},{6,14},{7,15},{8,16},{9,17... | collective-permute-start | bytes 1966088 | tf_op jit(solution)/shard_map/ppermute | solution.py:34
  162.1 5.7 %collective-permute-start.29 = (bf16[256,384]{1,0:T(8,128)(2,1)S(1)}, bf16[256,384]{1,0:T(8,128)(2,1)S(1)}, u32[]{:S(2)}, u32[]{:S(2)}) collective-permute-start(bf16[256,384]{1,0:T(8,128)(2,1)S(1)} %collective-permute-done.28.refs_4_), channel_id=1, source_target_pairs={{0,1},{1,2},{2,3},{3,4},{4,5},{5,6},{6,7},{7,0},{8,9},{9,10},{10,1... | collective-permute-start | bytes 589832 | tf_op jit(solution)/shard_map/ppermute | solution.py:34
  167.8 5.7 %collective-permute-start.30 = (bf16[256,384]{1,0:T(8,128)(2,1)S(1)}, bf16[256,384]{1,0:T(8,128)(2,1)S(1)}, u32[]{:S(2)}, u32[]{:S(2)}) collective-permute-start(bf16[256,384]{1,0:T(8,128)(2,1)S(1)} %collective-permute-done.29.refs_5_), channel_id=1, source_target_pairs={{0,1},{1,2},{2,3},{3,4},{4,5},{5,6},{6,7},{7,0},{8,9},{9,10},{10,1... | collective-permute-start | bytes 589832 | tf_op jit(solution)/shard_map/ppermute | solution.py:34
  173.5 6.0 %collective-permute-start.31 = (bf16[256,384]{1,0:T(8,128)(2,1)S(1)}, bf16[256,384]{1,0:T(8,128)(2,1)S(1)}, u32[]{:S(2)}, u32[]{:S(2)}) collective-permute-start(bf16[256,384]{1,0:T(8,128)(2,1)S(1)} %collective-permute-done.30.refs_6_), channel_id=1, source_target_pairs={{0,1},{1,2},{2,3},{3,4},{4,5},{5,6},{6,7},{7,0},{8,9},{9,10},{10,1... | collective-permute-start | bytes 589832 | tf_op jit(solution)/shard_map/ppermute | solution.py:34
  180.1 24.7 %collective-permute-start.35 = (bf16[128,1024]{1,0:T(8,128)(2,1)S(1)}, bf16[128,1024]{1,0:T(8,128)(2,1)S(1)}, u32[]{:S(2)}, u32[]{:S(2)}) collective-permute-start(bf16[128,1024]{1,0:T(8,128)(2,1)S(1)} %bitcast.22), channel_id=1, source_target_pairs={{0,32},{1,33},{2,34},{3,35},{4,36},{5,37},{6,38},{7,39},{8,40},{9,... | collective-permute-start | bytes 786440 | tf_op jit(solution)/shard_map/ppermute | solution.py:34
  (11 other events, 50.4 us)

commit v3 on v2

--- a/solution.py
+++ b/solution.py
@@ -9,8 +9,7 @@
 BLK = 64
 NX, NC, NY, NZ = 4, 2, 4, 8
 AXES = ("slab", "panel")
-TILE = 256
-SPLIT = 384
+SPLIT = 640
 PARTS = NZ + NY
 
 
@@ -44,26 +43,27 @@
 
 def gather(block):
     wide_a, wide_b = block[:, :SPLIT], block[:, SPLIT:]
-    for y_distance, z_distance in ((2, 4), (1, 2)):
-        more_a, more_b = lax.optimization_barrier(
-            (send(wide_a, hop("y", y_distance)), send(wide_b, hop("z", z_distance)))
-        )
-        wide_a = jnp.concatenate([wide_a, more_a])
-        wide_b = jnp.concatenate([wide_b, more_b])
-    next_a, more_b = lax.optimization_barrier(
-        (send(wide_a, hop("z", 1)), send(wide_b, hop("z", 1)))
-    )
-    wide_b = jnp.concatenate([wide_b, more_b])
-    parts_a, parts_b = [wide_a, next_a], [wide_b]
-    for _ in range(NZ - 2):
-        parts_a.append(send(parts_a[-1], hop("z", 1)))
-    for _ in range(NY - 1):
-        parts_b.append(send(parts_b[-1], hop("y", 1)))
+    wide_a = jnp.concatenate([wide_a] + [send(wide_a, hop("y", d)) for d in Y_BACK[1:]])
+    wide_b = jnp.concatenate([wide_b, send(wide_b, hop("z", 4))])
+    ahead, behind = send(wide_b, hop("z", 1)), send(wide_b, hop("z", -1))
+    wide_b = jnp.concatenate([wide_b, ahead, behind, send(ahead, hop("z", 1))])
+    parts_a, parts_b = [wide_a], [wide_b]
+    ahead, behind = wide_a, wide_a
+    for back in Z_BACK_A[1:]:
+        if back > 0:
+            ahead = send(ahead, hop("z", 1))
+            parts_a.append(ahead)
+        else:
+            behind = send(behind, hop("z", -1))
+            parts_a.append(behind)
+    ahead, behind = send(wide_b, hop("y", 1)), send(wide_b, hop("y", -1))
+    parts_b += [ahead, behind, send(ahead, hop("y", 1))]
     return parts_a, parts_b
 
 
-Y_BACK = (0, 2, 1, 3)
-Z_BACK = (0, 4, 2, 6, 1, 5, 3, 7)
+Y_BACK = (0, 1, -1, 2)
+Z_BACK_A = (0, 1, -1, 2, -2, 3, -3, 4)
+Z_BACK_B = (0, 4, 1, 5, -1, 3, 2, 6)
 
 
 def row_of(y, z):
@@ -73,27 +73,22 @@
 def order(where, parts, first, second):
     parts_a, parts_b = parts[:NZ], parts[NZ:]
     way, y, z = 1 - 2 * where[0], where[1], where[2]
-    for z_back, part in enumerate(parts_a):
+    for z_back, part in zip(Z_BACK_A, parts_a):
         for k, y_back in enumerate(Y_BACK):
             at = pl.ds(row_of(y - way * y_back, z - way * z_back), 32)
             first[at, :SPLIT] = part[pl.ds(k * 64, 32)]
             second[at, :SPLIT] = part[pl.ds(k * 64 + 32, 32)]
-    for y_back, part in enumerate(parts_b):
-        for k, z_back in enumerate(Z_BACK):
+    for y_back, part in zip(Y_BACK, parts_b):
+        for k, z_back in enumerate(Z_BACK_B):
             at = pl.ds(row_of(y - way * y_back, z - way * z_back), 32)
             first[at, SPLIT:] = part[pl.ds(k * 64, 32)]
             second[at, SPLIT:] = part[pl.ds(k * 64 + 32, 32)]
 
 
 def wide_dot(left, factor, out):
-    rows = left.shape[0]
-
-    @pl.loop(0, M // TILE)
-    def _(tile):
-        cols = pl.ds(pl.multiple_of(tile * TILE, TILE), TILE)
-        out[pl.ds(0, rows), cols] = jnp.dot(
-            left[...], factor[:, cols], preferred_element_type=jnp.float32
-        )
+    out[pl.ds(0, left.shape[0])] = jnp.dot(
+        left[...], factor[...], preferred_element_type=jnp.float32
+    )
 
 
 def chain_kernel(where, rows, *refs):

time: 211 us -> 149 us (0.71)
  waiting for transfers between devices: 98 us -> 67.5 us
  starting transfers between devices: 91.9 us -> 63.5 us
  Pallas kernels: 10 us -> 6.92 us
    ppermute x37 -> x41, waiting for transfers between devices: 98 us -> 67.5 us  [send(): return lax.ppermute(block, AXES, route(move))]
    ppermute x37 -> x41, starting transfers between devices: 91.9 us -> 63.5 us  [send(): return lax.ppermute(block, AXES, route(move))]
  transfers between devices with their start and end apart: 37 -> 41, of which waited for: 27 -> 23; matrix products, arithmetic and copies ran while one was open for 1% -> 3% of each run, Pallas kernels for 1% -> 1%
where the time goes in v3:
time: 149 us; the launch traced here: 148 us
  waiting for transfers between devices  67.5 us (45%)
  starting transfers between devices  63.5 us (43%)
  Pallas kernels  6.92 us (5%)
  other arithmetic  5.01 us (3%)
  local copies, waits for them, and re-layouts  4.75 us (3%)
    ppermute x41, waiting for transfers between devices, send(): return lax.ppermute(block, AXES, route(move))  67.5 us
    ppermute x41, starting transfers between devices, send(): return lax.ppermute(block, AXES, route(move))  63.5 us
    pallas_call x2, Pallas kernels, finish(): pl.pallas_call(finish_kernel, out_shape=jax.ShapeDtypeStruct((4, 32, M),...  3.19 us
  transfers between devices with their start and end apart: 41, of which 23 were waited for; matrix products, arithmetic and copies ran while one was open for 3% of the time, Pallas kernels for 1%

profile of v3, /device:TPU:1, one launch (start us, length us, event | category | flops | bytes accessed | tf_op | source)
XLA Modules:
  0.0 148.1 jit_solution(15187637893562268499)
XLA Ops:
  2.7 3.3 %collective-permute-start = (f32[2,32,1024]{2,1,0:T(8,128)S(1)}, f32[2,32,1024]{2,1,0:T(8,128)S(1)}, u32[]{:S(2)}, u32[]{:S(2)}) collective-permute-start(f32[2,32,1024]{2,1,0:T(8,128)S(1)} %pad_maximum_fusion.2), channel_id=1, source_target_pairs={{0,32},{1,33},{2,34},{3,35},{4,36},{5,37},{6,38},{7,39},{8,40},{9,... | collective-permute-start | bytes 786440 | tf_op jit(solution)/shard_map/ppermute | solution.py:33
  9.0 2.3 %collective-permute-start.1 = (bf16[64,640]{1,0:T(8,128)(2,1)S(1)}, bf16[64,640]{1,0:T(8,128)(2,1)S(1)}, u32[]{:S(2)}, u32[]{:S(2)}) collective-permute-start(bf16[64,640]{1,0:T(8,128)(2,1)S(1)} %fusion.1), channel_id=1, source_target_pairs={{0,8},{1,9},{2,10},{3,11},{4,12},{5,13},{6,14},{7,15},{8,16},{9,17... | collective-permute-start | bytes 245768 | tf_op jit(solution)/shard_map/ppermute | solution.py:33
  11.2 7.0 %collective-permute-start.11 = (bf16[64,384]{1,0:T(8,128)(2,1)S(1)}, bf16[64,384]{1,0:T(8,128)(2,1)S(1)}, u32[]{:S(2)}, u32[]{:S(2)}) collective-permute-start(bf16[64,384]{1,0:T(8,128)(2,1)S(1)} %get-tuple-element.14), channel_id=1, source_target_pairs={{0,4},{1,5},{2,6},{3,7},{4,0},{5,1},{6,2},{7,3},{8,12},{9,13},{10,... | collective-permute-start | bytes 147464 | tf_op jit(solution)/shard_map/ppermute | solution.py:33
  21.2 3.2 %collective-permute-start.12 = (bf16[128,384]{1,0:T(8,128)(2,1)S(1)}, bf16[128,384]{1,0:T(8,128)(2,1)S(1)}, u32[]{:S(2)}, u32[]{:S(2)}) collective-permute-start(bf16[128,384]{1,0:T(8,128)(2,1)S(1)} %pad_maximum_fusion.6), channel_id=1, source_target_pairs={{0,1},{1,2},{2,3},{3,4},{4,5},{5,6},{6,7},{7,0},{8,9},{9,10},{10,1... | collective-permute-start | bytes 294920 | tf_op jit(solution)/shard_map/ppermute | solution.py:33
  24.5 3.2 %collective-permute-done.12 = bf16[128,384]{1,0:T(8,128)(2,1)S(1)} collective-permute-done((bf16[128,384]{1,0:T(8,128)(2,1)S(1)}, bf16[128,384]{1,0:T(8,128)(2,1)S(1)}, u32[]{:S(2)}, u32[]{:S(2)}) %collective-permute-start.12) | collective-permute-done | bytes 98336 | tf_op jit(solution)/shard_map/ppermute | solution.py:33
  29.6 2.9 %collective-permute-done.14 = bf16[128,384]{1,0:T(8,128)(2,1)S(1)} collective-permute-done((bf16[128,384]{1,0:T(8,128)(2,1)S(1)}, bf16[128,384]{1,0:T(8,128)(2,1)S(1)}, u32[]{:S(2)}, u32[]{:S(2)}) %collective-permute-start.14) | collective-permute-done | bytes 98336 | tf_op jit(solution)/shard_map/ppermute | solution.py:33
  33.1 4.5 %collective-permute-done.6.refs_3_ = bf16[256,640]{1,0:T(8,128)(2,1)S(1)} collective-permute-done((bf16[256,640]{1,0:T(8,128)(2,1)S(1)}, bf16[256,640]{1,0:T(8,128)(2,1)S(1)}, u32[]{:S(2)}, u32[]{:S(2)}) %collective-permute-start.6) | collective-permute-done | bytes 327712 | tf_op jit(solution)/shard_map/ppermute | solution.py:33
  37.6 3.1 %collective-permute-start.8 = (bf16[256,640]{1,0:T(8,128)(2,1)S(1)}, bf16[256,640]{1,0:T(8,128)(2,1)S(1)}, u32[]{:S(2)}, u32[]{:S(2)}) collective-permute-start(bf16[256,640]{1,0:T(8,128)(2,1)S(1)} %collective-permute-done.6.refs_3_), channel_id=1, source_target_pairs={{0,1},{1,2},{2,3},{3,4},{4,5},{5,6},{6,7},{7,0},{8,9},{9,10},{10,1... | collective-permute-start | bytes 983048 | tf_op jit(solution)/shard_map/ppermute | solution.py:33
  41.0 2.5 %collective-permute-start.17 = (bf16[512,384]{1,0:T(8,128)(2,1)S(1)}, bf16[512,384]{1,0:T(8,128)(2,1)S(1)}, u32[]{:S(2)}, u32[]{:S(2)}) collective-permute-start(bf16[512,384]{1,0:T(8,128)(2,1)S(1)} %collective-permute-done.15.refs_9_), channel_id=1, source_target_pairs={{0,8},{1,9},{2,10},{3,11},{4,12},{5,13},{6,14},{7,15},{8,16},{9,17... | collective-permute-start | bytes 1179656 | tf_op jit(solution)/shard_map/ppermute | solution.py:33
  44.3 3.8 %collective-permute-done.8.refs_5_ = bf16[256,640]{1,0:T(8,128)(2,1)S(1)} collective-permute-done((bf16[256,640]{1,0:T(8,128)(2,1)S(1)}, bf16[256,640]{1,0:T(8,128)(2,1)S(1)}, u32[]{:S(2)}, u32[]{:S(2)}) %collective-permute-start.8) | collective-permute-done | bytes 327712 | tf_op jit(solution)/shard_map/ppermute | solution.py:33
  48.2 3.4 %collective-permute-start.10 = (bf16[256,640]{1,0:T(8,128)(2,1)S(1)}, bf16[256,640]{1,0:T(8,128)(2,1)S(1)}, u32[]{:S(2)}, u32[]{:S(2)}) collective-permute-start(bf16[256,640]{1,0:T(8,128)(2,1)S(1)} %collective-permute-done.8.refs_5_), channel_id=1, source_target_pairs={{0,1},{1,2},{2,3},{3,4},{4,5},{5,6},{6,7},{7,0},{8,9},{9,10},{10,1... | collective-permute-start | bytes 983048 | tf_op jit(solution)/shard_map/ppermute | solution.py:33
  51.6 1.7 %fusion.9 = (f32[1,32,1024]{2,1,0:T(8,128)}, f32[1,32,1024]{2,1,0:T(8,128)S(1)}) fusion(f32[2,32,1024]{2,1,0:T(8,128)} %copy-done.4), kind=kLoop, calls=%fused_computation.48 | loop fusion | bytes 524288 | tf_op jit(solution)/shard_map/slice | solution.py:217
  54.2 3.9 %collective-permute-done.10.refs_7_ = bf16[256,640]{1,0:T(8,128)(2,1)S(1)} collective-permute-done((bf16[256,640]{1,0:T(8,128)(2,1)S(1)}, bf16[256,640]{1,0:T(8,128)(2,1)S(1)}, u32[]{:S(2)}, u32[]{:S(2)}) %collective-permute-start.10) | collective-permute-done | bytes 327712 | tf_op jit(solution)/shard_map/ppermute | solution.py:33
  64.6 7.6 %collective-permute-done.18.lefts = bf16[128,1024]{1,0:T(8,128)(2,1)} collective-permute-done((bf16[128,1024]{1,0:T(8,128)(2,1)}, bf16[128,1024]{1,0:T(8,128)(2,1)}, u32[]{:S(2)}, u32[]{:S(2)}) %collective-permute-start.18) | collective-permute-done | bytes 262176 | tf_op jit(solution)/shard_map/ppermute | solution.py:33
  72.3 1.8 %finish.2 = f32[4,32,1024]{2,1,0:T(8,128)S(1)} custom-call(s32[3]{0:T(128)S(1)} %pad_add_fusion.where, bf16[128,1024]{1,0:T(8,128)(2,1)} %collective-permute-done.18.lefts, f32[2,32,1024]{2,1,0:T(8,128)S(1)} %pad_maximum_fusion.4.adds, bf16[1024,1024]{1,0:T(8,128)(2,1)S(1)} %get-tuple-element.9.first, bf16[1024,1024]{1,0:T(8,128)(2,1)S(1)} %get-tuple-element.10.second), custom_call_target="tpu_custom_call" | custom-call | tf_op jit(solution)/shard_map/finish/pallas_call | solution.py:182
  74.2 3.1 %collective-permute-start.21 = (bf16[2,32,1024]{2,1,0:T(8,128)(2,1)S(1)}, bf16[2,32,1024]{2,1,0:T(8,128)(2,1)S(1)}, u32[]{:S(2)}, u32[]{:S(2)}) collective-permute-start(bf16[2,32,1024]{2,1,0:T(8,128)(2,1)S(1)} %get-tuple-element.19), channel_id=1, source_target_pairs={{32,96},{33,97},{34,98},{35,99},{36,100},{37,101},{38,102},{39,103... | collective-permute-start | bytes 393224 | tf_op jit(solution)/shard_map/ppermute | solution.py:33
  77.3 2.6 %collective-permute-start.20 = (bf16[2,32,1024]{2,1,0:T(8,128)(2,1)S(1)}, bf16[2,32,1024]{2,1,0:T(8,128)(2,1)S(1)}, u32[]{:S(2)}, u32[]{:S(2)}) collective-permute-start(bf16[2,32,1024]{2,1,0:T(8,128)(2,1)S(1)} %get-tuple-element.20), channel_id=1, source_target_pairs={{32,64},{33,65},{34,66},{35,67},{36,68},{37,69},{38,70},{39,71},{4... | collective-permute-start | bytes 393224 | tf_op jit(solution)/shard_map/ppermute | solution.py:33
  83.1 2.6 %collective-permute-start.22 = (bf16[64,640]{1,0:T(8,128)(2,1)S(1)}, bf16[64,640]{1,0:T(8,128)(2,1)S(1)}, u32[]{:S(2)}, u32[]{:S(2)}) collective-permute-start(bf16[64,640]{1,0:T(8,128)(2,1)S(1)} %slice.116), channel_id=1, source_target_pairs={{0,8},{1,9},{2,10},{3,11},{4,12},{5,13},{6,14},{7,15},{8,16},{9,17... | collective-permute-start | bytes 245768 | tf_op jit(solution)/shard_map/ppermute | solution.py:33
  85.8 2.9 %collective-permute-start.32 = (bf16[64,384]{1,0:T(8,128)(2,1)S(1)}, bf16[64,384]{1,0:T(8,128)(2,1)S(1)}, u32[]{:S(2)}, u32[]{:S(2)}) collective-permute-start(bf16[64,384]{1,0:T(8,128)(2,1)S(1)} %get-tuple-element.33), channel_id=1, source_target_pairs={{0,4},{1,5},{2,6},{3,7},{4,0},{5,1},{6,2},{7,3},{8,12},{9,13},{10,... | collective-permute-start | bytes 147464 | tf_op jit(solution)/shard_map/ppermute | solution.py:33
  88.8 3.9 %collective-permute-done.32 = bf16[64,384]{1,0:T(8,128)(2,1)S(1)} collective-permute-done((bf16[64,384]{1,0:T(8,128)(2,1)S(1)}, bf16[64,384]{1,0:T(8,128)(2,1)S(1)}, u32[]{:S(2)}, u32[]{:S(2)}) %collective-permute-start.32) | collective-permute-done | bytes 49184 | tf_op jit(solution)/shard_map/ppermute | solution.py:33
  92.8 2.7 %collective-permute-start.33 = (bf16[128,384]{1,0:T(8,128)(2,1)S(1)}, bf16[128,384]{1,0:T(8,128)(2,1)S(1)}, u32[]{:S(2)}, u32[]{:S(2)}) collective-permute-start(bf16[128,384]{1,0:T(8,128)(2,1)S(1)} %pad_maximum_fusion.7), channel_id=1, source_target_pairs={{0,1},{1,2},{2,3},{3,4},{4,5},{5,6},{6,7},{7,0},{8,9},{9,10},{10,1... | collective-permute-start | bytes 294920 | tf_op jit(solution)/shard_map/ppermute | solution.py:33
  97.1 3.0 %collective-permute-start.35 = (bf16[128,384]{1,0:T(8,128)(2,1)S(1)}, bf16[128,384]{1,0:T(8,128)(2,1)S(1)}, u32[]{:S(2)}, u32[]{:S(2)}) collective-permute-start(bf16[128,384]{1,0:T(8,128)(2,1)S(1)} %collective-permute-done.33), channel_id=1, source_target_pairs={{0,1},{1,2},{2,3},{3,4},{4,5},{5,6},{6,7},{7,0},{8,9},{9,10},{10,1... | collective-permute-start | bytes 294920 | tf_op jit(solution)/shard_map/ppermute | solution.py:33
  100.3 2.5 %collective-permute-done.35 = bf16[128,384]{1,0:T(8,128)(2,1)S(1)} collective-permute-done((bf16[128,384]{1,0:T(8,128)(2,1)S(1)}, bf16[128,384]{1,0:T(8,128)(2,1)S(1)}, u32[]{:S(2)}, u32[]{:S(2)}) %collective-permute-start.35) | collective-permute-done | bytes 98336 | tf_op jit(solution)/shard_map/ppermute | solution.py:33
  103.0 2.5 %collective-permute-done.26.refs_2_ = bf16[256,640]{1,0:T(8,128)(2,1)S(1)} collective-permute-done((bf16[256,640]{1,0:T(8,128)(2,1)S(1)}, bf16[256,640]{1,0:T(8,128)(2,1)S(1)}, u32[]{:S(2)}, u32[]{:S(2)}) %collective-permute-start.26) | collective-permute-done | bytes 327712 | tf_op jit(solution)/shard_map/ppermute | solution.py:33
  105.5 3.0 %collective-permute-done.27.refs_3_ = bf16[256,640]{1,0:T(8,128)(2,1)S(1)} collective-permute-done((bf16[256,640]{1,0:T(8,128)(2,1)S(1)}, bf16[256,640]{1,0:T(8,128)(2,1)S(1)}, u32[]{:S(2)}, u32[]{:S(2)}) %collective-permute-start.27) | collective-permute-done | bytes 327712 | tf_op jit(solution)/shard_map/ppermute | solution.py:33
  108.6 3.1 %collective-permute-start.29 = (bf16[256,640]{1,0:T(8,128)(2,1)S(1)}, bf16[256,640]{1,0:T(8,128)(2,1)S(1)}, u32[]{:S(2)}, u32[]{:S(2)}) collective-permute-start(bf16[256,640]{1,0:T(8,128)(2,1)S(1)} %collective-permute-done.27.refs_3_), channel_id=1, source_target_pairs={{0,1},{1,2},{2,3},{3,4},{4,5},{5,6},{6,7},{7,0},{8,9},{9,10},{10,1... | collective-permute-start | bytes 983048 | tf_op jit(solution)/shard_map/ppermute | solution.py:33
  111.7 2.7 %collective-permute-start.38 = (bf16[512,384]{1,0:T(8,128)(2,1)S(1)}, bf16[512,384]{1,0:T(8,128)(2,1)S(1)}, u32[]{:S(2)}, u32[]{:S(2)}) collective-permute-start(bf16[512,384]{1,0:T(8,128)(2,1)S(1)} %collective-permute-done.36.refs_9_), channel_id=1, source_target_pairs={{0,8},{1,9},{2,10},{3,11},{4,12},{5,13},{6,14},{7,15},{8,16},{9,17... | collective-permute-start | bytes 1179656 | tf_op jit(solution)/shard_map/ppermute | solution.py:33
  114.4 1.8 %collective-permute-done.28.refs_4_ = bf16[256,640]{1,0:T(8,128)(2,1)S(1)} collective-permute-done((bf16[256,640]{1,0:T(8,128)(2,1)S(1)}, bf16[256,640]{1,0:T(8,128)(2,1)S(1)}, u32[]{:S(2)}, u32[]{:S(2)}) %collective-permute-start.28) | collective-permute-done | bytes 327712 | tf_op jit(solution)/shard_map/ppermute | solution.py:33
  116.2 1.8 %collective-permute-done.29.refs_5_ = bf16[256,640]{1,0:T(8,128)(2,1)S(1)} collective-permute-done((bf16[256,640]{1,0:T(8,128)(2,1)S(1)}, bf16[256,640]{1,0:T(8,128)(2,1)S(1)}, u32[]{:S(2)}, u32[]{:S(2)}) %collective-permute-start.29) | collective-permute-done | bytes 327712 | tf_op jit(solution)/shard_map/ppermute | solution.py:33
  118.0 3.4 %collective-permute-start.31 = (bf16[256,640]{1,0:T(8,128)(2,1)S(1)}, bf16[256,640]{1,0:T(8,128)(2,1)S(1)}, u32[]{:S(2)}, u32[]{:S(2)}) collective-permute-start(bf16[256,640]{1,0:T(8,128)(2,1)S(1)} %collective-permute-done.29.refs_5_), channel_id=1, source_target_pairs={{0,1},{1,2},{2,3},{3,4},{4,5},{5,6},{6,7},{7,0},{8,9},{9,10},{10,1... | collective-permute-start | bytes 983048 | tf_op jit(solution)/shard_map/ppermute | solution.py:33
  122.8 1.9 %collective-permute-done.30.refs_6_ = bf16[256,640]{1,0:T(8,128)(2,1)S(1)} collective-permute-done((bf16[256,640]{1,0:T(8,128)(2,1)S(1)}, bf16[256,640]{1,0:T(8,128)(2,1)S(1)}, u32[]{:S(2)}, u32[]{:S(2)}) %collective-permute-start.30) | collective-permute-done | bytes 327712 | tf_op jit(solution)/shard_map/ppermute | solution.py:33
  128.3 14.8 %collective-permute-done.39.lefts = bf16[128,1024]{1,0:T(8,128)(2,1)S(1)} collective-permute-done((bf16[128,1024]{1,0:T(8,128)(2,1)S(1)}, bf16[128,1024]{1,0:T(8,128)(2,1)S(1)}, u32[]{:S(2)}, u32[]{:S(2)}) %collective-permute-start.39) | collective-permute-done | bytes 262176 | tf_op jit(solution)/shard_map/ppermute | solution.py:33
  (105 shorter events, 35.1 us)
Async XLA Ops:
  7.3 11.0 %collective-permute-start.3 = (bf16[64,640]{1,0:T(8,128)(2,1)S(1)}, bf16[64,640]{1,0:T(8,128)(2,1)S(1)}, u32[]{:S(2)}, u32[]{:S(2)}) collective-permute-start(bf16[64,640]{1,0:T(8,128)(2,1)S(1)} %fusion.1), channel_id=1, source_target_pairs={{0,16},{1,17},{2,18},{3,19},{4,20},{5,21},{6,22},{7,23},{8,24},{9,... | collective-permute-start | bytes 245768 | tf_op jit(solution)/shard_map/ppermute | solution.py:33
  8.6 9.7 %collective-permute-start.2 = (bf16[64,640]{1,0:T(8,128)(2,1)S(1)}, bf16[64,640]{1,0:T(8,128)(2,1)S(1)}, u32[]{:S(2)}, u32[]{:S(2)}) collective-permute-start(bf16[64,640]{1,0:T(8,128)(2,1)S(1)} %fusion.1), channel_id=1, source_target_pairs={{0,24},{1,25},{2,26},{3,27},{4,28},{5,29},{6,30},{7,31},{8,0},{9,1... | collective-permute-start | bytes 245768 | tf_op jit(solution)/shard_map/ppermute | solution.py:33
  9.0 9.3 %collective-permute-start.1 = (bf16[64,640]{1,0:T(8,128)(2,1)S(1)}, bf16[64,640]{1,0:T(8,128)(2,1)S(1)}, u32[]{:S(2)}, u32[]{:S(2)}) collective-permute-start(bf16[64,640]{1,0:T(8,128)(2,1)S(1)} %fusion.1), channel_id=1, source_target_pairs={{0,8},{1,9},{2,10},{3,11},{4,12},{5,13},{6,14},{7,15},{8,16},{9,17... | collective-permute-start | bytes 245768 | tf_op jit(solution)/shard_map/ppermute | solution.py:33
  11.2 9.1 %collective-permute-start.11 = (bf16[64,384]{1,0:T(8,128)(2,1)S(1)}, bf16[64,384]{1,0:T(8,128)(2,1)S(1)}, u32[]{:S(2)}, u32[]{:S(2)}) collective-permute-start(bf16[64,384]{1,0:T(8,128)(2,1)S(1)} %get-tuple-element.14), channel_id=1, source_target_pairs={{0,4},{1,5},{2,6},{3,7},{4,0},{5,1},{6,2},{7,3},{8,12},{9,13},{10,... | collective-permute-start | bytes 147464 | tf_op jit(solution)/shard_map/ppermute | solution.py:33
  18.3 10.8 %collective-permute-start.4 = (bf16[256,640]{1,0:T(8,128)(2,1)S(1)}, bf16[256,640]{1,0:T(8,128)(2,1)S(1)}, u32[]{:S(2)}, u32[]{:S(2)}) collective-permute-start(bf16[256,640]{1,0:T(8,128)(2,1)S(1)} %pad_maximum_fusion.refs_0_), channel_id=1, source_target_pairs={{0,1},{1,2},{2,3},{3,4},{4,5},{5,6},{6,7},{7,0},{8,9},{9,10},{10,1... | collective-permute-start | bytes 983048 | tf_op jit(solution)/shard_map/ppermute | solution.py:33
  20.4 9.2 %collective-permute-start.13 = (bf16[128,384]{1,0:T(8,128)(2,1)S(1)}, bf16[128,384]{1,0:T(8,128)(2,1)S(1)}, u32[]{:S(2)}, u32[]{:S(2)}) collective-permute-start(bf16[128,384]{1,0:T(8,128)(2,1)S(1)} %pad_maximum_fusion.6), channel_id=1, source_target_pairs={{0,7},{1,0},{2,1},{3,2},{4,3},{5,4},{6,5},{7,6},{8,15},{9,8},{10,9... | collective-permute-start | bytes 294920 | tf_op jit(solution)/shard_map/ppermute | solution.py:33
  21.2 6.5 %collective-permute-start.12 = (bf16[128,384]{1,0:T(8,128)(2,1)S(1)}, bf16[128,384]{1,0:T(8,128)(2,1)S(1)}, u32[]{:S(2)}, u32[]{:S(2)}) collective-permute-start(bf16[128,384]{1,0:T(8,128)(2,1)S(1)} %pad_maximum_fusion.6), channel_id=1, source_target_pairs={{0,1},{1,2},{2,3},{3,4},{4,5},{5,6},{6,7},{7,0},{8,9},{9,10},{10,1... | collective-permute-start | bytes 294920 | tf_op jit(solution)/shard_map/ppermute | solution.py:33
  24.4 8.7 %collective-permute-start.5 = (bf16[256,640]{1,0:T(8,128)(2,1)S(1)}, bf16[256,640]{1,0:T(8,128)(2,1)S(1)}, u32[]{:S(2)}, u32[]{:S(2)}) collective-permute-start(bf16[256,640]{1,0:T(8,128)(2,1)S(1)} %pad_maximum_fusion.refs_0_), channel_id=1, source_target_pairs={{0,7},{1,0},{2,1},{3,2},{4,3},{5,4},{6,5},{7,6},{8,15},{9,8},{10,9... | collective-permute-start | bytes 983048 | tf_op jit(solution)/shard_map/ppermute | solution.py:33
  29.1 8.6 %collective-permute-start.6 = (bf16[256,640]{1,0:T(8,128)(2,1)S(1)}, bf16[256,640]{1,0:T(8,128)(2,1)S(1)}, u32[]{:S(2)}, u32[]{:S(2)}) collective-permute-start(bf16[256,640]{1,0:T(8,128)(2,1)S(1)} %collective-permute-done.4.refs_1_), channel_id=1, source_target_pairs={{0,1},{1,2},{2,3},{3,4},{4,5},{5,6},{6,7},{7,0},{8,9},{9,10},{10,1... | collective-permute-start | bytes 983048 | tf_op jit(solution)/shard_map/ppermute | solution.py:33
  32.6 8.4 %collective-permute-start.15 = (bf16[512,384]{1,0:T(8,128)(2,1)S(1)}, bf16[512,384]{1,0:T(8,128)(2,1)S(1)}, u32[]{:S(2)}, u32[]{:S(2)}) collective-permute-start(bf16[512,384]{1,0:T(8,128)(2,1)S(1)} %constant_dynamic-update-slice_fusion.refs_8_), channel_id=1, source_target_pairs={{0,8},{1,9},{2,10},{3,11},{4,12},{5,13},{6,14},{7,15},{8,16},{9,17... | collective-permute-start | bytes 1179656 | tf_op jit(solution)/shard_map/ppermute | solution.py:33
  33.1 11.2 %collective-permute-start.7 = (bf16[256,640]{1,0:T(8,128)(2,1)S(1)}, bf16[256,640]{1,0:T(8,128)(2,1)S(1)}, u32[]{:S(2)}, u32[]{:S(2)}) collective-permute-start(bf16[256,640]{1,0:T(8,128)(2,1)S(1)} %collective-permute-done.5.refs_2_), channel_id=1, source_target_pairs={{0,7},{1,0},{2,1},{3,2},{4,3},{5,4},{6,5},{7,6},{8,15},{9,8},{10,9... | collective-permute-start | bytes 983048 | tf_op jit(solution)/shard_map/ppermute | solution.py:33
  37.6 10.5 %collective-permute-start.8 = (bf16[256,640]{1,0:T(8,128)(2,1)S(1)}, bf16[256,640]{1,0:T(8,128)(2,1)S(1)}, u32[]{:S(2)}, u32[]{:S(2)}) collective-permute-start(bf16[256,640]{1,0:T(8,128)(2,1)S(1)} %collective-permute-done.6.refs_3_), channel_id=1, source_target_pairs={{0,1},{1,2},{2,3},{3,4},{4,5},{5,6},{6,7},{7,0},{8,9},{9,10},{10,1... | collective-permute-start | bytes 983048 | tf_op jit(solution)/shard_map/ppermute | solution.py:33
  40.7 13.4 %collective-permute-start.16 = (bf16[512,384]{1,0:T(8,128)(2,1)S(1)}, bf16[512,384]{1,0:T(8,128)(2,1)S(1)}, u32[]{:S(2)}, u32[]{:S(2)}) collective-permute-start(bf16[512,384]{1,0:T(8,128)(2,1)S(1)} %constant_dynamic-update-slice_fusion.refs_8_), channel_id=1, source_target_pairs={{0,24},{1,25},{2,26},{3,27},{4,28},{5,29},{6,30},{7,31},{8,0},{9,1... | collective-permute-start | bytes 1179656 | tf_op jit(solution)/shard_map/ppermute | solution.py:33
  41.0 13.2 %collective-permute-start.17 = (bf16[512,384]{1,0:T(8,128)(2,1)S(1)}, bf16[512,384]{1,0:T(8,128)(2,1)S(1)}, u32[]{:S(2)}, u32[]{:S(2)}) collective-permute-start(bf16[512,384]{1,0:T(8,128)(2,1)S(1)} %collective-permute-done.15.refs_9_), channel_id=1, source_target_pairs={{0,8},{1,9},{2,10},{3,11},{4,12},{5,13},{6,14},{7,15},{8,16},{9,17... | collective-permute-start | bytes 1179656 | tf_op jit(solution)/shard_map/ppermute | solution.py:33
  44.3 9.9 %collective-permute-start.9 = (bf16[256,640]{1,0:T(8,128)(2,1)S(1)}, bf16[256,640]{1,0:T(8,128)(2,1)S(1)}, u32[]{:S(2)}, u32[]{:S(2)}) collective-permute-start(bf16[256,640]{1,0:T(8,128)(2,1)S(1)} %collective-permute-done.7.refs_4_), channel_id=1, source_target_pairs={{0,7},{1,0},{2,1},{3,2},{4,3},{5,4},{6,5},{7,6},{8,15},{9,8},{10,9... | collective-permute-start | bytes 983048 | tf_op jit(solution)/shard_map/ppermute | solution.py:33
  48.2 10.0 %collective-permute-start.10 = (bf16[256,640]{1,0:T(8,128)(2,1)S(1)}, bf16[256,640]{1,0:T(8,128)(2,1)S(1)}, u32[]{:S(2)}, u32[]{:S(2)}) collective-permute-start(bf16[256,640]{1,0:T(8,128)(2,1)S(1)} %collective-permute-done.8.refs_5_), channel_id=1, source_target_pairs={{0,1},{1,2},{2,3},{3,4},{4,5},{5,6},{6,7},{7,0},{8,9},{9,10},{10,1... | collective-permute-start | bytes 983048 | tf_op jit(solution)/shard_map/ppermute | solution.py:33
  59.4 12.9 %collective-permute-start.18 = (bf16[128,1024]{1,0:T(8,128)(2,1)}, bf16[128,1024]{1,0:T(8,128)(2,1)}, u32[]{:S(2)}, u32[]{:S(2)}) collective-permute-start(bf16[128,1024]{1,0:T(8,128)(2,1)} %bitcast.7), channel_id=1, source_target_pairs={{0,32},{1,33},{2,34},{3,35},{4,36},{5,37},{6,38},{7,39},{8,40},{9,... | collective-permute-start | bytes 786440 | tf_op jit(solution)/shard_map/ppermute | solution.py:33
  74.2 7.0 %collective-permute-start.21 = (bf16[2,32,1024]{2,1,0:T(8,128)(2,1)S(1)}, bf16[2,32,1024]{2,1,0:T(8,128)(2,1)S(1)}, u32[]{:S(2)}, u32[]{:S(2)}) collective-permute-start(bf16[2,32,1024]{2,1,0:T(8,128)(2,1)S(1)} %get-tuple-element.19), channel_id=1, source_target_pairs={{32,96},{33,97},{34,98},{35,99},{36,100},{37,101},{38,102},{39,103... | collective-permute-start | bytes 393224 | tf_op jit(solution)/shard_map/ppermute | solution.py:33
  82.3 6.4 %collective-permute-start.24 = (bf16[64,640]{1,0:T(8,128)(2,1)S(1)}, bf16[64,640]{1,0:T(8,128)(2,1)S(1)}, u32[]{:S(2)}, u32[]{:S(2)}) collective-permute-start(bf16[64,640]{1,0:T(8,128)(2,1)S(1)} %slice.116), channel_id=1, source_target_pairs={{0,16},{1,17},{2,18},{3,19},{4,20},{5,21},{6,22},{7,23},{8,24},{9,... | collective-permute-start | bytes 245768 | tf_op jit(solution)/shard_map/ppermute | solution.py:33
  85.8 6.9 %collective-permute-start.32 = (bf16[64,384]{1,0:T(8,128)(2,1)S(1)}, bf16[64,384]{1,0:T(8,128)(2,1)S(1)}, u32[]{:S(2)}, u32[]{:S(2)}) collective-permute-start(bf16[64,384]{1,0:T(8,128)(2,1)S(1)} %get-tuple-element.33), channel_id=1, source_target_pairs={{0,4},{1,5},{2,6},{3,7},{4,0},{5,1},{6,2},{7,3},{8,12},{9,13},{10,... | collective-permute-start | bytes 147464 | tf_op jit(solution)/shard_map/ppermute | solution.py:33
  88.7 11.4 %collective-permute-start.25 = (bf16[256,640]{1,0:T(8,128)(2,1)S(1)}, bf16[256,640]{1,0:T(8,128)(2,1)S(1)}, u32[]{:S(2)}, u32[]{:S(2)}) collective-permute-start(bf16[256,640]{1,0:T(8,128)(2,1)S(1)} %pad_maximum_fusion.1.refs_0_), channel_id=1, source_target_pairs={{0,1},{1,2},{2,3},{3,4},{4,5},{5,6},{6,7},{7,0},{8,9},{9,10},{10,1... | collective-permute-start | bytes 983048 | tf_op jit(solution)/shard_map/ppermute | solution.py:33
  92.7 7.6 %collective-permute-start.34 = (bf16[128,384]{1,0:T(8,128)(2,1)S(1)}, bf16[128,384]{1,0:T(8,128)(2,1)S(1)}, u32[]{:S(2)}, u32[]{:S(2)}) collective-permute-start(bf16[128,384]{1,0:T(8,128)(2,1)S(1)} %pad_maximum_fusion.7), channel_id=1, source_target_pairs={{0,7},{1,0},{2,1},{3,2},{4,3},{5,4},{6,5},{7,6},{8,15},{9,8},{10,9... | collective-permute-start | bytes 294920 | tf_op jit(solution)/shard_map/ppermute | solution.py:33
  95.5 10.1 %collective-permute-start.26 = (bf16[256,640]{1,0:T(8,128)(2,1)S(1)}, bf16[256,640]{1,0:T(8,128)(2,1)S(1)}, u32[]{:S(2)}, u32[]{:S(2)}) collective-permute-start(bf16[256,640]{1,0:T(8,128)(2,1)S(1)} %pad_maximum_fusion.1.refs_0_), channel_id=1, source_target_pairs={{0,7},{1,0},{2,1},{3,2},{4,3},{5,4},{6,5},{7,6},{8,15},{9,8},{10,9... | collective-permute-start | bytes 983048 | tf_op jit(solution)/shard_map/ppermute | solution.py:33
  100.2 8.4 %collective-permute-start.27 = (bf16[256,640]{1,0:T(8,128)(2,1)S(1)}, bf16[256,640]{1,0:T(8,128)(2,1)S(1)}, u32[]{:S(2)}, u32[]{:S(2)}) collective-permute-start(bf16[256,640]{1,0:T(8,128)(2,1)S(1)} %collective-permute-done.25.refs_1_), channel_id=1, source_target_pairs={{0,1},{1,2},{2,3},{3,4},{4,5},{5,6},{6,7},{7,0},{8,9},{9,10},{10,1... | collective-permute-start | bytes 983048 | tf_op jit(solution)/shard_map/ppermute | solution.py:33
  102.8 8.9 %collective-permute-start.36 = (bf16[512,384]{1,0:T(8,128)(2,1)S(1)}, bf16[512,384]{1,0:T(8,128)(2,1)S(1)}, u32[]{:S(2)}, u32[]{:S(2)}) collective-permute-start(bf16[512,384]{1,0:T(8,128)(2,1)S(1)} %constant_dynamic-update-slice_fusion.5.refs_8_), channel_id=1, source_target_pairs={{0,8},{1,9},{2,10},{3,11},{4,12},{5,13},{6,14},{7,15},{8,16},{9,17... | collective-permute-start | bytes 1179656 | tf_op jit(solution)/shard_map/ppermute | solution.py:33
  105.5 10.6 %collective-permute-start.28 = (bf16[256,640]{1,0:T(8,128)(2,1)S(1)}, bf16[256,640]{1,0:T(8,128)(2,1)S(1)}, u32[]{:S(2)}, u32[]{:S(2)}) collective-permute-start(bf16[256,640]{1,0:T(8,128)(2,1)S(1)} %collective-permute-done.26.refs_2_), channel_id=1, source_target_pairs={{0,7},{1,0},{2,1},{3,2},{4,3},{5,4},{6,5},{7,6},{8,15},{9,8},{10,9... | collective-permute-start | bytes 983048 | tf_op jit(solution)/shard_map/ppermute | solution.py:33
  108.6 9.4 %collective-permute-start.29 = (bf16[256,640]{1,0:T(8,128)(2,1)S(1)}, bf16[256,640]{1,0:T(8,128)(2,1)S(1)}, u32[]{:S(2)}, u32[]{:S(2)}) collective-permute-start(bf16[256,640]{1,0:T(8,128)(2,1)S(1)} %collective-permute-done.27.refs_3_), channel_id=1, source_target_pairs={{0,1},{1,2},{2,3},{3,4},{4,5},{5,6},{6,7},{7,0},{8,9},{9,10},{10,1... | collective-permute-start | bytes 983048 | tf_op jit(solution)/shard_map/ppermute | solution.py:33
  111.7 11.1 %collective-permute-start.37 = (bf16[512,384]{1,0:T(8,128)(2,1)S(1)}, bf16[512,384]{1,0:T(8,128)(2,1)S(1)}, u32[]{:S(2)}, u32[]{:S(2)}) collective-permute-start(bf16[512,384]{1,0:T(8,128)(2,1)S(1)} %constant_dynamic-update-slice_fusion.5.refs_8_), channel_id=1, source_target_pairs={{0,24},{1,25},{2,26},{3,27},{4,28},{5,29},{6,30},{7,31},{8,0},{9,1... | collective-permute-start | bytes 1179656 | tf_op jit(solution)/shard_map/ppermute | solution.py:33
  111.7 11.1 %collective-permute-start.38 = (bf16[512,384]{1,0:T(8,128)(2,1)S(1)}, bf16[512,384]{1,0:T(8,128)(2,1)S(1)}, u32[]{:S(2)}, u32[]{:S(2)}) collective-permute-start(bf16[512,384]{1,0:T(8,128)(2,1)S(1)} %collective-permute-done.36.refs_9_), channel_id=1, source_target_pairs={{0,8},{1,9},{2,10},{3,11},{4,12},{5,13},{6,14},{7,15},{8,16},{9,17... | collective-permute-start | bytes 1179656 | tf_op jit(solution)/shard_map/ppermute | solution.py:33
  116.1 8.6 %collective-permute-start.30 = (bf16[256,640]{1,0:T(8,128)(2,1)S(1)}, bf16[256,640]{1,0:T(8,128)(2,1)S(1)}, u32[]{:S(2)}, u32[]{:S(2)}) collective-permute-start(bf16[256,640]{1,0:T(8,128)(2,1)S(1)} %collective-permute-done.28.refs_4_), channel_id=1, source_target_pairs={{0,7},{1,0},{2,1},{3,2},{4,3},{5,4},{6,5},{7,6},{8,15},{9,8},{10,9... | collective-permute-start | bytes 983048 | tf_op jit(solution)/shard_map/ppermute | solution.py:33
  118.0 7.4 %collective-permute-start.31 = (bf16[256,640]{1,0:T(8,128)(2,1)S(1)}, bf16[256,640]{1,0:T(8,128)(2,1)S(1)}, u32[]{:S(2)}, u32[]{:S(2)}) collective-permute-start(bf16[256,640]{1,0:T(8,128)(2,1)S(1)} %collective-permute-done.29.refs_5_), channel_id=1, source_target_pairs={{0,1},{1,2},{2,3},{3,4},{4,5},{5,6},{6,7},{7,0},{8,9},{9,10},{10,1... | collective-permute-start | bytes 983048 | tf_op jit(solution)/shard_map/ppermute | solution.py:33
  125.9 17.1 %collective-permute-start.39 = (bf16[128,1024]{1,0:T(8,128)(2,1)S(1)}, bf16[128,1024]{1,0:T(8,128)(2,1)S(1)}, u32[]{:S(2)}, u32[]{:S(2)}) collective-permute-start(bf16[128,1024]{1,0:T(8,128)(2,1)S(1)} %bitcast.22), channel_id=1, source_target_pairs={{0,32},{1,33},{2,34},{3,35},{4,36},{5,37},{6,38},{7,39},{8,40},{9,... | collective-permute-start | bytes 786440 | tf_op jit(solution)/shard_map/ppermute | solution.py:33
  (14 other events, 59.6 us)

commit v4 on v3

v4 whole, which is shorter than its diff:
```python
import functools
import jax
import jax.numpy as jnp
from jax import lax
from jax.experimental import pallas as pl
from jax.experimental.pallas import tpu as pltpu
from jax.sharding import PartitionSpec as P

M = 1024
BLK = 64
NX, NC, NY, NZ = 4, 2, 4, 8
AXES = ("slab", "panel")
SPLIT = 640
PARTS = NZ + NY


def device(x, c, y, z):
    return ((x % NX) * NC + c) * NY * NZ + (y % NY) * NZ + z % NZ


def route(move):
    pairs = []
    for x in range(NX):
        for c in range(NC):
            for y in range(NY):
                for z in range(NZ):
                    target = move(x, c, y, z)
                    if target is not None:
                        pairs.append((device(x, c, y, z), device(*target)))
    return pairs


def send(block, move):
    return lax.ppermute(block, AXES, route(move))


def hop(axis, distance):
    def move(x, c, y, z):
        ahead = distance if c == 0 else -distance
        return (x, c, y + ahead, z) if axis == "y" else (x, c, y, z + ahead)

    return move


def gather(block):
    wide_a, wide_b = block[:, :SPLIT], block[:, SPLIT:]
    wide_a = jnp.concatenate([wide_a] + [send(wide_a, hop("y", d)) for d in Y_BACK[1:]])
    wide_b = jnp.concatenate([wide_b, send(wide_b, hop("z", 4))])
    ahead, behind = send(wide_b, hop("z", 1)), send(wide_b, hop("z", -1))
    wide_b = jnp.concatenate([wide_b, ahead, behind, send(ahead, hop("z", 1))])
    parts_a, parts_b = [wide_a], [wide_b]
    ahead, behind = wide_a, wide_a
    for back in Z_BACK_A[1:]:
        if back > 0:
            ahead = send(ahead, hop("z", 1))
            parts_a.append(ahead)
        else:
            behind = send(behind, hop("z", -1))
            parts_a.append(behind)
    ahead, behind = send(wide_b, hop("y", 1)), send(wide_b, hop("y", -1))
    parts_b += [ahead, behind, send(ahead, hop("y", 1))]
    return parts_a, parts_b


Y_BACK = (0, 1, -1, 2)
Z_BACK_A = (0, 1, -1, 2, -2, 3, -3, 4)
Z_BACK_B = (0, 4, 1, 5, -1, 3, 2, 6)


def row_of(y, z):
    return pl.multiple_of((lax.rem(y + 2 * NY, NY) * NZ + lax.rem(z + 2 * NZ, NZ)) * 32, 32)


def order(where, parts, first, second):
    parts_a, parts_b = parts[:NZ], parts[NZ:]
    way, y, z = 1 - 2 * where[0], where[1], where[2]
    for z_back, part in zip(Z_BACK_A, parts_a):
        for k, y_back in enumerate(Y_BACK):
            at = pl.ds(row_of(y - way * y_back, z - way * z_back), 32)
            first[at, :SPLIT] = part[pl.ds(k * 64, 32)]
            second[at, :SPLIT] = part[pl.ds(k * 64 + 32, 32)]
    for y_back, part in zip(Y_BACK, parts_b):
        for k, z_back in enumerate(Z_BACK_B):
            at = pl.ds(row_of(y - way * y_back, z - way * z_back), 32)
            first[at, SPLIT:] = part[pl.ds(k * 64, 32)]
            second[at, SPLIT:] = part[pl.ds(k * 64 + 32, 32)]


def wide_dot(left, factor, out):
    out[pl.ds(0, left.shape[0])] = jnp.dot(
        left[...], factor[...], preferred_element_type=jnp.float32
    )


def mask_kernel(where, pattern, ranges, keep, give):
    block_row = pl.ds(lax.div(where[1] * NZ + where[2], BLK // 32), 1)
    count = M // BLK
    spread = (
        lax.broadcasted_iota(jnp.int32, (count, M), 0)
        == lax.div(lax.broadcasted_iota(jnp.int32, (count, M), 1), BLK)
    ).astype(jnp.bfloat16)
    for b, (out, at) in enumerate(((keep, 0), (give, 0), (keep, 1), (give, 1))):
        present = pattern[b, block_row, :].astype(jnp.float32).astype(jnp.bfloat16)
        mask = jnp.dot(present, spread, preferred_element_type=jnp.float32)
        out[at] = ranges[b] * mask


VMEM = pl.BlockSpec(memory_space=pltpu.VMEM)
SMEM = pl.BlockSpec(memory_space=pltpu.SMEM)


def masked(where, pattern, ranges):
    return pl.pallas_call(
        mask_kernel,
        out_shape=[jax.ShapeDtypeStruct((2, 32, M), jnp.float32)] * 2,
        in_specs=[SMEM, VMEM, VMEM],
        out_specs=[VMEM, VMEM],
        compiler_params=pltpu.CompilerParams(vmem_limit_bytes=8 << 20),
        name="masked",
    )(where, pattern, ranges)


def chain_kernel(where, keep, other, *refs):
    parts, (out, first, second, left, prod, sums) = refs[:PARTS], refs[PARTS:]
    order(where, parts, first, second)

    @pl.when(where[0] == 1)
    def _():
        half = jnp.bfloat16
        down, up = keep[1].astype(jnp.float32), other[0].astype(jnp.float32)
        left[pl.ds(0, 32)] = down.astype(half)
        left[pl.ds(32, 32)] = up.astype(half)
        wide_dot(left, second, prod)
        reach = prod[pl.ds(0, 32)]
        left[pl.ds(0, 32)] = reach.astype(half)
        sums[pl.ds(0, 32)] = reach
        sums[pl.ds(32, 32)] = up
        sums[pl.ds(64, 32)] = down
        sums[pl.ds(96, 32)] = jnp.zeros((32, M), jnp.float32)

        @pl.loop(0, 4)
        def _(n):
            wide_dot(left, first, prod)
            sums[pl.ds(64, 64)] += prod[...]
            left[...] = prod[...].astype(half)
            wide_dot(left, second, prod)
            sums[pl.ds(0, 32)] += prod[pl.ds(0, 32)]

            @pl.when(n < 3)
            def _():
                sums[pl.ds(32, 32)] += prod[pl.ds(32, 32)]

            left[...] = prod[...].astype(half)

        out[...] = sums[...].astype(half)


def chain(where, keep, other, parts):
    return pl.pallas_call(
        chain_kernel,
        out_shape=[
            jax.ShapeDtypeStruct((128, M), jnp.bfloat16),
            jax.ShapeDtypeStruct((M, M), jnp.bfloat16),
            jax.ShapeDtypeStruct((M, M), jnp.bfloat16),
        ],
        in_specs=[SMEM] + [VMEM] * (2 + PARTS),
        out_specs=[VMEM] * 3,
        scratch_shapes=[
            pltpu.VMEM((64, M), jnp.bfloat16),
            pltpu.VMEM((64, M), jnp.float32),
            pltpu.VMEM((128, M), jnp.float32),
        ],
        compiler_params=pltpu.CompilerParams(vmem_limit_bytes=20 << 20),
        name="chain",
    )(where, keep, other, *parts)


def finish_kernel(last, where, lefts, keep, other, first, second, *refs):
    outs, prod = refs[:-1], refs[-1]

    @pl.when(where[0] == 0)
    def _():
        wide_dot(lefts.at[pl.ds(0, 64)], first, prod.at[0])
        wide_dot(lefts.at[pl.ds(64, 64)], second, prod.at[1])
        top = keep[0].astype(jnp.float32) + prod[1, pl.ds(32, 32)]
        up = prod[0, pl.ds(32, 32)]
        down = prod[1, pl.ds(0, 32)]
        bottom = other[1].astype(jnp.float32) + prod[0, pl.ds(0, 32)]
        if last:
            for at, block in enumerate((top, up, down, bottom)):
                outs[0][at] = block
            return
        mine, mine_half, rest_half = outs
        for odd, pair, rest in ((0, (top, down), (up, bottom)), (1, (up, bottom), (top, down))):

            @pl.when(where[3] == odd)
            def _(pair=pair, rest=rest):
                for at in range(2):
                    mine[at] = pair[at]
                    mine_half[at] = pair[at].astype(jnp.bfloat16)
                    rest_half[at] = rest[at].astype(jnp.bfloat16)


def finish(last, where, lefts, keep, other, first, second):
    pair = (2, 32, M)
    if last:
        shapes = [jax.ShapeDtypeStruct((4, 32, M), jnp.float32)]
    else:
        shapes = [
            jax.ShapeDtypeStruct(pair, kind) for kind in (jnp.float32, jnp.bfloat16, jnp.bfloat16)
        ]
    return pl.pallas_call(
        functools.partial(finish_kernel, last),
        out_shape=shapes,
        in_specs=[SMEM] + [VMEM] * 5,
        out_specs=[VMEM] * len(shapes),
        scratch_shapes=[pltpu.VMEM((2, 64, M), jnp.float32)],
        compiler_params=pltpu.CompilerParams(vmem_limit_bytes=16 << 20),
        name="finish",
    )(where, lefts, keep, other, first, second)


def star(last, where, keep, other):
    block = jnp.where(
        where[0] == 1,
        jnp.concatenate([keep[0], other[1]]),
        jnp.concatenate([other[0], keep[1]]),
    ).astype(jnp.bfloat16)
    parts_a, parts_b = gather(block)
    sums, first, second = chain(where, keep, other, parts_a + parts_b)
    lefts = send(sums, lambda x, c, y, z: (x, 0, y, z) if c == 1 else None)
    return finish(last, where, lefts, keep, other, first, second)


def body(ranges, pattern):
    slab = lax.axis_index("slab")
    panel = lax.axis_index("panel")
    core, odd = slab % NC, (slab // NC) % 2
    where = jnp.stack([core, panel // NZ, panel % NZ, odd]).astype(jnp.int32)

    keep, give = masked(where, pattern[0], ranges[0])
    other = send(give, lambda x, c, y, z: (x, 1 - c, y, z))
    mine, mine_half, rest_half = star(False, where, keep, other)

    near = send(rest_half, lambda x, c, y, z: (x, 1, y, z) if c == 0 else None)
    across = send(rest_half, lambda x, c, y, z: (x ^ 1, 1, y, z) if c == 0 else None)
    far = send(mine_half, lambda x, c, y, z: (x ^ 1, 0, y, z) if c == 0 else None)
    this = jnp.where(core == 0, mine, across.astype(jnp.float32))
    that = jnp.where(core == 0, far, near).astype(jnp.float32)
    keep, other = jnp.where(odd == 1, that, this), jnp.where(odd == 1, this, that)
    (joint,) = star(True, where, keep, other)
    shared = send(joint, lambda x, c, y, z: (x, 1, y, z) if c == 0 else None)
    return jnp.where(core == 1, shared, joint)[None]


def solution(mesh):
    return jax.shard_map(
        body,
        mesh=mesh,
        in_specs=(P("slab", None, "panel", None), P("slab", None, None, None)),
        out_specs=P("slab", None, "panel", None),
        check_vma=False,
    )
```

time: 149 us -> 140 us (0.940)
  waiting for transfers between devices: 67.5 us -> 56.4 us
  Pallas kernels: 6.92 us -> 11.8 us
  starting transfers between devices: 63.5 us -> 68.1 us
  other arithmetic: 5.01 us -> 1.15 us
  local copies, waits for them, and re-layouts: 4.75 us -> 2.03 us
    ppermute x41, waiting for transfers between devices: 67.5 us -> 56.4 us  [send(): return lax.ppermute(block, AXES, route(move))]
    pallas_call x6 -> x5, Pallas kernels: 6.92 us -> 11.8 us  [the longest x2 10 us: chain(): pl.pallas_call(chain_kernel, out_shape=[jax.ShapeDtypeStruct((128, M), jn...]
    ppermute x41, starting transfers between devices: 63.5 us -> 68.1 us  [send(): return lax.ppermute(block, AXES, route(move))]
    slice x5 -> x0, local copies, waits for them, and re-layouts: 2.45 us -> none  [the longest x1 1.65 us: body(): other[0]]
    another operation x5 -> x1, other arithmetic: 2.03 us -> 0.08 us  [body(): where = jnp.stack([core, panel // NZ, panel % NZ, odd]).astype(jnp.int32)]
  transfers between devices with their start and end apart: 41 -> 41, of which waited for: 23 -> 26; matrix products, arithmetic and copies ran while one was open for 3% -> 0% of each run, Pallas kernels for 1% -> 0%
where the time goes in v4:
time: 140 us
  starting transfers between devices  68.1 us (49%)
  waiting for transfers between devices  56.4 us (40%)
  Pallas kernels  11.8 us (8%)
  local copies, waits for them, and re-layouts  2.03 us (1%)
    ppermute x41, starting transfers between devices, send(): return lax.ppermute(block, AXES, route(move))  68.1 us
    ppermute x41, waiting for transfers between devices, send(): return lax.ppermute(block, AXES, route(move))  56.4 us
    pallas_call x2, Pallas kernels, chain(): pl.pallas_call(chain_kernel, out_shape=[jax.ShapeDtypeStruct((128, M), jn...  10 us
  transfers between devices with their start and end apart: 41, of which 26 were waited for; matrix products, arithmetic and copies ran while one was open for 0% of the time, Pallas kernels for 0%

profile of v4, /device:TPU:1, one launch (start us, length us, event | category | flops | bytes accessed | tf_op | source)
XLA Modules:
  0.0 139.8 jit_solution(17040427063562598326)
XLA Ops:
  2.6 3.3 %collective-permute-start = (f32[2,32,1024]{2,1,0:T(8,128)S(1)}, f32[2,32,1024]{2,1,0:T(8,128)S(1)}, u32[]{:S(2)}, u32[]{:S(2)}) collective-permute-start(f32[2,32,1024]{2,1,0:T(8,128)S(1)} %get-tuple-element.17), channel_id=1, source_target_pairs={{0,32},{1,33},{2,34},{3,35},{4,36},{5,37},{6,38},{7,39},{8,40},{9,... | collective-permute-start | bytes 786440 | tf_op jit(solution)/shard_map/ppermute | solution.py:34
  8.8 2.3 %collective-permute-start.1 = (bf16[64,640]{1,0:T(8,128)(2,1)S(1)}, bf16[64,640]{1,0:T(8,128)(2,1)S(1)}, u32[]{:S(2)}, u32[]{:S(2)}) collective-permute-start(bf16[64,640]{1,0:T(8,128)(2,1)S(1)} %slice.50), channel_id=1, source_target_pairs={{0,8},{1,9},{2,10},{3,11},{4,12},{5,13},{6,14},{7,15},{8,16},{9,17... | collective-permute-start | bytes 245768 | tf_op jit(solution)/shard_map/ppermute | solution.py:34
  11.1 7.0 %collective-permute-start.11 = (bf16[64,384]{1,0:T(8,128)(2,1)S(1)}, bf16[64,384]{1,0:T(8,128)(2,1)S(1)}, u32[]{:S(2)}, u32[]{:S(2)}) collective-permute-start(bf16[64,384]{1,0:T(8,128)(2,1)S(1)} %get-tuple-element.39), channel_id=1, source_target_pairs={{0,4},{1,5},{2,6},{3,7},{4,0},{5,1},{6,2},{7,3},{8,12},{9,13},{10,... | collective-permute-start | bytes 147464 | tf_op jit(solution)/shard_map/ppermute | solution.py:34
  21.1 3.2 %collective-permute-start.12 = (bf16[128,384]{1,0:T(8,128)(2,1)S(1)}, bf16[128,384]{1,0:T(8,128)(2,1)S(1)}, u32[]{:S(2)}, u32[]{:S(2)}) collective-permute-start(bf16[128,384]{1,0:T(8,128)(2,1)S(1)} %pad_maximum_fusion.2), channel_id=1, source_target_pairs={{0,1},{1,2},{2,3},{3,4},{4,5},{5,6},{6,7},{7,0},{8,9},{9,10},{10,1... | collective-permute-start | bytes 294920 | tf_op jit(solution)/shard_map/ppermute | solution.py:34
  24.3 3.2 %collective-permute-done.12 = bf16[128,384]{1,0:T(8,128)(2,1)S(1)} collective-permute-done((bf16[128,384]{1,0:T(8,128)(2,1)S(1)}, bf16[128,384]{1,0:T(8,128)(2,1)S(1)}, u32[]{:S(2)}, u32[]{:S(2)}) %collective-permute-start.12) | collective-permute-done | bytes 98336 | tf_op jit(solution)/shard_map/ppermute | solution.py:34
  29.5 2.9 %collective-permute-done.14 = bf16[128,384]{1,0:T(8,128)(2,1)S(1)} collective-permute-done((bf16[128,384]{1,0:T(8,128)(2,1)S(1)}, bf16[128,384]{1,0:T(8,128)(2,1)S(1)}, u32[]{:S(2)}, u32[]{:S(2)}) %collective-permute-start.14) | collective-permute-done | bytes 98336 | tf_op jit(solution)/shard_map/ppermute | solution.py:34
  32.9 4.6 %collective-permute-done.6.refs_3_ = bf16[256,640]{1,0:T(8,128)(2,1)S(1)} collective-permute-done((bf16[256,640]{1,0:T(8,128)(2,1)S(1)}, bf16[256,640]{1,0:T(8,128)(2,1)S(1)}, u32[]{:S(2)}, u32[]{:S(2)}) %collective-permute-start.6) | collective-permute-done | bytes 327712 | tf_op jit(solution)/shard_map/ppermute | solution.py:34
  37.5 3.1 %collective-permute-start.8 = (bf16[256,640]{1,0:T(8,128)(2,1)S(1)}, bf16[256,640]{1,0:T(8,128)(2,1)S(1)}, u32[]{:S(2)}, u32[]{:S(2)}) collective-permute-start(bf16[256,640]{1,0:T(8,128)(2,1)S(1)} %collective-permute-done.6.refs_3_), channel_id=1, source_target_pairs={{0,1},{1,2},{2,3},{3,4},{4,5},{5,6},{6,7},{7,0},{8,9},{9,10},{10,1... | collective-permute-start | bytes 983048 | tf_op jit(solution)/shard_map/ppermute | solution.py:34
  40.8 2.5 %collective-permute-start.17 = (bf16[512,384]{1,0:T(8,128)(2,1)S(1)}, bf16[512,384]{1,0:T(8,128)(2,1)S(1)}, u32[]{:S(2)}, u32[]{:S(2)}) collective-permute-start(bf16[512,384]{1,0:T(8,128)(2,1)S(1)} %collective-permute-done.15.refs_9_), channel_id=1, source_target_pairs={{0,8},{1,9},{2,10},{3,11},{4,12},{5,13},{6,14},{7,15},{8,16},{9,17... | collective-permute-start | bytes 1179656 | tf_op jit(solution)/shard_map/ppermute | solution.py:34
  44.3 3.8 %collective-permute-done.8.refs_5_ = bf16[256,640]{1,0:T(8,128)(2,1)S(1)} collective-permute-done((bf16[256,640]{1,0:T(8,128)(2,1)S(1)}, bf16[256,640]{1,0:T(8,128)(2,1)S(1)}, u32[]{:S(2)}, u32[]{:S(2)}) %collective-permute-start.8) | collective-permute-done | bytes 327712 | tf_op jit(solution)/shard_map/ppermute | solution.py:34
  48.0 3.4 %collective-permute-start.10 = (bf16[256,640]{1,0:T(8,128)(2,1)S(1)}, bf16[256,640]{1,0:T(8,128)(2,1)S(1)}, u32[]{:S(2)}, u32[]{:S(2)}) collective-permute-start(bf16[256,640]{1,0:T(8,128)(2,1)S(1)} %collective-permute-done.8.refs_5_), channel_id=1, source_target_pairs={{0,1},{1,2},{2,3},{3,4},{4,5},{5,6},{6,7},{7,0},{8,9},{9,10},{10,1... | collective-permute-start | bytes 983048 | tf_op jit(solution)/shard_map/ppermute | solution.py:34
  51.7 2.0 %collective-permute-done.9.refs_6_ = bf16[256,640]{1,0:T(8,128)(2,1)S(1)} collective-permute-done((bf16[256,640]{1,0:T(8,128)(2,1)S(1)}, bf16[256,640]{1,0:T(8,128)(2,1)S(1)}, u32[]{:S(2)}, u32[]{:S(2)}) %collective-permute-start.9) | collective-permute-done | bytes 327712 | tf_op jit(solution)/shard_map/ppermute | solution.py:34
  53.7 4.3 %collective-permute-done.10.refs_7_ = bf16[256,640]{1,0:T(8,128)(2,1)S(1)} collective-permute-done((bf16[256,640]{1,0:T(8,128)(2,1)S(1)}, bf16[256,640]{1,0:T(8,128)(2,1)S(1)}, u32[]{:S(2)}, u32[]{:S(2)}) %collective-permute-start.10) | collective-permute-done | bytes 327712 | tf_op jit(solution)/shard_map/ppermute | solution.py:34
  58.0 5.0 %chain.2 = (bf16[128,1024]{1,0:T(8,128)(2,1)S(1)}, bf16[1024,1024]{1,0:T(8,128)(2,1)S(1)}, bf16[1024,1024]{1,0:T(8,128)(2,1)S(1)}) custom-call(s32[4]{0:T(128)S(1)} %pad_add_fusion.where, f32[2,32,1024]{2,1,0:T(8,128)S(1)} %get-tuple-element.16.keep, f32[2,32,1024]{2,1,0:T(8,128)S(1)} %collective-permute-done.other, ...), custom_call_target="tpu_custom_call" | custom-call | tf_op jit(solution)/shard_map/chain/pallas_call | solution.py:159
  63.0 3.7 %collective-permute-start.18 = (bf16[128,1024]{1,0:T(8,128)(2,1)S(1)}, bf16[128,1024]{1,0:T(8,128)(2,1)S(1)}, u32[]{:S(2)}, u32[]{:S(2)}) collective-permute-start(bf16[128,1024]{1,0:T(8,128)(2,1)S(1)} %get-tuple-element.18), channel_id=1, source_target_pairs={{32,0},{33,1},{34,2},{35,3},{36,4},{37,5},{38,6},{39,7},{40,8},{41... | collective-permute-start | bytes 786440 | tf_op jit(solution)/shard_map/ppermute | solution.py:34
  71.7 5.5 %collective-permute-done.21 = bf16[2,32,1024]{2,1,0:T(8,128)(2,1)S(1)} collective-permute-done((bf16[2,32,1024]{2,1,0:T(8,128)(2,1)S(1)}, bf16[2,32,1024]{2,1,0:T(8,128)(2,1)S(1)}, u32[]{:S(2)}, u32[]{:S(2)}) %collective-permute-start.21) | collective-permute-done | bytes 131104 | tf_op jit(solution)/shard_map/ppermute | solution.py:34
  78.2 2.6 %collective-permute-start.22 = (bf16[64,640]{1,0:T(8,128)(2,1)S(1)}, bf16[64,640]{1,0:T(8,128)(2,1)S(1)}, u32[]{:S(2)}, u32[]{:S(2)}) collective-permute-start(bf16[64,640]{1,0:T(8,128)(2,1)S(1)} %slice.56), channel_id=1, source_target_pairs={{0,8},{1,9},{2,10},{3,11},{4,12},{5,13},{6,14},{7,15},{8,16},{9,17... | collective-permute-start | bytes 245768 | tf_op jit(solution)/shard_map/ppermute | solution.py:34
  80.8 3.0 %collective-permute-start.32 = (bf16[64,384]{1,0:T(8,128)(2,1)S(1)}, bf16[64,384]{1,0:T(8,128)(2,1)S(1)}, u32[]{:S(2)}, u32[]{:S(2)}) collective-permute-start(bf16[64,384]{1,0:T(8,128)(2,1)S(1)} %get-tuple-element.37), channel_id=1, source_target_pairs={{0,4},{1,5},{2,6},{3,7},{4,0},{5,1},{6,2},{7,3},{8,12},{9,13},{10,... | collective-permute-start | bytes 147464 | tf_op jit(solution)/shard_map/ppermute | solution.py:34
  85.4 2.9 %collective-permute-done.32 = bf16[64,384]{1,0:T(8,128)(2,1)S(1)} collective-permute-done((bf16[64,384]{1,0:T(8,128)(2,1)S(1)}, bf16[64,384]{1,0:T(8,128)(2,1)S(1)}, u32[]{:S(2)}, u32[]{:S(2)}) %collective-permute-start.32) | collective-permute-done | bytes 49184 | tf_op jit(solution)/shard_map/ppermute | solution.py:34
  88.6 2.4 %collective-permute-start.33 = (bf16[128,384]{1,0:T(8,128)(2,1)S(1)}, bf16[128,384]{1,0:T(8,128)(2,1)S(1)}, u32[]{:S(2)}, u32[]{:S(2)}) collective-permute-start(bf16[128,384]{1,0:T(8,128)(2,1)S(1)} %pad_maximum_fusion.3), channel_id=1, source_target_pairs={{0,1},{1,2},{2,3},{3,4},{4,5},{5,6},{6,7},{7,0},{8,9},{9,10},{10,1... | collective-permute-start | bytes 294920 | tf_op jit(solution)/shard_map/ppermute | solution.py:34
  91.1 2.1 %collective-permute-done.33 = bf16[128,384]{1,0:T(8,128)(2,1)S(1)} collective-permute-done((bf16[128,384]{1,0:T(8,128)(2,1)S(1)}, bf16[128,384]{1,0:T(8,128)(2,1)S(1)}, u32[]{:S(2)}, u32[]{:S(2)}) %collective-permute-start.33) | collective-permute-done | bytes 98336 | tf_op jit(solution)/shard_map/ppermute | solution.py:34
  93.2 3.1 %collective-permute-start.35 = (bf16[128,384]{1,0:T(8,128)(2,1)S(1)}, bf16[128,384]{1,0:T(8,128)(2,1)S(1)}, u32[]{:S(2)}, u32[]{:S(2)}) collective-permute-start(bf16[128,384]{1,0:T(8,128)(2,1)S(1)} %collective-permute-done.33), channel_id=1, source_target_pairs={{0,1},{1,2},{2,3},{3,4},{4,5},{5,6},{6,7},{7,0},{8,9},{9,10},{10,1... | collective-permute-start | bytes 294920 | tf_op jit(solution)/shard_map/ppermute | solution.py:34
  96.5 2.5 %collective-permute-done.35 = bf16[128,384]{1,0:T(8,128)(2,1)S(1)} collective-permute-done((bf16[128,384]{1,0:T(8,128)(2,1)S(1)}, bf16[128,384]{1,0:T(8,128)(2,1)S(1)}, u32[]{:S(2)}, u32[]{:S(2)}) %collective-permute-start.35) | collective-permute-done | bytes 98336 | tf_op jit(solution)/shard_map/ppermute | solution.py:34
  99.8 2.8 %collective-permute-done.27.refs_3_ = bf16[256,640]{1,0:T(8,128)(2,1)S(1)} collective-permute-done((bf16[256,640]{1,0:T(8,128)(2,1)S(1)}, bf16[256,640]{1,0:T(8,128)(2,1)S(1)}, u32[]{:S(2)}, u32[]{:S(2)}) %collective-permute-start.27) | collective-permute-done | bytes 327712 | tf_op jit(solution)/shard_map/ppermute | solution.py:34
  102.5 3.1 %collective-permute-start.29 = (bf16[256,640]{1,0:T(8,128)(2,1)S(1)}, bf16[256,640]{1,0:T(8,128)(2,1)S(1)}, u32[]{:S(2)}, u32[]{:S(2)}) collective-permute-start(bf16[256,640]{1,0:T(8,128)(2,1)S(1)} %collective-permute-done.27.refs_3_), channel_id=1, source_target_pairs={{0,1},{1,2},{2,3},{3,4},{4,5},{5,6},{6,7},{7,0},{8,9},{9,10},{10,1... | collective-permute-start | bytes 983048 | tf_op jit(solution)/shard_map/ppermute | solution.py:34
  106.1 2.3 %collective-permute-start.38 = (bf16[512,384]{1,0:T(8,128)(2,1)S(1)}, bf16[512,384]{1,0:T(8,128)(2,1)S(1)}, u32[]{:S(2)}, u32[]{:S(2)}) collective-permute-start(bf16[512,384]{1,0:T(8,128)(2,1)S(1)} %collective-permute-done.36.refs_9_), channel_id=1, source_target_pairs={{0,8},{1,9},{2,10},{3,11},{4,12},{5,13},{6,14},{7,15},{8,16},{9,17... | collective-permute-start | bytes 1179656 | tf_op jit(solution)/shard_map/ppermute | solution.py:34
  108.3 2.6 %collective-permute-done.28.refs_4_ = bf16[256,640]{1,0:T(8,128)(2,1)S(1)} collective-permute-done((bf16[256,640]{1,0:T(8,128)(2,1)S(1)}, bf16[256,640]{1,0:T(8,128)(2,1)S(1)}, u32[]{:S(2)}, u32[]{:S(2)}) %collective-permute-start.28) | collective-permute-done | bytes 327712 | tf_op jit(solution)/shard_map/ppermute | solution.py:34
  112.4 3.1 %collective-permute-start.31 = (bf16[256,640]{1,0:T(8,128)(2,1)S(1)}, bf16[256,640]{1,0:T(8,128)(2,1)S(1)}, u32[]{:S(2)}, u32[]{:S(2)}) collective-permute-start(bf16[256,640]{1,0:T(8,128)(2,1)S(1)} %collective-permute-done.29.refs_5_), channel_id=1, source_target_pairs={{0,1},{1,2},{2,3},{3,4},{4,5},{5,6},{6,7},{7,0},{8,9},{9,10},{10,1... | collective-permute-start | bytes 983048 | tf_op jit(solution)/shard_map/ppermute | solution.py:34
  117.2 4.1 %collective-permute-done.30.refs_6_ = bf16[256,640]{1,0:T(8,128)(2,1)S(1)} collective-permute-done((bf16[256,640]{1,0:T(8,128)(2,1)S(1)}, bf16[256,640]{1,0:T(8,128)(2,1)S(1)}, u32[]{:S(2)}, u32[]{:S(2)}) %collective-permute-start.30) | collective-permute-done | bytes 327712 | tf_op jit(solution)/shard_map/ppermute | solution.py:34
  121.6 5.0 %chain.3 = (bf16[128,1024]{1,0:T(8,128)(2,1)S(1)}, bf16[1024,1024]{1,0:T(8,128)(2,1)S(1)}, bf16[1024,1024]{1,0:T(8,128)(2,1)S(1)}) custom-call(s32[4]{0:T(128)S(1)} %pad_add_fusion.where, f32[2,32,1024]{2,1,0:T(8,128)S(1)} %get-tuple-element.28.keep, f32[2,32,1024]{2,1,0:T(8,128)S(1)} %get-tuple-element.27.other, ...), custom_call_target="tpu_custom_call" | custom-call | tf_op jit(solution)/shard_map/chain/pallas_call | solution.py:159
  126.6 6.8 %collective-permute-start.39 = (bf16[128,1024]{1,0:T(8,128)(2,1)S(1)}, bf16[128,1024]{1,0:T(8,128)(2,1)S(1)}, u32[]{:S(2)}, u32[]{:S(2)}) collective-permute-start(bf16[128,1024]{1,0:T(8,128)(2,1)S(1)} %get-tuple-element.24), channel_id=1, source_target_pairs={{32,0},{33,1},{34,2},{35,3},{36,4},{37,5},{38,6},{39,7},{40,8},{41... | collective-permute-start | bytes 786440 | tf_op jit(solution)/shard_map/ppermute | solution.py:34
  136.4 2.6 %collective-permute-done.40 = f32[4,32,1024]{2,1,0:T(8,128)S(1)} collective-permute-done((f32[4,32,1024]{2,1,0:T(8,128)S(1)}, f32[4,32,1024]{2,1,0:T(8,128)S(1)}, u32[]{:S(2)}, u32[]{:S(2)}) %collective-permute-start.40) | collective-permute-done | bytes 524320 | tf_op jit(solution)/shard_map/ppermute | solution.py:34
  (83 shorter events, 28.8 us)
Async XLA Ops:
  7.2 11.0 %collective-permute-start.3 = (bf16[64,640]{1,0:T(8,128)(2,1)S(1)}, bf16[64,640]{1,0:T(8,128)(2,1)S(1)}, u32[]{:S(2)}, u32[]{:S(2)}) collective-permute-start(bf16[64,640]{1,0:T(8,128)(2,1)S(1)} %slice.50), channel_id=1, source_target_pairs={{0,16},{1,17},{2,18},{3,19},{4,20},{5,21},{6,22},{7,23},{8,24},{9,... | collective-permute-start | bytes 245768 | tf_op jit(solution)/shard_map/ppermute | solution.py:34
  8.4 9.7 %collective-permute-start.2 = (bf16[64,640]{1,0:T(8,128)(2,1)S(1)}, bf16[64,640]{1,0:T(8,128)(2,1)S(1)}, u32[]{:S(2)}, u32[]{:S(2)}) collective-permute-start(bf16[64,640]{1,0:T(8,128)(2,1)S(1)} %slice.50), channel_id=1, source_target_pairs={{0,24},{1,25},{2,26},{3,27},{4,28},{5,29},{6,30},{7,31},{8,0},{9,1... | collective-permute-start | bytes 245768 | tf_op jit(solution)/shard_map/ppermute | solution.py:34
  8.8 9.3 %collective-permute-start.1 = (bf16[64,640]{1,0:T(8,128)(2,1)S(1)}, bf16[64,640]{1,0:T(8,128)(2,1)S(1)}, u32[]{:S(2)}, u32[]{:S(2)}) collective-permute-start(bf16[64,640]{1,0:T(8,128)(2,1)S(1)} %slice.50), channel_id=1, source_target_pairs={{0,8},{1,9},{2,10},{3,11},{4,12},{5,13},{6,14},{7,15},{8,16},{9,17... | collective-permute-start | bytes 245768 | tf_op jit(solution)/shard_map/ppermute | solution.py:34
  11.1 9.1 %collective-permute-start.11 = (bf16[64,384]{1,0:T(8,128)(2,1)S(1)}, bf16[64,384]{1,0:T(8,128)(2,1)S(1)}, u32[]{:S(2)}, u32[]{:S(2)}) collective-permute-start(bf16[64,384]{1,0:T(8,128)(2,1)S(1)} %get-tuple-element.39), channel_id=1, source_target_pairs={{0,4},{1,5},{2,6},{3,7},{4,0},{5,1},{6,2},{7,3},{8,12},{9,13},{10,... | collective-permute-start | bytes 147464 | tf_op jit(solution)/shard_map/ppermute | solution.py:34
  18.2 10.8 %collective-permute-start.4 = (bf16[256,640]{1,0:T(8,128)(2,1)S(1)}, bf16[256,640]{1,0:T(8,128)(2,1)S(1)}, u32[]{:S(2)}, u32[]{:S(2)}) collective-permute-start(bf16[256,640]{1,0:T(8,128)(2,1)S(1)} %pad_maximum_fusion.refs_0_), channel_id=1, source_target_pairs={{0,1},{1,2},{2,3},{3,4},{4,5},{5,6},{6,7},{7,0},{8,9},{9,10},{10,1... | collective-permute-start | bytes 983048 | tf_op jit(solution)/shard_map/ppermute | solution.py:34
  20.2 9.2 %collective-permute-start.13 = (bf16[128,384]{1,0:T(8,128)(2,1)S(1)}, bf16[128,384]{1,0:T(8,128)(2,1)S(1)}, u32[]{:S(2)}, u32[]{:S(2)}) collective-permute-start(bf16[128,384]{1,0:T(8,128)(2,1)S(1)} %pad_maximum_fusion.2), channel_id=1, source_target_pairs={{0,7},{1,0},{2,1},{3,2},{4,3},{5,4},{6,5},{7,6},{8,15},{9,8},{10,9... | collective-permute-start | bytes 294920 | tf_op jit(solution)/shard_map/ppermute | solution.py:34
  21.1 6.5 %collective-permute-start.12 = (bf16[128,384]{1,0:T(8,128)(2,1)S(1)}, bf16[128,384]{1,0:T(8,128)(2,1)S(1)}, u32[]{:S(2)}, u32[]{:S(2)}) collective-permute-start(bf16[128,384]{1,0:T(8,128)(2,1)S(1)} %pad_maximum_fusion.2), channel_id=1, source_target_pairs={{0,1},{1,2},{2,3},{3,4},{4,5},{5,6},{6,7},{7,0},{8,9},{9,10},{10,1... | collective-permute-start | bytes 294920 | tf_op jit(solution)/shard_map/ppermute | solution.py:34
  24.3 8.7 %collective-permute-start.5 = (bf16[256,640]{1,0:T(8,128)(2,1)S(1)}, bf16[256,640]{1,0:T(8,128)(2,1)S(1)}, u32[]{:S(2)}, u32[]{:S(2)}) collective-permute-start(bf16[256,640]{1,0:T(8,128)(2,1)S(1)} %pad_maximum_fusion.refs_0_), channel_id=1, source_target_pairs={{0,7},{1,0},{2,1},{3,2},{4,3},{5,4},{6,5},{7,6},{8,15},{9,8},{10,9... | collective-permute-start | bytes 983048 | tf_op jit(solution)/shard_map/ppermute | solution.py:34
  29.0 8.6 %collective-permute-start.6 = (bf16[256,640]{1,0:T(8,128)(2,1)S(1)}, bf16[256,640]{1,0:T(8,128)(2,1)S(1)}, u32[]{:S(2)}, u32[]{:S(2)}) collective-permute-start(bf16[256,640]{1,0:T(8,128)(2,1)S(1)} %collective-permute-done.4.refs_1_), channel_id=1, source_target_pairs={{0,1},{1,2},{2,3},{3,4},{4,5},{5,6},{6,7},{7,0},{8,9},{9,10},{10,1... | collective-permute-start | bytes 983048 | tf_op jit(solution)/shard_map/ppermute | solution.py:34
  32.4 8.4 %collective-permute-start.15 = (bf16[512,384]{1,0:T(8,128)(2,1)S(1)}, bf16[512,384]{1,0:T(8,128)(2,1)S(1)}, u32[]{:S(2)}, u32[]{:S(2)}) collective-permute-start(bf16[512,384]{1,0:T(8,128)(2,1)S(1)} %constant_dynamic-update-slice_fusion.refs_8_), channel_id=1, source_target_pairs={{0,8},{1,9},{2,10},{3,11},{4,12},{5,13},{6,14},{7,15},{8,16},{9,17... | collective-permute-start | bytes 1179656 | tf_op jit(solution)/shard_map/ppermute | solution.py:34
  32.9 11.3 %collective-permute-start.7 = (bf16[256,640]{1,0:T(8,128)(2,1)S(1)}, bf16[256,640]{1,0:T(8,128)(2,1)S(1)}, u32[]{:S(2)}, u32[]{:S(2)}) collective-permute-start(bf16[256,640]{1,0:T(8,128)(2,1)S(1)} %collective-permute-done.5.refs_2_), channel_id=1, source_target_pairs={{0,7},{1,0},{2,1},{3,2},{4,3},{5,4},{6,5},{7,6},{8,15},{9,8},{10,9... | collective-permute-start | bytes 983048 | tf_op jit(solution)/shard_map/ppermute | solution.py:34
  37.5 10.5 %collective-permute-start.8 = (bf16[256,640]{1,0:T(8,128)(2,1)S(1)}, bf16[256,640]{1,0:T(8,128)(2,1)S(1)}, u32[]{:S(2)}, u32[]{:S(2)}) collective-permute-start(bf16[256,640]{1,0:T(8,128)(2,1)S(1)} %collective-permute-done.6.refs_3_), channel_id=1, source_target_pairs={{0,1},{1,2},{2,3},{3,4},{4,5},{5,6},{6,7},{7,0},{8,9},{9,10},{10,1... | collective-permute-start | bytes 983048 | tf_op jit(solution)/shard_map/ppermute | solution.py:34
  40.6 11.1 %collective-permute-start.16 = (bf16[512,384]{1,0:T(8,128)(2,1)S(1)}, bf16[512,384]{1,0:T(8,128)(2,1)S(1)}, u32[]{:S(2)}, u32[]{:S(2)}) collective-permute-start(bf16[512,384]{1,0:T(8,128)(2,1)S(1)} %constant_dynamic-update-slice_fusion.refs_8_), channel_id=1, source_target_pairs={{0,24},{1,25},{2,26},{3,27},{4,28},{5,29},{6,30},{7,31},{8,0},{9,1... | collective-permute-start | bytes 1179656 | tf_op jit(solution)/shard_map/ppermute | solution.py:34
  40.8 10.8 %collective-permute-start.17 = (bf16[512,384]{1,0:T(8,128)(2,1)S(1)}, bf16[512,384]{1,0:T(8,128)(2,1)S(1)}, u32[]{:S(2)}, u32[]{:S(2)}) collective-permute-start(bf16[512,384]{1,0:T(8,128)(2,1)S(1)} %collective-permute-done.15.refs_9_), channel_id=1, source_target_pairs={{0,8},{1,9},{2,10},{3,11},{4,12},{5,13},{6,14},{7,15},{8,16},{9,17... | collective-permute-start | bytes 1179656 | tf_op jit(solution)/shard_map/ppermute | solution.py:34
  44.3 9.4 %collective-permute-start.9 = (bf16[256,640]{1,0:T(8,128)(2,1)S(1)}, bf16[256,640]{1,0:T(8,128)(2,1)S(1)}, u32[]{:S(2)}, u32[]{:S(2)}) collective-permute-start(bf16[256,640]{1,0:T(8,128)(2,1)S(1)} %collective-permute-done.7.refs_4_), channel_id=1, source_target_pairs={{0,7},{1,0},{2,1},{3,2},{4,3},{5,4},{6,5},{7,6},{8,15},{9,8},{10,9... | collective-permute-start | bytes 983048 | tf_op jit(solution)/shard_map/ppermute | solution.py:34
  48.0 10.0 %collective-permute-start.10 = (bf16[256,640]{1,0:T(8,128)(2,1)S(1)}, bf16[256,640]{1,0:T(8,128)(2,1)S(1)}, u32[]{:S(2)}, u32[]{:S(2)}) collective-permute-start(bf16[256,640]{1,0:T(8,128)(2,1)S(1)} %collective-permute-done.8.refs_5_), channel_id=1, source_target_pairs={{0,1},{1,2},{2,3},{3,4},{4,5},{5,6},{6,7},{7,0},{8,9},{9,10},{10,1... | collective-permute-start | bytes 983048 | tf_op jit(solution)/shard_map/ppermute | solution.py:34
  69.1 8.1 %collective-permute-start.21 = (bf16[2,32,1024]{2,1,0:T(8,128)(2,1)S(1)}, bf16[2,32,1024]{2,1,0:T(8,128)(2,1)S(1)}, u32[]{:S(2)}, u32[]{:S(2)}) collective-permute-start(bf16[2,32,1024]{2,1,0:T(8,128)(2,1)S(1)} %get-tuple-element.22), channel_id=1, source_target_pairs={{0,96},{1,97},{2,98},{3,99},{4,100},{5,101},{6,102},{7,103},{8,104... | collective-permute-start | bytes 393224 | tf_op jit(solution)/shard_map/ppermute | solution.py:34
  70.4 6.9 %collective-permute-start.20 = (bf16[2,32,1024]{2,1,0:T(8,128)(2,1)S(1)}, bf16[2,32,1024]{2,1,0:T(8,128)(2,1)S(1)}, u32[]{:S(2)}, u32[]{:S(2)}) collective-permute-start(bf16[2,32,1024]{2,1,0:T(8,128)(2,1)S(1)} %get-tuple-element.22), channel_id=1, source_target_pairs={{0,32},{1,33},{2,34},{3,35},{4,36},{5,37},{6,38},{7,39},{8,40},{9,... | collective-permute-start | bytes 393224 | tf_op jit(solution)/shard_map/ppermute | solution.py:34
  77.4 6.4 %collective-permute-start.24 = (bf16[64,640]{1,0:T(8,128)(2,1)S(1)}, bf16[64,640]{1,0:T(8,128)(2,1)S(1)}, u32[]{:S(2)}, u32[]{:S(2)}) collective-permute-start(bf16[64,640]{1,0:T(8,128)(2,1)S(1)} %slice.56), channel_id=1, source_target_pairs={{0,16},{1,17},{2,18},{3,19},{4,20},{5,21},{6,22},{7,23},{8,24},{9,... | collective-permute-start | bytes 245768 | tf_op jit(solution)/shard_map/ppermute | solution.py:34
  80.8 7.4 %collective-permute-start.32 = (bf16[64,384]{1,0:T(8,128)(2,1)S(1)}, bf16[64,384]{1,0:T(8,128)(2,1)S(1)}, u32[]{:S(2)}, u32[]{:S(2)}) collective-permute-start(bf16[64,384]{1,0:T(8,128)(2,1)S(1)} %get-tuple-element.37), channel_id=1, source_target_pairs={{0,4},{1,5},{2,6},{3,7},{4,0},{5,1},{6,2},{7,3},{8,12},{9,13},{10,... | collective-permute-start | bytes 147464 | tf_op jit(solution)/shard_map/ppermute | solution.py:34
  84.1 12.3 %collective-permute-start.25 = (bf16[256,640]{1,0:T(8,128)(2,1)S(1)}, bf16[256,640]{1,0:T(8,128)(2,1)S(1)}, u32[]{:S(2)}, u32[]{:S(2)}) collective-permute-start(bf16[256,640]{1,0:T(8,128)(2,1)S(1)} %pad_maximum_fusion.1.refs_0_), channel_id=1, source_target_pairs={{0,1},{1,2},{2,3},{3,4},{4,5},{5,6},{6,7},{7,0},{8,9},{9,10},{10,1... | collective-permute-start | bytes 983048 | tf_op jit(solution)/shard_map/ppermute | solution.py:34
  88.3 8.2 %collective-permute-start.34 = (bf16[128,384]{1,0:T(8,128)(2,1)S(1)}, bf16[128,384]{1,0:T(8,128)(2,1)S(1)}, u32[]{:S(2)}, u32[]{:S(2)}) collective-permute-start(bf16[128,384]{1,0:T(8,128)(2,1)S(1)} %pad_maximum_fusion.3), channel_id=1, source_target_pairs={{0,7},{1,0},{2,1},{3,2},{4,3},{5,4},{6,5},{7,6},{8,15},{9,8},{10,9... | collective-permute-start | bytes 294920 | tf_op jit(solution)/shard_map/ppermute | solution.py:34
  91.0 8.8 %collective-permute-start.26 = (bf16[256,640]{1,0:T(8,128)(2,1)S(1)}, bf16[256,640]{1,0:T(8,128)(2,1)S(1)}, u32[]{:S(2)}, u32[]{:S(2)}) collective-permute-start(bf16[256,640]{1,0:T(8,128)(2,1)S(1)} %pad_maximum_fusion.1.refs_0_), channel_id=1, source_target_pairs={{0,7},{1,0},{2,1},{3,2},{4,3},{5,4},{6,5},{7,6},{8,15},{9,8},{10,9... | collective-permute-start | bytes 983048 | tf_op jit(solution)/shard_map/ppermute | solution.py:34
  96.4 6.1 %collective-permute-start.27 = (bf16[256,640]{1,0:T(8,128)(2,1)S(1)}, bf16[256,640]{1,0:T(8,128)(2,1)S(1)}, u32[]{:S(2)}, u32[]{:S(2)}) collective-permute-start(bf16[256,640]{1,0:T(8,128)(2,1)S(1)} %collective-permute-done.25.refs_1_), channel_id=1, source_target_pairs={{0,1},{1,2},{2,3},{3,4},{4,5},{5,6},{6,7},{7,0},{8,9},{9,10},{10,1... | collective-permute-start | bytes 983048 | tf_op jit(solution)/shard_map/ppermute | solution.py:34
  99.1 7.0 %collective-permute-start.36 = (bf16[512,384]{1,0:T(8,128)(2,1)S(1)}, bf16[512,384]{1,0:T(8,128)(2,1)S(1)}, u32[]{:S(2)}, u32[]{:S(2)}) collective-permute-start(bf16[512,384]{1,0:T(8,128)(2,1)S(1)} %constant_dynamic-update-slice_fusion.5.refs_8_), channel_id=1, source_target_pairs={{0,8},{1,9},{2,10},{3,11},{4,12},{5,13},{6,14},{7,15},{8,16},{9,17... | collective-permute-start | bytes 1179656 | tf_op jit(solution)/shard_map/ppermute | solution.py:34
  99.8 11.1 %collective-permute-start.28 = (bf16[256,640]{1,0:T(8,128)(2,1)S(1)}, bf16[256,640]{1,0:T(8,128)(2,1)S(1)}, u32[]{:S(2)}, u32[]{:S(2)}) collective-permute-start(bf16[256,640]{1,0:T(8,128)(2,1)S(1)} %collective-permute-done.26.refs_2_), channel_id=1, source_target_pairs={{0,7},{1,0},{2,1},{3,2},{4,3},{5,4},{6,5},{7,6},{8,15},{9,8},{10,9... | collective-permute-start | bytes 983048 | tf_op jit(solution)/shard_map/ppermute | solution.py:34
  102.5 9.9 %collective-permute-start.29 = (bf16[256,640]{1,0:T(8,128)(2,1)S(1)}, bf16[256,640]{1,0:T(8,128)(2,1)S(1)}, u32[]{:S(2)}, u32[]{:S(2)}) collective-permute-start(bf16[256,640]{1,0:T(8,128)(2,1)S(1)} %collective-permute-done.27.refs_3_), channel_id=1, source_target_pairs={{0,1},{1,2},{2,3},{3,4},{4,5},{5,6},{6,7},{7,0},{8,9},{9,10},{10,1... | collective-permute-start | bytes 983048 | tf_op jit(solution)/shard_map/ppermute | solution.py:34
  105.7 11.5 %collective-permute-start.37 = (bf16[512,384]{1,0:T(8,128)(2,1)S(1)}, bf16[512,384]{1,0:T(8,128)(2,1)S(1)}, u32[]{:S(2)}, u32[]{:S(2)}) collective-permute-start(bf16[512,384]{1,0:T(8,128)(2,1)S(1)} %constant_dynamic-update-slice_fusion.5.refs_8_), channel_id=1, source_target_pairs={{0,24},{1,25},{2,26},{3,27},{4,28},{5,29},{6,30},{7,31},{8,0},{9,1... | collective-permute-start | bytes 1179656 | tf_op jit(solution)/shard_map/ppermute | solution.py:34
  106.1 11.1 %collective-permute-start.38 = (bf16[512,384]{1,0:T(8,128)(2,1)S(1)}, bf16[512,384]{1,0:T(8,128)(2,1)S(1)}, u32[]{:S(2)}, u32[]{:S(2)}) collective-permute-start(bf16[512,384]{1,0:T(8,128)(2,1)S(1)} %collective-permute-done.36.refs_9_), channel_id=1, source_target_pairs={{0,8},{1,9},{2,10},{3,11},{4,12},{5,13},{6,14},{7,15},{8,16},{9,17... | collective-permute-start | bytes 1179656 | tf_op jit(solution)/shard_map/ppermute | solution.py:34
  110.9 10.4 %collective-permute-start.30 = (bf16[256,640]{1,0:T(8,128)(2,1)S(1)}, bf16[256,640]{1,0:T(8,128)(2,1)S(1)}, u32[]{:S(2)}, u32[]{:S(2)}) collective-permute-start(bf16[256,640]{1,0:T(8,128)(2,1)S(1)} %collective-permute-done.28.refs_4_), channel_id=1, source_target_pairs={{0,7},{1,0},{2,1},{3,2},{4,3},{5,4},{6,5},{7,6},{8,15},{9,8},{10,9... | collective-permute-start | bytes 983048 | tf_op jit(solution)/shard_map/ppermute | solution.py:34
  112.4 9.1 %collective-permute-start.31 = (bf16[256,640]{1,0:T(8,128)(2,1)S(1)}, bf16[256,640]{1,0:T(8,128)(2,1)S(1)}, u32[]{:S(2)}, u32[]{:S(2)}) collective-permute-start(bf16[256,640]{1,0:T(8,128)(2,1)S(1)} %collective-permute-done.29.refs_5_), channel_id=1, source_target_pairs={{0,1},{1,2},{2,3},{3,4},{4,5},{5,6},{6,7},{7,0},{8,9},{9,10},{10,1... | collective-permute-start | bytes 983048 | tf_op jit(solution)/shard_map/ppermute | solution.py:34
  126.6 8.0 %collective-permute-start.39 = (bf16[128,1024]{1,0:T(8,128)(2,1)S(1)}, bf16[128,1024]{1,0:T(8,128)(2,1)S(1)}, u32[]{:S(2)}, u32[]{:S(2)}) collective-permute-start(bf16[128,1024]{1,0:T(8,128)(2,1)S(1)} %get-tuple-element.24), channel_id=1, source_target_pairs={{32,0},{33,1},{34,2},{35,3},{36,4},{37,5},{38,6},{39,7},{40,8},{41... | collective-permute-start | bytes 786440 | tf_op jit(solution)/shard_map/ppermute | solution.py:34
  (11 other events, 45.4 us)

commit v5 on v4

--- a/solution.py
+++ b/solution.py
@@ -10,8 +10,7 @@
 BLK = 64
 NX, NC, NY, NZ = 4, 2, 4, 8
 AXES = ("slab", "panel")
-SPLIT = 640
-PARTS = NZ + NY
+PARTS = 8
 
 
 def device(x, c, y, z):
@@ -43,28 +42,21 @@
 
 
 def gather(block):
-    wide_a, wide_b = block[:, :SPLIT], block[:, SPLIT:]
-    wide_a = jnp.concatenate([wide_a] + [send(wide_a, hop("y", d)) for d in Y_BACK[1:]])
-    wide_b = jnp.concatenate([wide_b, send(wide_b, hop("z", 4))])
+    pair = send(block, hop("z", NZ // 2))
+    wide_a = jnp.concatenate([block[:32], pair[:32]])
+    wide_b = jnp.concatenate([block[32:], pair[32:]])
+    ahead, behind = send(wide_a, hop("y", 1)), send(wide_a, hop("y", -1))
+    wide_a = jnp.concatenate([wide_a, ahead, behind, send(wide_a, hop("y", 2))])
     ahead, behind = send(wide_b, hop("z", 1)), send(wide_b, hop("z", -1))
     wide_b = jnp.concatenate([wide_b, ahead, behind, send(ahead, hop("z", 1))])
-    parts_a, parts_b = [wide_a], [wide_b]
-    ahead, behind = wide_a, wide_a
-    for back in Z_BACK_A[1:]:
-        if back > 0:
-            ahead = send(ahead, hop("z", 1))
-            parts_a.append(ahead)
-        else:
-            behind = send(behind, hop("z", -1))
-            parts_a.append(behind)
+    ahead, behind = send(wide_a, hop("z", 1)), send(wide_a, hop("z", -1))
+    parts_a = [wide_a, ahead, behind, send(ahead, hop("z", 1))]
     ahead, behind = send(wide_b, hop("y", 1)), send(wide_b, hop("y", -1))
-    parts_b += [ahead, behind, send(ahead, hop("y", 1))]
+    parts_b = [wide_b, ahead, behind, send(ahead, hop("y", 1))]
     return parts_a, parts_b
 
 
-Y_BACK = (0, 1, -1, 2)
-Z_BACK_A = (0, 1, -1, 2, -2, 3, -3, 4)
-Z_BACK_B = (0, 4, 1, 5, -1, 3, 2, 6)
+BACK = (0, 1, -1, 2)
 
 
 def row_of(y, z):
@@ -72,18 +64,15 @@
 
 
 def order(where, parts, first, second):
-    parts_a, parts_b = parts[:NZ], parts[NZ:]
     way, y, z = 1 - 2 * where[0], where[1], where[2]
-    for z_back, part in zip(Z_BACK_A, parts_a):
-        for k, y_back in enumerate(Y_BACK):
-            at = pl.ds(row_of(y - way * y_back, z - way * z_back), 32)
-            first[at, :SPLIT] = part[pl.ds(k * 64, 32)]
-            second[at, :SPLIT] = part[pl.ds(k * 64 + 32, 32)]
-    for y_back, part in zip(Y_BACK, parts_b):
-        for k, z_back in enumerate(Z_BACK_B):
-            at = pl.ds(row_of(y - way * y_back, z - way * z_back), 32)
-            first[at, SPLIT:] = part[pl.ds(k * 64, 32)]
-            second[at, SPLIT:] = part[pl.ds(k * 64 + 32, 32)]
+    for part_a, part_b, outer in zip(parts[:4], parts[4:], BACK):
+        for k, inner in enumerate(BACK):
+            for j, far in enumerate((0, NZ // 2)):
+                piece = pl.ds((2 * k + j) * 32, 32)
+                at = pl.ds(row_of(y - way * inner, z - way * (outer + far)), 32)
+                first[at] = part_a[piece]
+                at = pl.ds(row_of(y - way * outer, z - way * (inner + far)), 32)
+                second[at] = part_b[piece]
 
 
 def wide_dot(left, factor, out):
@@ -92,7 +81,15 @@
     )
 
 
-def mask_kernel(where, pattern, ranges, keep, give):
+def mask_kernel(where, pattern_hbm, ranges_hbm, keep, give, pattern, ranges, sems):
+    copies = [
+        pltpu.make_async_copy(pattern_hbm, pattern, sems.at[0]),
+        pltpu.make_async_copy(ranges_hbm, ranges, sems.at[1]),
+    ]
+    for copy in copies:
+        copy.start()
+    for copy in copies:
+        copy.wait()
     block_row = pl.ds(lax.div(where[1] * NZ + where[2], BLK // 32), 1)
     count = M // BLK
     spread = (
@@ -113,8 +110,13 @@
     return pl.pallas_call(
         mask_kernel,
         out_shape=[jax.ShapeDtypeStruct((2, 32, M), jnp.float32)] * 2,
-        in_specs=[SMEM, VMEM, VMEM],
+        in_specs=[SMEM] + [pl.BlockSpec(memory_space=pl.ANY)] * 2,
         out_specs=[VMEM, VMEM],
+        scratch_shapes=[
+            pltpu.VMEM((4, M // BLK, M // BLK), jnp.int32),
+            pltpu.VMEM((4, 32, M), jnp.float32),
+            pltpu.SemaphoreType.DMA((2,)),
+        ],
         compiler_params=pltpu.CompilerParams(vmem_limit_bytes=8 << 20),
         name="masked",
     )(where, pattern, ranges)

time: 140 us -> 150 us (1.071)
  waiting for transfers between devices: 56.4 us -> 65.3 us
    ppermute x41 -> x33, waiting for transfers between devices: 56.4 us -> 65.3 us  [send(): return lax.ppermute(block, AXES, route(move))]
    ppermute x41 -> x33, starting transfers between devices: 68.1 us -> 68.8 us  [send(): return lax.ppermute(block, AXES, route(move))]
  transfers between devices with their start and end apart: 41 -> 33, of which waited for: 26 -> 20; matrix products, arithmetic and copies ran while one was open for 0% -> 0% of each run, Pallas kernels for 0% -> 0%
where the time goes in v5:
time: 150 us
  starting transfers between devices  68.8 us (46%)
  waiting for transfers between devices  65.3 us (44%)
  Pallas kernels  12.1 us (8%)
  local copies, waits for them, and re-layouts  2.05 us (1%)
    ppermute x33, starting transfers between devices, send(): return lax.ppermute(block, AXES, route(move))  68.8 us
    ppermute x33, waiting for transfers between devices, send(): return lax.ppermute(block, AXES, route(move))  65.3 us
    pallas_call x2, Pallas kernels, chain(): pl.pallas_call(chain_kernel, out_shape=[jax.ShapeDtypeStruct((128, M), jn...  10 us
  transfers between devices with their start and end apart: 33, of which 20 were waited for; matrix products, arithmetic and copies ran while one was open for 0% of the time, Pallas kernels for 0%

profile of v5, /device:TPU:1, one launch (start us, length us, event | category | flops | bytes accessed | tf_op | source)
XLA Modules:
  0.0 149.6 jit_solution(17892541200193449973)
XLA Ops:
  2.7 3.3 %collective-permute-start = (f32[2,32,1024]{2,1,0:T(8,128)S(1)}, f32[2,32,1024]{2,1,0:T(8,128)S(1)}, u32[]{:S(2)}, u32[]{:S(2)}) collective-permute-start(f32[2,32,1024]{2,1,0:T(8,128)S(1)} %get-tuple-element.17), channel_id=1, source_target_pairs={{0,32},{1,33},{2,34},{3,35},{4,36},{5,37},{6,38},{7,39},{8,40},{9,... | collective-permute-start | bytes 786440 | tf_op jit(solution)/shard_map/ppermute | solution.py:33
  7.2 5.3 %collective-permute-start.1 = (bf16[64,1024]{1,0:T(8,128)(2,1)S(1)}, bf16[64,1024]{1,0:T(8,128)(2,1)S(1)}, u32[]{:S(2)}, u32[]{:S(2)}) collective-permute-start(bf16[64,1024]{1,0:T(8,128)(2,1)S(1)} %fusion), channel_id=1, source_target_pairs={{0,4},{1,5},{2,6},{3,7},{4,0},{5,1},{6,2},{7,3},{8,12},{9,13},{10,... | collective-permute-start | bytes 393224 | tf_op jit(solution)/shard_map/ppermute | solution.py:33
  12.5 3.4 %collective-permute-done.1 = bf16[64,1024]{1,0:T(8,128)(2,1)S(1)} collective-permute-done((bf16[64,1024]{1,0:T(8,128)(2,1)S(1)}, bf16[64,1024]{1,0:T(8,128)(2,1)S(1)}, u32[]{:S(2)}, u32[]{:S(2)}) %collective-permute-start.1) | collective-permute-done | bytes 131104 | tf_op jit(solution)/shard_map/ppermute | solution.py:33
  16.0 2.9 %collective-permute-start.2 = (bf16[64,1024]{1,0:T(8,128)(2,1)S(1)}, bf16[64,1024]{1,0:T(8,128)(2,1)S(1)}, u32[]{:S(2)}, u32[]{:S(2)}) collective-permute-start(bf16[64,1024]{1,0:T(8,128)(2,1)S(1)} %pad_maximum_fusion), channel_id=1, source_target_pairs={{0,8},{1,9},{2,10},{3,11},{4,12},{5,13},{6,14},{7,15},{8,16},{9,17... | collective-permute-start | bytes 393224 | tf_op jit(solution)/shard_map/ppermute | solution.py:33
  20.0 3.6 %collective-permute-start.9 = (bf16[64,1024]{1,0:T(8,128)(2,1)S(1)}, bf16[64,1024]{1,0:T(8,128)(2,1)S(1)}, u32[]{:S(2)}, u32[]{:S(2)}) collective-permute-start(bf16[64,1024]{1,0:T(8,128)(2,1)S(1)} %pad_maximum_fusion.1), channel_id=1, source_target_pairs={{0,7},{1,0},{2,1},{3,2},{4,3},{5,4},{6,5},{7,6},{8,15},{9,8},{10,9... | collective-permute-start | bytes 393224 | tf_op jit(solution)/shard_map/ppermute | solution.py:33
  23.6 2.0 %collective-permute-start.8 = (bf16[64,1024]{1,0:T(8,128)(2,1)S(1)}, bf16[64,1024]{1,0:T(8,128)(2,1)S(1)}, u32[]{:S(2)}, u32[]{:S(2)}) collective-permute-start(bf16[64,1024]{1,0:T(8,128)(2,1)S(1)} %pad_maximum_fusion.1), channel_id=1, source_target_pairs={{0,1},{1,2},{2,3},{3,4},{4,5},{5,6},{6,7},{7,0},{8,9},{9,10},{10,1... | collective-permute-start | bytes 393224 | tf_op jit(solution)/shard_map/ppermute | solution.py:33
  26.6 6.3 %collective-permute-start.5 = (bf16[256,1024]{1,0:T(8,128)(2,1)S(1)}, bf16[256,1024]{1,0:T(8,128)(2,1)S(1)}, u32[]{:S(2)}, u32[]{:S(2)}) collective-permute-start(bf16[256,1024]{1,0:T(8,128)(2,1)S(1)} %constant_dynamic-update-slice_fusion.refs_0_), channel_id=1, source_target_pairs={{0,1},{1,2},{2,3},{3,4},{4,5},{5,6},{6,7},{7,0},{8,9},{9,10},{10,1... | collective-permute-start | bytes 1572872 | tf_op jit(solution)/shard_map/ppermute | solution.py:33
  33.8 6.7 %collective-permute-done.10 = bf16[64,1024]{1,0:T(8,128)(2,1)S(1)} collective-permute-done((bf16[64,1024]{1,0:T(8,128)(2,1)S(1)}, bf16[64,1024]{1,0:T(8,128)(2,1)S(1)}, u32[]{:S(2)}, u32[]{:S(2)}) %collective-permute-start.10) | collective-permute-done | bytes 131104 | tf_op jit(solution)/shard_map/ppermute | solution.py:33
  42.1 3.0 %collective-permute-start.7 = (bf16[256,1024]{1,0:T(8,128)(2,1)S(1)}, bf16[256,1024]{1,0:T(8,128)(2,1)S(1)}, u32[]{:S(2)}, u32[]{:S(2)}) collective-permute-start(bf16[256,1024]{1,0:T(8,128)(2,1)S(1)} %collective-permute-done.5.refs_1_), channel_id=1, source_target_pairs={{0,1},{1,2},{2,3},{3,4},{4,5},{5,6},{6,7},{7,0},{8,9},{9,10},{10,1... | collective-permute-start | bytes 1572872 | tf_op jit(solution)/shard_map/ppermute | solution.py:33
  45.1 3.9 %collective-permute-done.11.refs_5_ = bf16[256,1024]{1,0:T(8,128)(2,1)S(1)} collective-permute-done((bf16[256,1024]{1,0:T(8,128)(2,1)S(1)}, bf16[256,1024]{1,0:T(8,128)(2,1)S(1)}, u32[]{:S(2)}, u32[]{:S(2)}) %collective-permute-start.11) | collective-permute-done | bytes 524320 | tf_op jit(solution)/shard_map/ppermute | solution.py:33
  49.0 1.7 %collective-permute-start.13 = (bf16[256,1024]{1,0:T(8,128)(2,1)S(1)}, bf16[256,1024]{1,0:T(8,128)(2,1)S(1)}, u32[]{:S(2)}, u32[]{:S(2)}) collective-permute-start(bf16[256,1024]{1,0:T(8,128)(2,1)S(1)} %collective-permute-done.11.refs_5_), channel_id=1, source_target_pairs={{0,8},{1,9},{2,10},{3,11},{4,12},{5,13},{6,14},{7,15},{8,16},{9,17... | collective-permute-start | bytes 1572872 | tf_op jit(solution)/shard_map/ppermute | solution.py:33
  51.5 5.4 %collective-permute-done.12.refs_6_ = bf16[256,1024]{1,0:T(8,128)(2,1)S(1)} collective-permute-done((bf16[256,1024]{1,0:T(8,128)(2,1)S(1)}, bf16[256,1024]{1,0:T(8,128)(2,1)S(1)}, u32[]{:S(2)}, u32[]{:S(2)}) %collective-permute-start.12) | collective-permute-done | bytes 524320 | tf_op jit(solution)/shard_map/ppermute | solution.py:33
  56.9 3.7 %collective-permute-done.13.refs_7_ = bf16[256,1024]{1,0:T(8,128)(2,1)S(1)} collective-permute-done((bf16[256,1024]{1,0:T(8,128)(2,1)S(1)}, bf16[256,1024]{1,0:T(8,128)(2,1)S(1)}, u32[]{:S(2)}, u32[]{:S(2)}) %collective-permute-start.13) | collective-permute-done | bytes 524320 | tf_op jit(solution)/shard_map/ppermute | solution.py:33
  60.5 5.0 %chain.2 = (bf16[128,1024]{1,0:T(8,128)(2,1)S(1)}, bf16[1024,1024]{1,0:T(8,128)(2,1)S(1)}, bf16[1024,1024]{1,0:T(8,128)(2,1)S(1)}) custom-call(s32[4]{0:T(128)S(1)} %pad_add_fusion.where, f32[2,32,1024]{2,1,0:T(8,128)S(1)} %get-tuple-element.16.keep, f32[2,32,1024]{2,1,0:T(8,128)S(1)} %collective-permute-done.other, ...), custom_call_target="tpu_custom_call" | custom-call | tf_op jit(solution)/shard_map/chain/pallas_call | solution.py:161
  65.6 5.4 %collective-permute-start.14 = (bf16[128,1024]{1,0:T(8,128)(2,1)S(1)}, bf16[128,1024]{1,0:T(8,128)(2,1)S(1)}, u32[]{:S(2)}, u32[]{:S(2)}) collective-permute-start(bf16[128,1024]{1,0:T(8,128)(2,1)S(1)} %get-tuple-element.18), channel_id=1, source_target_pairs={{32,0},{33,1},{34,2},{35,3},{36,4},{37,5},{38,6},{39,7},{40,8},{41... | collective-permute-start | bytes 786440 | tf_op jit(solution)/shard_map/ppermute | solution.py:33
  76.1 5.5 %collective-permute-done.17 = bf16[2,32,1024]{2,1,0:T(8,128)(2,1)S(1)} collective-permute-done((bf16[2,32,1024]{2,1,0:T(8,128)(2,1)S(1)}, bf16[2,32,1024]{2,1,0:T(8,128)(2,1)S(1)}, u32[]{:S(2)}, u32[]{:S(2)}) %collective-permute-start.17) | collective-permute-done | bytes 131104 | tf_op jit(solution)/shard_map/ppermute | solution.py:33
  81.8 4.0 %collective-permute-start.18 = (bf16[64,1024]{1,0:T(8,128)(2,1)S(1)}, bf16[64,1024]{1,0:T(8,128)(2,1)S(1)}, u32[]{:S(2)}, u32[]{:S(2)}) collective-permute-start(bf16[64,1024]{1,0:T(8,128)(2,1)S(1)} %fusion.1), channel_id=1, source_target_pairs={{0,4},{1,5},{2,6},{3,7},{4,0},{5,1},{6,2},{7,3},{8,12},{9,13},{10,... | collective-permute-start | bytes 393224 | tf_op jit(solution)/shard_map/ppermute | solution.py:33
  85.8 5.3 %collective-permute-done.18 = bf16[64,1024]{1,0:T(8,128)(2,1)S(1)} collective-permute-done((bf16[64,1024]{1,0:T(8,128)(2,1)S(1)}, bf16[64,1024]{1,0:T(8,128)(2,1)S(1)}, u32[]{:S(2)}, u32[]{:S(2)}) %collective-permute-start.18) | collective-permute-done | bytes 131104 | tf_op jit(solution)/shard_map/ppermute | solution.py:33
  92.7 3.0 %collective-permute-start.26 = (bf16[64,1024]{1,0:T(8,128)(2,1)S(1)}, bf16[64,1024]{1,0:T(8,128)(2,1)S(1)}, u32[]{:S(2)}, u32[]{:S(2)}) collective-permute-start(bf16[64,1024]{1,0:T(8,128)(2,1)S(1)} %pad_maximum_fusion.3), channel_id=1, source_target_pairs={{0,7},{1,0},{2,1},{3,2},{4,3},{5,4},{6,5},{7,6},{8,15},{9,8},{10,9... | collective-permute-start | bytes 393224 | tf_op jit(solution)/shard_map/ppermute | solution.py:33
  95.8 2.4 %collective-permute-start.25 = (bf16[64,1024]{1,0:T(8,128)(2,1)S(1)}, bf16[64,1024]{1,0:T(8,128)(2,1)S(1)}, u32[]{:S(2)}, u32[]{:S(2)}) collective-permute-start(bf16[64,1024]{1,0:T(8,128)(2,1)S(1)} %pad_maximum_fusion.3), channel_id=1, source_target_pairs={{0,1},{1,2},{2,3},{3,4},{4,5},{5,6},{6,7},{7,0},{8,9},{9,10},{10,1... | collective-permute-start | bytes 393224 | tf_op jit(solution)/shard_map/ppermute | solution.py:33
  98.2 3.0 %collective-permute-done.20 = bf16[64,1024]{1,0:T(8,128)(2,1)S(1)} collective-permute-done((bf16[64,1024]{1,0:T(8,128)(2,1)S(1)}, bf16[64,1024]{1,0:T(8,128)(2,1)S(1)}, u32[]{:S(2)}, u32[]{:S(2)}) %collective-permute-start.20) | collective-permute-done | bytes 131104 | tf_op jit(solution)/shard_map/ppermute | solution.py:33
  101.2 5.4 %collective-permute-start.22 = (bf16[256,1024]{1,0:T(8,128)(2,1)S(1)}, bf16[256,1024]{1,0:T(8,128)(2,1)S(1)}, u32[]{:S(2)}, u32[]{:S(2)}) collective-permute-start(bf16[256,1024]{1,0:T(8,128)(2,1)S(1)} %constant_dynamic-update-slice_fusion.10.refs_0_), channel_id=1, source_target_pairs={{0,1},{1,2},{2,3},{3,4},{4,5},{5,6},{6,7},{7,0},{8,9},{9,10},{10,1... | collective-permute-start | bytes 1572872 | tf_op jit(solution)/shard_map/ppermute | solution.py:33
  106.6 1.5 collective-permute-start.27
  108.1 6.0 %collective-permute-done.27 = bf16[64,1024]{1,0:T(8,128)(2,1)S(1)} collective-permute-done((bf16[64,1024]{1,0:T(8,128)(2,1)S(1)}, bf16[64,1024]{1,0:T(8,128)(2,1)S(1)}, u32[]{:S(2)}, u32[]{:S(2)}) %collective-permute-start.27) | collective-permute-done | bytes 131104 | tf_op jit(solution)/shard_map/ppermute | solution.py:33
  115.7 3.1 %collective-permute-start.24 = (bf16[256,1024]{1,0:T(8,128)(2,1)S(1)}, bf16[256,1024]{1,0:T(8,128)(2,1)S(1)}, u32[]{:S(2)}, u32[]{:S(2)}) collective-permute-start(bf16[256,1024]{1,0:T(8,128)(2,1)S(1)} %collective-permute-done.22.refs_1_), channel_id=1, source_target_pairs={{0,1},{1,2},{2,3},{3,4},{4,5},{5,6},{6,7},{7,0},{8,9},{9,10},{10,1... | collective-permute-start | bytes 1572872 | tf_op jit(solution)/shard_map/ppermute | solution.py:33
  118.8 5.0 %collective-permute-done.28.refs_5_ = bf16[256,1024]{1,0:T(8,128)(2,1)S(1)} collective-permute-done((bf16[256,1024]{1,0:T(8,128)(2,1)S(1)}, bf16[256,1024]{1,0:T(8,128)(2,1)S(1)}, u32[]{:S(2)}, u32[]{:S(2)}) %collective-permute-start.28) | collective-permute-done | bytes 524320 | tf_op jit(solution)/shard_map/ppermute | solution.py:33
  124.3 3.2 %collective-permute-done.29.refs_6_ = bf16[256,1024]{1,0:T(8,128)(2,1)S(1)} collective-permute-done((bf16[256,1024]{1,0:T(8,128)(2,1)S(1)}, bf16[256,1024]{1,0:T(8,128)(2,1)S(1)}, u32[]{:S(2)}, u32[]{:S(2)}) %collective-permute-start.29) | collective-permute-done | bytes 524320 | tf_op jit(solution)/shard_map/ppermute | solution.py:33
  127.5 2.5 %collective-permute-done.24.refs_3_ = bf16[256,1024]{1,0:T(8,128)(2,1)S(1)} collective-permute-done((bf16[256,1024]{1,0:T(8,128)(2,1)S(1)}, bf16[256,1024]{1,0:T(8,128)(2,1)S(1)}, u32[]{:S(2)}, u32[]{:S(2)}) %collective-permute-start.24) | collective-permute-done | bytes 524320 | tf_op jit(solution)/shard_map/ppermute | solution.py:33
  130.0 3.5 %collective-permute-done.30.refs_7_ = bf16[256,1024]{1,0:T(8,128)(2,1)S(1)} collective-permute-done((bf16[256,1024]{1,0:T(8,128)(2,1)S(1)}, bf16[256,1024]{1,0:T(8,128)(2,1)S(1)}, u32[]{:S(2)}, u32[]{:S(2)}) %collective-permute-start.30) | collective-permute-done | bytes 524320 | tf_op jit(solution)/shard_map/ppermute | solution.py:33
  133.5 5.0 %chain.3 = (bf16[128,1024]{1,0:T(8,128)(2,1)S(1)}, bf16[1024,1024]{1,0:T(8,128)(2,1)S(1)}, bf16[1024,1024]{1,0:T(8,128)(2,1)S(1)}) custom-call(s32[4]{0:T(128)S(1)} %pad_add_fusion.where, f32[2,32,1024]{2,1,0:T(8,128)S(1)} %get-tuple-element.28.keep, f32[2,32,1024]{2,1,0:T(8,128)S(1)} %get-tuple-element.27.other, ...), custom_call_target="tpu_custom_call" | custom-call | tf_op jit(solution)/shard_map/chain/pallas_call | solution.py:161
  138.5 4.7 %collective-permute-start.31 = (bf16[128,1024]{1,0:T(8,128)(2,1)S(1)}, bf16[128,1024]{1,0:T(8,128)(2,1)S(1)}, u32[]{:S(2)}, u32[]{:S(2)}) collective-permute-start(bf16[128,1024]{1,0:T(8,128)(2,1)S(1)} %get-tuple-element.24), channel_id=1, source_target_pairs={{32,0},{33,1},{34,2},{35,3},{36,4},{37,5},{38,6},{39,7},{40,8},{41... | collective-permute-start | bytes 786440 | tf_op jit(solution)/shard_map/ppermute | solution.py:33
  146.2 2.6 %collective-permute-done.32 = f32[4,32,1024]{2,1,0:T(8,128)S(1)} collective-permute-done((f32[4,32,1024]{2,1,0:T(8,128)S(1)}, f32[4,32,1024]{2,1,0:T(8,128)S(1)}, u32[]{:S(2)}, u32[]{:S(2)}) %collective-permute-start.32) | collective-permute-done | bytes 524320 | tf_op jit(solution)/shard_map/ppermute | solution.py:33
  (71 shorter events, 22.1 us)
Async XLA Ops:
  2.7 4.5 %collective-permute-start = (f32[2,32,1024]{2,1,0:T(8,128)S(1)}, f32[2,32,1024]{2,1,0:T(8,128)S(1)}, u32[]{:S(2)}, u32[]{:S(2)}) collective-permute-start(f32[2,32,1024]{2,1,0:T(8,128)S(1)} %get-tuple-element.17), channel_id=1, source_target_pairs={{0,32},{1,33},{2,34},{3,35},{4,36},{5,37},{6,38},{7,39},{8,40},{9,... | collective-permute-start | bytes 786440 | tf_op jit(solution)/shard_map/ppermute | solution.py:33
  7.2 8.7 %collective-permute-start.1 = (bf16[64,1024]{1,0:T(8,128)(2,1)S(1)}, bf16[64,1024]{1,0:T(8,128)(2,1)S(1)}, u32[]{:S(2)}, u32[]{:S(2)}) collective-permute-start(bf16[64,1024]{1,0:T(8,128)(2,1)S(1)} %fusion), channel_id=1, source_target_pairs={{0,4},{1,5},{2,6},{3,7},{4,0},{5,1},{6,2},{7,3},{8,12},{9,13},{10,... | collective-permute-start | bytes 393224 | tf_op jit(solution)/shard_map/ppermute | solution.py:33
  16.0 9.6 %collective-permute-start.2 = (bf16[64,1024]{1,0:T(8,128)(2,1)S(1)}, bf16[64,1024]{1,0:T(8,128)(2,1)S(1)}, u32[]{:S(2)}, u32[]{:S(2)}) collective-permute-start(bf16[64,1024]{1,0:T(8,128)(2,1)S(1)} %pad_maximum_fusion), channel_id=1, source_target_pairs={{0,8},{1,9},{2,10},{3,11},{4,12},{5,13},{6,14},{7,15},{8,16},{9,17... | collective-permute-start | bytes 393224 | tf_op jit(solution)/shard_map/ppermute | solution.py:33
  18.9 7.7 %collective-permute-start.4 = (bf16[64,1024]{1,0:T(8,128)(2,1)S(1)}, bf16[64,1024]{1,0:T(8,128)(2,1)S(1)}, u32[]{:S(2)}, u32[]{:S(2)}) collective-permute-start(bf16[64,1024]{1,0:T(8,128)(2,1)S(1)} %pad_maximum_fusion), channel_id=1, source_target_pairs={{0,16},{1,17},{2,18},{3,19},{4,20},{5,21},{6,22},{7,23},{8,24},{9,... | collective-permute-start | bytes 393224 | tf_op jit(solution)/shard_map/ppermute | solution.py:33
  19.3 7.3 %collective-permute-start.3 = (bf16[64,1024]{1,0:T(8,128)(2,1)S(1)}, bf16[64,1024]{1,0:T(8,128)(2,1)S(1)}, u32[]{:S(2)}, u32[]{:S(2)}) collective-permute-start(bf16[64,1024]{1,0:T(8,128)(2,1)S(1)} %pad_maximum_fusion), channel_id=1, source_target_pairs={{0,24},{1,25},{2,26},{3,27},{4,28},{5,29},{6,30},{7,31},{8,0},{9,1... | collective-permute-start | bytes 393224 | tf_op jit(solution)/shard_map/ppermute | solution.py:33
  20.0 13.8 %collective-permute-start.9 = (bf16[64,1024]{1,0:T(8,128)(2,1)S(1)}, bf16[64,1024]{1,0:T(8,128)(2,1)S(1)}, u32[]{:S(2)}, u32[]{:S(2)}) collective-permute-start(bf16[64,1024]{1,0:T(8,128)(2,1)S(1)} %pad_maximum_fusion.1), channel_id=1, source_target_pairs={{0,7},{1,0},{2,1},{3,2},{4,3},{5,4},{6,5},{7,6},{8,15},{9,8},{10,9... | collective-permute-start | bytes 393224 | tf_op jit(solution)/shard_map/ppermute | solution.py:33
  23.6 9.3 %collective-permute-start.8 = (bf16[64,1024]{1,0:T(8,128)(2,1)S(1)}, bf16[64,1024]{1,0:T(8,128)(2,1)S(1)}, u32[]{:S(2)}, u32[]{:S(2)}) collective-permute-start(bf16[64,1024]{1,0:T(8,128)(2,1)S(1)} %pad_maximum_fusion.1), channel_id=1, source_target_pairs={{0,1},{1,2},{2,3},{3,4},{4,5},{5,6},{6,7},{7,0},{8,9},{9,10},{10,1... | collective-permute-start | bytes 393224 | tf_op jit(solution)/shard_map/ppermute | solution.py:33
  26.6 15.5 %collective-permute-start.5 = (bf16[256,1024]{1,0:T(8,128)(2,1)S(1)}, bf16[256,1024]{1,0:T(8,128)(2,1)S(1)}, u32[]{:S(2)}, u32[]{:S(2)}) collective-permute-start(bf16[256,1024]{1,0:T(8,128)(2,1)S(1)} %constant_dynamic-update-slice_fusion.refs_0_), channel_id=1, source_target_pairs={{0,1},{1,2},{2,3},{3,4},{4,5},{5,6},{6,7},{7,0},{8,9},{9,10},{10,1... | collective-permute-start | bytes 1572872 | tf_op jit(solution)/shard_map/ppermute | solution.py:33
  32.9 7.5 %collective-permute-start.10 = (bf16[64,1024]{1,0:T(8,128)(2,1)S(1)}, bf16[64,1024]{1,0:T(8,128)(2,1)S(1)}, u32[]{:S(2)}, u32[]{:S(2)}) collective-permute-start(bf16[64,1024]{1,0:T(8,128)(2,1)S(1)} %collective-permute-done.8), channel_id=1, source_target_pairs={{0,1},{1,2},{2,3},{3,4},{4,5},{5,6},{6,7},{7,0},{8,9},{9,10},{10,1... | collective-permute-start | bytes 393224 | tf_op jit(solution)/shard_map/ppermute | solution.py:33
  40.4 8.5 %collective-permute-start.11 = (bf16[256,1024]{1,0:T(8,128)(2,1)S(1)}, bf16[256,1024]{1,0:T(8,128)(2,1)S(1)}, u32[]{:S(2)}, u32[]{:S(2)}) collective-permute-start(bf16[256,1024]{1,0:T(8,128)(2,1)S(1)} %constant_dynamic-update-slice_fusion.5.refs_4_), channel_id=1, source_target_pairs={{0,8},{1,9},{2,10},{3,11},{4,12},{5,13},{6,14},{7,15},{8,16},{9,17... | collective-permute-start | bytes 1572872 | tf_op jit(solution)/shard_map/ppermute | solution.py:33
  41.5 10.0 %collective-permute-start.6 = (bf16[256,1024]{1,0:T(8,128)(2,1)S(1)}, bf16[256,1024]{1,0:T(8,128)(2,1)S(1)}, u32[]{:S(2)}, u32[]{:S(2)}) collective-permute-start(bf16[256,1024]{1,0:T(8,128)(2,1)S(1)} %constant_dynamic-update-slice_fusion.refs_0_), channel_id=1, source_target_pairs={{0,7},{1,0},{2,1},{3,2},{4,3},{5,4},{6,5},{7,6},{8,15},{9,8},{10,9... | collective-permute-start | bytes 1572872 | tf_op jit(solution)/shard_map/ppermute | solution.py:33
  42.1 14.7 %collective-permute-start.12 = (bf16[256,1024]{1,0:T(8,128)(2,1)S(1)}, bf16[256,1024]{1,0:T(8,128)(2,1)S(1)}, u32[]{:S(2)}, u32[]{:S(2)}) collective-permute-start(bf16[256,1024]{1,0:T(8,128)(2,1)S(1)} %constant_dynamic-update-slice_fusion.5.refs_4_), channel_id=1, source_target_pairs={{0,24},{1,25},{2,26},{3,27},{4,28},{5,29},{6,30},{7,31},{8,0},{9,1... | collective-permute-start | bytes 1572872 | tf_op jit(solution)/shard_map/ppermute | solution.py:33
  42.1 14.7 %collective-permute-start.7 = (bf16[256,1024]{1,0:T(8,128)(2,1)S(1)}, bf16[256,1024]{1,0:T(8,128)(2,1)S(1)}, u32[]{:S(2)}, u32[]{:S(2)}) collective-permute-start(bf16[256,1024]{1,0:T(8,128)(2,1)S(1)} %collective-permute-done.5.refs_1_), channel_id=1, source_target_pairs={{0,1},{1,2},{2,3},{3,4},{4,5},{5,6},{6,7},{7,0},{8,9},{9,10},{10,1... | collective-permute-start | bytes 1572872 | tf_op jit(solution)/shard_map/ppermute | solution.py:33
  49.0 11.5 %collective-permute-start.13 = (bf16[256,1024]{1,0:T(8,128)(2,1)S(1)}, bf16[256,1024]{1,0:T(8,128)(2,1)S(1)}, u32[]{:S(2)}, u32[]{:S(2)}) collective-permute-start(bf16[256,1024]{1,0:T(8,128)(2,1)S(1)} %collective-permute-done.11.refs_5_), channel_id=1, source_target_pairs={{0,8},{1,9},{2,10},{3,11},{4,12},{5,13},{6,14},{7,15},{8,16},{9,17... | collective-permute-start | bytes 1572872 | tf_op jit(solution)/shard_map/ppermute | solution.py:33
  65.6 6.5 %collective-permute-start.14 = (bf16[128,1024]{1,0:T(8,128)(2,1)S(1)}, bf16[128,1024]{1,0:T(8,128)(2,1)S(1)}, u32[]{:S(2)}, u32[]{:S(2)}) collective-permute-start(bf16[128,1024]{1,0:T(8,128)(2,1)S(1)} %get-tuple-element.18), channel_id=1, source_target_pairs={{32,0},{33,1},{34,2},{35,3},{36,4},{37,5},{38,6},{39,7},{40,8},{41... | collective-permute-start | bytes 786440 | tf_op jit(solution)/shard_map/ppermute | solution.py:33
  73.5 8.1 %collective-permute-start.17 = (bf16[2,32,1024]{2,1,0:T(8,128)(2,1)S(1)}, bf16[2,32,1024]{2,1,0:T(8,128)(2,1)S(1)}, u32[]{:S(2)}, u32[]{:S(2)}) collective-permute-start(bf16[2,32,1024]{2,1,0:T(8,128)(2,1)S(1)} %get-tuple-element.22), channel_id=1, source_target_pairs={{0,96},{1,97},{2,98},{3,99},{4,100},{5,101},{6,102},{7,103},{8,104... | collective-permute-start | bytes 393224 | tf_op jit(solution)/shard_map/ppermute | solution.py:33
  74.8 6.9 %collective-permute-start.16 = (bf16[2,32,1024]{2,1,0:T(8,128)(2,1)S(1)}, bf16[2,32,1024]{2,1,0:T(8,128)(2,1)S(1)}, u32[]{:S(2)}, u32[]{:S(2)}) collective-permute-start(bf16[2,32,1024]{2,1,0:T(8,128)(2,1)S(1)} %get-tuple-element.22), channel_id=1, source_target_pairs={{0,32},{1,33},{2,34},{3,35},{4,36},{5,37},{6,38},{7,39},{8,40},{9,... | collective-permute-start | bytes 393224 | tf_op jit(solution)/shard_map/ppermute | solution.py:33
  81.8 9.3 %collective-permute-start.18 = (bf16[64,1024]{1,0:T(8,128)(2,1)S(1)}, bf16[64,1024]{1,0:T(8,128)(2,1)S(1)}, u32[]{:S(2)}, u32[]{:S(2)}) collective-permute-start(bf16[64,1024]{1,0:T(8,128)(2,1)S(1)} %fusion.1), channel_id=1, source_target_pairs={{0,4},{1,5},{2,6},{3,7},{4,0},{5,1},{6,2},{7,3},{8,12},{9,13},{10,... | collective-permute-start | bytes 393224 | tf_op jit(solution)/shard_map/ppermute | solution.py:33
  91.2 7.0 %collective-permute-start.19 = (bf16[64,1024]{1,0:T(8,128)(2,1)S(1)}, bf16[64,1024]{1,0:T(8,128)(2,1)S(1)}, u32[]{:S(2)}, u32[]{:S(2)}) collective-permute-start(bf16[64,1024]{1,0:T(8,128)(2,1)S(1)} %pad_maximum_fusion.2), channel_id=1, source_target_pairs={{0,8},{1,9},{2,10},{3,11},{4,12},{5,13},{6,14},{7,15},{8,16},{9,17... | collective-permute-start | bytes 393224 | tf_op jit(solution)/shard_map/ppermute | solution.py:33
  91.3 9.9 %collective-permute-start.21 = (bf16[64,1024]{1,0:T(8,128)(2,1)S(1)}, bf16[64,1024]{1,0:T(8,128)(2,1)S(1)}, u32[]{:S(2)}, u32[]{:S(2)}) collective-permute-start(bf16[64,1024]{1,0:T(8,128)(2,1)S(1)} %pad_maximum_fusion.2), channel_id=1, source_target_pairs={{0,16},{1,17},{2,18},{3,19},{4,20},{5,21},{6,22},{7,23},{8,24},{9,... | collective-permute-start | bytes 393224 | tf_op jit(solution)/shard_map/ppermute | solution.py:33
  91.5 9.6 %collective-permute-start.20 = (bf16[64,1024]{1,0:T(8,128)(2,1)S(1)}, bf16[64,1024]{1,0:T(8,128)(2,1)S(1)}, u32[]{:S(2)}, u32[]{:S(2)}) collective-permute-start(bf16[64,1024]{1,0:T(8,128)(2,1)S(1)} %pad_maximum_fusion.2), channel_id=1, source_target_pairs={{0,24},{1,25},{2,26},{3,27},{4,28},{5,29},{6,30},{7,31},{8,0},{9,1... | collective-permute-start | bytes 393224 | tf_op jit(solution)/shard_map/ppermute | solution.py:33
  92.7 15.3 %collective-permute-start.26 = (bf16[64,1024]{1,0:T(8,128)(2,1)S(1)}, bf16[64,1024]{1,0:T(8,128)(2,1)S(1)}, u32[]{:S(2)}, u32[]{:S(2)}) collective-permute-start(bf16[64,1024]{1,0:T(8,128)(2,1)S(1)} %pad_maximum_fusion.3), channel_id=1, source_target_pairs={{0,7},{1,0},{2,1},{3,2},{4,3},{5,4},{6,5},{7,6},{8,15},{9,8},{10,9... | collective-permute-start | bytes 393224 | tf_op jit(solution)/shard_map/ppermute | solution.py:33
  95.8 10.8 %collective-permute-start.25 = (bf16[64,1024]{1,0:T(8,128)(2,1)S(1)}, bf16[64,1024]{1,0:T(8,128)(2,1)S(1)}, u32[]{:S(2)}, u32[]{:S(2)}) collective-permute-start(bf16[64,1024]{1,0:T(8,128)(2,1)S(1)} %pad_maximum_fusion.3), channel_id=1, source_target_pairs={{0,1},{1,2},{2,3},{3,4},{4,5},{5,6},{6,7},{7,0},{8,9},{9,10},{10,1... | collective-permute-start | bytes 393224 | tf_op jit(solution)/shard_map/ppermute | solution.py:33
  101.2 14.5 %collective-permute-start.22 = (bf16[256,1024]{1,0:T(8,128)(2,1)S(1)}, bf16[256,1024]{1,0:T(8,128)(2,1)S(1)}, u32[]{:S(2)}, u32[]{:S(2)}) collective-permute-start(bf16[256,1024]{1,0:T(8,128)(2,1)S(1)} %constant_dynamic-update-slice_fusion.10.refs_0_), channel_id=1, source_target_pairs={{0,1},{1,2},{2,3},{3,4},{4,5},{5,6},{6,7},{7,0},{8,9},{9,10},{10,1... | collective-permute-start | bytes 1572872 | tf_op jit(solution)/shard_map/ppermute | solution.py:33
  106.6 7.5 %collective-permute-start.27 = (bf16[64,1024]{1,0:T(8,128)(2,1)S(1)}, bf16[64,1024]{1,0:T(8,128)(2,1)S(1)}, u32[]{:S(2)}, u32[]{:S(2)}) collective-permute-start(bf16[64,1024]{1,0:T(8,128)(2,1)S(1)} %collective-permute-done.25), channel_id=1, source_target_pairs={{0,1},{1,2},{2,3},{3,4},{4,5},{5,6},{6,7},{7,0},{8,9},{9,10},{10,1... | collective-permute-start | bytes 393224 | tf_op jit(solution)/shard_map/ppermute | solution.py:33
  114.1 9.6 %collective-permute-start.28 = (bf16[256,1024]{1,0:T(8,128)(2,1)S(1)}, bf16[256,1024]{1,0:T(8,128)(2,1)S(1)}, u32[]{:S(2)}, u32[]{:S(2)}) collective-permute-start(bf16[256,1024]{1,0:T(8,128)(2,1)S(1)} %constant_dynamic-update-slice_fusion.15.refs_4_), channel_id=1, source_target_pairs={{0,8},{1,9},{2,10},{3,11},{4,12},{5,13},{6,14},{7,15},{8,16},{9,17... | collective-permute-start | bytes 1572872 | tf_op jit(solution)/shard_map/ppermute | solution.py:33
  114.2 10.1 %collective-permute-start.23 = (bf16[256,1024]{1,0:T(8,128)(2,1)S(1)}, bf16[256,1024]{1,0:T(8,128)(2,1)S(1)}, u32[]{:S(2)}, u32[]{:S(2)}) collective-permute-start(bf16[256,1024]{1,0:T(8,128)(2,1)S(1)} %constant_dynamic-update-slice_fusion.10.refs_0_), channel_id=1, source_target_pairs={{0,7},{1,0},{2,1},{3,2},{4,3},{5,4},{6,5},{7,6},{8,15},{9,8},{10,9... | collective-permute-start | bytes 1572872 | tf_op jit(solution)/shard_map/ppermute | solution.py:33
  114.3 13.1 %collective-permute-start.29 = (bf16[256,1024]{1,0:T(8,128)(2,1)S(1)}, bf16[256,1024]{1,0:T(8,128)(2,1)S(1)}, u32[]{:S(2)}, u32[]{:S(2)}) collective-permute-start(bf16[256,1024]{1,0:T(8,128)(2,1)S(1)} %constant_dynamic-update-slice_fusion.15.refs_4_), channel_id=1, source_target_pairs={{0,24},{1,25},{2,26},{3,27},{4,28},{5,29},{6,30},{7,31},{8,0},{9,1... | collective-permute-start | bytes 1572872 | tf_op jit(solution)/shard_map/ppermute | solution.py:33
  115.7 14.3 %collective-permute-start.24 = (bf16[256,1024]{1,0:T(8,128)(2,1)S(1)}, bf16[256,1024]{1,0:T(8,128)(2,1)S(1)}, u32[]{:S(2)}, u32[]{:S(2)}) collective-permute-start(bf16[256,1024]{1,0:T(8,128)(2,1)S(1)} %collective-permute-done.22.refs_1_), channel_id=1, source_target_pairs={{0,1},{1,2},{2,3},{3,4},{4,5},{5,6},{6,7},{7,0},{8,9},{9,10},{10,1... | collective-permute-start | bytes 1572872 | tf_op jit(solution)/shard_map/ppermute | solution.py:33
  123.8 9.7 %collective-permute-start.30 = (bf16[256,1024]{1,0:T(8,128)(2,1)S(1)}, bf16[256,1024]{1,0:T(8,128)(2,1)S(1)}, u32[]{:S(2)}, u32[]{:S(2)}) collective-permute-start(bf16[256,1024]{1,0:T(8,128)(2,1)S(1)} %collective-permute-done.28.refs_5_), channel_id=1, source_target_pairs={{0,8},{1,9},{2,10},{3,11},{4,12},{5,13},{6,14},{7,15},{8,16},{9,17... | collective-permute-start | bytes 1572872 | tf_op jit(solution)/shard_map/ppermute | solution.py:33
  138.5 5.8 %collective-permute-start.31 = (bf16[128,1024]{1,0:T(8,128)(2,1)S(1)}, bf16[128,1024]{1,0:T(8,128)(2,1)S(1)}, u32[]{:S(2)}, u32[]{:S(2)}) collective-permute-start(bf16[128,1024]{1,0:T(8,128)(2,1)S(1)} %get-tuple-element.24), channel_id=1, source_target_pairs={{32,0},{33,1},{34,2},{35,3},{36,4},{37,5},{38,6},{39,7},{40,8},{41... | collective-permute-start | bytes 786440 | tf_op jit(solution)/shard_map/ppermute | solution.py:33
  144.9 3.9 %collective-permute-start.32 = (f32[4,32,1024]{2,1,0:T(8,128)S(1)}, f32[4,32,1024]{2,1,0:T(8,128)S(1)}, u32[]{:S(2)}, u32[]{:S(2)}) collective-permute-start(f32[4,32,1024]{2,1,0:T(8,128)S(1)} %finish.3), channel_id=1, source_target_pairs={{0,32},{1,33},{2,34},{3,35},{4,36},{5,37},{6,38},{7,39},{8,40},{9,... | collective-permute-start | bytes 1572872 | tf_op jit(solution)/shard_map/ppermute | solution.py:33
  (3 other events, 5.1 us)

commit v6 on v5

--- a/solution.py
+++ b/solution.py
@@ -49,6 +49,7 @@
     wide_a = jnp.concatenate([wide_a, ahead, behind, send(wide_a, hop("y", 2))])
     ahead, behind = send(wide_b, hop("z", 1)), send(wide_b, hop("z", -1))
     wide_b = jnp.concatenate([wide_b, ahead, behind, send(ahead, hop("z", 1))])
+    wide_a, wide_b = lax.optimization_barrier((wide_a, wide_b))
     ahead, behind = send(wide_a, hop("z", 1)), send(wide_a, hop("z", -1))
     parts_a = [wide_a, ahead, behind, send(ahead, hop("z", 1))]
     ahead, behind = send(wide_b, hop("y", 1)), send(wide_b, hop("y", -1))

time: 150 us -> 135 us (0.900)
  starting transfers between devices: 68.8 us -> 61.1 us
  waiting for transfers between devices: 65.3 us -> 58.4 us
    ppermute x33, starting transfers between devices: 68.8 us -> 61.1 us  [send(): return lax.ppermute(block, AXES, route(move))]
    ppermute x33, waiting for transfers between devices: 65.3 us -> 58.4 us  [send(): return lax.ppermute(block, AXES, route(move))]
  transfers between devices with their start and end apart: 33 -> 33, of which waited for: 20 -> 23; matrix products, arithmetic and copies ran while one was open for 0% -> 0% of each run, Pallas kernels for 0% -> 0%
where the time goes in v6:
time: 135 us
  starting transfers between devices  61.1 us (45%)
  waiting for transfers between devices  58.4 us (43%)
  Pallas kernels  12.1 us (9%)
  local copies, waits for them, and re-layouts  2.06 us (2%)
    ppermute x33, starting transfers between devices, send(): return lax.ppermute(block, AXES, route(move))  61.1 us
    ppermute x33, waiting for transfers between devices, send(): return lax.ppermute(block, AXES, route(move))  58.4 us
    pallas_call x2, Pallas kernels, chain(): pl.pallas_call(chain_kernel, out_shape=[jax.ShapeDtypeStruct((128, M), jn...  10 us
  transfers between devices with their start and end apart: 33, of which 23 were waited for; matrix products, arithmetic and copies ran while one was open for 0% of the time, Pallas kernels for 0%

profile of v6, /device:TPU:1, one launch (start us, length us, event | category | flops | bytes accessed | tf_op | source)
XLA Modules:
  0.0 135.0 jit_solution(9139152981306166913)
XLA Ops:
  2.7 3.3 %collective-permute-start = (f32[2,32,1024]{2,1,0:T(8,128)S(1)}, f32[2,32,1024]{2,1,0:T(8,128)S(1)}, u32[]{:S(2)}, u32[]{:S(2)}) collective-permute-start(f32[2,32,1024]{2,1,0:T(8,128)S(1)} %get-tuple-element.21), channel_id=1, source_target_pairs={{0,32},{1,33},{2,34},{3,35},{4,36},{5,37},{6,38},{7,39},{8,40},{9,... | collective-permute-start | bytes 786440 | tf_op jit(solution)/shard_map/ppermute | solution.py:33
  7.2 5.3 %collective-permute-start.1 = (bf16[64,1024]{1,0:T(8,128)(2,1)S(1)}, bf16[64,1024]{1,0:T(8,128)(2,1)S(1)}, u32[]{:S(2)}, u32[]{:S(2)}) collective-permute-start(bf16[64,1024]{1,0:T(8,128)(2,1)S(1)} %fusion), channel_id=1, source_target_pairs={{0,4},{1,5},{2,6},{3,7},{4,0},{5,1},{6,2},{7,3},{8,12},{9,13},{10,... | collective-permute-start | bytes 393224 | tf_op jit(solution)/shard_map/ppermute | solution.py:33
  12.5 3.4 %collective-permute-done.1 = bf16[64,1024]{1,0:T(8,128)(2,1)S(1)} collective-permute-done((bf16[64,1024]{1,0:T(8,128)(2,1)S(1)}, bf16[64,1024]{1,0:T(8,128)(2,1)S(1)}, u32[]{:S(2)}, u32[]{:S(2)}) %collective-permute-start.1) | collective-permute-done | bytes 131104 | tf_op jit(solution)/shard_map/ppermute | solution.py:33
  16.0 5.6 %collective-permute-start.5 = (bf16[64,1024]{1,0:T(8,128)(2,1)S(1)}, bf16[64,1024]{1,0:T(8,128)(2,1)S(1)}, u32[]{:S(2)}, u32[]{:S(2)}) collective-permute-start(bf16[64,1024]{1,0:T(8,128)(2,1)S(1)} %pad_maximum_fusion.1), channel_id=1, source_target_pairs={{0,1},{1,2},{2,3},{3,4},{4,5},{5,6},{6,7},{7,0},{8,9},{9,10},{10,1... | collective-permute-start | bytes 393224 | tf_op jit(solution)/shard_map/ppermute | solution.py:33
  21.6 2.8 %collective-permute-start.2 = (bf16[64,1024]{1,0:T(8,128)(2,1)S(1)}, bf16[64,1024]{1,0:T(8,128)(2,1)S(1)}, u32[]{:S(2)}, u32[]{:S(2)}) collective-permute-start(bf16[64,1024]{1,0:T(8,128)(2,1)S(1)} %pad_maximum_fusion), channel_id=1, source_target_pairs={{0,8},{1,9},{2,10},{3,11},{4,12},{5,13},{6,14},{7,15},{8,16},{9,17... | collective-permute-start | bytes 393224 | tf_op jit(solution)/shard_map/ppermute | solution.py:33
  25.5 2.7 %collective-permute-start.7 = (bf16[64,1024]{1,0:T(8,128)(2,1)S(1)}, bf16[64,1024]{1,0:T(8,128)(2,1)S(1)}, u32[]{:S(2)}, u32[]{:S(2)}) collective-permute-start(bf16[64,1024]{1,0:T(8,128)(2,1)S(1)} %collective-permute-done.5), channel_id=1, source_target_pairs={{0,1},{1,2},{2,3},{3,4},{4,5},{5,6},{6,7},{7,0},{8,9},{9,10},{10,1... | collective-permute-start | bytes 393224 | tf_op jit(solution)/shard_map/ppermute | solution.py:33
  28.2 1.9 %collective-permute-done.2 = bf16[64,1024]{1,0:T(8,128)(2,1)S(1)} collective-permute-done((bf16[64,1024]{1,0:T(8,128)(2,1)S(1)}, bf16[64,1024]{1,0:T(8,128)(2,1)S(1)}, u32[]{:S(2)}, u32[]{:S(2)}) %collective-permute-start.2) | collective-permute-done | bytes 131104 | tf_op jit(solution)/shard_map/ppermute | solution.py:33
  30.1 1.9 %collective-permute-done.3 = bf16[64,1024]{1,0:T(8,128)(2,1)S(1)} collective-permute-done((bf16[64,1024]{1,0:T(8,128)(2,1)S(1)}, bf16[64,1024]{1,0:T(8,128)(2,1)S(1)}, u32[]{:S(2)}, u32[]{:S(2)}) %collective-permute-start.3) | collective-permute-done | bytes 131104 | tf_op jit(solution)/shard_map/ppermute | solution.py:33
  32.1 2.5 %collective-permute-start.8 = (bf16[256,1024]{1,0:T(8,128)(2,1)S(1)}, bf16[256,1024]{1,0:T(8,128)(2,1)S(1)}, u32[]{:S(2)}, u32[]{:S(2)}) collective-permute-start(bf16[256,1024]{1,0:T(8,128)(2,1)S(1)} %constant_dynamic-update-slice_fusion.refs_0_), channel_id=1, source_target_pairs={{0,1},{1,2},{2,3},{3,4},{4,5},{5,6},{6,7},{7,0},{8,9},{9,10},{10,1... | collective-permute-start | bytes 1572872 | tf_op jit(solution)/shard_map/ppermute | solution.py:33
  36.1 6.2 %collective-permute-done.8.refs_1_ = bf16[256,1024]{1,0:T(8,128)(2,1)S(1)} collective-permute-done((bf16[256,1024]{1,0:T(8,128)(2,1)S(1)}, bf16[256,1024]{1,0:T(8,128)(2,1)S(1)}, u32[]{:S(2)}, u32[]{:S(2)}) %collective-permute-start.8) | collective-permute-done | bytes 524320 | tf_op jit(solution)/shard_map/ppermute | solution.py:33
  42.3 3.3 %collective-permute-start.10 = (bf16[256,1024]{1,0:T(8,128)(2,1)S(1)}, bf16[256,1024]{1,0:T(8,128)(2,1)S(1)}, u32[]{:S(2)}, u32[]{:S(2)}) collective-permute-start(bf16[256,1024]{1,0:T(8,128)(2,1)S(1)} %collective-permute-done.8.refs_1_), channel_id=1, source_target_pairs={{0,1},{1,2},{2,3},{3,4},{4,5},{5,6},{6,7},{7,0},{8,9},{9,10},{10,1... | collective-permute-start | bytes 1572872 | tf_op jit(solution)/shard_map/ppermute | solution.py:33
  45.6 4.4 %collective-permute-done.9.refs_2_ = bf16[256,1024]{1,0:T(8,128)(2,1)S(1)} collective-permute-done((bf16[256,1024]{1,0:T(8,128)(2,1)S(1)}, bf16[256,1024]{1,0:T(8,128)(2,1)S(1)}, u32[]{:S(2)}, u32[]{:S(2)}) %collective-permute-start.9) | collective-permute-done | bytes 524320 | tf_op jit(solution)/shard_map/ppermute | solution.py:33
  50.1 1.9 %collective-permute-done.10.refs_3_ = bf16[256,1024]{1,0:T(8,128)(2,1)S(1)} collective-permute-done((bf16[256,1024]{1,0:T(8,128)(2,1)S(1)}, bf16[256,1024]{1,0:T(8,128)(2,1)S(1)}, u32[]{:S(2)}, u32[]{:S(2)}) %collective-permute-start.10) | collective-permute-done | bytes 524320 | tf_op jit(solution)/shard_map/ppermute | solution.py:33
  52.0 2.2 %collective-permute-done.13.refs_7_ = bf16[256,1024]{1,0:T(8,128)(2,1)S(1)} collective-permute-done((bf16[256,1024]{1,0:T(8,128)(2,1)S(1)}, bf16[256,1024]{1,0:T(8,128)(2,1)S(1)}, u32[]{:S(2)}, u32[]{:S(2)}) %collective-permute-start.13) | collective-permute-done | bytes 524320 | tf_op jit(solution)/shard_map/ppermute | solution.py:33
  54.2 5.0 %chain.2 = (bf16[128,1024]{1,0:T(8,128)(2,1)S(1)}, bf16[1024,1024]{1,0:T(8,128)(2,1)S(1)}, bf16[1024,1024]{1,0:T(8,128)(2,1)S(1)}) custom-call(s32[4]{0:T(128)S(1)} %pad_add_fusion.where, f32[2,32,1024]{2,1,0:T(8,128)S(1)} %get-tuple-element.20.keep, f32[2,32,1024]{2,1,0:T(8,128)S(1)} %collective-permute-done.other, ...), custom_call_target="tpu_custom_call" | custom-call | tf_op jit(solution)/shard_map/chain/pallas_call | solution.py:162
  59.2 4.4 %collective-permute-start.14 = (bf16[128,1024]{1,0:T(8,128)(2,1)S(1)}, bf16[128,1024]{1,0:T(8,128)(2,1)S(1)}, u32[]{:S(2)}, u32[]{:S(2)}) collective-permute-start(bf16[128,1024]{1,0:T(8,128)(2,1)S(1)} %get-tuple-element.24), channel_id=1, source_target_pairs={{32,0},{33,1},{34,2},{35,3},{36,4},{37,5},{38,6},{39,7},{40,8},{41... | collective-permute-start | bytes 786440 | tf_op jit(solution)/shard_map/ppermute | solution.py:33
  66.1 1.3 collective-permute-start.17
  68.7 5.5 %collective-permute-done.17 = bf16[2,32,1024]{2,1,0:T(8,128)(2,1)S(1)} collective-permute-done((bf16[2,32,1024]{2,1,0:T(8,128)(2,1)S(1)}, bf16[2,32,1024]{2,1,0:T(8,128)(2,1)S(1)}, u32[]{:S(2)}, u32[]{:S(2)}) %collective-permute-start.17) | collective-permute-done | bytes 131104 | tf_op jit(solution)/shard_map/ppermute | solution.py:33
  74.4 2.6 %collective-permute-start.18 = (bf16[64,1024]{1,0:T(8,128)(2,1)S(1)}, bf16[64,1024]{1,0:T(8,128)(2,1)S(1)}, u32[]{:S(2)}, u32[]{:S(2)}) collective-permute-start(bf16[64,1024]{1,0:T(8,128)(2,1)S(1)} %fusion.1), channel_id=1, source_target_pairs={{0,4},{1,5},{2,6},{3,7},{4,0},{5,1},{6,2},{7,3},{8,12},{9,13},{10,... | collective-permute-start | bytes 393224 | tf_op jit(solution)/shard_map/ppermute | solution.py:33
  77.0 6.6 %collective-permute-done.18 = bf16[64,1024]{1,0:T(8,128)(2,1)S(1)} collective-permute-done((bf16[64,1024]{1,0:T(8,128)(2,1)S(1)}, bf16[64,1024]{1,0:T(8,128)(2,1)S(1)}, u32[]{:S(2)}, u32[]{:S(2)}) %collective-permute-start.18) | collective-permute-done | bytes 131104 | tf_op jit(solution)/shard_map/ppermute | solution.py:33
  83.7 5.7 %collective-permute-start.22 = (bf16[64,1024]{1,0:T(8,128)(2,1)S(1)}, bf16[64,1024]{1,0:T(8,128)(2,1)S(1)}, u32[]{:S(2)}, u32[]{:S(2)}) collective-permute-start(bf16[64,1024]{1,0:T(8,128)(2,1)S(1)} %pad_maximum_fusion.3), channel_id=1, source_target_pairs={{0,1},{1,2},{2,3},{3,4},{4,5},{5,6},{6,7},{7,0},{8,9},{9,10},{10,1... | collective-permute-start | bytes 393224 | tf_op jit(solution)/shard_map/ppermute | solution.py:33
  91.3 3.4 %collective-permute-start.24 = (bf16[64,1024]{1,0:T(8,128)(2,1)S(1)}, bf16[64,1024]{1,0:T(8,128)(2,1)S(1)}, u32[]{:S(2)}, u32[]{:S(2)}) collective-permute-start(bf16[64,1024]{1,0:T(8,128)(2,1)S(1)} %collective-permute-done.22), channel_id=1, source_target_pairs={{0,1},{1,2},{2,3},{3,4},{4,5},{5,6},{6,7},{7,0},{8,9},{9,10},{10,1... | collective-permute-start | bytes 393224 | tf_op jit(solution)/shard_map/ppermute | solution.py:33
  94.8 2.0 %collective-permute-done.20 = bf16[64,1024]{1,0:T(8,128)(2,1)S(1)} collective-permute-done((bf16[64,1024]{1,0:T(8,128)(2,1)S(1)}, bf16[64,1024]{1,0:T(8,128)(2,1)S(1)}, u32[]{:S(2)}, u32[]{:S(2)}) %collective-permute-start.20) | collective-permute-done | bytes 131104 | tf_op jit(solution)/shard_map/ppermute | solution.py:33
  97.4 3.2 %collective-permute-start.25 = (bf16[256,1024]{1,0:T(8,128)(2,1)S(1)}, bf16[256,1024]{1,0:T(8,128)(2,1)S(1)}, u32[]{:S(2)}, u32[]{:S(2)}) collective-permute-start(bf16[256,1024]{1,0:T(8,128)(2,1)S(1)} %constant_dynamic-update-slice_fusion.10.refs_0_), channel_id=1, source_target_pairs={{0,1},{1,2},{2,3},{3,4},{4,5},{5,6},{6,7},{7,0},{8,9},{9,10},{10,1... | collective-permute-start | bytes 1572872 | tf_op jit(solution)/shard_map/ppermute | solution.py:33
  102.1 6.9 %collective-permute-done.25.refs_1_ = bf16[256,1024]{1,0:T(8,128)(2,1)S(1)} collective-permute-done((bf16[256,1024]{1,0:T(8,128)(2,1)S(1)}, bf16[256,1024]{1,0:T(8,128)(2,1)S(1)}, u32[]{:S(2)}, u32[]{:S(2)}) %collective-permute-start.25) | collective-permute-done | bytes 524320 | tf_op jit(solution)/shard_map/ppermute | solution.py:33
  109.0 3.4 %collective-permute-start.27 = (bf16[256,1024]{1,0:T(8,128)(2,1)S(1)}, bf16[256,1024]{1,0:T(8,128)(2,1)S(1)}, u32[]{:S(2)}, u32[]{:S(2)}) collective-permute-start(bf16[256,1024]{1,0:T(8,128)(2,1)S(1)} %collective-permute-done.25.refs_1_), channel_id=1, source_target_pairs={{0,1},{1,2},{2,3},{3,4},{4,5},{5,6},{6,7},{7,0},{8,9},{9,10},{10,1... | collective-permute-start | bytes 1572872 | tf_op jit(solution)/shard_map/ppermute | solution.py:33
  112.4 3.1 %collective-permute-done.26.refs_2_ = bf16[256,1024]{1,0:T(8,128)(2,1)S(1)} collective-permute-done((bf16[256,1024]{1,0:T(8,128)(2,1)S(1)}, bf16[256,1024]{1,0:T(8,128)(2,1)S(1)}, u32[]{:S(2)}, u32[]{:S(2)}) %collective-permute-start.26) | collective-permute-done | bytes 524320 | tf_op jit(solution)/shard_map/ppermute | solution.py:33
  115.6 2.9 %collective-permute-done.27.refs_3_ = bf16[256,1024]{1,0:T(8,128)(2,1)S(1)} collective-permute-done((bf16[256,1024]{1,0:T(8,128)(2,1)S(1)}, bf16[256,1024]{1,0:T(8,128)(2,1)S(1)}, u32[]{:S(2)}, u32[]{:S(2)}) %collective-permute-start.27) | collective-permute-done | bytes 524320 | tf_op jit(solution)/shard_map/ppermute | solution.py:33
  118.5 2.2 %collective-permute-done.30.refs_7_ = bf16[256,1024]{1,0:T(8,128)(2,1)S(1)} collective-permute-done((bf16[256,1024]{1,0:T(8,128)(2,1)S(1)}, bf16[256,1024]{1,0:T(8,128)(2,1)S(1)}, u32[]{:S(2)}, u32[]{:S(2)}) %collective-permute-start.30) | collective-permute-done | bytes 524320 | tf_op jit(solution)/shard_map/ppermute | solution.py:33
  120.7 5.0 %chain.3 = (bf16[128,1024]{1,0:T(8,128)(2,1)S(1)}, bf16[1024,1024]{1,0:T(8,128)(2,1)S(1)}, bf16[1024,1024]{1,0:T(8,128)(2,1)S(1)}) custom-call(s32[4]{0:T(128)S(1)} %pad_add_fusion.where, f32[2,32,1024]{2,1,0:T(8,128)S(1)} %get-tuple-element.36.keep, f32[2,32,1024]{2,1,0:T(8,128)S(1)} %get-tuple-element.35.other, ...), custom_call_target="tpu_custom_call" | custom-call | tf_op jit(solution)/shard_map/chain/pallas_call | solution.py:162
  125.7 2.9 %collective-permute-start.31 = (bf16[128,1024]{1,0:T(8,128)(2,1)S(1)}, bf16[128,1024]{1,0:T(8,128)(2,1)S(1)}, u32[]{:S(2)}, u32[]{:S(2)}) collective-permute-start(bf16[128,1024]{1,0:T(8,128)(2,1)S(1)} %get-tuple-element.32), channel_id=1, source_target_pairs={{32,0},{33,1},{34,2},{35,3},{36,4},{37,5},{38,6},{39,7},{40,8},{41... | collective-permute-start | bytes 786440 | tf_op jit(solution)/shard_map/ppermute | solution.py:33
  131.6 2.6 %collective-permute-done.32 = f32[4,32,1024]{2,1,0:T(8,128)S(1)} collective-permute-done((f32[4,32,1024]{2,1,0:T(8,128)S(1)}, f32[4,32,1024]{2,1,0:T(8,128)S(1)}, u32[]{:S(2)}, u32[]{:S(2)}) %collective-permute-start.32) | collective-permute-done | bytes 524320 | tf_op jit(solution)/shard_map/ppermute | solution.py:33
  (71 shorter events, 18.6 us)
Async XLA Ops:
  2.7 4.5 %collective-permute-start = (f32[2,32,1024]{2,1,0:T(8,128)S(1)}, f32[2,32,1024]{2,1,0:T(8,128)S(1)}, u32[]{:S(2)}, u32[]{:S(2)}) collective-permute-start(f32[2,32,1024]{2,1,0:T(8,128)S(1)} %get-tuple-element.21), channel_id=1, source_target_pairs={{0,32},{1,33},{2,34},{3,35},{4,36},{5,37},{6,38},{7,39},{8,40},{9,... | collective-permute-start | bytes 786440 | tf_op jit(solution)/shard_map/ppermute | solution.py:33
  7.2 8.7 %collective-permute-start.1 = (bf16[64,1024]{1,0:T(8,128)(2,1)S(1)}, bf16[64,1024]{1,0:T(8,128)(2,1)S(1)}, u32[]{:S(2)}, u32[]{:S(2)}) collective-permute-start(bf16[64,1024]{1,0:T(8,128)(2,1)S(1)} %fusion), channel_id=1, source_target_pairs={{0,4},{1,5},{2,6},{3,7},{4,0},{5,1},{6,2},{7,3},{8,12},{9,13},{10,... | collective-permute-start | bytes 393224 | tf_op jit(solution)/shard_map/ppermute | solution.py:33
  16.0 9.5 %collective-permute-start.5 = (bf16[64,1024]{1,0:T(8,128)(2,1)S(1)}, bf16[64,1024]{1,0:T(8,128)(2,1)S(1)}, u32[]{:S(2)}, u32[]{:S(2)}) collective-permute-start(bf16[64,1024]{1,0:T(8,128)(2,1)S(1)} %pad_maximum_fusion.1), channel_id=1, source_target_pairs={{0,1},{1,2},{2,3},{3,4},{4,5},{5,6},{6,7},{7,0},{8,9},{9,10},{10,1... | collective-permute-start | bytes 393224 | tf_op jit(solution)/shard_map/ppermute | solution.py:33
  21.6 8.5 %collective-permute-start.2 = (bf16[64,1024]{1,0:T(8,128)(2,1)S(1)}, bf16[64,1024]{1,0:T(8,128)(2,1)S(1)}, u32[]{:S(2)}, u32[]{:S(2)}) collective-permute-start(bf16[64,1024]{1,0:T(8,128)(2,1)S(1)} %pad_maximum_fusion), channel_id=1, source_target_pairs={{0,8},{1,9},{2,10},{3,11},{4,12},{5,13},{6,14},{7,15},{8,16},{9,17... | collective-permute-start | bytes 393224 | tf_op jit(solution)/shard_map/ppermute | solution.py:33
  24.4 7.6 %collective-permute-start.4 = (bf16[64,1024]{1,0:T(8,128)(2,1)S(1)}, bf16[64,1024]{1,0:T(8,128)(2,1)S(1)}, u32[]{:S(2)}, u32[]{:S(2)}) collective-permute-start(bf16[64,1024]{1,0:T(8,128)(2,1)S(1)} %pad_maximum_fusion), channel_id=1, source_target_pairs={{0,16},{1,17},{2,18},{3,19},{4,20},{5,21},{6,22},{7,23},{8,24},{9,... | collective-permute-start | bytes 393224 | tf_op jit(solution)/shard_map/ppermute | solution.py:33
  24.8 7.2 %collective-permute-start.3 = (bf16[64,1024]{1,0:T(8,128)(2,1)S(1)}, bf16[64,1024]{1,0:T(8,128)(2,1)S(1)}, u32[]{:S(2)}, u32[]{:S(2)}) collective-permute-start(bf16[64,1024]{1,0:T(8,128)(2,1)S(1)} %pad_maximum_fusion), channel_id=1, source_target_pairs={{0,24},{1,25},{2,26},{3,27},{4,28},{5,29},{6,30},{7,31},{8,0},{9,1... | collective-permute-start | bytes 393224 | tf_op jit(solution)/shard_map/ppermute | solution.py:33
  25.5 6.5 %collective-permute-start.6 = (bf16[64,1024]{1,0:T(8,128)(2,1)S(1)}, bf16[64,1024]{1,0:T(8,128)(2,1)S(1)}, u32[]{:S(2)}, u32[]{:S(2)}) collective-permute-start(bf16[64,1024]{1,0:T(8,128)(2,1)S(1)} %pad_maximum_fusion.1), channel_id=1, source_target_pairs={{0,7},{1,0},{2,1},{3,2},{4,3},{5,4},{6,5},{7,6},{8,15},{9,8},{10,9... | collective-permute-start | bytes 393224 | tf_op jit(solution)/shard_map/ppermute | solution.py:33
  25.5 6.6 %collective-permute-start.7 = (bf16[64,1024]{1,0:T(8,128)(2,1)S(1)}, bf16[64,1024]{1,0:T(8,128)(2,1)S(1)}, u32[]{:S(2)}, u32[]{:S(2)}) collective-permute-start(bf16[64,1024]{1,0:T(8,128)(2,1)S(1)} %collective-permute-done.5), channel_id=1, source_target_pairs={{0,1},{1,2},{2,3},{3,4},{4,5},{5,6},{6,7},{7,0},{8,9},{9,10},{10,1... | collective-permute-start | bytes 393224 | tf_op jit(solution)/shard_map/ppermute | solution.py:33
  32.1 10.2 %collective-permute-start.8 = (bf16[256,1024]{1,0:T(8,128)(2,1)S(1)}, bf16[256,1024]{1,0:T(8,128)(2,1)S(1)}, u32[]{:S(2)}, u32[]{:S(2)}) collective-permute-start(bf16[256,1024]{1,0:T(8,128)(2,1)S(1)} %constant_dynamic-update-slice_fusion.refs_0_), channel_id=1, source_target_pairs={{0,1},{1,2},{2,3},{3,4},{4,5},{5,6},{6,7},{7,0},{8,9},{9,10},{10,1... | collective-permute-start | bytes 1572872 | tf_op jit(solution)/shard_map/ppermute | solution.py:33
  34.6 10.9 %collective-permute-start.11 = (bf16[256,1024]{1,0:T(8,128)(2,1)S(1)}, bf16[256,1024]{1,0:T(8,128)(2,1)S(1)}, u32[]{:S(2)}, u32[]{:S(2)}) collective-permute-start(bf16[256,1024]{1,0:T(8,128)(2,1)S(1)} %constant_dynamic-update-slice_fusion.5.refs_4_), channel_id=1, source_target_pairs={{0,8},{1,9},{2,10},{3,11},{4,12},{5,13},{6,14},{7,15},{8,16},{9,17... | collective-permute-start | bytes 1572872 | tf_op jit(solution)/shard_map/ppermute | solution.py:33
  35.8 14.2 %collective-permute-start.9 = (bf16[256,1024]{1,0:T(8,128)(2,1)S(1)}, bf16[256,1024]{1,0:T(8,128)(2,1)S(1)}, u32[]{:S(2)}, u32[]{:S(2)}) collective-permute-start(bf16[256,1024]{1,0:T(8,128)(2,1)S(1)} %constant_dynamic-update-slice_fusion.refs_0_), channel_id=1, source_target_pairs={{0,7},{1,0},{2,1},{3,2},{4,3},{5,4},{6,5},{7,6},{8,15},{9,8},{10,9... | collective-permute-start | bytes 1572872 | tf_op jit(solution)/shard_map/ppermute | solution.py:33
  35.8 14.3 %collective-permute-start.12 = (bf16[256,1024]{1,0:T(8,128)(2,1)S(1)}, bf16[256,1024]{1,0:T(8,128)(2,1)S(1)}, u32[]{:S(2)}, u32[]{:S(2)}) collective-permute-start(bf16[256,1024]{1,0:T(8,128)(2,1)S(1)} %constant_dynamic-update-slice_fusion.5.refs_4_), channel_id=1, source_target_pairs={{0,24},{1,25},{2,26},{3,27},{4,28},{5,29},{6,30},{7,31},{8,0},{9,1... | collective-permute-start | bytes 1572872 | tf_op jit(solution)/shard_map/ppermute | solution.py:33
  42.3 9.7 %collective-permute-start.10 = (bf16[256,1024]{1,0:T(8,128)(2,1)S(1)}, bf16[256,1024]{1,0:T(8,128)(2,1)S(1)}, u32[]{:S(2)}, u32[]{:S(2)}) collective-permute-start(bf16[256,1024]{1,0:T(8,128)(2,1)S(1)} %collective-permute-done.8.refs_1_), channel_id=1, source_target_pairs={{0,1},{1,2},{2,3},{3,4},{4,5},{5,6},{6,7},{7,0},{8,9},{9,10},{10,1... | collective-permute-start | bytes 1572872 | tf_op jit(solution)/shard_map/ppermute | solution.py:33
  45.6 8.6 %collective-permute-start.13 = (bf16[256,1024]{1,0:T(8,128)(2,1)S(1)}, bf16[256,1024]{1,0:T(8,128)(2,1)S(1)}, u32[]{:S(2)}, u32[]{:S(2)}) collective-permute-start(bf16[256,1024]{1,0:T(8,128)(2,1)S(1)} %collective-permute-done.11.refs_5_), channel_id=1, source_target_pairs={{0,8},{1,9},{2,10},{3,11},{4,12},{5,13},{6,14},{7,15},{8,16},{9,17... | collective-permute-start | bytes 1572872 | tf_op jit(solution)/shard_map/ppermute | solution.py:33
  59.2 5.5 %collective-permute-start.14 = (bf16[128,1024]{1,0:T(8,128)(2,1)S(1)}, bf16[128,1024]{1,0:T(8,128)(2,1)S(1)}, u32[]{:S(2)}, u32[]{:S(2)}) collective-permute-start(bf16[128,1024]{1,0:T(8,128)(2,1)S(1)} %get-tuple-element.24), channel_id=1, source_target_pairs={{32,0},{33,1},{34,2},{35,3},{36,4},{37,5},{38,6},{39,7},{40,8},{41... | collective-permute-start | bytes 786440 | tf_op jit(solution)/shard_map/ppermute | solution.py:33
  66.1 8.1 %collective-permute-start.17 = (bf16[2,32,1024]{2,1,0:T(8,128)(2,1)S(1)}, bf16[2,32,1024]{2,1,0:T(8,128)(2,1)S(1)}, u32[]{:S(2)}, u32[]{:S(2)}) collective-permute-start(bf16[2,32,1024]{2,1,0:T(8,128)(2,1)S(1)} %get-tuple-element.28), channel_id=1, source_target_pairs={{0,96},{1,97},{2,98},{3,99},{4,100},{5,101},{6,102},{7,103},{8,104... | collective-permute-start | bytes 393224 | tf_op jit(solution)/shard_map/ppermute | solution.py:33
  67.4 6.9 %collective-permute-start.16 = (bf16[2,32,1024]{2,1,0:T(8,128)(2,1)S(1)}, bf16[2,32,1024]{2,1,0:T(8,128)(2,1)S(1)}, u32[]{:S(2)}, u32[]{:S(2)}) collective-permute-start(bf16[2,32,1024]{2,1,0:T(8,128)(2,1)S(1)} %get-tuple-element.28), channel_id=1, source_target_pairs={{0,32},{1,33},{2,34},{3,35},{4,36},{5,37},{6,38},{7,39},{8,40},{9,... | collective-permute-start | bytes 393224 | tf_op jit(solution)/shard_map/ppermute | solution.py:33
  74.4 9.3 %collective-permute-start.18 = (bf16[64,1024]{1,0:T(8,128)(2,1)S(1)}, bf16[64,1024]{1,0:T(8,128)(2,1)S(1)}, u32[]{:S(2)}, u32[]{:S(2)}) collective-permute-start(bf16[64,1024]{1,0:T(8,128)(2,1)S(1)} %fusion.1), channel_id=1, source_target_pairs={{0,4},{1,5},{2,6},{3,7},{4,0},{5,1},{6,2},{7,3},{8,12},{9,13},{10,... | collective-permute-start | bytes 393224 | tf_op jit(solution)/shard_map/ppermute | solution.py:33
  83.7 7.6 %collective-permute-start.22 = (bf16[64,1024]{1,0:T(8,128)(2,1)S(1)}, bf16[64,1024]{1,0:T(8,128)(2,1)S(1)}, u32[]{:S(2)}, u32[]{:S(2)}) collective-permute-start(bf16[64,1024]{1,0:T(8,128)(2,1)S(1)} %pad_maximum_fusion.3), channel_id=1, source_target_pairs={{0,1},{1,2},{2,3},{3,4},{4,5},{5,6},{6,7},{7,0},{8,9},{9,10},{10,1... | collective-permute-start | bytes 393224 | tf_op jit(solution)/shard_map/ppermute | solution.py:33
  89.4 5.4 %collective-permute-start.19 = (bf16[64,1024]{1,0:T(8,128)(2,1)S(1)}, bf16[64,1024]{1,0:T(8,128)(2,1)S(1)}, u32[]{:S(2)}, u32[]{:S(2)}) collective-permute-start(bf16[64,1024]{1,0:T(8,128)(2,1)S(1)} %pad_maximum_fusion.2), channel_id=1, source_target_pairs={{0,8},{1,9},{2,10},{3,11},{4,12},{5,13},{6,14},{7,15},{8,16},{9,17... | collective-permute-start | bytes 393224 | tf_op jit(solution)/shard_map/ppermute | solution.py:33
  89.5 7.4 %collective-permute-start.21 = (bf16[64,1024]{1,0:T(8,128)(2,1)S(1)}, bf16[64,1024]{1,0:T(8,128)(2,1)S(1)}, u32[]{:S(2)}, u32[]{:S(2)}) collective-permute-start(bf16[64,1024]{1,0:T(8,128)(2,1)S(1)} %pad_maximum_fusion.2), channel_id=1, source_target_pairs={{0,16},{1,17},{2,18},{3,19},{4,20},{5,21},{6,22},{7,23},{8,24},{9,... | collective-permute-start | bytes 393224 | tf_op jit(solution)/shard_map/ppermute | solution.py:33
  89.7 7.1 %collective-permute-start.20 = (bf16[64,1024]{1,0:T(8,128)(2,1)S(1)}, bf16[64,1024]{1,0:T(8,128)(2,1)S(1)}, u32[]{:S(2)}, u32[]{:S(2)}) collective-permute-start(bf16[64,1024]{1,0:T(8,128)(2,1)S(1)} %pad_maximum_fusion.2), channel_id=1, source_target_pairs={{0,24},{1,25},{2,26},{3,27},{4,28},{5,29},{6,30},{7,31},{8,0},{9,1... | collective-permute-start | bytes 393224 | tf_op jit(solution)/shard_map/ppermute | solution.py:33
  90.9 5.9 %collective-permute-start.23 = (bf16[64,1024]{1,0:T(8,128)(2,1)S(1)}, bf16[64,1024]{1,0:T(8,128)(2,1)S(1)}, u32[]{:S(2)}, u32[]{:S(2)}) collective-permute-start(bf16[64,1024]{1,0:T(8,128)(2,1)S(1)} %pad_maximum_fusion.3), channel_id=1, source_target_pairs={{0,7},{1,0},{2,1},{3,2},{4,3},{5,4},{6,5},{7,6},{8,15},{9,8},{10,9... | collective-permute-start | bytes 393224 | tf_op jit(solution)/shard_map/ppermute | solution.py:33
  91.3 6.1 %collective-permute-start.24 = (bf16[64,1024]{1,0:T(8,128)(2,1)S(1)}, bf16[64,1024]{1,0:T(8,128)(2,1)S(1)}, u32[]{:S(2)}, u32[]{:S(2)}) collective-permute-start(bf16[64,1024]{1,0:T(8,128)(2,1)S(1)} %collective-permute-done.22), channel_id=1, source_target_pairs={{0,1},{1,2},{2,3},{3,4},{4,5},{5,6},{6,7},{7,0},{8,9},{9,10},{10,1... | collective-permute-start | bytes 393224 | tf_op jit(solution)/shard_map/ppermute | solution.py:33
  97.4 11.5 %collective-permute-start.25 = (bf16[256,1024]{1,0:T(8,128)(2,1)S(1)}, bf16[256,1024]{1,0:T(8,128)(2,1)S(1)}, u32[]{:S(2)}, u32[]{:S(2)}) collective-permute-start(bf16[256,1024]{1,0:T(8,128)(2,1)S(1)} %constant_dynamic-update-slice_fusion.10.refs_0_), channel_id=1, source_target_pairs={{0,1},{1,2},{2,3},{3,4},{4,5},{5,6},{6,7},{7,0},{8,9},{9,10},{10,1... | collective-permute-start | bytes 1572872 | tf_op jit(solution)/shard_map/ppermute | solution.py:33
  100.6 11.8 %collective-permute-start.28 = (bf16[256,1024]{1,0:T(8,128)(2,1)S(1)}, bf16[256,1024]{1,0:T(8,128)(2,1)S(1)}, u32[]{:S(2)}, u32[]{:S(2)}) collective-permute-start(bf16[256,1024]{1,0:T(8,128)(2,1)S(1)} %constant_dynamic-update-slice_fusion.15.refs_4_), channel_id=1, source_target_pairs={{0,8},{1,9},{2,10},{3,11},{4,12},{5,13},{6,14},{7,15},{8,16},{9,17... | collective-permute-start | bytes 1572872 | tf_op jit(solution)/shard_map/ppermute | solution.py:33
  101.7 13.8 %collective-permute-start.26 = (bf16[256,1024]{1,0:T(8,128)(2,1)S(1)}, bf16[256,1024]{1,0:T(8,128)(2,1)S(1)}, u32[]{:S(2)}, u32[]{:S(2)}) collective-permute-start(bf16[256,1024]{1,0:T(8,128)(2,1)S(1)} %constant_dynamic-update-slice_fusion.10.refs_0_), channel_id=1, source_target_pairs={{0,7},{1,0},{2,1},{3,2},{4,3},{5,4},{6,5},{7,6},{8,15},{9,8},{10,9... | collective-permute-start | bytes 1572872 | tf_op jit(solution)/shard_map/ppermute | solution.py:33
  101.7 13.9 %collective-permute-start.29 = (bf16[256,1024]{1,0:T(8,128)(2,1)S(1)}, bf16[256,1024]{1,0:T(8,128)(2,1)S(1)}, u32[]{:S(2)}, u32[]{:S(2)}) collective-permute-start(bf16[256,1024]{1,0:T(8,128)(2,1)S(1)} %constant_dynamic-update-slice_fusion.15.refs_4_), channel_id=1, source_target_pairs={{0,24},{1,25},{2,26},{3,27},{4,28},{5,29},{6,30},{7,31},{8,0},{9,1... | collective-permute-start | bytes 1572872 | tf_op jit(solution)/shard_map/ppermute | solution.py:33
  109.0 9.5 %collective-permute-start.27 = (bf16[256,1024]{1,0:T(8,128)(2,1)S(1)}, bf16[256,1024]{1,0:T(8,128)(2,1)S(1)}, u32[]{:S(2)}, u32[]{:S(2)}) collective-permute-start(bf16[256,1024]{1,0:T(8,128)(2,1)S(1)} %collective-permute-done.25.refs_1_), channel_id=1, source_target_pairs={{0,1},{1,2},{2,3},{3,4},{4,5},{5,6},{6,7},{7,0},{8,9},{9,10},{10,1... | collective-permute-start | bytes 1572872 | tf_op jit(solution)/shard_map/ppermute | solution.py:33
  112.4 8.3 %collective-permute-start.30 = (bf16[256,1024]{1,0:T(8,128)(2,1)S(1)}, bf16[256,1024]{1,0:T(8,128)(2,1)S(1)}, u32[]{:S(2)}, u32[]{:S(2)}) collective-permute-start(bf16[256,1024]{1,0:T(8,128)(2,1)S(1)} %collective-permute-done.28.refs_5_), channel_id=1, source_target_pairs={{0,8},{1,9},{2,10},{3,11},{4,12},{5,13},{6,14},{7,15},{8,16},{9,17... | collective-permute-start | bytes 1572872 | tf_op jit(solution)/shard_map/ppermute | solution.py:33
  125.7 4.0 %collective-permute-start.31 = (bf16[128,1024]{1,0:T(8,128)(2,1)S(1)}, bf16[128,1024]{1,0:T(8,128)(2,1)S(1)}, u32[]{:S(2)}, u32[]{:S(2)}) collective-permute-start(bf16[128,1024]{1,0:T(8,128)(2,1)S(1)} %get-tuple-element.32), channel_id=1, source_target_pairs={{32,0},{33,1},{34,2},{35,3},{36,4},{37,5},{38,6},{39,7},{40,8},{41... | collective-permute-start | bytes 786440 | tf_op jit(solution)/shard_map/ppermute | solution.py:33
  130.3 3.9 %collective-permute-start.32 = (f32[4,32,1024]{2,1,0:T(8,128)S(1)}, f32[4,32,1024]{2,1,0:T(8,128)S(1)}, u32[]{:S(2)}, u32[]{:S(2)}) collective-permute-start(f32[4,32,1024]{2,1,0:T(8,128)S(1)} %finish.3), channel_id=1, source_target_pairs={{0,32},{1,33},{2,34},{3,35},{4,36},{5,37},{6,38},{7,39},{8,40},{9,... | collective-permute-start | bytes 1572872 | tf_op jit(solution)/shard_map/ppermute | solution.py:33
  (3 other events, 5.1 us)

commit v7 on v6

--- a/solution.py
+++ b/solution.py
@@ -111,14 +111,14 @@
     return pl.pallas_call(
         mask_kernel,
         out_shape=[jax.ShapeDtypeStruct((2, 32, M), jnp.float32)] * 2,
-        in_specs=[SMEM] + [pl.BlockSpec(memory_space=pl.ANY)] * 2,
+        in_specs=[SMEM] + [pl.BlockSpec(memory_space=pltpu.HBM)] * 2,
         out_specs=[VMEM, VMEM],
         scratch_shapes=[
             pltpu.VMEM((4, M // BLK, M // BLK), jnp.int32),
             pltpu.VMEM((4, 32, M), jnp.float32),
             pltpu.SemaphoreType.DMA((2,)),
         ],
-        compiler_params=pltpu.CompilerParams(vmem_limit_bytes=8 << 20),
+        compiler_params=pltpu.CompilerParams(vmem_limit_bytes=60 << 20),
         name="masked",
     )(where, pattern, ranges)
 
@@ -246,11 +246,12 @@
     mine, mine_half, rest_half = star(False, where, keep, other)
 
     near = send(rest_half, lambda x, c, y, z: (x, 1, y, z) if c == 0 else None)
-    across = send(rest_half, lambda x, c, y, z: (x ^ 1, 1, y, z) if c == 0 else None)
-    far = send(mine_half, lambda x, c, y, z: (x ^ 1, 0, y, z) if c == 0 else None)
-    this = jnp.where(core == 0, mine, across.astype(jnp.float32))
-    that = jnp.where(core == 0, far, near).astype(jnp.float32)
-    keep, other = jnp.where(odd == 1, that, this), jnp.where(odd == 1, this, that)
+    far = send(
+        jnp.where(core == 0, mine_half, near), lambda x, c, y, z: (x ^ 1, c, y, z)
+    ).astype(jnp.float32)
+    local = jnp.where(core == 0, mine, near.astype(jnp.float32))
+    swap = (odd == 1) == (core == 0)
+    keep, other = jnp.where(swap, far, local), jnp.where(swap, local, far)
     (joint,) = star(True, where, keep, other)
     shared = send(joint, lambda x, c, y, z: (x, 1, y, z) if c == 0 else None)
     return jnp.where(core == 1, shared, joint)[None]

time: 135 us -> 136 us (level)
  Pallas kernels: 12.1 us -> 14.1 us
  waiting for transfers between devices: 58.4 us -> 56.6 us
    pallas_call x1, Pallas kernels: 0.81 us -> 2.82 us  [masked(): pl.pallas_call(mask_kernel, out_shape=[jax.ShapeDtypeStruct((2, 32, M), j...]
    unnamed x12, local copies, waits for them, and re-layouts: 1.88 us -> 0.09 us
    ppermute x33 -> x32, waiting for transfers between devices: 58.4 us -> 56.6 us  [send(): return lax.ppermute(block, AXES, route(move))]
    ppermute x33 -> x32, starting transfers between devices: 61.1 us -> 61.6 us  [send(): return lax.ppermute(block, AXES, route(move))]
  transfers between devices with their start and end apart: 33 -> 32, of which waited for: 23 -> 23; matrix products, arithmetic and copies ran while one was open for 0% -> 1% of each run, Pallas kernels for 0% -> 0%
where the time goes in v7:
time: 136 us
  starting transfers between devices  61.6 us (45%)
  waiting for transfers between devices  56.6 us (42%)
  Pallas kernels  14.1 us (10%)
  other arithmetic  1.69 us (1%)
    ppermute x32, starting transfers between devices, send(): return lax.ppermute(block, AXES, route(move))  61.6 us
    ppermute x32, waiting for transfers between devices, send(): return lax.ppermute(block, AXES, route(move))  56.6 us
    pallas_call x2, Pallas kernels, chain(): pl.pallas_call(chain_kernel, out_shape=[jax.ShapeDtypeStruct((128, M), jn...  10 us
    pallas_call x1, Pallas kernels, masked(): pl.pallas_call(mask_kernel, out_shape=[jax.ShapeDtypeStruct((2, 32, M), j...  2.82 us
  transfers between devices with their start and end apart: 32, of which 23 were waited for; matrix products, arithmetic and copies ran while one was open for 1% of the time, Pallas kernels for 0%

profile of v7, /device:TPU:1, one launch (start us, length us, event | category | flops | bytes accessed | tf_op | source)
XLA Modules:
  0.0 135.6 jit_solution(3311424452801418482)
XLA Ops:
  0.7 2.8 %masked.1 = (f32[2,32,1024]{2,1,0:T(8,128)}, f32[2,32,1024]{2,1,0:T(8,128)}) custom-call(s32[4]{0:T(128)} %pad_add_fusion.where, s32[4,16,16]{2,1,0:T(8,128)} %bitcast.25, f32[4,32,1024]{2,1,0:T(8,128)} %bitcast.24), custom_call_target="tpu_custom_call" | custom-call | tf_op jit(solution)/shard_map/masked/pallas_call | solution.py:111
  3.5 3.3 %collective-permute-start = (f32[2,32,1024]{2,1,0:T(8,128)}, f32[2,32,1024]{2,1,0:T(8,128)S(1)}, u32[]{:S(2)}, u32[]{:S(2)}) collective-permute-start(f32[2,32,1024]{2,1,0:T(8,128)} %get-tuple-element.21), channel_id=1, source_target_pairs={{0,32},{1,33},{2,34},{3,35},{4,36},{5,37},{6,38},{7,39},{8,40},{9,... | collective-permute-start | bytes 786440 | tf_op jit(solution)/shard_map/ppermute | solution.py:33
  8.3 5.3 %collective-permute-start.1 = (bf16[64,1024]{1,0:T(8,128)(2,1)S(1)}, bf16[64,1024]{1,0:T(8,128)(2,1)S(1)}, u32[]{:S(2)}, u32[]{:S(2)}) collective-permute-start(bf16[64,1024]{1,0:T(8,128)(2,1)S(1)} %fusion), channel_id=1, source_target_pairs={{0,4},{1,5},{2,6},{3,7},{4,0},{5,1},{6,2},{7,3},{8,12},{9,13},{10,... | collective-permute-start | bytes 393224 | tf_op jit(solution)/shard_map/ppermute | solution.py:33
  13.6 3.4 %collective-permute-done.1 = bf16[64,1024]{1,0:T(8,128)(2,1)S(1)} collective-permute-done((bf16[64,1024]{1,0:T(8,128)(2,1)S(1)}, bf16[64,1024]{1,0:T(8,128)(2,1)S(1)}, u32[]{:S(2)}, u32[]{:S(2)}) %collective-permute-start.1) | collective-permute-done | bytes 131104 | tf_op jit(solution)/shard_map/ppermute | solution.py:33
  17.0 5.6 %collective-permute-start.5 = (bf16[64,1024]{1,0:T(8,128)(2,1)S(1)}, bf16[64,1024]{1,0:T(8,128)(2,1)S(1)}, u32[]{:S(2)}, u32[]{:S(2)}) collective-permute-start(bf16[64,1024]{1,0:T(8,128)(2,1)S(1)} %pad_maximum_fusion.1), channel_id=1, source_target_pairs={{0,1},{1,2},{2,3},{3,4},{4,5},{5,6},{6,7},{7,0},{8,9},{9,10},{10,1... | collective-permute-start | bytes 393224 | tf_op jit(solution)/shard_map/ppermute | solution.py:33
  22.6 2.8 %collective-permute-start.2 = (bf16[64,1024]{1,0:T(8,128)(2,1)S(1)}, bf16[64,1024]{1,0:T(8,128)(2,1)S(1)}, u32[]{:S(2)}, u32[]{:S(2)}) collective-permute-start(bf16[64,1024]{1,0:T(8,128)(2,1)S(1)} %pad_maximum_fusion), channel_id=1, source_target_pairs={{0,8},{1,9},{2,10},{3,11},{4,12},{5,13},{6,14},{7,15},{8,16},{9,17... | collective-permute-start | bytes 393224 | tf_op jit(solution)/shard_map/ppermute | solution.py:33
  26.5 2.7 %collective-permute-start.7 = (bf16[64,1024]{1,0:T(8,128)(2,1)S(1)}, bf16[64,1024]{1,0:T(8,128)(2,1)S(1)}, u32[]{:S(2)}, u32[]{:S(2)}) collective-permute-start(bf16[64,1024]{1,0:T(8,128)(2,1)S(1)} %collective-permute-done.5), channel_id=1, source_target_pairs={{0,1},{1,2},{2,3},{3,4},{4,5},{5,6},{6,7},{7,0},{8,9},{9,10},{10,1... | collective-permute-start | bytes 393224 | tf_op jit(solution)/shard_map/ppermute | solution.py:33
  29.2 1.9 %collective-permute-done.2 = bf16[64,1024]{1,0:T(8,128)(2,1)S(1)} collective-permute-done((bf16[64,1024]{1,0:T(8,128)(2,1)S(1)}, bf16[64,1024]{1,0:T(8,128)(2,1)S(1)}, u32[]{:S(2)}, u32[]{:S(2)}) %collective-permute-start.2) | collective-permute-done | bytes 131104 | tf_op jit(solution)/shard_map/ppermute | solution.py:33
  33.1 2.5 %collective-permute-start.8 = (bf16[256,1024]{1,0:T(8,128)(2,1)S(1)}, bf16[256,1024]{1,0:T(8,128)(2,1)S(1)}, u32[]{:S(2)}, u32[]{:S(2)}) collective-permute-start(bf16[256,1024]{1,0:T(8,128)(2,1)S(1)} %constant_dynamic-update-slice_fusion.refs_0_), channel_id=1, source_target_pairs={{0,1},{1,2},{2,3},{3,4},{4,5},{5,6},{6,7},{7,0},{8,9},{9,10},{10,1... | collective-permute-start | bytes 1572872 | tf_op jit(solution)/shard_map/ppermute | solution.py:33
  37.1 6.2 %collective-permute-done.8.refs_1_ = bf16[256,1024]{1,0:T(8,128)(2,1)S(1)} collective-permute-done((bf16[256,1024]{1,0:T(8,128)(2,1)S(1)}, bf16[256,1024]{1,0:T(8,128)(2,1)S(1)}, u32[]{:S(2)}, u32[]{:S(2)}) %collective-permute-start.8) | collective-permute-done | bytes 524320 | tf_op jit(solution)/shard_map/ppermute | solution.py:33
  43.3 3.3 %collective-permute-start.10 = (bf16[256,1024]{1,0:T(8,128)(2,1)S(1)}, bf16[256,1024]{1,0:T(8,128)(2,1)S(1)}, u32[]{:S(2)}, u32[]{:S(2)}) collective-permute-start(bf16[256,1024]{1,0:T(8,128)(2,1)S(1)} %collective-permute-done.8.refs_1_), channel_id=1, source_target_pairs={{0,1},{1,2},{2,3},{3,4},{4,5},{5,6},{6,7},{7,0},{8,9},{9,10},{10,1... | collective-permute-start | bytes 1572872 | tf_op jit(solution)/shard_map/ppermute | solution.py:33
  46.6 4.4 %collective-permute-done.9.refs_2_ = bf16[256,1024]{1,0:T(8,128)(2,1)S(1)} collective-permute-done((bf16[256,1024]{1,0:T(8,128)(2,1)S(1)}, bf16[256,1024]{1,0:T(8,128)(2,1)S(1)}, u32[]{:S(2)}, u32[]{:S(2)}) %collective-permute-start.9) | collective-permute-done | bytes 524320 | tf_op jit(solution)/shard_map/ppermute | solution.py:33
  51.1 1.9 %collective-permute-done.10.refs_3_ = bf16[256,1024]{1,0:T(8,128)(2,1)S(1)} collective-permute-done((bf16[256,1024]{1,0:T(8,128)(2,1)S(1)}, bf16[256,1024]{1,0:T(8,128)(2,1)S(1)}, u32[]{:S(2)}, u32[]{:S(2)}) %collective-permute-start.10) | collective-permute-done | bytes 524320 | tf_op jit(solution)/shard_map/ppermute | solution.py:33
  53.0 2.2 %collective-permute-done.13.refs_7_ = bf16[256,1024]{1,0:T(8,128)(2,1)S(1)} collective-permute-done((bf16[256,1024]{1,0:T(8,128)(2,1)S(1)}, bf16[256,1024]{1,0:T(8,128)(2,1)S(1)}, u32[]{:S(2)}, u32[]{:S(2)}) %collective-permute-start.13) | collective-permute-done | bytes 524320 | tf_op jit(solution)/shard_map/ppermute | solution.py:33
  55.2 5.0 %chain.2 = (bf16[128,1024]{1,0:T(8,128)(2,1)S(1)}, bf16[1024,1024]{1,0:T(8,128)(2,1)S(1)}, bf16[1024,1024]{1,0:T(8,128)(2,1)S(1)}) custom-call(s32[4]{0:T(128)S(1)} %copy-done.1, f32[2,32,1024]{2,1,0:T(8,128)S(1)} %copy-done, f32[2,32,1024]{2,1,0:T(8,128)S(1)} %collective-permute-done.other, bf16[256,1024]{1,0:T(8,128)(2,1)S(1)} %constant_dynamic-update-slice_fusion.refs_0_, ...), custom_call_target="tpu_custom_call" | custom-call | tf_op jit(solution)/shard_map/chain/pallas_call | solution.py:162
  60.2 4.3 %collective-permute-start.14 = (bf16[128,1024]{1,0:T(8,128)(2,1)S(1)}, bf16[128,1024]{1,0:T(8,128)(2,1)S(1)}, u32[]{:S(2)}, u32[]{:S(2)}) collective-permute-start(bf16[128,1024]{1,0:T(8,128)(2,1)S(1)} %get-tuple-element.24), channel_id=1, source_target_pairs={{32,0},{33,1},{34,2},{35,3},{36,4},{37,5},{38,6},{39,7},{40,8},{41... | collective-permute-start | bytes 786440 | tf_op jit(solution)/shard_map/ppermute | solution.py:33
  67.7 2.1 %collective-permute-done.15 = bf16[2,32,1024]{2,1,0:T(8,128)(2,1)S(1)} collective-permute-done((bf16[2,32,1024]{2,1,0:T(8,128)(2,1)S(1)}, bf16[2,32,1024]{2,1,0:T(8,128)(2,1)S(1)}, u32[]{:S(2)}, u32[]{:S(2)}) %collective-permute-start.15) | collective-permute-done | bytes 131104 | tf_op jit(solution)/shard_map/ppermute | solution.py:33
  71.2 3.6 %collective-permute-done.16 = bf16[2,32,1024]{2,1,0:T(8,128)(2,1)S(1)} collective-permute-done((bf16[2,32,1024]{2,1,0:T(8,128)(2,1)S(1)}, bf16[2,32,1024]{2,1,0:T(8,128)(2,1)S(1)}, u32[]{:S(2)}, u32[]{:S(2)}) %collective-permute-start.16) | collective-permute-done | bytes 131104 | tf_op jit(solution)/shard_map/ppermute | solution.py:33
  75.0 2.6 %collective-permute-start.17 = (bf16[64,1024]{1,0:T(8,128)(2,1)S(1)}, bf16[64,1024]{1,0:T(8,128)(2,1)S(1)}, u32[]{:S(2)}, u32[]{:S(2)}) collective-permute-start(bf16[64,1024]{1,0:T(8,128)(2,1)S(1)} %fusion.1), channel_id=1, source_target_pairs={{0,4},{1,5},{2,6},{3,7},{4,0},{5,1},{6,2},{7,3},{8,12},{9,13},{10,... | collective-permute-start | bytes 393224 | tf_op jit(solution)/shard_map/ppermute | solution.py:33
  77.6 5.3 %collective-permute-done.17 = bf16[64,1024]{1,0:T(8,128)(2,1)S(1)} collective-permute-done((bf16[64,1024]{1,0:T(8,128)(2,1)S(1)}, bf16[64,1024]{1,0:T(8,128)(2,1)S(1)}, u32[]{:S(2)}, u32[]{:S(2)}) %collective-permute-start.17) | collective-permute-done | bytes 131104 | tf_op jit(solution)/shard_map/ppermute | solution.py:33
  83.0 6.5 %collective-permute-start.21 = (bf16[64,1024]{1,0:T(8,128)(2,1)S(1)}, bf16[64,1024]{1,0:T(8,128)(2,1)S(1)}, u32[]{:S(2)}, u32[]{:S(2)}) collective-permute-start(bf16[64,1024]{1,0:T(8,128)(2,1)S(1)} %pad_maximum_fusion.3), channel_id=1, source_target_pairs={{0,1},{1,2},{2,3},{3,4},{4,5},{5,6},{6,7},{7,0},{8,9},{9,10},{10,1... | collective-permute-start | bytes 393224 | tf_op jit(solution)/shard_map/ppermute | solution.py:33
  91.4 3.1 %collective-permute-start.23 = (bf16[64,1024]{1,0:T(8,128)(2,1)S(1)}, bf16[64,1024]{1,0:T(8,128)(2,1)S(1)}, u32[]{:S(2)}, u32[]{:S(2)}) collective-permute-start(bf16[64,1024]{1,0:T(8,128)(2,1)S(1)} %collective-permute-done.21), channel_id=1, source_target_pairs={{0,1},{1,2},{2,3},{3,4},{4,5},{5,6},{6,7},{7,0},{8,9},{9,10},{10,1... | collective-permute-start | bytes 393224 | tf_op jit(solution)/shard_map/ppermute | solution.py:33
  94.6 2.9 %collective-permute-done.19 = bf16[64,1024]{1,0:T(8,128)(2,1)S(1)} collective-permute-done((bf16[64,1024]{1,0:T(8,128)(2,1)S(1)}, bf16[64,1024]{1,0:T(8,128)(2,1)S(1)}, u32[]{:S(2)}, u32[]{:S(2)}) %collective-permute-start.19) | collective-permute-done | bytes 131104 | tf_op jit(solution)/shard_map/ppermute | solution.py:33
  97.7 3.5 %collective-permute-start.24 = (bf16[256,1024]{1,0:T(8,128)(2,1)S(1)}, bf16[256,1024]{1,0:T(8,128)(2,1)S(1)}, u32[]{:S(2)}, u32[]{:S(2)}) collective-permute-start(bf16[256,1024]{1,0:T(8,128)(2,1)S(1)} %constant_dynamic-update-slice_fusion.10.refs_0_), channel_id=1, source_target_pairs={{0,1},{1,2},{2,3},{3,4},{4,5},{5,6},{6,7},{7,0},{8,9},{9,10},{10,1... | collective-permute-start | bytes 1572872 | tf_op jit(solution)/shard_map/ppermute | solution.py:33
  102.6 6.6 %collective-permute-done.24.refs_1_ = bf16[256,1024]{1,0:T(8,128)(2,1)S(1)} collective-permute-done((bf16[256,1024]{1,0:T(8,128)(2,1)S(1)}, bf16[256,1024]{1,0:T(8,128)(2,1)S(1)}, u32[]{:S(2)}, u32[]{:S(2)}) %collective-permute-start.24) | collective-permute-done | bytes 524320 | tf_op jit(solution)/shard_map/ppermute | solution.py:33
  109.3 3.4 %collective-permute-start.26 = (bf16[256,1024]{1,0:T(8,128)(2,1)S(1)}, bf16[256,1024]{1,0:T(8,128)(2,1)S(1)}, u32[]{:S(2)}, u32[]{:S(2)}) collective-permute-start(bf16[256,1024]{1,0:T(8,128)(2,1)S(1)} %collective-permute-done.24.refs_1_), channel_id=1, source_target_pairs={{0,1},{1,2},{2,3},{3,4},{4,5},{5,6},{6,7},{7,0},{8,9},{9,10},{10,1... | collective-permute-start | bytes 1572872 | tf_op jit(solution)/shard_map/ppermute | solution.py:33
  112.7 3.4 %collective-permute-done.25.refs_2_ = bf16[256,1024]{1,0:T(8,128)(2,1)S(1)} collective-permute-done((bf16[256,1024]{1,0:T(8,128)(2,1)S(1)}, bf16[256,1024]{1,0:T(8,128)(2,1)S(1)}, u32[]{:S(2)}, u32[]{:S(2)}) %collective-permute-start.25) | collective-permute-done | bytes 524320 | tf_op jit(solution)/shard_map/ppermute | solution.py:33
  116.2 2.6 %collective-permute-done.26.refs_3_ = bf16[256,1024]{1,0:T(8,128)(2,1)S(1)} collective-permute-done((bf16[256,1024]{1,0:T(8,128)(2,1)S(1)}, bf16[256,1024]{1,0:T(8,128)(2,1)S(1)}, u32[]{:S(2)}, u32[]{:S(2)}) %collective-permute-start.26) | collective-permute-done | bytes 524320 | tf_op jit(solution)/shard_map/ppermute | solution.py:33
  118.8 2.2 %collective-permute-done.29.refs_7_ = bf16[256,1024]{1,0:T(8,128)(2,1)S(1)} collective-permute-done((bf16[256,1024]{1,0:T(8,128)(2,1)S(1)}, bf16[256,1024]{1,0:T(8,128)(2,1)S(1)}, u32[]{:S(2)}, u32[]{:S(2)}) %collective-permute-start.29) | collective-permute-done | bytes 524320 | tf_op jit(solution)/shard_map/ppermute | solution.py:33
  121.0 5.0 %chain.3 = (bf16[128,1024]{1,0:T(8,128)(2,1)S(1)}, bf16[1024,1024]{1,0:T(8,128)(2,1)S(1)}, bf16[1024,1024]{1,0:T(8,128)(2,1)S(1)}) custom-call(s32[4]{0:T(128)S(1)} %copy-done.1, f32[2,32,1024]{2,1,0:T(8,128)S(1)} %get-tuple-element.36.keep, f32[2,32,1024]{2,1,0:T(8,128)S(1)} %get-tuple-element.35.other, ...), custom_call_target="tpu_custom_call" | custom-call | tf_op jit(solution)/shard_map/chain/pallas_call | solution.py:162
  126.0 3.1 %collective-permute-start.30 = (bf16[128,1024]{1,0:T(8,128)(2,1)S(1)}, bf16[128,1024]{1,0:T(8,128)(2,1)S(1)}, u32[]{:S(2)}, u32[]{:S(2)}) collective-permute-start(bf16[128,1024]{1,0:T(8,128)(2,1)S(1)} %get-tuple-element.32), channel_id=1, source_target_pairs={{32,0},{33,1},{34,2},{35,3},{36,4},{37,5},{38,6},{39,7},{40,8},{41... | collective-permute-start | bytes 786440 | tf_op jit(solution)/shard_map/ppermute | solution.py:33
  132.2 2.6 %collective-permute-done.31 = f32[4,32,1024]{2,1,0:T(8,128)S(1)} collective-permute-done((f32[4,32,1024]{2,1,0:T(8,128)S(1)}, f32[4,32,1024]{2,1,0:T(8,128)S(1)}, u32[]{:S(2)}, u32[]{:S(2)}) %collective-permute-start.31) | collective-permute-done | bytes 524320 | tf_op jit(solution)/shard_map/ppermute | solution.py:33
  (70 shorter events, 19.0 us)
Async XLA Ops:
  3.5 4.7 %collective-permute-start = (f32[2,32,1024]{2,1,0:T(8,128)}, f32[2,32,1024]{2,1,0:T(8,128)S(1)}, u32[]{:S(2)}, u32[]{:S(2)}) collective-permute-start(f32[2,32,1024]{2,1,0:T(8,128)} %get-tuple-element.21), channel_id=1, source_target_pairs={{0,32},{1,33},{2,34},{3,35},{4,36},{5,37},{6,38},{7,39},{8,40},{9,... | collective-permute-start | bytes 786440 | tf_op jit(solution)/shard_map/ppermute | solution.py:33
  8.3 8.7 %collective-permute-start.1 = (bf16[64,1024]{1,0:T(8,128)(2,1)S(1)}, bf16[64,1024]{1,0:T(8,128)(2,1)S(1)}, u32[]{:S(2)}, u32[]{:S(2)}) collective-permute-start(bf16[64,1024]{1,0:T(8,128)(2,1)S(1)} %fusion), channel_id=1, source_target_pairs={{0,4},{1,5},{2,6},{3,7},{4,0},{5,1},{6,2},{7,3},{8,12},{9,13},{10,... | collective-permute-start | bytes 393224 | tf_op jit(solution)/shard_map/ppermute | solution.py:33
  17.0 9.5 %collective-permute-start.5 = (bf16[64,1024]{1,0:T(8,128)(2,1)S(1)}, bf16[64,1024]{1,0:T(8,128)(2,1)S(1)}, u32[]{:S(2)}, u32[]{:S(2)}) collective-permute-start(bf16[64,1024]{1,0:T(8,128)(2,1)S(1)} %pad_maximum_fusion.1), channel_id=1, source_target_pairs={{0,1},{1,2},{2,3},{3,4},{4,5},{5,6},{6,7},{7,0},{8,9},{9,10},{10,1... | collective-permute-start | bytes 393224 | tf_op jit(solution)/shard_map/ppermute | solution.py:33
  22.6 8.5 %collective-permute-start.2 = (bf16[64,1024]{1,0:T(8,128)(2,1)S(1)}, bf16[64,1024]{1,0:T(8,128)(2,1)S(1)}, u32[]{:S(2)}, u32[]{:S(2)}) collective-permute-start(bf16[64,1024]{1,0:T(8,128)(2,1)S(1)} %pad_maximum_fusion), channel_id=1, source_target_pairs={{0,8},{1,9},{2,10},{3,11},{4,12},{5,13},{6,14},{7,15},{8,16},{9,17... | collective-permute-start | bytes 393224 | tf_op jit(solution)/shard_map/ppermute | solution.py:33
  25.5 7.6 %collective-permute-start.4 = (bf16[64,1024]{1,0:T(8,128)(2,1)S(1)}, bf16[64,1024]{1,0:T(8,128)(2,1)S(1)}, u32[]{:S(2)}, u32[]{:S(2)}) collective-permute-start(bf16[64,1024]{1,0:T(8,128)(2,1)S(1)} %pad_maximum_fusion), channel_id=1, source_target_pairs={{0,16},{1,17},{2,18},{3,19},{4,20},{5,21},{6,22},{7,23},{8,24},{9,... | collective-permute-start | bytes 393224 | tf_op jit(solution)/shard_map/ppermute | solution.py:33
  25.8 7.2 %collective-permute-start.3 = (bf16[64,1024]{1,0:T(8,128)(2,1)S(1)}, bf16[64,1024]{1,0:T(8,128)(2,1)S(1)}, u32[]{:S(2)}, u32[]{:S(2)}) collective-permute-start(bf16[64,1024]{1,0:T(8,128)(2,1)S(1)} %pad_maximum_fusion), channel_id=1, source_target_pairs={{0,24},{1,25},{2,26},{3,27},{4,28},{5,29},{6,30},{7,31},{8,0},{9,1... | collective-permute-start | bytes 393224 | tf_op jit(solution)/shard_map/ppermute | solution.py:33
  26.5 6.6 %collective-permute-start.6 = (bf16[64,1024]{1,0:T(8,128)(2,1)S(1)}, bf16[64,1024]{1,0:T(8,128)(2,1)S(1)}, u32[]{:S(2)}, u32[]{:S(2)}) collective-permute-start(bf16[64,1024]{1,0:T(8,128)(2,1)S(1)} %pad_maximum_fusion.1), channel_id=1, source_target_pairs={{0,7},{1,0},{2,1},{3,2},{4,3},{5,4},{6,5},{7,6},{8,15},{9,8},{10,9... | collective-permute-start | bytes 393224 | tf_op jit(solution)/shard_map/ppermute | solution.py:33
  26.5 6.6 %collective-permute-start.7 = (bf16[64,1024]{1,0:T(8,128)(2,1)S(1)}, bf16[64,1024]{1,0:T(8,128)(2,1)S(1)}, u32[]{:S(2)}, u32[]{:S(2)}) collective-permute-start(bf16[64,1024]{1,0:T(8,128)(2,1)S(1)} %collective-permute-done.5), channel_id=1, source_target_pairs={{0,1},{1,2},{2,3},{3,4},{4,5},{5,6},{6,7},{7,0},{8,9},{9,10},{10,1... | collective-permute-start | bytes 393224 | tf_op jit(solution)/shard_map/ppermute | solution.py:33
  33.1 10.2 %collective-permute-start.8 = (bf16[256,1024]{1,0:T(8,128)(2,1)S(1)}, bf16[256,1024]{1,0:T(8,128)(2,1)S(1)}, u32[]{:S(2)}, u32[]{:S(2)}) collective-permute-start(bf16[256,1024]{1,0:T(8,128)(2,1)S(1)} %constant_dynamic-update-slice_fusion.refs_0_), channel_id=1, source_target_pairs={{0,1},{1,2},{2,3},{3,4},{4,5},{5,6},{6,7},{7,0},{8,9},{9,10},{10,1... | collective-permute-start | bytes 1572872 | tf_op jit(solution)/shard_map/ppermute | solution.py:33
  35.7 10.9 %collective-permute-start.11 = (bf16[256,1024]{1,0:T(8,128)(2,1)S(1)}, bf16[256,1024]{1,0:T(8,128)(2,1)S(1)}, u32[]{:S(2)}, u32[]{:S(2)}) collective-permute-start(bf16[256,1024]{1,0:T(8,128)(2,1)S(1)} %constant_dynamic-update-slice_fusion.5.refs_4_), channel_id=1, source_target_pairs={{0,8},{1,9},{2,10},{3,11},{4,12},{5,13},{6,14},{7,15},{8,16},{9,17... | collective-permute-start | bytes 1572872 | tf_op jit(solution)/shard_map/ppermute | solution.py:33
  36.8 14.2 %collective-permute-start.9 = (bf16[256,1024]{1,0:T(8,128)(2,1)S(1)}, bf16[256,1024]{1,0:T(8,128)(2,1)S(1)}, u32[]{:S(2)}, u32[]{:S(2)}) collective-permute-start(bf16[256,1024]{1,0:T(8,128)(2,1)S(1)} %constant_dynamic-update-slice_fusion.refs_0_), channel_id=1, source_target_pairs={{0,7},{1,0},{2,1},{3,2},{4,3},{5,4},{6,5},{7,6},{8,15},{9,8},{10,9... | collective-permute-start | bytes 1572872 | tf_op jit(solution)/shard_map/ppermute | solution.py:33
  36.8 14.3 %collective-permute-start.12 = (bf16[256,1024]{1,0:T(8,128)(2,1)S(1)}, bf16[256,1024]{1,0:T(8,128)(2,1)S(1)}, u32[]{:S(2)}, u32[]{:S(2)}) collective-permute-start(bf16[256,1024]{1,0:T(8,128)(2,1)S(1)} %constant_dynamic-update-slice_fusion.5.refs_4_), channel_id=1, source_target_pairs={{0,24},{1,25},{2,26},{3,27},{4,28},{5,29},{6,30},{7,31},{8,0},{9,1... | collective-permute-start | bytes 1572872 | tf_op jit(solution)/shard_map/ppermute | solution.py:33
  43.3 9.7 %collective-permute-start.10 = (bf16[256,1024]{1,0:T(8,128)(2,1)S(1)}, bf16[256,1024]{1,0:T(8,128)(2,1)S(1)}, u32[]{:S(2)}, u32[]{:S(2)}) collective-permute-start(bf16[256,1024]{1,0:T(8,128)(2,1)S(1)} %collective-permute-done.8.refs_1_), channel_id=1, source_target_pairs={{0,1},{1,2},{2,3},{3,4},{4,5},{5,6},{6,7},{7,0},{8,9},{9,10},{10,1... | collective-permute-start | bytes 1572872 | tf_op jit(solution)/shard_map/ppermute | solution.py:33
  46.6 8.6 %collective-permute-start.13 = (bf16[256,1024]{1,0:T(8,128)(2,1)S(1)}, bf16[256,1024]{1,0:T(8,128)(2,1)S(1)}, u32[]{:S(2)}, u32[]{:S(2)}) collective-permute-start(bf16[256,1024]{1,0:T(8,128)(2,1)S(1)} %collective-permute-done.11.refs_5_), channel_id=1, source_target_pairs={{0,8},{1,9},{2,10},{3,11},{4,12},{5,13},{6,14},{7,15},{8,16},{9,17... | collective-permute-start | bytes 1572872 | tf_op jit(solution)/shard_map/ppermute | solution.py:33
  60.2 5.5 %collective-permute-start.14 = (bf16[128,1024]{1,0:T(8,128)(2,1)S(1)}, bf16[128,1024]{1,0:T(8,128)(2,1)S(1)}, u32[]{:S(2)}, u32[]{:S(2)}) collective-permute-start(bf16[128,1024]{1,0:T(8,128)(2,1)S(1)} %get-tuple-element.24), channel_id=1, source_target_pairs={{32,0},{33,1},{34,2},{35,3},{36,4},{37,5},{38,6},{39,7},{40,8},{41... | collective-permute-start | bytes 786440 | tf_op jit(solution)/shard_map/ppermute | solution.py:33
  66.4 3.4 %collective-permute-start.15 = (bf16[2,32,1024]{2,1,0:T(8,128)(2,1)S(1)}, bf16[2,32,1024]{2,1,0:T(8,128)(2,1)S(1)}, u32[]{:S(2)}, u32[]{:S(2)}) collective-permute-start(bf16[2,32,1024]{2,1,0:T(8,128)(2,1)S(1)} %get-tuple-element.28), channel_id=1, source_target_pairs={{0,32},{1,33},{2,34},{3,35},{4,36},{5,37},{6,38},{7,39},{8,40},{9,... | collective-permute-start | bytes 393224 | tf_op jit(solution)/shard_map/ppermute | solution.py:33
  69.8 5.0 %collective-permute-start.16 = (bf16[2,32,1024]{2,1,0:T(8,128)(2,1)S(1)}, bf16[2,32,1024]{2,1,0:T(8,128)(2,1)S(1)}, u32[]{:S(2)}, u32[]{:S(2)}) collective-permute-start(bf16[2,32,1024]{2,1,0:T(8,128)(2,1)S(1)} %broadcast_select_fusion), channel_id=1, source_target_pairs={{0,64},{1,65},{2,66},{3,67},{4,68},{5,69},{6,70},{7,71},{8,72},{9,... | collective-permute-start | bytes 393224 | tf_op jit(solution)/shard_map/ppermute | solution.py:33
  75.0 7.9 %collective-permute-start.17 = (bf16[64,1024]{1,0:T(8,128)(2,1)S(1)}, bf16[64,1024]{1,0:T(8,128)(2,1)S(1)}, u32[]{:S(2)}, u32[]{:S(2)}) collective-permute-start(bf16[64,1024]{1,0:T(8,128)(2,1)S(1)} %fusion.1), channel_id=1, source_target_pairs={{0,4},{1,5},{2,6},{3,7},{4,0},{5,1},{6,2},{7,3},{8,12},{9,13},{10,... | collective-permute-start | bytes 393224 | tf_op jit(solution)/shard_map/ppermute | solution.py:33
  83.0 8.5 %collective-permute-start.21 = (bf16[64,1024]{1,0:T(8,128)(2,1)S(1)}, bf16[64,1024]{1,0:T(8,128)(2,1)S(1)}, u32[]{:S(2)}, u32[]{:S(2)}) collective-permute-start(bf16[64,1024]{1,0:T(8,128)(2,1)S(1)} %pad_maximum_fusion.3), channel_id=1, source_target_pairs={{0,1},{1,2},{2,3},{3,4},{4,5},{5,6},{6,7},{7,0},{8,9},{9,10},{10,1... | collective-permute-start | bytes 393224 | tf_op jit(solution)/shard_map/ppermute | solution.py:33
  89.5 5.0 %collective-permute-start.18 = (bf16[64,1024]{1,0:T(8,128)(2,1)S(1)}, bf16[64,1024]{1,0:T(8,128)(2,1)S(1)}, u32[]{:S(2)}, u32[]{:S(2)}) collective-permute-start(bf16[64,1024]{1,0:T(8,128)(2,1)S(1)} %pad_maximum_fusion.2), channel_id=1, source_target_pairs={{0,8},{1,9},{2,10},{3,11},{4,12},{5,13},{6,14},{7,15},{8,16},{9,17... | collective-permute-start | bytes 393224 | tf_op jit(solution)/shard_map/ppermute | solution.py:33
  89.6 7.9 %collective-permute-start.20 = (bf16[64,1024]{1,0:T(8,128)(2,1)S(1)}, bf16[64,1024]{1,0:T(8,128)(2,1)S(1)}, u32[]{:S(2)}, u32[]{:S(2)}) collective-permute-start(bf16[64,1024]{1,0:T(8,128)(2,1)S(1)} %pad_maximum_fusion.2), channel_id=1, source_target_pairs={{0,16},{1,17},{2,18},{3,19},{4,20},{5,21},{6,22},{7,23},{8,24},{9,... | collective-permute-start | bytes 393224 | tf_op jit(solution)/shard_map/ppermute | solution.py:33
  90.3 7.2 %collective-permute-start.19 = (bf16[64,1024]{1,0:T(8,128)(2,1)S(1)}, bf16[64,1024]{1,0:T(8,128)(2,1)S(1)}, u32[]{:S(2)}, u32[]{:S(2)}) collective-permute-start(bf16[64,1024]{1,0:T(8,128)(2,1)S(1)} %pad_maximum_fusion.2), channel_id=1, source_target_pairs={{0,24},{1,25},{2,26},{3,27},{4,28},{5,29},{6,30},{7,31},{8,0},{9,1... | collective-permute-start | bytes 393224 | tf_op jit(solution)/shard_map/ppermute | solution.py:33
  91.1 6.5 %collective-permute-start.22 = (bf16[64,1024]{1,0:T(8,128)(2,1)S(1)}, bf16[64,1024]{1,0:T(8,128)(2,1)S(1)}, u32[]{:S(2)}, u32[]{:S(2)}) collective-permute-start(bf16[64,1024]{1,0:T(8,128)(2,1)S(1)} %pad_maximum_fusion.3), channel_id=1, source_target_pairs={{0,7},{1,0},{2,1},{3,2},{4,3},{5,4},{6,5},{7,6},{8,15},{9,8},{10,9... | collective-permute-start | bytes 393224 | tf_op jit(solution)/shard_map/ppermute | solution.py:33
  91.4 6.2 %collective-permute-start.23 = (bf16[64,1024]{1,0:T(8,128)(2,1)S(1)}, bf16[64,1024]{1,0:T(8,128)(2,1)S(1)}, u32[]{:S(2)}, u32[]{:S(2)}) collective-permute-start(bf16[64,1024]{1,0:T(8,128)(2,1)S(1)} %collective-permute-done.21), channel_id=1, source_target_pairs={{0,1},{1,2},{2,3},{3,4},{4,5},{5,6},{6,7},{7,0},{8,9},{9,10},{10,1... | collective-permute-start | bytes 393224 | tf_op jit(solution)/shard_map/ppermute | solution.py:33
  97.7 11.6 %collective-permute-start.24 = (bf16[256,1024]{1,0:T(8,128)(2,1)S(1)}, bf16[256,1024]{1,0:T(8,128)(2,1)S(1)}, u32[]{:S(2)}, u32[]{:S(2)}) collective-permute-start(bf16[256,1024]{1,0:T(8,128)(2,1)S(1)} %constant_dynamic-update-slice_fusion.10.refs_0_), channel_id=1, source_target_pairs={{0,1},{1,2},{2,3},{3,4},{4,5},{5,6},{6,7},{7,0},{8,9},{9,10},{10,1... | collective-permute-start | bytes 1572872 | tf_op jit(solution)/shard_map/ppermute | solution.py:33
  101.2 11.5 %collective-permute-start.27 = (bf16[256,1024]{1,0:T(8,128)(2,1)S(1)}, bf16[256,1024]{1,0:T(8,128)(2,1)S(1)}, u32[]{:S(2)}, u32[]{:S(2)}) collective-permute-start(bf16[256,1024]{1,0:T(8,128)(2,1)S(1)} %constant_dynamic-update-slice_fusion.15.refs_4_), channel_id=1, source_target_pairs={{0,8},{1,9},{2,10},{3,11},{4,12},{5,13},{6,14},{7,15},{8,16},{9,17... | collective-permute-start | bytes 1572872 | tf_op jit(solution)/shard_map/ppermute | solution.py:33
  102.3 13.8 %collective-permute-start.25 = (bf16[256,1024]{1,0:T(8,128)(2,1)S(1)}, bf16[256,1024]{1,0:T(8,128)(2,1)S(1)}, u32[]{:S(2)}, u32[]{:S(2)}) collective-permute-start(bf16[256,1024]{1,0:T(8,128)(2,1)S(1)} %constant_dynamic-update-slice_fusion.10.refs_0_), channel_id=1, source_target_pairs={{0,7},{1,0},{2,1},{3,2},{4,3},{5,4},{6,5},{7,6},{8,15},{9,8},{10,9... | collective-permute-start | bytes 1572872 | tf_op jit(solution)/shard_map/ppermute | solution.py:33
  102.3 13.9 %collective-permute-start.28 = (bf16[256,1024]{1,0:T(8,128)(2,1)S(1)}, bf16[256,1024]{1,0:T(8,128)(2,1)S(1)}, u32[]{:S(2)}, u32[]{:S(2)}) collective-permute-start(bf16[256,1024]{1,0:T(8,128)(2,1)S(1)} %constant_dynamic-update-slice_fusion.15.refs_4_), channel_id=1, source_target_pairs={{0,24},{1,25},{2,26},{3,27},{4,28},{5,29},{6,30},{7,31},{8,0},{9,1... | collective-permute-start | bytes 1572872 | tf_op jit(solution)/shard_map/ppermute | solution.py:33
  109.3 9.5 %collective-permute-start.26 = (bf16[256,1024]{1,0:T(8,128)(2,1)S(1)}, bf16[256,1024]{1,0:T(8,128)(2,1)S(1)}, u32[]{:S(2)}, u32[]{:S(2)}) collective-permute-start(bf16[256,1024]{1,0:T(8,128)(2,1)S(1)} %collective-permute-done.24.refs_1_), channel_id=1, source_target_pairs={{0,1},{1,2},{2,3},{3,4},{4,5},{5,6},{6,7},{7,0},{8,9},{9,10},{10,1... | collective-permute-start | bytes 1572872 | tf_op jit(solution)/shard_map/ppermute | solution.py:33
  112.7 8.3 %collective-permute-start.29 = (bf16[256,1024]{1,0:T(8,128)(2,1)S(1)}, bf16[256,1024]{1,0:T(8,128)(2,1)S(1)}, u32[]{:S(2)}, u32[]{:S(2)}) collective-permute-start(bf16[256,1024]{1,0:T(8,128)(2,1)S(1)} %collective-permute-done.27.refs_5_), channel_id=1, source_target_pairs={{0,8},{1,9},{2,10},{3,11},{4,12},{5,13},{6,14},{7,15},{8,16},{9,17... | collective-permute-start | bytes 1572872 | tf_op jit(solution)/shard_map/ppermute | solution.py:33
  126.0 4.3 %collective-permute-start.30 = (bf16[128,1024]{1,0:T(8,128)(2,1)S(1)}, bf16[128,1024]{1,0:T(8,128)(2,1)S(1)}, u32[]{:S(2)}, u32[]{:S(2)}) collective-permute-start(bf16[128,1024]{1,0:T(8,128)(2,1)S(1)} %get-tuple-element.32), channel_id=1, source_target_pairs={{32,0},{33,1},{34,2},{35,3},{36,4},{37,5},{38,6},{39,7},{40,8},{41... | collective-permute-start | bytes 786440 | tf_op jit(solution)/shard_map/ppermute | solution.py:33
  130.9 3.9 %collective-permute-start.31 = (f32[4,32,1024]{2,1,0:T(8,128)S(1)}, f32[4,32,1024]{2,1,0:T(8,128)S(1)}, u32[]{:S(2)}, u32[]{:S(2)}) collective-permute-start(f32[4,32,1024]{2,1,0:T(8,128)S(1)} %finish.3), channel_id=1, source_target_pairs={{0,32},{1,33},{2,34},{3,35},{4,36},{5,37},{6,38},{7,39},{8,40},{9,... | collective-permute-start | bytes 1572872 | tf_op jit(solution)/shard_map/ppermute | solution.py:33
  (2 other events, 106.2 us)

commit v8 on v7

--- a/solution.py
+++ b/solution.py
@@ -50,11 +50,11 @@
     ahead, behind = send(wide_b, hop("z", 1)), send(wide_b, hop("z", -1))
     wide_b = jnp.concatenate([wide_b, ahead, behind, send(ahead, hop("z", 1))])
     wide_a, wide_b = lax.optimization_barrier((wide_a, wide_b))
-    ahead, behind = send(wide_a, hop("z", 1)), send(wide_a, hop("z", -1))
-    parts_a = [wide_a, ahead, behind, send(ahead, hop("z", 1))]
-    ahead, behind = send(wide_b, hop("y", 1)), send(wide_b, hop("y", -1))
-    parts_b = [wide_b, ahead, behind, send(ahead, hop("y", 1))]
-    return parts_a, parts_b
+    parts = []
+    for wide, axis in ((wide_a, "z"), (wide_b, "y")):
+        ahead, wide = lax.optimization_barrier((send(wide, hop(axis, 1)), wide))
+        parts.append([wide, ahead, send(wide, hop(axis, -1)), send(ahead, hop(axis, 1))])
+    return parts
 
 
 BACK = (0, 1, -1, 2)
@@ -82,15 +82,7 @@
     )
 
 
-def mask_kernel(where, pattern_hbm, ranges_hbm, keep, give, pattern, ranges, sems):
-    copies = [
-        pltpu.make_async_copy(pattern_hbm, pattern, sems.at[0]),
-        pltpu.make_async_copy(ranges_hbm, ranges, sems.at[1]),
-    ]
-    for copy in copies:
-        copy.start()
-    for copy in copies:
-        copy.wait()
+def mask_kernel(where, pattern, ranges, keep, give):
     block_row = pl.ds(lax.div(where[1] * NZ + where[2], BLK // 32), 1)
     count = M // BLK
     spread = (
@@ -111,14 +103,9 @@
     return pl.pallas_call(
         mask_kernel,
         out_shape=[jax.ShapeDtypeStruct((2, 32, M), jnp.float32)] * 2,
-        in_specs=[SMEM] + [pl.BlockSpec(memory_space=pltpu.HBM)] * 2,
+        in_specs=[SMEM, VMEM, VMEM],
         out_specs=[VMEM, VMEM],
-        scratch_shapes=[
-            pltpu.VMEM((4, M // BLK, M // BLK), jnp.int32),
-            pltpu.VMEM((4, 32, M), jnp.float32),
-            pltpu.SemaphoreType.DMA((2,)),
-        ],
-        compiler_params=pltpu.CompilerParams(vmem_limit_bytes=60 << 20),
+        compiler_params=pltpu.CompilerParams(vmem_limit_bytes=8 << 20),
         name="masked",
     )(where, pattern, ranges)
 

time: 136 us -> 136 us (level)
  waiting for transfers between devices: 56.6 us -> 59.2 us
  Pallas kernels: 14.1 us -> 12 us
    ppermute x32, waiting for transfers between devices: 56.6 us -> 59.2 us  [send(): return lax.ppermute(block, AXES, route(move))]
    pallas_call x1, Pallas kernels: 2.82 us -> 0.7 us  [masked(): pl.pallas_call(mask_kernel, out_shape=[jax.ShapeDtypeStruct((2, 32, M), j...]
    unnamed x12, local copies, waits for them, and re-layouts: 0.09 us -> 1.88 us
  transfers between devices with their start and end apart: 32 -> 32, of which waited for: 23 -> 21; matrix products, arithmetic and copies ran while one was open for 1% -> 0% of each run, Pallas kernels for 0% -> 0%
where the time goes in v8:
time: 136 us; the launch traced here: 135 us
  starting transfers between devices  60.8 us (45%)
  waiting for transfers between devices  59.2 us (44%)
  Pallas kernels  12 us (9%)
  local copies, waits for them, and re-layouts  2.06 us (2%)
    ppermute x32, starting transfers between devices, send(): return lax.ppermute(block, AXES, route(move))  60.8 us
    ppermute x32, waiting for transfers between devices, send(): return lax.ppermute(block, AXES, route(move))  59.2 us
    pallas_call x2, Pallas kernels, chain(): pl.pallas_call(chain_kernel, out_shape=[jax.ShapeDtypeStruct((128, M), jn...  10 us
  transfers between devices with their start and end apart: 32, of which 21 were waited for; matrix products, arithmetic and copies ran while one was open for 0% of the time, Pallas kernels for 0%

profile of v8, /device:TPU:1, one launch (start us, length us, event | category | flops | bytes accessed | tf_op | source)
XLA Modules:
  0.0 135.5 jit_solution(17538367991306005175)
XLA Ops:
  2.6 3.3 %collective-permute-start = (f32[2,32,1024]{2,1,0:T(8,128)S(1)}, f32[2,32,1024]{2,1,0:T(8,128)S(1)}, u32[]{:S(2)}, u32[]{:S(2)}) collective-permute-start(f32[2,32,1024]{2,1,0:T(8,128)S(1)} %get-tuple-element.29), channel_id=1, source_target_pairs={{0,32},{1,33},{2,34},{3,35},{4,36},{5,37},{6,38},{7,39},{8,40},{9,... | collective-permute-start | bytes 786440 | tf_op jit(solution)/shard_map/ppermute | solution.py:33
  7.1 5.3 %collective-permute-start.1 = (bf16[64,1024]{1,0:T(8,128)(2,1)S(1)}, bf16[64,1024]{1,0:T(8,128)(2,1)S(1)}, u32[]{:S(2)}, u32[]{:S(2)}) collective-permute-start(bf16[64,1024]{1,0:T(8,128)(2,1)S(1)} %fusion), channel_id=1, source_target_pairs={{0,4},{1,5},{2,6},{3,7},{4,0},{5,1},{6,2},{7,3},{8,12},{9,13},{10,... | collective-permute-start | bytes 393224 | tf_op jit(solution)/shard_map/ppermute | solution.py:33
  12.4 3.4 %collective-permute-done.1 = bf16[64,1024]{1,0:T(8,128)(2,1)S(1)} collective-permute-done((bf16[64,1024]{1,0:T(8,128)(2,1)S(1)}, bf16[64,1024]{1,0:T(8,128)(2,1)S(1)}, u32[]{:S(2)}, u32[]{:S(2)}) %collective-permute-start.1) | collective-permute-done | bytes 131104 | tf_op jit(solution)/shard_map/ppermute | solution.py:33
  15.9 5.6 %collective-permute-start.5 = (bf16[64,1024]{1,0:T(8,128)(2,1)S(1)}, bf16[64,1024]{1,0:T(8,128)(2,1)S(1)}, u32[]{:S(2)}, u32[]{:S(2)}) collective-permute-start(bf16[64,1024]{1,0:T(8,128)(2,1)S(1)} %pad_maximum_fusion.1), channel_id=1, source_target_pairs={{0,1},{1,2},{2,3},{3,4},{4,5},{5,6},{6,7},{7,0},{8,9},{9,10},{10,1... | collective-permute-start | bytes 393224 | tf_op jit(solution)/shard_map/ppermute | solution.py:33
  21.5 2.8 %collective-permute-start.2 = (bf16[64,1024]{1,0:T(8,128)(2,1)S(1)}, bf16[64,1024]{1,0:T(8,128)(2,1)S(1)}, u32[]{:S(2)}, u32[]{:S(2)}) collective-permute-start(bf16[64,1024]{1,0:T(8,128)(2,1)S(1)} %pad_maximum_fusion), channel_id=1, source_target_pairs={{0,8},{1,9},{2,10},{3,11},{4,12},{5,13},{6,14},{7,15},{8,16},{9,17... | collective-permute-start | bytes 393224 | tf_op jit(solution)/shard_map/ppermute | solution.py:33
  25.4 2.7 %collective-permute-start.7 = (bf16[64,1024]{1,0:T(8,128)(2,1)S(1)}, bf16[64,1024]{1,0:T(8,128)(2,1)S(1)}, u32[]{:S(2)}, u32[]{:S(2)}) collective-permute-start(bf16[64,1024]{1,0:T(8,128)(2,1)S(1)} %collective-permute-done.5), channel_id=1, source_target_pairs={{0,1},{1,2},{2,3},{3,4},{4,5},{5,6},{6,7},{7,0},{8,9},{9,10},{10,1... | collective-permute-start | bytes 393224 | tf_op jit(solution)/shard_map/ppermute | solution.py:33
  28.1 1.9 %collective-permute-done.2 = bf16[64,1024]{1,0:T(8,128)(2,1)S(1)} collective-permute-done((bf16[64,1024]{1,0:T(8,128)(2,1)S(1)}, bf16[64,1024]{1,0:T(8,128)(2,1)S(1)}, u32[]{:S(2)}, u32[]{:S(2)}) %collective-permute-start.2) | collective-permute-done | bytes 131104 | tf_op jit(solution)/shard_map/ppermute | solution.py:33
  30.0 1.9 %collective-permute-done.3 = bf16[64,1024]{1,0:T(8,128)(2,1)S(1)} collective-permute-done((bf16[64,1024]{1,0:T(8,128)(2,1)S(1)}, bf16[64,1024]{1,0:T(8,128)(2,1)S(1)}, u32[]{:S(2)}, u32[]{:S(2)}) %collective-permute-start.3) | collective-permute-done | bytes 131104 | tf_op jit(solution)/shard_map/ppermute | solution.py:33
  32.0 2.5 %collective-permute-start.8 = (bf16[256,1024]{1,0:T(8,128)(2,1)S(1)}, bf16[256,1024]{1,0:T(8,128)(2,1)S(1)}, u32[]{:S(2)}, u32[]{:S(2)}) collective-permute-start(bf16[256,1024]{1,0:T(8,128)(2,1)S(1)} %constant_dynamic-update-slice_fusion.refs_0_), channel_id=1, source_target_pairs={{0,1},{1,2},{2,3},{3,4},{4,5},{5,6},{6,7},{7,0},{8,9},{9,10},{10,1... | collective-permute-start | bytes 1572872 | tf_op jit(solution)/shard_map/ppermute | solution.py:33
  35.7 5.0 %collective-permute-done.8.refs_1_ = bf16[256,1024]{1,0:T(8,128)(2,1)S(1)} collective-permute-done((bf16[256,1024]{1,0:T(8,128)(2,1)S(1)}, bf16[256,1024]{1,0:T(8,128)(2,1)S(1)}, u32[]{:S(2)}, u32[]{:S(2)}) %collective-permute-start.8) | collective-permute-done | bytes 524320 | tf_op jit(solution)/shard_map/ppermute | solution.py:33
  40.7 3.4 %collective-permute-start.10 = (bf16[256,1024]{1,0:T(8,128)(2,1)S(1)}, bf16[256,1024]{1,0:T(8,128)(2,1)S(1)}, u32[]{:S(2)}, u32[]{:S(2)}) collective-permute-start(bf16[256,1024]{1,0:T(8,128)(2,1)S(1)} %collective-permute-done.8.refs_1_), channel_id=1, source_target_pairs={{0,1},{1,2},{2,3},{3,4},{4,5},{5,6},{6,7},{7,0},{8,9},{9,10},{10,1... | collective-permute-start | bytes 1572872 | tf_op jit(solution)/shard_map/ppermute | solution.py:33
  44.7 2.1 %collective-permute-start.13 = (bf16[256,1024]{1,0:T(8,128)(2,1)S(1)}, bf16[256,1024]{1,0:T(8,128)(2,1)S(1)}, u32[]{:S(2)}, u32[]{:S(2)}) collective-permute-start(bf16[256,1024]{1,0:T(8,128)(2,1)S(1)} %collective-permute-done.11.refs_5_), channel_id=1, source_target_pairs={{0,8},{1,9},{2,10},{3,11},{4,12},{5,13},{6,14},{7,15},{8,16},{9,17... | collective-permute-start | bytes 1572872 | tf_op jit(solution)/shard_map/ppermute | solution.py:33
  46.8 5.5 %collective-permute-done.9.refs_2_ = bf16[256,1024]{1,0:T(8,128)(2,1)S(1)} collective-permute-done((bf16[256,1024]{1,0:T(8,128)(2,1)S(1)}, bf16[256,1024]{1,0:T(8,128)(2,1)S(1)}, u32[]{:S(2)}, u32[]{:S(2)}) %collective-permute-start.9) | collective-permute-done | bytes 524320 | tf_op jit(solution)/shard_map/ppermute | solution.py:33
  52.2 2.2 %collective-permute-done.10.refs_3_ = bf16[256,1024]{1,0:T(8,128)(2,1)S(1)} collective-permute-done((bf16[256,1024]{1,0:T(8,128)(2,1)S(1)}, bf16[256,1024]{1,0:T(8,128)(2,1)S(1)}, u32[]{:S(2)}, u32[]{:S(2)}) %collective-permute-start.10) | collective-permute-done | bytes 524320 | tf_op jit(solution)/shard_map/ppermute | solution.py:33
  55.5 2.3 %collective-permute-done.13.refs_7_ = bf16[256,1024]{1,0:T(8,128)(2,1)S(1)} collective-permute-done((bf16[256,1024]{1,0:T(8,128)(2,1)S(1)}, bf16[256,1024]{1,0:T(8,128)(2,1)S(1)}, u32[]{:S(2)}, u32[]{:S(2)}) %collective-permute-start.13) | collective-permute-done | bytes 524320 | tf_op jit(solution)/shard_map/ppermute | solution.py:33
  57.8 5.0 %chain.2 = (bf16[128,1024]{1,0:T(8,128)(2,1)S(1)}, bf16[1024,1024]{1,0:T(8,128)(2,1)S(1)}, bf16[1024,1024]{1,0:T(8,128)(2,1)S(1)}) custom-call(s32[4]{0:T(128)S(1)} %pad_add_fusion.where, f32[2,32,1024]{2,1,0:T(8,128)S(1)} %get-tuple-element.28.keep, f32[2,32,1024]{2,1,0:T(8,128)S(1)} %collective-permute-done.other, ...), custom_call_target="tpu_custom_call" | custom-call | tf_op jit(solution)/shard_map/chain/pallas_call | solution.py:149
  67.3 2.1 %collective-permute-done.15 = bf16[2,32,1024]{2,1,0:T(8,128)(2,1)S(1)} collective-permute-done((bf16[2,32,1024]{2,1,0:T(8,128)(2,1)S(1)}, bf16[2,32,1024]{2,1,0:T(8,128)(2,1)S(1)}, u32[]{:S(2)}, u32[]{:S(2)}) %collective-permute-start.15) | collective-permute-done | bytes 131104 | tf_op jit(solution)/shard_map/ppermute | solution.py:33
  70.7 3.7 %collective-permute-done.16 = bf16[2,32,1024]{2,1,0:T(8,128)(2,1)S(1)} collective-permute-done((bf16[2,32,1024]{2,1,0:T(8,128)(2,1)S(1)}, bf16[2,32,1024]{2,1,0:T(8,128)(2,1)S(1)}, u32[]{:S(2)}, u32[]{:S(2)}) %collective-permute-start.16) | collective-permute-done | bytes 131104 | tf_op jit(solution)/shard_map/ppermute | solution.py:33
  74.6 4.8 %collective-permute-start.17 = (bf16[64,1024]{1,0:T(8,128)(2,1)S(1)}, bf16[64,1024]{1,0:T(8,128)(2,1)S(1)}, u32[]{:S(2)}, u32[]{:S(2)}) collective-permute-start(bf16[64,1024]{1,0:T(8,128)(2,1)S(1)} %fusion.1), channel_id=1, source_target_pairs={{0,4},{1,5},{2,6},{3,7},{4,0},{5,1},{6,2},{7,3},{8,12},{9,13},{10,... | collective-permute-start | bytes 393224 | tf_op jit(solution)/shard_map/ppermute | solution.py:33
  79.4 7.1 %collective-permute-done.17 = bf16[64,1024]{1,0:T(8,128)(2,1)S(1)} collective-permute-done((bf16[64,1024]{1,0:T(8,128)(2,1)S(1)}, bf16[64,1024]{1,0:T(8,128)(2,1)S(1)}, u32[]{:S(2)}, u32[]{:S(2)}) %collective-permute-start.17) | collective-permute-done | bytes 131104 | tf_op jit(solution)/shard_map/ppermute | solution.py:33
  86.5 1.6 %collective-permute-start.21 = (bf16[64,1024]{1,0:T(8,128)(2,1)S(1)}, bf16[64,1024]{1,0:T(8,128)(2,1)S(1)}, u32[]{:S(2)}, u32[]{:S(2)}) collective-permute-start(bf16[64,1024]{1,0:T(8,128)(2,1)S(1)} %pad_maximum_fusion.3), channel_id=1, source_target_pairs={{0,1},{1,2},{2,3},{3,4},{4,5},{5,6},{6,7},{7,0},{8,9},{9,10},{10,1... | collective-permute-start | bytes 393224 | tf_op jit(solution)/shard_map/ppermute | solution.py:33
  88.2 1.8 %collective-permute-start.18 = (bf16[64,1024]{1,0:T(8,128)(2,1)S(1)}, bf16[64,1024]{1,0:T(8,128)(2,1)S(1)}, u32[]{:S(2)}, u32[]{:S(2)}) collective-permute-start(bf16[64,1024]{1,0:T(8,128)(2,1)S(1)} %pad_maximum_fusion.2), channel_id=1, source_target_pairs={{0,8},{1,9},{2,10},{3,11},{4,12},{5,13},{6,14},{7,15},{8,16},{9,17... | collective-permute-start | bytes 393224 | tf_op jit(solution)/shard_map/ppermute | solution.py:33
  94.9 3.2 %collective-permute-done.19 = bf16[64,1024]{1,0:T(8,128)(2,1)S(1)} collective-permute-done((bf16[64,1024]{1,0:T(8,128)(2,1)S(1)}, bf16[64,1024]{1,0:T(8,128)(2,1)S(1)}, u32[]{:S(2)}, u32[]{:S(2)}) %collective-permute-start.19) | collective-permute-done | bytes 131104 | tf_op jit(solution)/shard_map/ppermute | solution.py:33
  99.0 3.0 %collective-permute-start.27 = (bf16[256,1024]{1,0:T(8,128)(2,1)S(1)}, bf16[256,1024]{1,0:T(8,128)(2,1)S(1)}, u32[]{:S(2)}, u32[]{:S(2)}) collective-permute-start(bf16[256,1024]{1,0:T(8,128)(2,1)S(1)} %constant_dynamic-update-slice_fusion.15.refs_4_), channel_id=1, source_target_pairs={{0,8},{1,9},{2,10},{3,11},{4,12},{5,13},{6,14},{7,15},{8,16},{9,17... | collective-permute-start | bytes 1572872 | tf_op jit(solution)/shard_map/ppermute | solution.py:33
  102.0 4.7 %collective-permute-done.24.refs_1_ = bf16[256,1024]{1,0:T(8,128)(2,1)S(1)} collective-permute-done((bf16[256,1024]{1,0:T(8,128)(2,1)S(1)}, bf16[256,1024]{1,0:T(8,128)(2,1)S(1)}, u32[]{:S(2)}, u32[]{:S(2)}) %collective-permute-start.24) | collective-permute-done | bytes 524320 | tf_op jit(solution)/shard_map/ppermute | solution.py:33
  106.7 2.7 %collective-permute-start.26 = (bf16[256,1024]{1,0:T(8,128)(2,1)S(1)}, bf16[256,1024]{1,0:T(8,128)(2,1)S(1)}, u32[]{:S(2)}, u32[]{:S(2)}) collective-permute-start(bf16[256,1024]{1,0:T(8,128)(2,1)S(1)} %collective-permute-done.24.refs_1_), channel_id=1, source_target_pairs={{0,1},{1,2},{2,3},{3,4},{4,5},{5,6},{6,7},{7,0},{8,9},{9,10},{10,1... | collective-permute-start | bytes 1572872 | tf_op jit(solution)/shard_map/ppermute | solution.py:33
  110.4 1.7 %collective-permute-start.29 = (bf16[256,1024]{1,0:T(8,128)(2,1)S(1)}, bf16[256,1024]{1,0:T(8,128)(2,1)S(1)}, u32[]{:S(2)}, u32[]{:S(2)}) collective-permute-start(bf16[256,1024]{1,0:T(8,128)(2,1)S(1)} %collective-permute-done.27.refs_5_), channel_id=1, source_target_pairs={{0,8},{1,9},{2,10},{3,11},{4,12},{5,13},{6,14},{7,15},{8,16},{9,17... | collective-permute-start | bytes 1572872 | tf_op jit(solution)/shard_map/ppermute | solution.py:33
  112.0 5.0 %collective-permute-done.25.refs_2_ = bf16[256,1024]{1,0:T(8,128)(2,1)S(1)} collective-permute-done((bf16[256,1024]{1,0:T(8,128)(2,1)S(1)}, bf16[256,1024]{1,0:T(8,128)(2,1)S(1)}, u32[]{:S(2)}, u32[]{:S(2)}) %collective-permute-start.25) | collective-permute-done | bytes 524320 | tf_op jit(solution)/shard_map/ppermute | solution.py:33
  117.0 1.9 %collective-permute-done.28.refs_6_ = bf16[256,1024]{1,0:T(8,128)(2,1)S(1)} collective-permute-done((bf16[256,1024]{1,0:T(8,128)(2,1)S(1)}, bf16[256,1024]{1,0:T(8,128)(2,1)S(1)}, u32[]{:S(2)}, u32[]{:S(2)}) %collective-permute-start.28) | collective-permute-done | bytes 524320 | tf_op jit(solution)/shard_map/ppermute | solution.py:33
  119.7 5.0 %chain.3 = (bf16[128,1024]{1,0:T(8,128)(2,1)S(1)}, bf16[1024,1024]{1,0:T(8,128)(2,1)S(1)}, bf16[1024,1024]{1,0:T(8,128)(2,1)S(1)}) custom-call(s32[4]{0:T(128)S(1)} %pad_add_fusion.where, f32[2,32,1024]{2,1,0:T(8,128)S(1)} %get-tuple-element.52.keep, f32[2,32,1024]{2,1,0:T(8,128)S(1)} %get-tuple-element.51.other, ...), custom_call_target="tpu_custom_call" | custom-call | tf_op jit(solution)/shard_map/chain/pallas_call | solution.py:149
  124.8 4.3 %collective-permute-start.30 = (bf16[128,1024]{1,0:T(8,128)(2,1)S(1)}, bf16[128,1024]{1,0:T(8,128)(2,1)S(1)}, u32[]{:S(2)}, u32[]{:S(2)}) collective-permute-start(bf16[128,1024]{1,0:T(8,128)(2,1)S(1)} %get-tuple-element.48), channel_id=1, source_target_pairs={{32,0},{33,1},{34,2},{35,3},{36,4},{37,5},{38,6},{39,7},{40,8},{41... | collective-permute-start | bytes 786440 | tf_op jit(solution)/shard_map/ppermute | solution.py:33
  132.0 2.6 %collective-permute-done.31 = f32[4,32,1024]{2,1,0:T(8,128)S(1)} collective-permute-done((f32[4,32,1024]{2,1,0:T(8,128)S(1)}, f32[4,32,1024]{2,1,0:T(8,128)S(1)}, u32[]{:S(2)}, u32[]{:S(2)}) %collective-permute-start.31) | collective-permute-done | bytes 524320 | tf_op jit(solution)/shard_map/ppermute | solution.py:33
  (70 shorter events, 25.1 us)
Async XLA Ops:
  2.6 4.5 %collective-permute-start = (f32[2,32,1024]{2,1,0:T(8,128)S(1)}, f32[2,32,1024]{2,1,0:T(8,128)S(1)}, u32[]{:S(2)}, u32[]{:S(2)}) collective-permute-start(f32[2,32,1024]{2,1,0:T(8,128)S(1)} %get-tuple-element.29), channel_id=1, source_target_pairs={{0,32},{1,33},{2,34},{3,35},{4,36},{5,37},{6,38},{7,39},{8,40},{9,... | collective-permute-start | bytes 786440 | tf_op jit(solution)/shard_map/ppermute | solution.py:33
  7.1 8.7 %collective-permute-start.1 = (bf16[64,1024]{1,0:T(8,128)(2,1)S(1)}, bf16[64,1024]{1,0:T(8,128)(2,1)S(1)}, u32[]{:S(2)}, u32[]{:S(2)}) collective-permute-start(bf16[64,1024]{1,0:T(8,128)(2,1)S(1)} %fusion), channel_id=1, source_target_pairs={{0,4},{1,5},{2,6},{3,7},{4,0},{5,1},{6,2},{7,3},{8,12},{9,13},{10,... | collective-permute-start | bytes 393224 | tf_op jit(solution)/shard_map/ppermute | solution.py:33
  15.9 9.5 %collective-permute-start.5 = (bf16[64,1024]{1,0:T(8,128)(2,1)S(1)}, bf16[64,1024]{1,0:T(8,128)(2,1)S(1)}, u32[]{:S(2)}, u32[]{:S(2)}) collective-permute-start(bf16[64,1024]{1,0:T(8,128)(2,1)S(1)} %pad_maximum_fusion.1), channel_id=1, source_target_pairs={{0,1},{1,2},{2,3},{3,4},{4,5},{5,6},{6,7},{7,0},{8,9},{9,10},{10,1... | collective-permute-start | bytes 393224 | tf_op jit(solution)/shard_map/ppermute | solution.py:33
  21.5 8.5 %collective-permute-start.2 = (bf16[64,1024]{1,0:T(8,128)(2,1)S(1)}, bf16[64,1024]{1,0:T(8,128)(2,1)S(1)}, u32[]{:S(2)}, u32[]{:S(2)}) collective-permute-start(bf16[64,1024]{1,0:T(8,128)(2,1)S(1)} %pad_maximum_fusion), channel_id=1, source_target_pairs={{0,8},{1,9},{2,10},{3,11},{4,12},{5,13},{6,14},{7,15},{8,16},{9,17... | collective-permute-start | bytes 393224 | tf_op jit(solution)/shard_map/ppermute | solution.py:33
  24.3 7.6 %collective-permute-start.4 = (bf16[64,1024]{1,0:T(8,128)(2,1)S(1)}, bf16[64,1024]{1,0:T(8,128)(2,1)S(1)}, u32[]{:S(2)}, u32[]{:S(2)}) collective-permute-start(bf16[64,1024]{1,0:T(8,128)(2,1)S(1)} %pad_maximum_fusion), channel_id=1, source_target_pairs={{0,16},{1,17},{2,18},{3,19},{4,20},{5,21},{6,22},{7,23},{8,24},{9,... | collective-permute-start | bytes 393224 | tf_op jit(solution)/shard_map/ppermute | solution.py:33
  24.7 7.2 %collective-permute-start.3 = (bf16[64,1024]{1,0:T(8,128)(2,1)S(1)}, bf16[64,1024]{1,0:T(8,128)(2,1)S(1)}, u32[]{:S(2)}, u32[]{:S(2)}) collective-permute-start(bf16[64,1024]{1,0:T(8,128)(2,1)S(1)} %pad_maximum_fusion), channel_id=1, source_target_pairs={{0,24},{1,25},{2,26},{3,27},{4,28},{5,29},{6,30},{7,31},{8,0},{9,1... | collective-permute-start | bytes 393224 | tf_op jit(solution)/shard_map/ppermute | solution.py:33
  25.4 6.5 %collective-permute-start.6 = (bf16[64,1024]{1,0:T(8,128)(2,1)S(1)}, bf16[64,1024]{1,0:T(8,128)(2,1)S(1)}, u32[]{:S(2)}, u32[]{:S(2)}) collective-permute-start(bf16[64,1024]{1,0:T(8,128)(2,1)S(1)} %pad_maximum_fusion.1), channel_id=1, source_target_pairs={{0,7},{1,0},{2,1},{3,2},{4,3},{5,4},{6,5},{7,6},{8,15},{9,8},{10,9... | collective-permute-start | bytes 393224 | tf_op jit(solution)/shard_map/ppermute | solution.py:33
  25.4 6.6 %collective-permute-start.7 = (bf16[64,1024]{1,0:T(8,128)(2,1)S(1)}, bf16[64,1024]{1,0:T(8,128)(2,1)S(1)}, u32[]{:S(2)}, u32[]{:S(2)}) collective-permute-start(bf16[64,1024]{1,0:T(8,128)(2,1)S(1)} %collective-permute-done.5), channel_id=1, source_target_pairs={{0,1},{1,2},{2,3},{3,4},{4,5},{5,6},{6,7},{7,0},{8,9},{9,10},{10,1... | collective-permute-start | bytes 393224 | tf_op jit(solution)/shard_map/ppermute | solution.py:33
  32.0 8.7 %collective-permute-start.8 = (bf16[256,1024]{1,0:T(8,128)(2,1)S(1)}, bf16[256,1024]{1,0:T(8,128)(2,1)S(1)}, u32[]{:S(2)}, u32[]{:S(2)}) collective-permute-start(bf16[256,1024]{1,0:T(8,128)(2,1)S(1)} %constant_dynamic-update-slice_fusion.refs_0_), channel_id=1, source_target_pairs={{0,1},{1,2},{2,3},{3,4},{4,5},{5,6},{6,7},{7,0},{8,9},{9,10},{10,1... | collective-permute-start | bytes 1572872 | tf_op jit(solution)/shard_map/ppermute | solution.py:33
  34.5 9.5 %collective-permute-start.11 = (bf16[256,1024]{1,0:T(8,128)(2,1)S(1)}, bf16[256,1024]{1,0:T(8,128)(2,1)S(1)}, u32[]{:S(2)}, u32[]{:S(2)}) collective-permute-start(bf16[256,1024]{1,0:T(8,128)(2,1)S(1)} %constant_dynamic-update-slice_fusion.5.refs_4_), channel_id=1, source_target_pairs={{0,8},{1,9},{2,10},{3,11},{4,12},{5,13},{6,14},{7,15},{8,16},{9,17... | collective-permute-start | bytes 1572872 | tf_op jit(solution)/shard_map/ppermute | solution.py:33
  40.7 11.6 %collective-permute-start.9 = (bf16[256,1024]{1,0:T(8,128)(2,1)S(1)}, bf16[256,1024]{1,0:T(8,128)(2,1)S(1)}, u32[]{:S(2)}, u32[]{:S(2)}) collective-permute-start(bf16[256,1024]{1,0:T(8,128)(2,1)S(1)} %constant_dynamic-update-slice_fusion.refs_0_), channel_id=1, source_target_pairs={{0,7},{1,0},{2,1},{3,2},{4,3},{5,4},{6,5},{7,6},{8,15},{9,8},{10,9... | collective-permute-start | bytes 1572872 | tf_op jit(solution)/shard_map/ppermute | solution.py:33
  40.7 13.8 %collective-permute-start.10 = (bf16[256,1024]{1,0:T(8,128)(2,1)S(1)}, bf16[256,1024]{1,0:T(8,128)(2,1)S(1)}, u32[]{:S(2)}, u32[]{:S(2)}) collective-permute-start(bf16[256,1024]{1,0:T(8,128)(2,1)S(1)} %collective-permute-done.8.refs_1_), channel_id=1, source_target_pairs={{0,1},{1,2},{2,3},{3,4},{4,5},{5,6},{6,7},{7,0},{8,9},{9,10},{10,1... | collective-permute-start | bytes 1572872 | tf_op jit(solution)/shard_map/ppermute | solution.py:33
  44.1 11.4 %collective-permute-start.12 = (bf16[256,1024]{1,0:T(8,128)(2,1)S(1)}, bf16[256,1024]{1,0:T(8,128)(2,1)S(1)}, u32[]{:S(2)}, u32[]{:S(2)}) collective-permute-start(bf16[256,1024]{1,0:T(8,128)(2,1)S(1)} %constant_dynamic-update-slice_fusion.5.refs_4_), channel_id=1, source_target_pairs={{0,24},{1,25},{2,26},{3,27},{4,28},{5,29},{6,30},{7,31},{8,0},{9,1... | collective-permute-start | bytes 1572872 | tf_op jit(solution)/shard_map/ppermute | solution.py:33
  44.7 13.2 %collective-permute-start.13 = (bf16[256,1024]{1,0:T(8,128)(2,1)S(1)}, bf16[256,1024]{1,0:T(8,128)(2,1)S(1)}, u32[]{:S(2)}, u32[]{:S(2)}) collective-permute-start(bf16[256,1024]{1,0:T(8,128)(2,1)S(1)} %collective-permute-done.11.refs_5_), channel_id=1, source_target_pairs={{0,8},{1,9},{2,10},{3,11},{4,12},{5,13},{6,14},{7,15},{8,16},{9,17... | collective-permute-start | bytes 1572872 | tf_op jit(solution)/shard_map/ppermute | solution.py:33
  62.9 2.4 %collective-permute-start.14 = (bf16[128,1024]{1,0:T(8,128)(2,1)S(1)}, bf16[128,1024]{1,0:T(8,128)(2,1)S(1)}, u32[]{:S(2)}, u32[]{:S(2)}) collective-permute-start(bf16[128,1024]{1,0:T(8,128)(2,1)S(1)} %get-tuple-element.36), channel_id=1, source_target_pairs={{32,0},{33,1},{34,2},{35,3},{36,4},{37,5},{38,6},{39,7},{40,8},{41... | collective-permute-start | bytes 786440 | tf_op jit(solution)/shard_map/ppermute | solution.py:33
  66.0 3.4 %collective-permute-start.15 = (bf16[2,32,1024]{2,1,0:T(8,128)(2,1)S(1)}, bf16[2,32,1024]{2,1,0:T(8,128)(2,1)S(1)}, u32[]{:S(2)}, u32[]{:S(2)}) collective-permute-start(bf16[2,32,1024]{2,1,0:T(8,128)(2,1)S(1)} %get-tuple-element.40), channel_id=1, source_target_pairs={{0,32},{1,33},{2,34},{3,35},{4,36},{5,37},{6,38},{7,39},{8,40},{9,... | collective-permute-start | bytes 393224 | tf_op jit(solution)/shard_map/ppermute | solution.py:33
  69.4 5.0 %collective-permute-start.16 = (bf16[2,32,1024]{2,1,0:T(8,128)(2,1)S(1)}, bf16[2,32,1024]{2,1,0:T(8,128)(2,1)S(1)}, u32[]{:S(2)}, u32[]{:S(2)}) collective-permute-start(bf16[2,32,1024]{2,1,0:T(8,128)(2,1)S(1)} %broadcast_select_fusion), channel_id=1, source_target_pairs={{0,64},{1,65},{2,66},{3,67},{4,68},{5,69},{6,70},{7,71},{8,72},{9,... | collective-permute-start | bytes 393224 | tf_op jit(solution)/shard_map/ppermute | solution.py:33
  74.6 11.9 %collective-permute-start.17 = (bf16[64,1024]{1,0:T(8,128)(2,1)S(1)}, bf16[64,1024]{1,0:T(8,128)(2,1)S(1)}, u32[]{:S(2)}, u32[]{:S(2)}) collective-permute-start(bf16[64,1024]{1,0:T(8,128)(2,1)S(1)} %fusion.1), channel_id=1, source_target_pairs={{0,4},{1,5},{2,6},{3,7},{4,0},{5,1},{6,2},{7,3},{8,12},{9,13},{10,... | collective-permute-start | bytes 393224 | tf_op jit(solution)/shard_map/ppermute | solution.py:33
  86.5 5.6 %collective-permute-start.21 = (bf16[64,1024]{1,0:T(8,128)(2,1)S(1)}, bf16[64,1024]{1,0:T(8,128)(2,1)S(1)}, u32[]{:S(2)}, u32[]{:S(2)}) collective-permute-start(bf16[64,1024]{1,0:T(8,128)(2,1)S(1)} %pad_maximum_fusion.3), channel_id=1, source_target_pairs={{0,1},{1,2},{2,3},{3,4},{4,5},{5,6},{6,7},{7,0},{8,9},{9,10},{10,1... | collective-permute-start | bytes 393224 | tf_op jit(solution)/shard_map/ppermute | solution.py:33
  88.2 6.8 %collective-permute-start.18 = (bf16[64,1024]{1,0:T(8,128)(2,1)S(1)}, bf16[64,1024]{1,0:T(8,128)(2,1)S(1)}, u32[]{:S(2)}, u32[]{:S(2)}) collective-permute-start(bf16[64,1024]{1,0:T(8,128)(2,1)S(1)} %pad_maximum_fusion.2), channel_id=1, source_target_pairs={{0,8},{1,9},{2,10},{3,11},{4,12},{5,13},{6,14},{7,15},{8,16},{9,17... | collective-permute-start | bytes 393224 | tf_op jit(solution)/shard_map/ppermute | solution.py:33
  90.0 8.2 %collective-permute-start.20 = (bf16[64,1024]{1,0:T(8,128)(2,1)S(1)}, bf16[64,1024]{1,0:T(8,128)(2,1)S(1)}, u32[]{:S(2)}, u32[]{:S(2)}) collective-permute-start(bf16[64,1024]{1,0:T(8,128)(2,1)S(1)} %pad_maximum_fusion.2), channel_id=1, source_target_pairs={{0,16},{1,17},{2,18},{3,19},{4,20},{5,21},{6,22},{7,23},{8,24},{9,... | collective-permute-start | bytes 393224 | tf_op jit(solution)/shard_map/ppermute | solution.py:33
  90.1 8.0 %collective-permute-start.19 = (bf16[64,1024]{1,0:T(8,128)(2,1)S(1)}, bf16[64,1024]{1,0:T(8,128)(2,1)S(1)}, u32[]{:S(2)}, u32[]{:S(2)}) collective-permute-start(bf16[64,1024]{1,0:T(8,128)(2,1)S(1)} %pad_maximum_fusion.2), channel_id=1, source_target_pairs={{0,24},{1,25},{2,26},{3,27},{4,28},{5,29},{6,30},{7,31},{8,0},{9,1... | collective-permute-start | bytes 393224 | tf_op jit(solution)/shard_map/ppermute | solution.py:33
  90.9 7.3 %collective-permute-start.22 = (bf16[64,1024]{1,0:T(8,128)(2,1)S(1)}, bf16[64,1024]{1,0:T(8,128)(2,1)S(1)}, u32[]{:S(2)}, u32[]{:S(2)}) collective-permute-start(bf16[64,1024]{1,0:T(8,128)(2,1)S(1)} %pad_maximum_fusion.3), channel_id=1, source_target_pairs={{0,7},{1,0},{2,1},{3,2},{4,3},{5,4},{6,5},{7,6},{8,15},{9,8},{10,9... | collective-permute-start | bytes 393224 | tf_op jit(solution)/shard_map/ppermute | solution.py:33
  92.1 6.1 %collective-permute-start.23 = (bf16[64,1024]{1,0:T(8,128)(2,1)S(1)}, bf16[64,1024]{1,0:T(8,128)(2,1)S(1)}, u32[]{:S(2)}, u32[]{:S(2)}) collective-permute-start(bf16[64,1024]{1,0:T(8,128)(2,1)S(1)} %collective-permute-done.21), channel_id=1, source_target_pairs={{0,1},{1,2},{2,3},{3,4},{4,5},{5,6},{6,7},{7,0},{8,9},{9,10},{10,1... | collective-permute-start | bytes 393224 | tf_op jit(solution)/shard_map/ppermute | solution.py:33
  98.3 8.4 %collective-permute-start.24 = (bf16[256,1024]{1,0:T(8,128)(2,1)S(1)}, bf16[256,1024]{1,0:T(8,128)(2,1)S(1)}, u32[]{:S(2)}, u32[]{:S(2)}) collective-permute-start(bf16[256,1024]{1,0:T(8,128)(2,1)S(1)} %constant_dynamic-update-slice_fusion.10.refs_0_), channel_id=1, source_target_pairs={{0,1},{1,2},{2,3},{3,4},{4,5},{5,6},{6,7},{7,0},{8,9},{9,10},{10,1... | collective-permute-start | bytes 1572872 | tf_op jit(solution)/shard_map/ppermute | solution.py:33
  99.0 10.4 %collective-permute-start.27 = (bf16[256,1024]{1,0:T(8,128)(2,1)S(1)}, bf16[256,1024]{1,0:T(8,128)(2,1)S(1)}, u32[]{:S(2)}, u32[]{:S(2)}) collective-permute-start(bf16[256,1024]{1,0:T(8,128)(2,1)S(1)} %constant_dynamic-update-slice_fusion.15.refs_4_), channel_id=1, source_target_pairs={{0,8},{1,9},{2,10},{3,11},{4,12},{5,13},{6,14},{7,15},{8,16},{9,17... | collective-permute-start | bytes 1572872 | tf_op jit(solution)/shard_map/ppermute | solution.py:33
  106.7 10.4 %collective-permute-start.25 = (bf16[256,1024]{1,0:T(8,128)(2,1)S(1)}, bf16[256,1024]{1,0:T(8,128)(2,1)S(1)}, u32[]{:S(2)}, u32[]{:S(2)}) collective-permute-start(bf16[256,1024]{1,0:T(8,128)(2,1)S(1)} %constant_dynamic-update-slice_fusion.10.refs_0_), channel_id=1, source_target_pairs={{0,7},{1,0},{2,1},{3,2},{4,3},{5,4},{6,5},{7,6},{8,15},{9,8},{10,9... | collective-permute-start | bytes 1572872 | tf_op jit(solution)/shard_map/ppermute | solution.py:33
  106.7 10.4 %collective-permute-start.26 = (bf16[256,1024]{1,0:T(8,128)(2,1)S(1)}, bf16[256,1024]{1,0:T(8,128)(2,1)S(1)}, u32[]{:S(2)}, u32[]{:S(2)}) collective-permute-start(bf16[256,1024]{1,0:T(8,128)(2,1)S(1)} %collective-permute-done.24.refs_1_), channel_id=1, source_target_pairs={{0,1},{1,2},{2,3},{3,4},{4,5},{5,6},{6,7},{7,0},{8,9},{9,10},{10,1... | collective-permute-start | bytes 1572872 | tf_op jit(solution)/shard_map/ppermute | solution.py:33
  109.4 9.5 %collective-permute-start.28 = (bf16[256,1024]{1,0:T(8,128)(2,1)S(1)}, bf16[256,1024]{1,0:T(8,128)(2,1)S(1)}, u32[]{:S(2)}, u32[]{:S(2)}) collective-permute-start(bf16[256,1024]{1,0:T(8,128)(2,1)S(1)} %constant_dynamic-update-slice_fusion.15.refs_4_), channel_id=1, source_target_pairs={{0,24},{1,25},{2,26},{3,27},{4,28},{5,29},{6,30},{7,31},{8,0},{9,1... | collective-permute-start | bytes 1572872 | tf_op jit(solution)/shard_map/ppermute | solution.py:33
  110.4 9.4 %collective-permute-start.29 = (bf16[256,1024]{1,0:T(8,128)(2,1)S(1)}, bf16[256,1024]{1,0:T(8,128)(2,1)S(1)}, u32[]{:S(2)}, u32[]{:S(2)}) collective-permute-start(bf16[256,1024]{1,0:T(8,128)(2,1)S(1)} %collective-permute-done.27.refs_5_), channel_id=1, source_target_pairs={{0,8},{1,9},{2,10},{3,11},{4,12},{5,13},{6,14},{7,15},{8,16},{9,17... | collective-permute-start | bytes 1572872 | tf_op jit(solution)/shard_map/ppermute | solution.py:33
  124.8 5.4 %collective-permute-start.30 = (bf16[128,1024]{1,0:T(8,128)(2,1)S(1)}, bf16[128,1024]{1,0:T(8,128)(2,1)S(1)}, u32[]{:S(2)}, u32[]{:S(2)}) collective-permute-start(bf16[128,1024]{1,0:T(8,128)(2,1)S(1)} %get-tuple-element.48), channel_id=1, source_target_pairs={{32,0},{33,1},{34,2},{35,3},{36,4},{37,5},{38,6},{39,7},{40,8},{41... | collective-permute-start | bytes 786440 | tf_op jit(solution)/shard_map/ppermute | solution.py:33
  130.7 3.9 %collective-permute-start.31 = (f32[4,32,1024]{2,1,0:T(8,128)S(1)}, f32[4,32,1024]{2,1,0:T(8,128)S(1)}, u32[]{:S(2)}, u32[]{:S(2)}) collective-permute-start(f32[4,32,1024]{2,1,0:T(8,128)S(1)} %finish.3), channel_id=1, source_target_pairs={{0,32},{1,33},{2,34},{3,35},{4,36},{5,37},{6,38},{7,39},{8,40},{9,... | collective-permute-start | bytes 1572872 | tf_op jit(solution)/shard_map/ppermute | solution.py:33
  (2 other events, 1.8 us)

commit v9 on v8

--- a/solution.py
+++ b/solution.py
@@ -52,8 +52,8 @@
     wide_a, wide_b = lax.optimization_barrier((wide_a, wide_b))
     parts = []
     for wide, axis in ((wide_a, "z"), (wide_b, "y")):
-        ahead, wide = lax.optimization_barrier((send(wide, hop(axis, 1)), wide))
-        parts.append([wide, ahead, send(wide, hop(axis, -1)), send(ahead, hop(axis, 1))])
+        ahead, behind = send(wide, hop(axis, 1)), send(wide, hop(axis, -1))
+        parts.append([wide, ahead, behind, send(ahead, hop(axis, 1))])
     return parts
 
 

time: 136 us -> 135 us (level)
    ppermute x32, waiting for transfers between devices: 59.2 us -> 57.9 us  [send(): return lax.ppermute(block, AXES, route(move))]
  transfers between devices with their start and end apart: 32 -> 32, of which waited for: 21 -> 23; matrix products, arithmetic and copies ran while one was open for 0% -> 0% of each run, Pallas kernels for 0% -> 0%
where the time goes in v9:
time: 135 us
  starting transfers between devices  61.2 us (45%)
  waiting for transfers between devices  57.9 us (43%)
  Pallas kernels  12 us (9%)
  local copies, waits for them, and re-layouts  2.06 us (2%)
    ppermute x32, starting transfers between devices, send(): return lax.ppermute(block, AXES, route(move))  61.2 us
    ppermute x32, waiting for transfers between devices, send(): return lax.ppermute(block, AXES, route(move))  57.9 us
    pallas_call x2, Pallas kernels, chain(): pl.pallas_call(chain_kernel, out_shape=[jax.ShapeDtypeStruct((128, M), jn...  10 us
  transfers between devices with their start and end apart: 32, of which 23 were waited for; matrix products, arithmetic and copies ran while one was open for 0% of the time, Pallas kernels for 0%

profile of v9, /device:TPU:1, one launch (start us, length us, event | category | flops | bytes accessed | tf_op | source)
XLA Modules:
  0.0 134.5 jit_solution(17661078033459794667)
XLA Ops:
  2.6 3.3 %collective-permute-start = (f32[2,32,1024]{2,1,0:T(8,128)S(1)}, f32[2,32,1024]{2,1,0:T(8,128)S(1)}, u32[]{:S(2)}, u32[]{:S(2)}) collective-permute-start(f32[2,32,1024]{2,1,0:T(8,128)S(1)} %get-tuple-element.21), channel_id=1, source_target_pairs={{0,32},{1,33},{2,34},{3,35},{4,36},{5,37},{6,38},{7,39},{8,40},{9,... | collective-permute-start | bytes 786440 | tf_op jit(solution)/shard_map/ppermute | solution.py:33
  7.1 5.3 %collective-permute-start.1 = (bf16[64,1024]{1,0:T(8,128)(2,1)S(1)}, bf16[64,1024]{1,0:T(8,128)(2,1)S(1)}, u32[]{:S(2)}, u32[]{:S(2)}) collective-permute-start(bf16[64,1024]{1,0:T(8,128)(2,1)S(1)} %fusion), channel_id=1, source_target_pairs={{0,4},{1,5},{2,6},{3,7},{4,0},{5,1},{6,2},{7,3},{8,12},{9,13},{10,... | collective-permute-start | bytes 393224 | tf_op jit(solution)/shard_map/ppermute | solution.py:33
  12.4 3.4 %collective-permute-done.1 = bf16[64,1024]{1,0:T(8,128)(2,1)S(1)} collective-permute-done((bf16[64,1024]{1,0:T(8,128)(2,1)S(1)}, bf16[64,1024]{1,0:T(8,128)(2,1)S(1)}, u32[]{:S(2)}, u32[]{:S(2)}) %collective-permute-start.1) | collective-permute-done | bytes 131104 | tf_op jit(solution)/shard_map/ppermute | solution.py:33
  15.9 5.6 %collective-permute-start.5 = (bf16[64,1024]{1,0:T(8,128)(2,1)S(1)}, bf16[64,1024]{1,0:T(8,128)(2,1)S(1)}, u32[]{:S(2)}, u32[]{:S(2)}) collective-permute-start(bf16[64,1024]{1,0:T(8,128)(2,1)S(1)} %pad_maximum_fusion.1), channel_id=1, source_target_pairs={{0,1},{1,2},{2,3},{3,4},{4,5},{5,6},{6,7},{7,0},{8,9},{9,10},{10,1... | collective-permute-start | bytes 393224 | tf_op jit(solution)/shard_map/ppermute | solution.py:33
  21.5 2.8 %collective-permute-start.2 = (bf16[64,1024]{1,0:T(8,128)(2,1)S(1)}, bf16[64,1024]{1,0:T(8,128)(2,1)S(1)}, u32[]{:S(2)}, u32[]{:S(2)}) collective-permute-start(bf16[64,1024]{1,0:T(8,128)(2,1)S(1)} %pad_maximum_fusion), channel_id=1, source_target_pairs={{0,8},{1,9},{2,10},{3,11},{4,12},{5,13},{6,14},{7,15},{8,16},{9,17... | collective-permute-start | bytes 393224 | tf_op jit(solution)/shard_map/ppermute | solution.py:33
  25.4 2.7 %collective-permute-start.7 = (bf16[64,1024]{1,0:T(8,128)(2,1)S(1)}, bf16[64,1024]{1,0:T(8,128)(2,1)S(1)}, u32[]{:S(2)}, u32[]{:S(2)}) collective-permute-start(bf16[64,1024]{1,0:T(8,128)(2,1)S(1)} %collective-permute-done.5), channel_id=1, source_target_pairs={{0,1},{1,2},{2,3},{3,4},{4,5},{5,6},{6,7},{7,0},{8,9},{9,10},{10,1... | collective-permute-start | bytes 393224 | tf_op jit(solution)/shard_map/ppermute | solution.py:33
  28.1 1.9 %collective-permute-done.2 = bf16[64,1024]{1,0:T(8,128)(2,1)S(1)} collective-permute-done((bf16[64,1024]{1,0:T(8,128)(2,1)S(1)}, bf16[64,1024]{1,0:T(8,128)(2,1)S(1)}, u32[]{:S(2)}, u32[]{:S(2)}) %collective-permute-start.2) | collective-permute-done | bytes 131104 | tf_op jit(solution)/shard_map/ppermute | solution.py:33
  30.0 1.9 %collective-permute-done.3 = bf16[64,1024]{1,0:T(8,128)(2,1)S(1)} collective-permute-done((bf16[64,1024]{1,0:T(8,128)(2,1)S(1)}, bf16[64,1024]{1,0:T(8,128)(2,1)S(1)}, u32[]{:S(2)}, u32[]{:S(2)}) %collective-permute-start.3) | collective-permute-done | bytes 131104 | tf_op jit(solution)/shard_map/ppermute | solution.py:33
  32.0 2.5 %collective-permute-start.8 = (bf16[256,1024]{1,0:T(8,128)(2,1)S(1)}, bf16[256,1024]{1,0:T(8,128)(2,1)S(1)}, u32[]{:S(2)}, u32[]{:S(2)}) collective-permute-start(bf16[256,1024]{1,0:T(8,128)(2,1)S(1)} %constant_dynamic-update-slice_fusion.refs_0_), channel_id=1, source_target_pairs={{0,1},{1,2},{2,3},{3,4},{4,5},{5,6},{6,7},{7,0},{8,9},{9,10},{10,1... | collective-permute-start | bytes 1572872 | tf_op jit(solution)/shard_map/ppermute | solution.py:33
  36.0 6.2 %collective-permute-done.8.refs_1_ = bf16[256,1024]{1,0:T(8,128)(2,1)S(1)} collective-permute-done((bf16[256,1024]{1,0:T(8,128)(2,1)S(1)}, bf16[256,1024]{1,0:T(8,128)(2,1)S(1)}, u32[]{:S(2)}, u32[]{:S(2)}) %collective-permute-start.8) | collective-permute-done | bytes 524320 | tf_op jit(solution)/shard_map/ppermute | solution.py:33
  42.2 3.3 %collective-permute-start.10 = (bf16[256,1024]{1,0:T(8,128)(2,1)S(1)}, bf16[256,1024]{1,0:T(8,128)(2,1)S(1)}, u32[]{:S(2)}, u32[]{:S(2)}) collective-permute-start(bf16[256,1024]{1,0:T(8,128)(2,1)S(1)} %collective-permute-done.8.refs_1_), channel_id=1, source_target_pairs={{0,1},{1,2},{2,3},{3,4},{4,5},{5,6},{6,7},{7,0},{8,9},{9,10},{10,1... | collective-permute-start | bytes 1572872 | tf_op jit(solution)/shard_map/ppermute | solution.py:33
  45.5 4.4 %collective-permute-done.9.refs_2_ = bf16[256,1024]{1,0:T(8,128)(2,1)S(1)} collective-permute-done((bf16[256,1024]{1,0:T(8,128)(2,1)S(1)}, bf16[256,1024]{1,0:T(8,128)(2,1)S(1)}, u32[]{:S(2)}, u32[]{:S(2)}) %collective-permute-start.9) | collective-permute-done | bytes 524320 | tf_op jit(solution)/shard_map/ppermute | solution.py:33
  50.0 1.9 %collective-permute-done.10.refs_3_ = bf16[256,1024]{1,0:T(8,128)(2,1)S(1)} collective-permute-done((bf16[256,1024]{1,0:T(8,128)(2,1)S(1)}, bf16[256,1024]{1,0:T(8,128)(2,1)S(1)}, u32[]{:S(2)}, u32[]{:S(2)}) %collective-permute-start.10) | collective-permute-done | bytes 524320 | tf_op jit(solution)/shard_map/ppermute | solution.py:33
  51.9 2.2 %collective-permute-done.13.refs_7_ = bf16[256,1024]{1,0:T(8,128)(2,1)S(1)} collective-permute-done((bf16[256,1024]{1,0:T(8,128)(2,1)S(1)}, bf16[256,1024]{1,0:T(8,128)(2,1)S(1)}, u32[]{:S(2)}, u32[]{:S(2)}) %collective-permute-start.13) | collective-permute-done | bytes 524320 | tf_op jit(solution)/shard_map/ppermute | solution.py:33
  54.1 5.0 %chain.2 = (bf16[128,1024]{1,0:T(8,128)(2,1)S(1)}, bf16[1024,1024]{1,0:T(8,128)(2,1)S(1)}, bf16[1024,1024]{1,0:T(8,128)(2,1)S(1)}) custom-call(s32[4]{0:T(128)S(1)} %pad_add_fusion.where, f32[2,32,1024]{2,1,0:T(8,128)S(1)} %get-tuple-element.20.keep, f32[2,32,1024]{2,1,0:T(8,128)S(1)} %collective-permute-done.other, ...), custom_call_target="tpu_custom_call" | custom-call | tf_op jit(solution)/shard_map/chain/pallas_call | solution.py:149
  59.1 4.4 %collective-permute-start.14 = (bf16[128,1024]{1,0:T(8,128)(2,1)S(1)}, bf16[128,1024]{1,0:T(8,128)(2,1)S(1)}, u32[]{:S(2)}, u32[]{:S(2)}) collective-permute-start(bf16[128,1024]{1,0:T(8,128)(2,1)S(1)} %get-tuple-element.24), channel_id=1, source_target_pairs={{32,0},{33,1},{34,2},{35,3},{36,4},{37,5},{38,6},{39,7},{40,8},{41... | collective-permute-start | bytes 786440 | tf_op jit(solution)/shard_map/ppermute | solution.py:33
  66.6 2.1 %collective-permute-done.15 = bf16[2,32,1024]{2,1,0:T(8,128)(2,1)S(1)} collective-permute-done((bf16[2,32,1024]{2,1,0:T(8,128)(2,1)S(1)}, bf16[2,32,1024]{2,1,0:T(8,128)(2,1)S(1)}, u32[]{:S(2)}, u32[]{:S(2)}) %collective-permute-start.15) | collective-permute-done | bytes 131104 | tf_op jit(solution)/shard_map/ppermute | solution.py:33
  70.1 3.7 %collective-permute-done.16 = bf16[2,32,1024]{2,1,0:T(8,128)(2,1)S(1)} collective-permute-done((bf16[2,32,1024]{2,1,0:T(8,128)(2,1)S(1)}, bf16[2,32,1024]{2,1,0:T(8,128)(2,1)S(1)}, u32[]{:S(2)}, u32[]{:S(2)}) %collective-permute-start.16) | collective-permute-done | bytes 131104 | tf_op jit(solution)/shard_map/ppermute | solution.py:33
  73.9 2.6 %collective-permute-start.17 = (bf16[64,1024]{1,0:T(8,128)(2,1)S(1)}, bf16[64,1024]{1,0:T(8,128)(2,1)S(1)}, u32[]{:S(2)}, u32[]{:S(2)}) collective-permute-start(bf16[64,1024]{1,0:T(8,128)(2,1)S(1)} %fusion.1), channel_id=1, source_target_pairs={{0,4},{1,5},{2,6},{3,7},{4,0},{5,1},{6,2},{7,3},{8,12},{9,13},{10,... | collective-permute-start | bytes 393224 | tf_op jit(solution)/shard_map/ppermute | solution.py:33
  76.5 5.3 %collective-permute-done.17 = bf16[64,1024]{1,0:T(8,128)(2,1)S(1)} collective-permute-done((bf16[64,1024]{1,0:T(8,128)(2,1)S(1)}, bf16[64,1024]{1,0:T(8,128)(2,1)S(1)}, u32[]{:S(2)}, u32[]{:S(2)}) %collective-permute-start.17) | collective-permute-done | bytes 131104 | tf_op jit(solution)/shard_map/ppermute | solution.py:33
  81.9 6.6 %collective-permute-start.21 = (bf16[64,1024]{1,0:T(8,128)(2,1)S(1)}, bf16[64,1024]{1,0:T(8,128)(2,1)S(1)}, u32[]{:S(2)}, u32[]{:S(2)}) collective-permute-start(bf16[64,1024]{1,0:T(8,128)(2,1)S(1)} %pad_maximum_fusion.3), channel_id=1, source_target_pairs={{0,1},{1,2},{2,3},{3,4},{4,5},{5,6},{6,7},{7,0},{8,9},{9,10},{10,1... | collective-permute-start | bytes 393224 | tf_op jit(solution)/shard_map/ppermute | solution.py:33
  90.5 3.1 %collective-permute-start.23 = (bf16[64,1024]{1,0:T(8,128)(2,1)S(1)}, bf16[64,1024]{1,0:T(8,128)(2,1)S(1)}, u32[]{:S(2)}, u32[]{:S(2)}) collective-permute-start(bf16[64,1024]{1,0:T(8,128)(2,1)S(1)} %collective-permute-done.21), channel_id=1, source_target_pairs={{0,1},{1,2},{2,3},{3,4},{4,5},{5,6},{6,7},{7,0},{8,9},{9,10},{10,1... | collective-permute-start | bytes 393224 | tf_op jit(solution)/shard_map/ppermute | solution.py:33
  93.6 2.8 %collective-permute-done.19 = bf16[64,1024]{1,0:T(8,128)(2,1)S(1)} collective-permute-done((bf16[64,1024]{1,0:T(8,128)(2,1)S(1)}, bf16[64,1024]{1,0:T(8,128)(2,1)S(1)}, u32[]{:S(2)}, u32[]{:S(2)}) %collective-permute-start.19) | collective-permute-done | bytes 131104 | tf_op jit(solution)/shard_map/ppermute | solution.py:33
  96.8 3.5 %collective-permute-start.24 = (bf16[256,1024]{1,0:T(8,128)(2,1)S(1)}, bf16[256,1024]{1,0:T(8,128)(2,1)S(1)}, u32[]{:S(2)}, u32[]{:S(2)}) collective-permute-start(bf16[256,1024]{1,0:T(8,128)(2,1)S(1)} %constant_dynamic-update-slice_fusion.10.refs_0_), channel_id=1, source_target_pairs={{0,1},{1,2},{2,3},{3,4},{4,5},{5,6},{6,7},{7,0},{8,9},{9,10},{10,1... | collective-permute-start | bytes 1572872 | tf_op jit(solution)/shard_map/ppermute | solution.py:33
  101.8 6.9 %collective-permute-done.24.refs_1_ = bf16[256,1024]{1,0:T(8,128)(2,1)S(1)} collective-permute-done((bf16[256,1024]{1,0:T(8,128)(2,1)S(1)}, bf16[256,1024]{1,0:T(8,128)(2,1)S(1)}, u32[]{:S(2)}, u32[]{:S(2)}) %collective-permute-start.24) | collective-permute-done | bytes 524320 | tf_op jit(solution)/shard_map/ppermute | solution.py:33
  108.7 3.4 %collective-permute-start.26 = (bf16[256,1024]{1,0:T(8,128)(2,1)S(1)}, bf16[256,1024]{1,0:T(8,128)(2,1)S(1)}, u32[]{:S(2)}, u32[]{:S(2)}) collective-permute-start(bf16[256,1024]{1,0:T(8,128)(2,1)S(1)} %collective-permute-done.24.refs_1_), channel_id=1, source_target_pairs={{0,1},{1,2},{2,3},{3,4},{4,5},{5,6},{6,7},{7,0},{8,9},{9,10},{10,1... | collective-permute-start | bytes 1572872 | tf_op jit(solution)/shard_map/ppermute | solution.py:33
  112.1 2.9 %collective-permute-done.25.refs_2_ = bf16[256,1024]{1,0:T(8,128)(2,1)S(1)} collective-permute-done((bf16[256,1024]{1,0:T(8,128)(2,1)S(1)}, bf16[256,1024]{1,0:T(8,128)(2,1)S(1)}, u32[]{:S(2)}, u32[]{:S(2)}) %collective-permute-start.25) | collective-permute-done | bytes 524320 | tf_op jit(solution)/shard_map/ppermute | solution.py:33
  115.1 3.2 %collective-permute-done.26.refs_3_ = bf16[256,1024]{1,0:T(8,128)(2,1)S(1)} collective-permute-done((bf16[256,1024]{1,0:T(8,128)(2,1)S(1)}, bf16[256,1024]{1,0:T(8,128)(2,1)S(1)}, u32[]{:S(2)}, u32[]{:S(2)}) %collective-permute-start.26) | collective-permute-done | bytes 524320 | tf_op jit(solution)/shard_map/ppermute | solution.py:33
  118.2 2.2 %collective-permute-done.29.refs_7_ = bf16[256,1024]{1,0:T(8,128)(2,1)S(1)} collective-permute-done((bf16[256,1024]{1,0:T(8,128)(2,1)S(1)}, bf16[256,1024]{1,0:T(8,128)(2,1)S(1)}, u32[]{:S(2)}, u32[]{:S(2)}) %collective-permute-start.29) | collective-permute-done | bytes 524320 | tf_op jit(solution)/shard_map/ppermute | solution.py:33
  120.4 5.0 %chain.3 = (bf16[128,1024]{1,0:T(8,128)(2,1)S(1)}, bf16[1024,1024]{1,0:T(8,128)(2,1)S(1)}, bf16[1024,1024]{1,0:T(8,128)(2,1)S(1)}) custom-call(s32[4]{0:T(128)S(1)} %pad_add_fusion.where, f32[2,32,1024]{2,1,0:T(8,128)S(1)} %get-tuple-element.36.keep, f32[2,32,1024]{2,1,0:T(8,128)S(1)} %get-tuple-element.35.other, ...), custom_call_target="tpu_custom_call" | custom-call | tf_op jit(solution)/shard_map/chain/pallas_call | solution.py:149
  125.5 2.6 %collective-permute-start.30 = (bf16[128,1024]{1,0:T(8,128)(2,1)S(1)}, bf16[128,1024]{1,0:T(8,128)(2,1)S(1)}, u32[]{:S(2)}, u32[]{:S(2)}) collective-permute-start(bf16[128,1024]{1,0:T(8,128)(2,1)S(1)} %get-tuple-element.32), channel_id=1, source_target_pairs={{32,0},{33,1},{34,2},{35,3},{36,4},{37,5},{38,6},{39,7},{40,8},{41... | collective-permute-start | bytes 786440 | tf_op jit(solution)/shard_map/ppermute | solution.py:33
  131.1 2.6 %collective-permute-done.31 = f32[4,32,1024]{2,1,0:T(8,128)S(1)} collective-permute-done((f32[4,32,1024]{2,1,0:T(8,128)S(1)}, f32[4,32,1024]{2,1,0:T(8,128)S(1)}, u32[]{:S(2)}, u32[]{:S(2)}) %collective-permute-start.31) | collective-permute-done | bytes 524320 | tf_op jit(solution)/shard_map/ppermute | solution.py:33
  (70 shorter events, 19.0 us)
Async XLA Ops:
  2.6 4.5 %collective-permute-start = (f32[2,32,1024]{2,1,0:T(8,128)S(1)}, f32[2,32,1024]{2,1,0:T(8,128)S(1)}, u32[]{:S(2)}, u32[]{:S(2)}) collective-permute-start(f32[2,32,1024]{2,1,0:T(8,128)S(1)} %get-tuple-element.21), channel_id=1, source_target_pairs={{0,32},{1,33},{2,34},{3,35},{4,36},{5,37},{6,38},{7,39},{8,40},{9,... | collective-permute-start | bytes 786440 | tf_op jit(solution)/shard_map/ppermute | solution.py:33
  7.1 8.7 %collective-permute-start.1 = (bf16[64,1024]{1,0:T(8,128)(2,1)S(1)}, bf16[64,1024]{1,0:T(8,128)(2,1)S(1)}, u32[]{:S(2)}, u32[]{:S(2)}) collective-permute-start(bf16[64,1024]{1,0:T(8,128)(2,1)S(1)} %fusion), channel_id=1, source_target_pairs={{0,4},{1,5},{2,6},{3,7},{4,0},{5,1},{6,2},{7,3},{8,12},{9,13},{10,... | collective-permute-start | bytes 393224 | tf_op jit(solution)/shard_map/ppermute | solution.py:33
  15.9 9.5 %collective-permute-start.5 = (bf16[64,1024]{1,0:T(8,128)(2,1)S(1)}, bf16[64,1024]{1,0:T(8,128)(2,1)S(1)}, u32[]{:S(2)}, u32[]{:S(2)}) collective-permute-start(bf16[64,1024]{1,0:T(8,128)(2,1)S(1)} %pad_maximum_fusion.1), channel_id=1, source_target_pairs={{0,1},{1,2},{2,3},{3,4},{4,5},{5,6},{6,7},{7,0},{8,9},{9,10},{10,1... | collective-permute-start | bytes 393224 | tf_op jit(solution)/shard_map/ppermute | solution.py:33
  21.5 8.5 %collective-permute-start.2 = (bf16[64,1024]{1,0:T(8,128)(2,1)S(1)}, bf16[64,1024]{1,0:T(8,128)(2,1)S(1)}, u32[]{:S(2)}, u32[]{:S(2)}) collective-permute-start(bf16[64,1024]{1,0:T(8,128)(2,1)S(1)} %pad_maximum_fusion), channel_id=1, source_target_pairs={{0,8},{1,9},{2,10},{3,11},{4,12},{5,13},{6,14},{7,15},{8,16},{9,17... | collective-permute-start | bytes 393224 | tf_op jit(solution)/shard_map/ppermute | solution.py:33
  24.3 7.6 %collective-permute-start.4 = (bf16[64,1024]{1,0:T(8,128)(2,1)S(1)}, bf16[64,1024]{1,0:T(8,128)(2,1)S(1)}, u32[]{:S(2)}, u32[]{:S(2)}) collective-permute-start(bf16[64,1024]{1,0:T(8,128)(2,1)S(1)} %pad_maximum_fusion), channel_id=1, source_target_pairs={{0,16},{1,17},{2,18},{3,19},{4,20},{5,21},{6,22},{7,23},{8,24},{9,... | collective-permute-start | bytes 393224 | tf_op jit(solution)/shard_map/ppermute | solution.py:33
  24.7 7.2 %collective-permute-start.3 = (bf16[64,1024]{1,0:T(8,128)(2,1)S(1)}, bf16[64,1024]{1,0:T(8,128)(2,1)S(1)}, u32[]{:S(2)}, u32[]{:S(2)}) collective-permute-start(bf16[64,1024]{1,0:T(8,128)(2,1)S(1)} %pad_maximum_fusion), channel_id=1, source_target_pairs={{0,24},{1,25},{2,26},{3,27},{4,28},{5,29},{6,30},{7,31},{8,0},{9,1... | collective-permute-start | bytes 393224 | tf_op jit(solution)/shard_map/ppermute | solution.py:33
  25.4 6.5 %collective-permute-start.6 = (bf16[64,1024]{1,0:T(8,128)(2,1)S(1)}, bf16[64,1024]{1,0:T(8,128)(2,1)S(1)}, u32[]{:S(2)}, u32[]{:S(2)}) collective-permute-start(bf16[64,1024]{1,0:T(8,128)(2,1)S(1)} %pad_maximum_fusion.1), channel_id=1, source_target_pairs={{0,7},{1,0},{2,1},{3,2},{4,3},{5,4},{6,5},{7,6},{8,15},{9,8},{10,9... | collective-permute-start | bytes 393224 | tf_op jit(solution)/shard_map/ppermute | solution.py:33
  25.4 6.6 %collective-permute-start.7 = (bf16[64,1024]{1,0:T(8,128)(2,1)S(1)}, bf16[64,1024]{1,0:T(8,128)(2,1)S(1)}, u32[]{:S(2)}, u32[]{:S(2)}) collective-permute-start(bf16[64,1024]{1,0:T(8,128)(2,1)S(1)} %collective-permute-done.5), channel_id=1, source_target_pairs={{0,1},{1,2},{2,3},{3,4},{4,5},{5,6},{6,7},{7,0},{8,9},{9,10},{10,1... | collective-permute-start | bytes 393224 | tf_op jit(solution)/shard_map/ppermute | solution.py:33
  32.0 10.2 %collective-permute-start.8 = (bf16[256,1024]{1,0:T(8,128)(2,1)S(1)}, bf16[256,1024]{1,0:T(8,128)(2,1)S(1)}, u32[]{:S(2)}, u32[]{:S(2)}) collective-permute-start(bf16[256,1024]{1,0:T(8,128)(2,1)S(1)} %constant_dynamic-update-slice_fusion.refs_0_), channel_id=1, source_target_pairs={{0,1},{1,2},{2,3},{3,4},{4,5},{5,6},{6,7},{7,0},{8,9},{9,10},{10,1... | collective-permute-start | bytes 1572872 | tf_op jit(solution)/shard_map/ppermute | solution.py:33
  34.5 10.9 %collective-permute-start.11 = (bf16[256,1024]{1,0:T(8,128)(2,1)S(1)}, bf16[256,1024]{1,0:T(8,128)(2,1)S(1)}, u32[]{:S(2)}, u32[]{:S(2)}) collective-permute-start(bf16[256,1024]{1,0:T(8,128)(2,1)S(1)} %constant_dynamic-update-slice_fusion.5.refs_4_), channel_id=1, source_target_pairs={{0,8},{1,9},{2,10},{3,11},{4,12},{5,13},{6,14},{7,15},{8,16},{9,17... | collective-permute-start | bytes 1572872 | tf_op jit(solution)/shard_map/ppermute | solution.py:33
  35.7 14.2 %collective-permute-start.9 = (bf16[256,1024]{1,0:T(8,128)(2,1)S(1)}, bf16[256,1024]{1,0:T(8,128)(2,1)S(1)}, u32[]{:S(2)}, u32[]{:S(2)}) collective-permute-start(bf16[256,1024]{1,0:T(8,128)(2,1)S(1)} %constant_dynamic-update-slice_fusion.refs_0_), channel_id=1, source_target_pairs={{0,7},{1,0},{2,1},{3,2},{4,3},{5,4},{6,5},{7,6},{8,15},{9,8},{10,9... | collective-permute-start | bytes 1572872 | tf_op jit(solution)/shard_map/ppermute | solution.py:33
  35.7 14.3 %collective-permute-start.12 = (bf16[256,1024]{1,0:T(8,128)(2,1)S(1)}, bf16[256,1024]{1,0:T(8,128)(2,1)S(1)}, u32[]{:S(2)}, u32[]{:S(2)}) collective-permute-start(bf16[256,1024]{1,0:T(8,128)(2,1)S(1)} %constant_dynamic-update-slice_fusion.5.refs_4_), channel_id=1, source_target_pairs={{0,24},{1,25},{2,26},{3,27},{4,28},{5,29},{6,30},{7,31},{8,0},{9,1... | collective-permute-start | bytes 1572872 | tf_op jit(solution)/shard_map/ppermute | solution.py:33
  42.2 9.7 %collective-permute-start.10 = (bf16[256,1024]{1,0:T(8,128)(2,1)S(1)}, bf16[256,1024]{1,0:T(8,128)(2,1)S(1)}, u32[]{:S(2)}, u32[]{:S(2)}) collective-permute-start(bf16[256,1024]{1,0:T(8,128)(2,1)S(1)} %collective-permute-done.8.refs_1_), channel_id=1, source_target_pairs={{0,1},{1,2},{2,3},{3,4},{4,5},{5,6},{6,7},{7,0},{8,9},{9,10},{10,1... | collective-permute-start | bytes 1572872 | tf_op jit(solution)/shard_map/ppermute | solution.py:33
  45.5 8.6 %collective-permute-start.13 = (bf16[256,1024]{1,0:T(8,128)(2,1)S(1)}, bf16[256,1024]{1,0:T(8,128)(2,1)S(1)}, u32[]{:S(2)}, u32[]{:S(2)}) collective-permute-start(bf16[256,1024]{1,0:T(8,128)(2,1)S(1)} %collective-permute-done.11.refs_5_), channel_id=1, source_target_pairs={{0,8},{1,9},{2,10},{3,11},{4,12},{5,13},{6,14},{7,15},{8,16},{9,17... | collective-permute-start | bytes 1572872 | tf_op jit(solution)/shard_map/ppermute | solution.py:33
  59.1 5.5 %collective-permute-start.14 = (bf16[128,1024]{1,0:T(8,128)(2,1)S(1)}, bf16[128,1024]{1,0:T(8,128)(2,1)S(1)}, u32[]{:S(2)}, u32[]{:S(2)}) collective-permute-start(bf16[128,1024]{1,0:T(8,128)(2,1)S(1)} %get-tuple-element.24), channel_id=1, source_target_pairs={{32,0},{33,1},{34,2},{35,3},{36,4},{37,5},{38,6},{39,7},{40,8},{41... | collective-permute-start | bytes 786440 | tf_op jit(solution)/shard_map/ppermute | solution.py:33
  65.3 3.4 %collective-permute-start.15 = (bf16[2,32,1024]{2,1,0:T(8,128)(2,1)S(1)}, bf16[2,32,1024]{2,1,0:T(8,128)(2,1)S(1)}, u32[]{:S(2)}, u32[]{:S(2)}) collective-permute-start(bf16[2,32,1024]{2,1,0:T(8,128)(2,1)S(1)} %get-tuple-element.28), channel_id=1, source_target_pairs={{0,32},{1,33},{2,34},{3,35},{4,36},{5,37},{6,38},{7,39},{8,40},{9,... | collective-permute-start | bytes 393224 | tf_op jit(solution)/shard_map/ppermute | solution.py:33
  68.7 5.0 %collective-permute-start.16 = (bf16[2,32,1024]{2,1,0:T(8,128)(2,1)S(1)}, bf16[2,32,1024]{2,1,0:T(8,128)(2,1)S(1)}, u32[]{:S(2)}, u32[]{:S(2)}) collective-permute-start(bf16[2,32,1024]{2,1,0:T(8,128)(2,1)S(1)} %broadcast_select_fusion), channel_id=1, source_target_pairs={{0,64},{1,65},{2,66},{3,67},{4,68},{5,69},{6,70},{7,71},{8,72},{9,... | collective-permute-start | bytes 393224 | tf_op jit(solution)/shard_map/ppermute | solution.py:33
  73.9 7.9 %collective-permute-start.17 = (bf16[64,1024]{1,0:T(8,128)(2,1)S(1)}, bf16[64,1024]{1,0:T(8,128)(2,1)S(1)}, u32[]{:S(2)}, u32[]{:S(2)}) collective-permute-start(bf16[64,1024]{1,0:T(8,128)(2,1)S(1)} %fusion.1), channel_id=1, source_target_pairs={{0,4},{1,5},{2,6},{3,7},{4,0},{5,1},{6,2},{7,3},{8,12},{9,13},{10,... | collective-permute-start | bytes 393224 | tf_op jit(solution)/shard_map/ppermute | solution.py:33
  81.9 8.6 %collective-permute-start.21 = (bf16[64,1024]{1,0:T(8,128)(2,1)S(1)}, bf16[64,1024]{1,0:T(8,128)(2,1)S(1)}, u32[]{:S(2)}, u32[]{:S(2)}) collective-permute-start(bf16[64,1024]{1,0:T(8,128)(2,1)S(1)} %pad_maximum_fusion.3), channel_id=1, source_target_pairs={{0,1},{1,2},{2,3},{3,4},{4,5},{5,6},{6,7},{7,0},{8,9},{9,10},{10,1... | collective-permute-start | bytes 393224 | tf_op jit(solution)/shard_map/ppermute | solution.py:33
  88.5 5.1 %collective-permute-start.18 = (bf16[64,1024]{1,0:T(8,128)(2,1)S(1)}, bf16[64,1024]{1,0:T(8,128)(2,1)S(1)}, u32[]{:S(2)}, u32[]{:S(2)}) collective-permute-start(bf16[64,1024]{1,0:T(8,128)(2,1)S(1)} %pad_maximum_fusion.2), channel_id=1, source_target_pairs={{0,8},{1,9},{2,10},{3,11},{4,12},{5,13},{6,14},{7,15},{8,16},{9,17... | collective-permute-start | bytes 393224 | tf_op jit(solution)/shard_map/ppermute | solution.py:33
  88.6 7.8 %collective-permute-start.20 = (bf16[64,1024]{1,0:T(8,128)(2,1)S(1)}, bf16[64,1024]{1,0:T(8,128)(2,1)S(1)}, u32[]{:S(2)}, u32[]{:S(2)}) collective-permute-start(bf16[64,1024]{1,0:T(8,128)(2,1)S(1)} %pad_maximum_fusion.2), channel_id=1, source_target_pairs={{0,16},{1,17},{2,18},{3,19},{4,20},{5,21},{6,22},{7,23},{8,24},{9,... | collective-permute-start | bytes 393224 | tf_op jit(solution)/shard_map/ppermute | solution.py:33
  89.1 7.2 %collective-permute-start.19 = (bf16[64,1024]{1,0:T(8,128)(2,1)S(1)}, bf16[64,1024]{1,0:T(8,128)(2,1)S(1)}, u32[]{:S(2)}, u32[]{:S(2)}) collective-permute-start(bf16[64,1024]{1,0:T(8,128)(2,1)S(1)} %pad_maximum_fusion.2), channel_id=1, source_target_pairs={{0,24},{1,25},{2,26},{3,27},{4,28},{5,29},{6,30},{7,31},{8,0},{9,1... | collective-permute-start | bytes 393224 | tf_op jit(solution)/shard_map/ppermute | solution.py:33
  90.1 6.4 %collective-permute-start.22 = (bf16[64,1024]{1,0:T(8,128)(2,1)S(1)}, bf16[64,1024]{1,0:T(8,128)(2,1)S(1)}, u32[]{:S(2)}, u32[]{:S(2)}) collective-permute-start(bf16[64,1024]{1,0:T(8,128)(2,1)S(1)} %pad_maximum_fusion.3), channel_id=1, source_target_pairs={{0,7},{1,0},{2,1},{3,2},{4,3},{5,4},{6,5},{7,6},{8,15},{9,8},{10,9... | collective-permute-start | bytes 393224 | tf_op jit(solution)/shard_map/ppermute | solution.py:33
  90.5 6.4 %collective-permute-start.23 = (bf16[64,1024]{1,0:T(8,128)(2,1)S(1)}, bf16[64,1024]{1,0:T(8,128)(2,1)S(1)}, u32[]{:S(2)}, u32[]{:S(2)}) collective-permute-start(bf16[64,1024]{1,0:T(8,128)(2,1)S(1)} %collective-permute-done.21), channel_id=1, source_target_pairs={{0,1},{1,2},{2,3},{3,4},{4,5},{5,6},{6,7},{7,0},{8,9},{9,10},{10,1... | collective-permute-start | bytes 393224 | tf_op jit(solution)/shard_map/ppermute | solution.py:33
  96.8 11.9 %collective-permute-start.24 = (bf16[256,1024]{1,0:T(8,128)(2,1)S(1)}, bf16[256,1024]{1,0:T(8,128)(2,1)S(1)}, u32[]{:S(2)}, u32[]{:S(2)}) collective-permute-start(bf16[256,1024]{1,0:T(8,128)(2,1)S(1)} %constant_dynamic-update-slice_fusion.10.refs_0_), channel_id=1, source_target_pairs={{0,1},{1,2},{2,3},{3,4},{4,5},{5,6},{6,7},{7,0},{8,9},{9,10},{10,1... | collective-permute-start | bytes 1572872 | tf_op jit(solution)/shard_map/ppermute | solution.py:33
  100.3 11.8 %collective-permute-start.27 = (bf16[256,1024]{1,0:T(8,128)(2,1)S(1)}, bf16[256,1024]{1,0:T(8,128)(2,1)S(1)}, u32[]{:S(2)}, u32[]{:S(2)}) collective-permute-start(bf16[256,1024]{1,0:T(8,128)(2,1)S(1)} %constant_dynamic-update-slice_fusion.15.refs_4_), channel_id=1, source_target_pairs={{0,8},{1,9},{2,10},{3,11},{4,12},{5,13},{6,14},{7,15},{8,16},{9,17... | collective-permute-start | bytes 1572872 | tf_op jit(solution)/shard_map/ppermute | solution.py:33
  101.1 13.8 %collective-permute-start.25 = (bf16[256,1024]{1,0:T(8,128)(2,1)S(1)}, bf16[256,1024]{1,0:T(8,128)(2,1)S(1)}, u32[]{:S(2)}, u32[]{:S(2)}) collective-permute-start(bf16[256,1024]{1,0:T(8,128)(2,1)S(1)} %constant_dynamic-update-slice_fusion.10.refs_0_), channel_id=1, source_target_pairs={{0,7},{1,0},{2,1},{3,2},{4,3},{5,4},{6,5},{7,6},{8,15},{9,8},{10,9... | collective-permute-start | bytes 1572872 | tf_op jit(solution)/shard_map/ppermute | solution.py:33
  101.1 13.9 %collective-permute-start.28 = (bf16[256,1024]{1,0:T(8,128)(2,1)S(1)}, bf16[256,1024]{1,0:T(8,128)(2,1)S(1)}, u32[]{:S(2)}, u32[]{:S(2)}) collective-permute-start(bf16[256,1024]{1,0:T(8,128)(2,1)S(1)} %constant_dynamic-update-slice_fusion.15.refs_4_), channel_id=1, source_target_pairs={{0,24},{1,25},{2,26},{3,27},{4,28},{5,29},{6,30},{7,31},{8,0},{9,1... | collective-permute-start | bytes 1572872 | tf_op jit(solution)/shard_map/ppermute | solution.py:33
  108.7 9.5 %collective-permute-start.26 = (bf16[256,1024]{1,0:T(8,128)(2,1)S(1)}, bf16[256,1024]{1,0:T(8,128)(2,1)S(1)}, u32[]{:S(2)}, u32[]{:S(2)}) collective-permute-start(bf16[256,1024]{1,0:T(8,128)(2,1)S(1)} %collective-permute-done.24.refs_1_), channel_id=1, source_target_pairs={{0,1},{1,2},{2,3},{3,4},{4,5},{5,6},{6,7},{7,0},{8,9},{9,10},{10,1... | collective-permute-start | bytes 1572872 | tf_op jit(solution)/shard_map/ppermute | solution.py:33
  112.1 8.3 %collective-permute-start.29 = (bf16[256,1024]{1,0:T(8,128)(2,1)S(1)}, bf16[256,1024]{1,0:T(8,128)(2,1)S(1)}, u32[]{:S(2)}, u32[]{:S(2)}) collective-permute-start(bf16[256,1024]{1,0:T(8,128)(2,1)S(1)} %collective-permute-done.27.refs_5_), channel_id=1, source_target_pairs={{0,8},{1,9},{2,10},{3,11},{4,12},{5,13},{6,14},{7,15},{8,16},{9,17... | collective-permute-start | bytes 1572872 | tf_op jit(solution)/shard_map/ppermute | solution.py:33
  125.5 3.8 %collective-permute-start.30 = (bf16[128,1024]{1,0:T(8,128)(2,1)S(1)}, bf16[128,1024]{1,0:T(8,128)(2,1)S(1)}, u32[]{:S(2)}, u32[]{:S(2)}) collective-permute-start(bf16[128,1024]{1,0:T(8,128)(2,1)S(1)} %get-tuple-element.32), channel_id=1, source_target_pairs={{32,0},{33,1},{34,2},{35,3},{36,4},{37,5},{38,6},{39,7},{40,8},{41... | collective-permute-start | bytes 786440 | tf_op jit(solution)/shard_map/ppermute | solution.py:33
  129.8 3.9 %collective-permute-start.31 = (f32[4,32,1024]{2,1,0:T(8,128)S(1)}, f32[4,32,1024]{2,1,0:T(8,128)S(1)}, u32[]{:S(2)}, u32[]{:S(2)}) collective-permute-start(f32[4,32,1024]{2,1,0:T(8,128)S(1)} %finish.3), channel_id=1, source_target_pairs={{0,32},{1,33},{2,34},{3,35},{4,36},{5,37},{6,38},{7,39},{8,40},{9,... | collective-permute-start | bytes 1572872 | tf_op jit(solution)/shard_map/ppermute | solution.py:33
  (2 other events, 1.8 us)

commit v10 on v9

--- a/solution.py
+++ b/solution.py
@@ -42,9 +42,9 @@
 
 
 def gather(block):
-    pair = send(block, hop("z", NZ // 2))
-    wide_a = jnp.concatenate([block[:32], pair[:32]])
-    wide_b = jnp.concatenate([block[32:], pair[32:]])
+    wide_a, wide_b = block[:32], block[32:]
+    wide_a = jnp.concatenate([wide_a, send(wide_a, hop("z", NZ // 2))])
+    wide_b = jnp.concatenate([wide_b, send(wide_b, hop("z", NZ // 2))])
     ahead, behind = send(wide_a, hop("y", 1)), send(wide_a, hop("y", -1))
     wide_a = jnp.concatenate([wide_a, ahead, behind, send(wide_a, hop("y", 2))])
     ahead, behind = send(wide_b, hop("z", 1)), send(wide_b, hop("z", -1))

time: 135 us -> 137 us (1.015)
    ppermute x32 -> x34, waiting for transfers between devices: 57.9 us -> 58.5 us  [send(): return lax.ppermute(block, AXES, route(move))]
    ppermute x32 -> x34, starting transfers between devices: 61.2 us -> 61.8 us  [send(): return lax.ppermute(block, AXES, route(move))]
  transfers between devices with their start and end apart: 32 -> 34, of which waited for: 23 -> 22; matrix products, arithmetic and copies ran while one was open for 0% -> 0% of each run, Pallas kernels for 0% -> 0%
where the time goes in v10:
time: 137 us; the launch traced here: 136 us
  starting transfers between devices  61.8 us (45%)
  waiting for transfers between devices  58.5 us (43%)
  Pallas kernels  12 us (9%)
  local copies, waits for them, and re-layouts  2.05 us (1%)
    ppermute x34, starting transfers between devices, send(): return lax.ppermute(block, AXES, route(move))  61.8 us
    ppermute x34, waiting for transfers between devices, send(): return lax.ppermute(block, AXES, route(move))  58.5 us
    pallas_call x2, Pallas kernels, chain(): pl.pallas_call(chain_kernel, out_shape=[jax.ShapeDtypeStruct((128, M), jn...  10.2 us
  transfers between devices with their start and end apart: 34, of which 22 were waited for; matrix products, arithmetic and copies ran while one was open for 0% of the time, Pallas kernels for 0%

profile of v10, /device:TPU:1, one launch (start us, length us, event | category | flops | bytes accessed | tf_op | source)
XLA Modules:
  0.0 135.8 jit_solution(1899775120801283711)
XLA Ops:
  2.6 3.3 %collective-permute-start = (f32[2,32,1024]{2,1,0:T(8,128)S(1)}, f32[2,32,1024]{2,1,0:T(8,128)S(1)}, u32[]{:S(2)}, u32[]{:S(2)}) collective-permute-start(f32[2,32,1024]{2,1,0:T(8,128)S(1)} %get-tuple-element.21), channel_id=1, source_target_pairs={{0,32},{1,33},{2,34},{3,35},{4,36},{5,37},{6,38},{7,39},{8,40},{9,... | collective-permute-start | bytes 786440 | tf_op jit(solution)/shard_map/ppermute | solution.py:33
  7.2 5.3 %collective-permute-start.1 = (bf16[32,1024]{1,0:T(8,128)(2,1)S(1)}, bf16[32,1024]{1,0:T(8,128)(2,1)S(1)}, u32[]{:S(2)}, u32[]{:S(2)}) collective-permute-start(bf16[32,1024]{1,0:T(8,128)(2,1)S(1)} %get-tuple-element.52), channel_id=1, source_target_pairs={{0,4},{1,5},{2,6},{3,7},{4,0},{5,1},{6,2},{7,3},{8,12},{9,13},{10,... | collective-permute-start | bytes 196616 | tf_op jit(solution)/shard_map/ppermute | solution.py:33
  12.6 1.7 %collective-permute-done.1 = bf16[32,1024]{1,0:T(8,128)(2,1)S(1)} collective-permute-done((bf16[32,1024]{1,0:T(8,128)(2,1)S(1)}, bf16[32,1024]{1,0:T(8,128)(2,1)S(1)}, u32[]{:S(2)}, u32[]{:S(2)}) %collective-permute-start.1) | collective-permute-done | bytes 65568 | tf_op jit(solution)/shard_map/ppermute | solution.py:33
  14.4 3.2 %collective-permute-start.4 = (bf16[64,1024]{1,0:T(8,128)(2,1)S(1)}, bf16[64,1024]{1,0:T(8,128)(2,1)S(1)}, u32[]{:S(2)}, u32[]{:S(2)}) collective-permute-start(bf16[64,1024]{1,0:T(8,128)(2,1)S(1)} %pad_maximum_fusion), channel_id=1, source_target_pairs={{0,16},{1,17},{2,18},{3,19},{4,20},{5,21},{6,22},{7,23},{8,24},{9,... | collective-permute-start | bytes 393224 | tf_op jit(solution)/shard_map/ppermute | solution.py:33
  18.0 2.3 %collective-permute-start.2 = (bf16[64,1024]{1,0:T(8,128)(2,1)S(1)}, bf16[64,1024]{1,0:T(8,128)(2,1)S(1)}, u32[]{:S(2)}, u32[]{:S(2)}) collective-permute-start(bf16[64,1024]{1,0:T(8,128)(2,1)S(1)} %pad_maximum_fusion), channel_id=1, source_target_pairs={{0,8},{1,9},{2,10},{3,11},{4,12},{5,13},{6,14},{7,15},{8,16},{9,17... | collective-permute-start | bytes 393224 | tf_op jit(solution)/shard_map/ppermute | solution.py:33
  21.1 3.5 %collective-permute-start.6 = (bf16[64,1024]{1,0:T(8,128)(2,1)S(1)}, bf16[64,1024]{1,0:T(8,128)(2,1)S(1)}, u32[]{:S(2)}, u32[]{:S(2)}) collective-permute-start(bf16[64,1024]{1,0:T(8,128)(2,1)S(1)} %pad_maximum_fusion.1), channel_id=1, source_target_pairs={{0,1},{1,2},{2,3},{3,4},{4,5},{5,6},{6,7},{7,0},{8,9},{9,10},{10,1... | collective-permute-start | bytes 393224 | tf_op jit(solution)/shard_map/ppermute | solution.py:33
  24.6 1.9 %collective-permute-done.6 = bf16[64,1024]{1,0:T(8,128)(2,1)S(1)} collective-permute-done((bf16[64,1024]{1,0:T(8,128)(2,1)S(1)}, bf16[64,1024]{1,0:T(8,128)(2,1)S(1)}, u32[]{:S(2)}, u32[]{:S(2)}) %collective-permute-start.6) | collective-permute-done | bytes 131104 | tf_op jit(solution)/shard_map/ppermute | solution.py:33
  26.6 3.4 %collective-permute-start.8 = (bf16[64,1024]{1,0:T(8,128)(2,1)S(1)}, bf16[64,1024]{1,0:T(8,128)(2,1)S(1)}, u32[]{:S(2)}, u32[]{:S(2)}) collective-permute-start(bf16[64,1024]{1,0:T(8,128)(2,1)S(1)} %collective-permute-done.6), channel_id=1, source_target_pairs={{0,1},{1,2},{2,3},{3,4},{4,5},{5,6},{6,7},{7,0},{8,9},{9,10},{10,1... | collective-permute-start | bytes 393224 | tf_op jit(solution)/shard_map/ppermute | solution.py:33
  30.1 1.8 %collective-permute-done.8 = bf16[64,1024]{1,0:T(8,128)(2,1)S(1)} collective-permute-done((bf16[64,1024]{1,0:T(8,128)(2,1)S(1)}, bf16[64,1024]{1,0:T(8,128)(2,1)S(1)}, u32[]{:S(2)}, u32[]{:S(2)}) %collective-permute-start.8) | collective-permute-done | bytes 131104 | tf_op jit(solution)/shard_map/ppermute | solution.py:33
  31.9 3.2 %collective-permute-start.9 = (bf16[256,1024]{1,0:T(8,128)(2,1)S(1)}, bf16[256,1024]{1,0:T(8,128)(2,1)S(1)}, u32[]{:S(2)}, u32[]{:S(2)}) collective-permute-start(bf16[256,1024]{1,0:T(8,128)(2,1)S(1)} %constant_dynamic-update-slice_fusion.refs_0_), channel_id=1, source_target_pairs={{0,1},{1,2},{2,3},{3,4},{4,5},{5,6},{6,7},{7,0},{8,9},{9,10},{10,1... | collective-permute-start | bytes 1572872 | tf_op jit(solution)/shard_map/ppermute | solution.py:33
  36.5 4.7 %collective-permute-done.9.refs_1_ = bf16[256,1024]{1,0:T(8,128)(2,1)S(1)} collective-permute-done((bf16[256,1024]{1,0:T(8,128)(2,1)S(1)}, bf16[256,1024]{1,0:T(8,128)(2,1)S(1)}, u32[]{:S(2)}, u32[]{:S(2)}) %collective-permute-start.9) | collective-permute-done | bytes 524320 | tf_op jit(solution)/shard_map/ppermute | solution.py:33
  41.2 3.1 %collective-permute-start.11 = (bf16[256,1024]{1,0:T(8,128)(2,1)S(1)}, bf16[256,1024]{1,0:T(8,128)(2,1)S(1)}, u32[]{:S(2)}, u32[]{:S(2)}) collective-permute-start(bf16[256,1024]{1,0:T(8,128)(2,1)S(1)} %collective-permute-done.9.refs_1_), channel_id=1, source_target_pairs={{0,1},{1,2},{2,3},{3,4},{4,5},{5,6},{6,7},{7,0},{8,9},{9,10},{10,1... | collective-permute-start | bytes 1572872 | tf_op jit(solution)/shard_map/ppermute | solution.py:33
  44.7 1.9 %collective-permute-done.10.refs_2_ = bf16[256,1024]{1,0:T(8,128)(2,1)S(1)} collective-permute-done((bf16[256,1024]{1,0:T(8,128)(2,1)S(1)}, bf16[256,1024]{1,0:T(8,128)(2,1)S(1)}, u32[]{:S(2)}, u32[]{:S(2)}) %collective-permute-start.10) | collective-permute-done | bytes 524320 | tf_op jit(solution)/shard_map/ppermute | solution.py:33
  46.6 8.2 %collective-permute-done.11.refs_3_ = bf16[256,1024]{1,0:T(8,128)(2,1)S(1)} collective-permute-done((bf16[256,1024]{1,0:T(8,128)(2,1)S(1)}, bf16[256,1024]{1,0:T(8,128)(2,1)S(1)}, u32[]{:S(2)}, u32[]{:S(2)}) %collective-permute-start.11) | collective-permute-done | bytes 524320 | tf_op jit(solution)/shard_map/ppermute | solution.py:33
  54.8 2.5 %collective-permute-done.14.refs_7_ = bf16[256,1024]{1,0:T(8,128)(2,1)S(1)} collective-permute-done((bf16[256,1024]{1,0:T(8,128)(2,1)S(1)}, bf16[256,1024]{1,0:T(8,128)(2,1)S(1)}, u32[]{:S(2)}, u32[]{:S(2)}) %collective-permute-start.14) | collective-permute-done | bytes 524320 | tf_op jit(solution)/shard_map/ppermute | solution.py:33
  57.3 5.2 %chain.2 = (bf16[128,1024]{1,0:T(8,128)(2,1)S(1)}, bf16[1024,1024]{1,0:T(8,128)(2,1)S(1)}, bf16[1024,1024]{1,0:T(8,128)(2,1)S(1)}) custom-call(s32[4]{0:T(128)S(1)} %pad_add_fusion.where, f32[2,32,1024]{2,1,0:T(8,128)S(1)} %get-tuple-element.20.keep, f32[2,32,1024]{2,1,0:T(8,128)S(1)} %collective-permute-done.other, ...), custom_call_target="tpu_custom_call" | custom-call | tf_op jit(solution)/shard_map/chain/pallas_call | solution.py:149
  62.5 2.0 %collective-permute-start.15 = (bf16[128,1024]{1,0:T(8,128)(2,1)S(1)}, bf16[128,1024]{1,0:T(8,128)(2,1)S(1)}, u32[]{:S(2)}, u32[]{:S(2)}) collective-permute-start(bf16[128,1024]{1,0:T(8,128)(2,1)S(1)} %get-tuple-element.24), channel_id=1, source_target_pairs={{32,0},{33,1},{34,2},{35,3},{36,4},{37,5},{38,6},{39,7},{40,8},{41... | collective-permute-start | bytes 786440 | tf_op jit(solution)/shard_map/ppermute | solution.py:33
  67.4 2.1 %collective-permute-done.16 = bf16[2,32,1024]{2,1,0:T(8,128)(2,1)S(1)} collective-permute-done((bf16[2,32,1024]{2,1,0:T(8,128)(2,1)S(1)}, bf16[2,32,1024]{2,1,0:T(8,128)(2,1)S(1)}, u32[]{:S(2)}, u32[]{:S(2)}) %collective-permute-start.16) | collective-permute-done | bytes 131104 | tf_op jit(solution)/shard_map/ppermute | solution.py:33
  70.8 3.7 %collective-permute-done.17 = bf16[2,32,1024]{2,1,0:T(8,128)(2,1)S(1)} collective-permute-done((bf16[2,32,1024]{2,1,0:T(8,128)(2,1)S(1)}, bf16[2,32,1024]{2,1,0:T(8,128)(2,1)S(1)}, u32[]{:S(2)}, u32[]{:S(2)}) %collective-permute-start.17) | collective-permute-done | bytes 131104 | tf_op jit(solution)/shard_map/ppermute | solution.py:33
  74.7 4.4 %collective-permute-start.18 = (bf16[32,1024]{1,0:T(8,128)(2,1)S(1)}, bf16[32,1024]{1,0:T(8,128)(2,1)S(1)}, u32[]{:S(2)}, u32[]{:S(2)}) collective-permute-start(bf16[32,1024]{1,0:T(8,128)(2,1)S(1)} %get-tuple-element.48), channel_id=1, source_target_pairs={{0,4},{1,5},{2,6},{3,7},{4,0},{5,1},{6,2},{7,3},{8,12},{9,13},{10,... | collective-permute-start | bytes 196616 | tf_op jit(solution)/shard_map/ppermute | solution.py:33
  86.3 3.4 %collective-permute-start.23 = (bf16[64,1024]{1,0:T(8,128)(2,1)S(1)}, bf16[64,1024]{1,0:T(8,128)(2,1)S(1)}, u32[]{:S(2)}, u32[]{:S(2)}) collective-permute-start(bf16[64,1024]{1,0:T(8,128)(2,1)S(1)} %pad_maximum_fusion.3), channel_id=1, source_target_pairs={{0,1},{1,2},{2,3},{3,4},{4,5},{5,6},{6,7},{7,0},{8,9},{9,10},{10,1... | collective-permute-start | bytes 393224 | tf_op jit(solution)/shard_map/ppermute | solution.py:33
  89.7 1.9 %collective-permute-done.23 = bf16[64,1024]{1,0:T(8,128)(2,1)S(1)} collective-permute-done((bf16[64,1024]{1,0:T(8,128)(2,1)S(1)}, bf16[64,1024]{1,0:T(8,128)(2,1)S(1)}, u32[]{:S(2)}, u32[]{:S(2)}) %collective-permute-start.23) | collective-permute-done | bytes 131104 | tf_op jit(solution)/shard_map/ppermute | solution.py:33
  91.6 3.4 %collective-permute-start.25 = (bf16[64,1024]{1,0:T(8,128)(2,1)S(1)}, bf16[64,1024]{1,0:T(8,128)(2,1)S(1)}, u32[]{:S(2)}, u32[]{:S(2)}) collective-permute-start(bf16[64,1024]{1,0:T(8,128)(2,1)S(1)} %collective-permute-done.23), channel_id=1, source_target_pairs={{0,1},{1,2},{2,3},{3,4},{4,5},{5,6},{6,7},{7,0},{8,9},{9,10},{10,1... | collective-permute-start | bytes 393224 | tf_op jit(solution)/shard_map/ppermute | solution.py:33
  95.2 2.5 %collective-permute-done.25 = bf16[64,1024]{1,0:T(8,128)(2,1)S(1)} collective-permute-done((bf16[64,1024]{1,0:T(8,128)(2,1)S(1)}, bf16[64,1024]{1,0:T(8,128)(2,1)S(1)}, u32[]{:S(2)}, u32[]{:S(2)}) %collective-permute-start.25) | collective-permute-done | bytes 131104 | tf_op jit(solution)/shard_map/ppermute | solution.py:33
  97.7 2.5 %collective-permute-start.26 = (bf16[256,1024]{1,0:T(8,128)(2,1)S(1)}, bf16[256,1024]{1,0:T(8,128)(2,1)S(1)}, u32[]{:S(2)}, u32[]{:S(2)}) collective-permute-start(bf16[256,1024]{1,0:T(8,128)(2,1)S(1)} %constant_dynamic-update-slice_fusion.10.refs_0_), channel_id=1, source_target_pairs={{0,1},{1,2},{2,3},{3,4},{4,5},{5,6},{6,7},{7,0},{8,9},{9,10},{10,1... | collective-permute-start | bytes 1572872 | tf_op jit(solution)/shard_map/ppermute | solution.py:33
  101.6 4.7 %collective-permute-done.26.refs_1_ = bf16[256,1024]{1,0:T(8,128)(2,1)S(1)} collective-permute-done((bf16[256,1024]{1,0:T(8,128)(2,1)S(1)}, bf16[256,1024]{1,0:T(8,128)(2,1)S(1)}, u32[]{:S(2)}, u32[]{:S(2)}) %collective-permute-start.26) | collective-permute-done | bytes 524320 | tf_op jit(solution)/shard_map/ppermute | solution.py:33
  106.3 3.1 %collective-permute-start.28 = (bf16[256,1024]{1,0:T(8,128)(2,1)S(1)}, bf16[256,1024]{1,0:T(8,128)(2,1)S(1)}, u32[]{:S(2)}, u32[]{:S(2)}) collective-permute-start(bf16[256,1024]{1,0:T(8,128)(2,1)S(1)} %collective-permute-done.26.refs_1_), channel_id=1, source_target_pairs={{0,1},{1,2},{2,3},{3,4},{4,5},{5,6},{6,7},{7,0},{8,9},{9,10},{10,1... | collective-permute-start | bytes 1572872 | tf_op jit(solution)/shard_map/ppermute | solution.py:33
  111.4 8.5 %collective-permute-done.28.refs_3_ = bf16[256,1024]{1,0:T(8,128)(2,1)S(1)} collective-permute-done((bf16[256,1024]{1,0:T(8,128)(2,1)S(1)}, bf16[256,1024]{1,0:T(8,128)(2,1)S(1)}, u32[]{:S(2)}, u32[]{:S(2)}) %collective-permute-start.28) | collective-permute-done | bytes 524320 | tf_op jit(solution)/shard_map/ppermute | solution.py:33
  119.9 2.5 %collective-permute-done.31.refs_7_ = bf16[256,1024]{1,0:T(8,128)(2,1)S(1)} collective-permute-done((bf16[256,1024]{1,0:T(8,128)(2,1)S(1)}, bf16[256,1024]{1,0:T(8,128)(2,1)S(1)}, u32[]{:S(2)}, u32[]{:S(2)}) %collective-permute-start.31) | collective-permute-done | bytes 524320 | tf_op jit(solution)/shard_map/ppermute | solution.py:33
  122.4 5.0 %chain.3 = (bf16[128,1024]{1,0:T(8,128)(2,1)S(1)}, bf16[1024,1024]{1,0:T(8,128)(2,1)S(1)}, bf16[1024,1024]{1,0:T(8,128)(2,1)S(1)}) custom-call(s32[4]{0:T(128)S(1)} %pad_add_fusion.where, f32[2,32,1024]{2,1,0:T(8,128)S(1)} %get-tuple-element.36.keep, f32[2,32,1024]{2,1,0:T(8,128)S(1)} %get-tuple-element.35.other, ...), custom_call_target="tpu_custom_call" | custom-call | tf_op jit(solution)/shard_map/chain/pallas_call | solution.py:149
  127.4 2.0 %collective-permute-start.32 = (bf16[128,1024]{1,0:T(8,128)(2,1)S(1)}, bf16[128,1024]{1,0:T(8,128)(2,1)S(1)}, u32[]{:S(2)}, u32[]{:S(2)}) collective-permute-start(bf16[128,1024]{1,0:T(8,128)(2,1)S(1)} %get-tuple-element.32), channel_id=1, source_target_pairs={{32,0},{33,1},{34,2},{35,3},{36,4},{37,5},{38,6},{39,7},{40,8},{41... | collective-permute-start | bytes 786440 | tf_op jit(solution)/shard_map/ppermute | solution.py:33
  132.4 2.6 %collective-permute-done.33 = f32[4,32,1024]{2,1,0:T(8,128)S(1)} collective-permute-done((f32[4,32,1024]{2,1,0:T(8,128)S(1)}, f32[4,32,1024]{2,1,0:T(8,128)S(1)}, u32[]{:S(2)}, u32[]{:S(2)}) %collective-permute-start.33) | collective-permute-done | bytes 524320 | tf_op jit(solution)/shard_map/ppermute | solution.py:33
  (76 shorter events, 26.1 us)
Async XLA Ops:
  2.6 4.5 %collective-permute-start = (f32[2,32,1024]{2,1,0:T(8,128)S(1)}, f32[2,32,1024]{2,1,0:T(8,128)S(1)}, u32[]{:S(2)}, u32[]{:S(2)}) collective-permute-start(f32[2,32,1024]{2,1,0:T(8,128)S(1)} %get-tuple-element.21), channel_id=1, source_target_pairs={{0,32},{1,33},{2,34},{3,35},{4,36},{5,37},{6,38},{7,39},{8,40},{9,... | collective-permute-start | bytes 786440 | tf_op jit(solution)/shard_map/ppermute | solution.py:33
  7.2 7.2 %collective-permute-start.1 = (bf16[32,1024]{1,0:T(8,128)(2,1)S(1)}, bf16[32,1024]{1,0:T(8,128)(2,1)S(1)}, u32[]{:S(2)}, u32[]{:S(2)}) collective-permute-start(bf16[32,1024]{1,0:T(8,128)(2,1)S(1)} %get-tuple-element.52), channel_id=1, source_target_pairs={{0,4},{1,5},{2,6},{3,7},{4,0},{5,1},{6,2},{7,3},{8,12},{9,13},{10,... | collective-permute-start | bytes 196616 | tf_op jit(solution)/shard_map/ppermute | solution.py:33
  12.4 7.9 %collective-permute-start.5 = (bf16[32,1024]{1,0:T(8,128)(2,1)S(1)}, bf16[32,1024]{1,0:T(8,128)(2,1)S(1)}, u32[]{:S(2)}, u32[]{:S(2)}) collective-permute-start(bf16[32,1024]{1,0:T(8,128)(2,1)S(1)} %get-tuple-element.49), channel_id=1, source_target_pairs={{0,4},{1,5},{2,6},{3,7},{4,0},{5,1},{6,2},{7,3},{8,12},{9,13},{10,... | collective-permute-start | bytes 196616 | tf_op jit(solution)/shard_map/ppermute | solution.py:33
  14.4 15.7 %collective-permute-start.4 = (bf16[64,1024]{1,0:T(8,128)(2,1)S(1)}, bf16[64,1024]{1,0:T(8,128)(2,1)S(1)}, u32[]{:S(2)}, u32[]{:S(2)}) collective-permute-start(bf16[64,1024]{1,0:T(8,128)(2,1)S(1)} %pad_maximum_fusion), channel_id=1, source_target_pairs={{0,16},{1,17},{2,18},{3,19},{4,20},{5,21},{6,22},{7,23},{8,24},{9,... | collective-permute-start | bytes 393224 | tf_op jit(solution)/shard_map/ppermute | solution.py:33
  17.6 12.4 %collective-permute-start.3 = (bf16[64,1024]{1,0:T(8,128)(2,1)S(1)}, bf16[64,1024]{1,0:T(8,128)(2,1)S(1)}, u32[]{:S(2)}, u32[]{:S(2)}) collective-permute-start(bf16[64,1024]{1,0:T(8,128)(2,1)S(1)} %pad_maximum_fusion), channel_id=1, source_target_pairs={{0,24},{1,25},{2,26},{3,27},{4,28},{5,29},{6,30},{7,31},{8,0},{9,1... | collective-permute-start | bytes 393224 | tf_op jit(solution)/shard_map/ppermute | solution.py:33
  18.0 12.0 %collective-permute-start.2 = (bf16[64,1024]{1,0:T(8,128)(2,1)S(1)}, bf16[64,1024]{1,0:T(8,128)(2,1)S(1)}, u32[]{:S(2)}, u32[]{:S(2)}) collective-permute-start(bf16[64,1024]{1,0:T(8,128)(2,1)S(1)} %pad_maximum_fusion), channel_id=1, source_target_pairs={{0,8},{1,9},{2,10},{3,11},{4,12},{5,13},{6,14},{7,15},{8,16},{9,17... | collective-permute-start | bytes 393224 | tf_op jit(solution)/shard_map/ppermute | solution.py:33
  20.3 9.7 %collective-permute-start.7 = (bf16[64,1024]{1,0:T(8,128)(2,1)S(1)}, bf16[64,1024]{1,0:T(8,128)(2,1)S(1)}, u32[]{:S(2)}, u32[]{:S(2)}) collective-permute-start(bf16[64,1024]{1,0:T(8,128)(2,1)S(1)} %pad_maximum_fusion.1), channel_id=1, source_target_pairs={{0,7},{1,0},{2,1},{3,2},{4,3},{5,4},{6,5},{7,6},{8,15},{9,8},{10,9... | collective-permute-start | bytes 393224 | tf_op jit(solution)/shard_map/ppermute | solution.py:33
  21.1 5.4 %collective-permute-start.6 = (bf16[64,1024]{1,0:T(8,128)(2,1)S(1)}, bf16[64,1024]{1,0:T(8,128)(2,1)S(1)}, u32[]{:S(2)}, u32[]{:S(2)}) collective-permute-start(bf16[64,1024]{1,0:T(8,128)(2,1)S(1)} %pad_maximum_fusion.1), channel_id=1, source_target_pairs={{0,1},{1,2},{2,3},{3,4},{4,5},{5,6},{6,7},{7,0},{8,9},{9,10},{10,1... | collective-permute-start | bytes 393224 | tf_op jit(solution)/shard_map/ppermute | solution.py:33
  26.6 5.3 %collective-permute-start.8 = (bf16[64,1024]{1,0:T(8,128)(2,1)S(1)}, bf16[64,1024]{1,0:T(8,128)(2,1)S(1)}, u32[]{:S(2)}, u32[]{:S(2)}) collective-permute-start(bf16[64,1024]{1,0:T(8,128)(2,1)S(1)} %collective-permute-done.6), channel_id=1, source_target_pairs={{0,1},{1,2},{2,3},{3,4},{4,5},{5,6},{6,7},{7,0},{8,9},{9,10},{10,1... | collective-permute-start | bytes 393224 | tf_op jit(solution)/shard_map/ppermute | solution.py:33
  31.9 9.3 %collective-permute-start.9 = (bf16[256,1024]{1,0:T(8,128)(2,1)S(1)}, bf16[256,1024]{1,0:T(8,128)(2,1)S(1)}, u32[]{:S(2)}, u32[]{:S(2)}) collective-permute-start(bf16[256,1024]{1,0:T(8,128)(2,1)S(1)} %constant_dynamic-update-slice_fusion.refs_0_), channel_id=1, source_target_pairs={{0,1},{1,2},{2,3},{3,4},{4,5},{5,6},{6,7},{7,0},{8,9},{9,10},{10,1... | collective-permute-start | bytes 1572872 | tf_op jit(solution)/shard_map/ppermute | solution.py:33
  35.1 9.2 %collective-permute-start.12 = (bf16[256,1024]{1,0:T(8,128)(2,1)S(1)}, bf16[256,1024]{1,0:T(8,128)(2,1)S(1)}, u32[]{:S(2)}, u32[]{:S(2)}) collective-permute-start(bf16[256,1024]{1,0:T(8,128)(2,1)S(1)} %constant_dynamic-update-slice_fusion.5.refs_4_), channel_id=1, source_target_pairs={{0,8},{1,9},{2,10},{3,11},{4,12},{5,13},{6,14},{7,15},{8,16},{9,17... | collective-permute-start | bytes 1572872 | tf_op jit(solution)/shard_map/ppermute | solution.py:33
  35.5 11.1 %collective-permute-start.10 = (bf16[256,1024]{1,0:T(8,128)(2,1)S(1)}, bf16[256,1024]{1,0:T(8,128)(2,1)S(1)}, u32[]{:S(2)}, u32[]{:S(2)}) collective-permute-start(bf16[256,1024]{1,0:T(8,128)(2,1)S(1)} %constant_dynamic-update-slice_fusion.refs_0_), channel_id=1, source_target_pairs={{0,7},{1,0},{2,1},{3,2},{4,3},{5,4},{6,5},{7,6},{8,15},{9,8},{10,9... | collective-permute-start | bytes 1572872 | tf_op jit(solution)/shard_map/ppermute | solution.py:33
  35.5 11.1 %collective-permute-start.13 = (bf16[256,1024]{1,0:T(8,128)(2,1)S(1)}, bf16[256,1024]{1,0:T(8,128)(2,1)S(1)}, u32[]{:S(2)}, u32[]{:S(2)}) collective-permute-start(bf16[256,1024]{1,0:T(8,128)(2,1)S(1)} %constant_dynamic-update-slice_fusion.5.refs_4_), channel_id=1, source_target_pairs={{0,24},{1,25},{2,26},{3,27},{4,28},{5,29},{6,30},{7,31},{8,0},{9,1... | collective-permute-start | bytes 1572872 | tf_op jit(solution)/shard_map/ppermute | solution.py:33
  41.2 13.6 %collective-permute-start.11 = (bf16[256,1024]{1,0:T(8,128)(2,1)S(1)}, bf16[256,1024]{1,0:T(8,128)(2,1)S(1)}, u32[]{:S(2)}, u32[]{:S(2)}) collective-permute-start(bf16[256,1024]{1,0:T(8,128)(2,1)S(1)} %collective-permute-done.9.refs_1_), channel_id=1, source_target_pairs={{0,1},{1,2},{2,3},{3,4},{4,5},{5,6},{6,7},{7,0},{8,9},{9,10},{10,1... | collective-permute-start | bytes 1572872 | tf_op jit(solution)/shard_map/ppermute | solution.py:33
  44.3 13.0 %collective-permute-start.14 = (bf16[256,1024]{1,0:T(8,128)(2,1)S(1)}, bf16[256,1024]{1,0:T(8,128)(2,1)S(1)}, u32[]{:S(2)}, u32[]{:S(2)}) collective-permute-start(bf16[256,1024]{1,0:T(8,128)(2,1)S(1)} %collective-permute-done.12.refs_5_), channel_id=1, source_target_pairs={{0,8},{1,9},{2,10},{3,11},{4,12},{5,13},{6,14},{7,15},{8,16},{9,17... | collective-permute-start | bytes 1572872 | tf_op jit(solution)/shard_map/ppermute | solution.py:33
  66.1 3.4 %collective-permute-start.16 = (bf16[2,32,1024]{2,1,0:T(8,128)(2,1)S(1)}, bf16[2,32,1024]{2,1,0:T(8,128)(2,1)S(1)}, u32[]{:S(2)}, u32[]{:S(2)}) collective-permute-start(bf16[2,32,1024]{2,1,0:T(8,128)(2,1)S(1)} %get-tuple-element.28), channel_id=1, source_target_pairs={{0,32},{1,33},{2,34},{3,35},{4,36},{5,37},{6,38},{7,39},{8,40},{9,... | collective-permute-start | bytes 393224 | tf_op jit(solution)/shard_map/ppermute | solution.py:33
  69.5 5.0 %collective-permute-start.17 = (bf16[2,32,1024]{2,1,0:T(8,128)(2,1)S(1)}, bf16[2,32,1024]{2,1,0:T(8,128)(2,1)S(1)}, u32[]{:S(2)}, u32[]{:S(2)}) collective-permute-start(bf16[2,32,1024]{2,1,0:T(8,128)(2,1)S(1)} %broadcast_select_fusion), channel_id=1, source_target_pairs={{0,64},{1,65},{2,66},{3,67},{4,68},{5,69},{6,70},{7,71},{8,72},{9,... | collective-permute-start | bytes 393224 | tf_op jit(solution)/shard_map/ppermute | solution.py:33
  74.7 7.1 %collective-permute-start.18 = (bf16[32,1024]{1,0:T(8,128)(2,1)S(1)}, bf16[32,1024]{1,0:T(8,128)(2,1)S(1)}, u32[]{:S(2)}, u32[]{:S(2)}) collective-permute-start(bf16[32,1024]{1,0:T(8,128)(2,1)S(1)} %get-tuple-element.48), channel_id=1, source_target_pairs={{0,4},{1,5},{2,6},{3,7},{4,0},{5,1},{6,2},{7,3},{8,12},{9,13},{10,... | collective-permute-start | bytes 196616 | tf_op jit(solution)/shard_map/ppermute | solution.py:33
  79.1 7.0 %collective-permute-start.22 = (bf16[32,1024]{1,0:T(8,128)(2,1)S(1)}, bf16[32,1024]{1,0:T(8,128)(2,1)S(1)}, u32[]{:S(2)}, u32[]{:S(2)}) collective-permute-start(bf16[32,1024]{1,0:T(8,128)(2,1)S(1)} %get-tuple-element.45), channel_id=1, source_target_pairs={{0,4},{1,5},{2,6},{3,7},{4,0},{5,1},{6,2},{7,3},{8,12},{9,13},{10,... | collective-permute-start | bytes 196616 | tf_op jit(solution)/shard_map/ppermute | solution.py:33
  81.9 13.2 %collective-permute-start.21 = (bf16[64,1024]{1,0:T(8,128)(2,1)S(1)}, bf16[64,1024]{1,0:T(8,128)(2,1)S(1)}, u32[]{:S(2)}, u32[]{:S(2)}) collective-permute-start(bf16[64,1024]{1,0:T(8,128)(2,1)S(1)} %pad_maximum_fusion.2), channel_id=1, source_target_pairs={{0,16},{1,17},{2,18},{3,19},{4,20},{5,21},{6,22},{7,23},{8,24},{9,... | collective-permute-start | bytes 393224 | tf_op jit(solution)/shard_map/ppermute | solution.py:33
  83.1 12.0 %collective-permute-start.20 = (bf16[64,1024]{1,0:T(8,128)(2,1)S(1)}, bf16[64,1024]{1,0:T(8,128)(2,1)S(1)}, u32[]{:S(2)}, u32[]{:S(2)}) collective-permute-start(bf16[64,1024]{1,0:T(8,128)(2,1)S(1)} %pad_maximum_fusion.2), channel_id=1, source_target_pairs={{0,24},{1,25},{2,26},{3,27},{4,28},{5,29},{6,30},{7,31},{8,0},{9,1... | collective-permute-start | bytes 393224 | tf_op jit(solution)/shard_map/ppermute | solution.py:33
  84.3 10.7 %collective-permute-start.19 = (bf16[64,1024]{1,0:T(8,128)(2,1)S(1)}, bf16[64,1024]{1,0:T(8,128)(2,1)S(1)}, u32[]{:S(2)}, u32[]{:S(2)}) collective-permute-start(bf16[64,1024]{1,0:T(8,128)(2,1)S(1)} %pad_maximum_fusion.2), channel_id=1, source_target_pairs={{0,8},{1,9},{2,10},{3,11},{4,12},{5,13},{6,14},{7,15},{8,16},{9,17... | collective-permute-start | bytes 393224 | tf_op jit(solution)/shard_map/ppermute | solution.py:33
  86.2 9.0 %collective-permute-start.24 = (bf16[64,1024]{1,0:T(8,128)(2,1)S(1)}, bf16[64,1024]{1,0:T(8,128)(2,1)S(1)}, u32[]{:S(2)}, u32[]{:S(2)}) collective-permute-start(bf16[64,1024]{1,0:T(8,128)(2,1)S(1)} %pad_maximum_fusion.3), channel_id=1, source_target_pairs={{0,7},{1,0},{2,1},{3,2},{4,3},{5,4},{6,5},{7,6},{8,15},{9,8},{10,9... | collective-permute-start | bytes 393224 | tf_op jit(solution)/shard_map/ppermute | solution.py:33
  86.3 5.4 %collective-permute-start.23 = (bf16[64,1024]{1,0:T(8,128)(2,1)S(1)}, bf16[64,1024]{1,0:T(8,128)(2,1)S(1)}, u32[]{:S(2)}, u32[]{:S(2)}) collective-permute-start(bf16[64,1024]{1,0:T(8,128)(2,1)S(1)} %pad_maximum_fusion.3), channel_id=1, source_target_pairs={{0,1},{1,2},{2,3},{3,4},{4,5},{5,6},{6,7},{7,0},{8,9},{9,10},{10,1... | collective-permute-start | bytes 393224 | tf_op jit(solution)/shard_map/ppermute | solution.py:33
  91.6 6.0 %collective-permute-start.25 = (bf16[64,1024]{1,0:T(8,128)(2,1)S(1)}, bf16[64,1024]{1,0:T(8,128)(2,1)S(1)}, u32[]{:S(2)}, u32[]{:S(2)}) collective-permute-start(bf16[64,1024]{1,0:T(8,128)(2,1)S(1)} %collective-permute-done.23), channel_id=1, source_target_pairs={{0,1},{1,2},{2,3},{3,4},{4,5},{5,6},{6,7},{7,0},{8,9},{9,10},{10,1... | collective-permute-start | bytes 393224 | tf_op jit(solution)/shard_map/ppermute | solution.py:33
  97.7 8.6 %collective-permute-start.26 = (bf16[256,1024]{1,0:T(8,128)(2,1)S(1)}, bf16[256,1024]{1,0:T(8,128)(2,1)S(1)}, u32[]{:S(2)}, u32[]{:S(2)}) collective-permute-start(bf16[256,1024]{1,0:T(8,128)(2,1)S(1)} %constant_dynamic-update-slice_fusion.10.refs_0_), channel_id=1, source_target_pairs={{0,1},{1,2},{2,3},{3,4},{4,5},{5,6},{6,7},{7,0},{8,9},{9,10},{10,1... | collective-permute-start | bytes 1572872 | tf_op jit(solution)/shard_map/ppermute | solution.py:33
  100.1 9.2 %collective-permute-start.29 = (bf16[256,1024]{1,0:T(8,128)(2,1)S(1)}, bf16[256,1024]{1,0:T(8,128)(2,1)S(1)}, u32[]{:S(2)}, u32[]{:S(2)}) collective-permute-start(bf16[256,1024]{1,0:T(8,128)(2,1)S(1)} %constant_dynamic-update-slice_fusion.15.refs_4_), channel_id=1, source_target_pairs={{0,8},{1,9},{2,10},{3,11},{4,12},{5,13},{6,14},{7,15},{8,16},{9,17... | collective-permute-start | bytes 1572872 | tf_op jit(solution)/shard_map/ppermute | solution.py:33
  100.2 10.6 %collective-permute-start.27 = (bf16[256,1024]{1,0:T(8,128)(2,1)S(1)}, bf16[256,1024]{1,0:T(8,128)(2,1)S(1)}, u32[]{:S(2)}, u32[]{:S(2)}) collective-permute-start(bf16[256,1024]{1,0:T(8,128)(2,1)S(1)} %constant_dynamic-update-slice_fusion.10.refs_0_), channel_id=1, source_target_pairs={{0,7},{1,0},{2,1},{3,2},{4,3},{5,4},{6,5},{7,6},{8,15},{9,8},{10,9... | collective-permute-start | bytes 1572872 | tf_op jit(solution)/shard_map/ppermute | solution.py:33
  100.6 10.8 %collective-permute-start.30 = (bf16[256,1024]{1,0:T(8,128)(2,1)S(1)}, bf16[256,1024]{1,0:T(8,128)(2,1)S(1)}, u32[]{:S(2)}, u32[]{:S(2)}) collective-permute-start(bf16[256,1024]{1,0:T(8,128)(2,1)S(1)} %constant_dynamic-update-slice_fusion.15.refs_4_), channel_id=1, source_target_pairs={{0,24},{1,25},{2,26},{3,27},{4,28},{5,29},{6,30},{7,31},{8,0},{9,1... | collective-permute-start | bytes 1572872 | tf_op jit(solution)/shard_map/ppermute | solution.py:33
  106.3 13.6 %collective-permute-start.28 = (bf16[256,1024]{1,0:T(8,128)(2,1)S(1)}, bf16[256,1024]{1,0:T(8,128)(2,1)S(1)}, u32[]{:S(2)}, u32[]{:S(2)}) collective-permute-start(bf16[256,1024]{1,0:T(8,128)(2,1)S(1)} %collective-permute-done.26.refs_1_), channel_id=1, source_target_pairs={{0,1},{1,2},{2,3},{3,4},{4,5},{5,6},{6,7},{7,0},{8,9},{9,10},{10,1... | collective-permute-start | bytes 1572872 | tf_op jit(solution)/shard_map/ppermute | solution.py:33
  109.4 13.0 %collective-permute-start.31 = (bf16[256,1024]{1,0:T(8,128)(2,1)S(1)}, bf16[256,1024]{1,0:T(8,128)(2,1)S(1)}, u32[]{:S(2)}, u32[]{:S(2)}) collective-permute-start(bf16[256,1024]{1,0:T(8,128)(2,1)S(1)} %collective-permute-done.29.refs_5_), channel_id=1, source_target_pairs={{0,8},{1,9},{2,10},{3,11},{4,12},{5,13},{6,14},{7,15},{8,16},{9,17... | collective-permute-start | bytes 1572872 | tf_op jit(solution)/shard_map/ppermute | solution.py:33
  131.1 3.9 %collective-permute-start.33 = (f32[4,32,1024]{2,1,0:T(8,128)S(1)}, f32[4,32,1024]{2,1,0:T(8,128)S(1)}, u32[]{:S(2)}, u32[]{:S(2)}) collective-permute-start(f32[4,32,1024]{2,1,0:T(8,128)S(1)} %finish.3), channel_id=1, source_target_pairs={{0,32},{1,33},{2,34},{3,35},{4,36},{5,37},{6,38},{7,39},{8,40},{9,... | collective-permute-start | bytes 1572872 | tf_op jit(solution)/shard_map/ppermute | solution.py:33
  (4 other events, 8.0 us)

commit v11 on v10

--- a/solution.py
+++ b/solution.py
@@ -47,7 +47,8 @@
     wide_b = jnp.concatenate([wide_b, send(wide_b, hop("z", NZ // 2))])
     ahead, behind = send(wide_a, hop("y", 1)), send(wide_a, hop("y", -1))
     wide_a = jnp.concatenate([wide_a, ahead, behind, send(wide_a, hop("y", 2))])
-    ahead, behind = send(wide_b, hop("z", 1)), send(wide_b, hop("z", -1))
+    ahead, wide_b = lax.optimization_barrier((send(wide_b, hop("z", 1)), wide_b))
+    behind = send(wide_b, hop("z", -1))
     wide_b = jnp.concatenate([wide_b, ahead, behind, send(ahead, hop("z", 1))])
     wide_a, wide_b = lax.optimization_barrier((wide_a, wide_b))
     parts = []

time: 137 us -> 133 us (0.971)
  waiting for transfers between devices: 58.5 us -> 56.8 us
  starting transfers between devices: 61.8 us -> 60.4 us
    ppermute x34, waiting for transfers between devices: 58.5 us -> 56.8 us  [send(): return lax.ppermute(block, AXES, route(move))]
    ppermute x34, starting transfers between devices: 61.8 us -> 60.4 us  [send(): return lax.ppermute(block, AXES, route(move))]
  transfers between devices with their start and end apart: 34 -> 34, of which waited for: 22 -> 20; matrix products, arithmetic and copies ran while one was open for 0% -> 0% of each run, Pallas kernels for 0% -> 0%
where the time goes in v11:
time: 133 us
  starting transfers between devices  60.4 us (45%)
  waiting for transfers between devices  56.8 us (43%)
  Pallas kernels  12 us (9%)
  local copies, waits for them, and re-layouts  1.96 us (1%)
    ppermute x34, starting transfers between devices, send(): return lax.ppermute(block, AXES, route(move))  60.4 us
    ppermute x34, waiting for transfers between devices, send(): return lax.ppermute(block, AXES, route(move))  56.8 us
    pallas_call x2, Pallas kernels, chain(): pl.pallas_call(chain_kernel, out_shape=[jax.ShapeDtypeStruct((128, M), jn...  10.2 us
  transfers between devices with their start and end apart: 34, of which 20 were waited for; matrix products, arithmetic and copies ran while one was open for 0% of the time, Pallas kernels for 0%

profile of v11, /device:TPU:1, one launch (start us, length us, event | category | flops | bytes accessed | tf_op | source)
XLA Modules:
  0.0 132.6 jit_solution(10796604913761683412)
XLA Ops:
  2.6 3.3 %collective-permute-start = (f32[2,32,1024]{2,1,0:T(8,128)S(1)}, f32[2,32,1024]{2,1,0:T(8,128)S(1)}, u32[]{:S(2)}, u32[]{:S(2)}) collective-permute-start(f32[2,32,1024]{2,1,0:T(8,128)S(1)} %get-tuple-element.25), channel_id=1, source_target_pairs={{0,32},{1,33},{2,34},{3,35},{4,36},{5,37},{6,38},{7,39},{8,40},{9,... | collective-permute-start | bytes 786440 | tf_op jit(solution)/shard_map/ppermute | solution.py:33
  7.2 5.3 %collective-permute-start.5 = (bf16[32,1024]{1,0:T(8,128)(2,1)S(1)}, bf16[32,1024]{1,0:T(8,128)(2,1)S(1)}, u32[]{:S(2)}, u32[]{:S(2)}) collective-permute-start(bf16[32,1024]{1,0:T(8,128)(2,1)S(1)} %get-tuple-element.56), channel_id=1, source_target_pairs={{0,4},{1,5},{2,6},{3,7},{4,0},{5,1},{6,2},{7,3},{8,12},{9,13},{10,... | collective-permute-start | bytes 196616 | tf_op jit(solution)/shard_map/ppermute | solution.py:33
  12.6 1.7 %collective-permute-done.5 = bf16[32,1024]{1,0:T(8,128)(2,1)S(1)} collective-permute-done((bf16[32,1024]{1,0:T(8,128)(2,1)S(1)}, bf16[32,1024]{1,0:T(8,128)(2,1)S(1)}, u32[]{:S(2)}, u32[]{:S(2)}) %collective-permute-start.5) | collective-permute-done | bytes 65568 | tf_op jit(solution)/shard_map/ppermute | solution.py:33
  14.4 4.5 %collective-permute-start.6 = (bf16[64,1024]{1,0:T(8,128)(2,1)S(1)}, bf16[64,1024]{1,0:T(8,128)(2,1)S(1)}, u32[]{:S(2)}, u32[]{:S(2)}) collective-permute-start(bf16[64,1024]{1,0:T(8,128)(2,1)S(1)} %pad_maximum_fusion.3), channel_id=1, source_target_pairs={{0,1},{1,2},{2,3},{3,4},{4,5},{5,6},{6,7},{7,0},{8,9},{9,10},{10,1... | collective-permute-start | bytes 393224 | tf_op jit(solution)/shard_map/ppermute | solution.py:33
  19.5 2.8 %collective-permute-start.2 = (bf16[64,1024]{1,0:T(8,128)(2,1)S(1)}, bf16[64,1024]{1,0:T(8,128)(2,1)S(1)}, u32[]{:S(2)}, u32[]{:S(2)}) collective-permute-start(bf16[64,1024]{1,0:T(8,128)(2,1)S(1)} %pad_maximum_fusion.2), channel_id=1, source_target_pairs={{0,8},{1,9},{2,10},{3,11},{4,12},{5,13},{6,14},{7,15},{8,16},{9,17... | collective-permute-start | bytes 393224 | tf_op jit(solution)/shard_map/ppermute | solution.py:33
  24.3 1.8 %collective-permute-start.8 = (bf16[64,1024]{1,0:T(8,128)(2,1)S(1)}, bf16[64,1024]{1,0:T(8,128)(2,1)S(1)}, u32[]{:S(2)}, u32[]{:S(2)}) collective-permute-start(bf16[64,1024]{1,0:T(8,128)(2,1)S(1)} %collective-permute-done.6), channel_id=1, source_target_pairs={{0,1},{1,2},{2,3},{3,4},{4,5},{5,6},{6,7},{7,0},{8,9},{9,10},{10,1... | collective-permute-start | bytes 393224 | tf_op jit(solution)/shard_map/ppermute | solution.py:33
  26.2 4.6 %collective-permute-done.3 = bf16[64,1024]{1,0:T(8,128)(2,1)S(1)} collective-permute-done((bf16[64,1024]{1,0:T(8,128)(2,1)S(1)}, bf16[64,1024]{1,0:T(8,128)(2,1)S(1)}, u32[]{:S(2)}, u32[]{:S(2)}) %collective-permute-start.3) | collective-permute-done | bytes 131104 | tf_op jit(solution)/shard_map/ppermute | solution.py:33
  31.6 1.7 %collective-permute-start.12 = (bf16[256,1024]{1,0:T(8,128)(2,1)S(1)}, bf16[256,1024]{1,0:T(8,128)(2,1)S(1)}, u32[]{:S(2)}, u32[]{:S(2)}) collective-permute-start(bf16[256,1024]{1,0:T(8,128)(2,1)S(1)} %pad_maximum_fusion.refs_4_), channel_id=1, source_target_pairs={{0,8},{1,9},{2,10},{3,11},{4,12},{5,13},{6,14},{7,15},{8,16},{9,17... | collective-permute-start | bytes 1572872 | tf_op jit(solution)/shard_map/ppermute | solution.py:33
  33.8 5.4 %collective-permute-done.9.refs_1_ = bf16[256,1024]{1,0:T(8,128)(2,1)S(1)} collective-permute-done((bf16[256,1024]{1,0:T(8,128)(2,1)S(1)}, bf16[256,1024]{1,0:T(8,128)(2,1)S(1)}, u32[]{:S(2)}, u32[]{:S(2)}) %collective-permute-start.9) | collective-permute-done | bytes 524320 | tf_op jit(solution)/shard_map/ppermute | solution.py:33
  40.8 2.4 %collective-permute-start.14 = (bf16[256,1024]{1,0:T(8,128)(2,1)S(1)}, bf16[256,1024]{1,0:T(8,128)(2,1)S(1)}, u32[]{:S(2)}, u32[]{:S(2)}) collective-permute-start(bf16[256,1024]{1,0:T(8,128)(2,1)S(1)} %collective-permute-done.12.refs_5_), channel_id=1, source_target_pairs={{0,8},{1,9},{2,10},{3,11},{4,12},{5,13},{6,14},{7,15},{8,16},{9,17... | collective-permute-start | bytes 1572872 | tf_op jit(solution)/shard_map/ppermute | solution.py:33
  43.2 4.3 %collective-permute-done.10.refs_2_ = bf16[256,1024]{1,0:T(8,128)(2,1)S(1)} collective-permute-done((bf16[256,1024]{1,0:T(8,128)(2,1)S(1)}, bf16[256,1024]{1,0:T(8,128)(2,1)S(1)}, u32[]{:S(2)}, u32[]{:S(2)}) %collective-permute-start.10) | collective-permute-done | bytes 524320 | tf_op jit(solution)/shard_map/ppermute | solution.py:33
  47.5 3.7 %collective-permute-done.11.refs_3_ = bf16[256,1024]{1,0:T(8,128)(2,1)S(1)} collective-permute-done((bf16[256,1024]{1,0:T(8,128)(2,1)S(1)}, bf16[256,1024]{1,0:T(8,128)(2,1)S(1)}, u32[]{:S(2)}, u32[]{:S(2)}) %collective-permute-start.11) | collective-permute-done | bytes 524320 | tf_op jit(solution)/shard_map/ppermute | solution.py:33
  52.8 5.2 %chain.2 = (bf16[128,1024]{1,0:T(8,128)(2,1)S(1)}, bf16[1024,1024]{1,0:T(8,128)(2,1)S(1)}, bf16[1024,1024]{1,0:T(8,128)(2,1)S(1)}) custom-call(s32[4]{0:T(128)S(1)} %pad_add_fusion.where, f32[2,32,1024]{2,1,0:T(8,128)S(1)} %get-tuple-element.24.keep, f32[2,32,1024]{2,1,0:T(8,128)S(1)} %collective-permute-done.other, ...), custom_call_target="tpu_custom_call" | custom-call | tf_op jit(solution)/shard_map/chain/pallas_call | solution.py:150
  58.0 4.6 %collective-permute-start.15 = (bf16[128,1024]{1,0:T(8,128)(2,1)S(1)}, bf16[128,1024]{1,0:T(8,128)(2,1)S(1)}, u32[]{:S(2)}, u32[]{:S(2)}) collective-permute-start(bf16[128,1024]{1,0:T(8,128)(2,1)S(1)} %get-tuple-element.30), channel_id=1, source_target_pairs={{32,0},{33,1},{34,2},{35,3},{36,4},{37,5},{38,6},{39,7},{40,8},{41... | collective-permute-start | bytes 786440 | tf_op jit(solution)/shard_map/ppermute | solution.py:33
  65.6 2.1 %collective-permute-done.16 = bf16[2,32,1024]{2,1,0:T(8,128)(2,1)S(1)} collective-permute-done((bf16[2,32,1024]{2,1,0:T(8,128)(2,1)S(1)}, bf16[2,32,1024]{2,1,0:T(8,128)(2,1)S(1)}, u32[]{:S(2)}, u32[]{:S(2)}) %collective-permute-start.16) | collective-permute-done | bytes 131104 | tf_op jit(solution)/shard_map/ppermute | solution.py:33
  68.9 3.7 %collective-permute-done.17 = bf16[2,32,1024]{2,1,0:T(8,128)(2,1)S(1)} collective-permute-done((bf16[2,32,1024]{2,1,0:T(8,128)(2,1)S(1)}, bf16[2,32,1024]{2,1,0:T(8,128)(2,1)S(1)}, u32[]{:S(2)}, u32[]{:S(2)}) %collective-permute-start.17) | collective-permute-done | bytes 131104 | tf_op jit(solution)/shard_map/ppermute | solution.py:33
  72.8 3.7 %collective-permute-start.22 = (bf16[32,1024]{1,0:T(8,128)(2,1)S(1)}, bf16[32,1024]{1,0:T(8,128)(2,1)S(1)}, u32[]{:S(2)}, u32[]{:S(2)}) collective-permute-start(bf16[32,1024]{1,0:T(8,128)(2,1)S(1)} %get-tuple-element.53), channel_id=1, source_target_pairs={{0,4},{1,5},{2,6},{3,7},{4,0},{5,1},{6,2},{7,3},{8,12},{9,13},{10,... | collective-permute-start | bytes 196616 | tf_op jit(solution)/shard_map/ppermute | solution.py:33
  76.5 1.8 %collective-permute-start.18 = (bf16[32,1024]{1,0:T(8,128)(2,1)S(1)}, bf16[32,1024]{1,0:T(8,128)(2,1)S(1)}, u32[]{:S(2)}, u32[]{:S(2)}) collective-permute-start(bf16[32,1024]{1,0:T(8,128)(2,1)S(1)} %get-tuple-element.55), channel_id=1, source_target_pairs={{0,4},{1,5},{2,6},{3,7},{4,0},{5,1},{6,2},{7,3},{8,12},{9,13},{10,... | collective-permute-start | bytes 196616 | tf_op jit(solution)/shard_map/ppermute | solution.py:33
  78.3 1.7 %collective-permute-done.22 = bf16[32,1024]{1,0:T(8,128)(2,1)S(1)} collective-permute-done((bf16[32,1024]{1,0:T(8,128)(2,1)S(1)}, bf16[32,1024]{1,0:T(8,128)(2,1)S(1)}, u32[]{:S(2)}, u32[]{:S(2)}) %collective-permute-start.22) | collective-permute-done | bytes 65568 | tf_op jit(solution)/shard_map/ppermute | solution.py:33
  80.0 3.8 %collective-permute-start.23 = (bf16[64,1024]{1,0:T(8,128)(2,1)S(1)}, bf16[64,1024]{1,0:T(8,128)(2,1)S(1)}, u32[]{:S(2)}, u32[]{:S(2)}) collective-permute-start(bf16[64,1024]{1,0:T(8,128)(2,1)S(1)} %pad_maximum_fusion.5), channel_id=1, source_target_pairs={{0,1},{1,2},{2,3},{3,4},{4,5},{5,6},{6,7},{7,0},{8,9},{9,10},{10,1... | collective-permute-start | bytes 393224 | tf_op jit(solution)/shard_map/ppermute | solution.py:33
  84.4 2.0 %collective-permute-start.21 = (bf16[64,1024]{1,0:T(8,128)(2,1)S(1)}, bf16[64,1024]{1,0:T(8,128)(2,1)S(1)}, u32[]{:S(2)}, u32[]{:S(2)}) collective-permute-start(bf16[64,1024]{1,0:T(8,128)(2,1)S(1)} %pad_maximum_fusion.4), channel_id=1, source_target_pairs={{0,16},{1,17},{2,18},{3,19},{4,20},{5,21},{6,22},{7,23},{8,24},{9,... | collective-permute-start | bytes 393224 | tf_op jit(solution)/shard_map/ppermute | solution.py:33
  87.3 2.7 %collective-permute-start.25 = (bf16[64,1024]{1,0:T(8,128)(2,1)S(1)}, bf16[64,1024]{1,0:T(8,128)(2,1)S(1)}, u32[]{:S(2)}, u32[]{:S(2)}) collective-permute-start(bf16[64,1024]{1,0:T(8,128)(2,1)S(1)} %collective-permute-done.23), channel_id=1, source_target_pairs={{0,1},{1,2},{2,3},{3,4},{4,5},{5,6},{6,7},{7,0},{8,9},{9,10},{10,1... | collective-permute-start | bytes 393224 | tf_op jit(solution)/shard_map/ppermute | solution.py:33
  90.0 4.7 %collective-permute-done.20 = bf16[64,1024]{1,0:T(8,128)(2,1)S(1)} collective-permute-done((bf16[64,1024]{1,0:T(8,128)(2,1)S(1)}, bf16[64,1024]{1,0:T(8,128)(2,1)S(1)}, u32[]{:S(2)}, u32[]{:S(2)}) %collective-permute-start.20) | collective-permute-done | bytes 131104 | tf_op jit(solution)/shard_map/ppermute | solution.py:33
  95.4 1.9 %collective-permute-start.29 = (bf16[256,1024]{1,0:T(8,128)(2,1)S(1)}, bf16[256,1024]{1,0:T(8,128)(2,1)S(1)}, u32[]{:S(2)}, u32[]{:S(2)}) collective-permute-start(bf16[256,1024]{1,0:T(8,128)(2,1)S(1)} %pad_maximum_fusion.1.refs_4_), channel_id=1, source_target_pairs={{0,8},{1,9},{2,10},{3,11},{4,12},{5,13},{6,14},{7,15},{8,16},{9,17... | collective-permute-start | bytes 1572872 | tf_op jit(solution)/shard_map/ppermute | solution.py:33
  97.8 5.1 %collective-permute-done.26.refs_1_ = bf16[256,1024]{1,0:T(8,128)(2,1)S(1)} collective-permute-done((bf16[256,1024]{1,0:T(8,128)(2,1)S(1)}, bf16[256,1024]{1,0:T(8,128)(2,1)S(1)}, u32[]{:S(2)}, u32[]{:S(2)}) %collective-permute-start.26) | collective-permute-done | bytes 524320 | tf_op jit(solution)/shard_map/ppermute | solution.py:33
  102.9 2.4 %collective-permute-start.28 = (bf16[256,1024]{1,0:T(8,128)(2,1)S(1)}, bf16[256,1024]{1,0:T(8,128)(2,1)S(1)}, u32[]{:S(2)}, u32[]{:S(2)}) collective-permute-start(bf16[256,1024]{1,0:T(8,128)(2,1)S(1)} %collective-permute-done.26.refs_1_), channel_id=1, source_target_pairs={{0,1},{1,2},{2,3},{3,4},{4,5},{5,6},{6,7},{7,0},{8,9},{9,10},{10,1... | collective-permute-start | bytes 1572872 | tf_op jit(solution)/shard_map/ppermute | solution.py:33
  106.9 3.1 %collective-permute-done.27.refs_2_ = bf16[256,1024]{1,0:T(8,128)(2,1)S(1)} collective-permute-done((bf16[256,1024]{1,0:T(8,128)(2,1)S(1)}, bf16[256,1024]{1,0:T(8,128)(2,1)S(1)}, u32[]{:S(2)}, u32[]{:S(2)}) %collective-permute-start.27) | collective-permute-done | bytes 524320 | tf_op jit(solution)/shard_map/ppermute | solution.py:33
  110.0 5.3 %collective-permute-done.28.refs_3_ = bf16[256,1024]{1,0:T(8,128)(2,1)S(1)} collective-permute-done((bf16[256,1024]{1,0:T(8,128)(2,1)S(1)}, bf16[256,1024]{1,0:T(8,128)(2,1)S(1)}, u32[]{:S(2)}, u32[]{:S(2)}) %collective-permute-start.28) | collective-permute-done | bytes 524320 | tf_op jit(solution)/shard_map/ppermute | solution.py:33
  115.4 2.6 %collective-permute-done.31.refs_7_ = bf16[256,1024]{1,0:T(8,128)(2,1)S(1)} collective-permute-done((bf16[256,1024]{1,0:T(8,128)(2,1)S(1)}, bf16[256,1024]{1,0:T(8,128)(2,1)S(1)}, u32[]{:S(2)}, u32[]{:S(2)}) %collective-permute-start.31) | collective-permute-done | bytes 524320 | tf_op jit(solution)/shard_map/ppermute | solution.py:33
  118.0 5.0 %chain.3 = (bf16[128,1024]{1,0:T(8,128)(2,1)S(1)}, bf16[1024,1024]{1,0:T(8,128)(2,1)S(1)}, bf16[1024,1024]{1,0:T(8,128)(2,1)S(1)}) custom-call(s32[4]{0:T(128)S(1)} %pad_add_fusion.where, f32[2,32,1024]{2,1,0:T(8,128)S(1)} %get-tuple-element.44.keep, f32[2,32,1024]{2,1,0:T(8,128)S(1)} %get-tuple-element.43.other, ...), custom_call_target="tpu_custom_call" | custom-call | tf_op jit(solution)/shard_map/chain/pallas_call | solution.py:150
  123.0 3.2 %collective-permute-start.32 = (bf16[128,1024]{1,0:T(8,128)(2,1)S(1)}, bf16[128,1024]{1,0:T(8,128)(2,1)S(1)}, u32[]{:S(2)}, u32[]{:S(2)}) collective-permute-start(bf16[128,1024]{1,0:T(8,128)(2,1)S(1)} %get-tuple-element.40), channel_id=1, source_target_pairs={{32,0},{33,1},{34,2},{35,3},{36,4},{37,5},{38,6},{39,7},{40,8},{41... | collective-permute-start | bytes 786440 | tf_op jit(solution)/shard_map/ppermute | solution.py:33
  129.2 2.6 %collective-permute-done.33 = f32[4,32,1024]{2,1,0:T(8,128)S(1)} collective-permute-done((f32[4,32,1024]{2,1,0:T(8,128)S(1)}, f32[4,32,1024]{2,1,0:T(8,128)S(1)}, u32[]{:S(2)}, u32[]{:S(2)}) %collective-permute-start.33) | collective-permute-done | bytes 524320 | tf_op jit(solution)/shard_map/ppermute | solution.py:33
  (70 shorter events, 23.8 us)
Async XLA Ops:
  2.6 4.5 %collective-permute-start = (f32[2,32,1024]{2,1,0:T(8,128)S(1)}, f32[2,32,1024]{2,1,0:T(8,128)S(1)}, u32[]{:S(2)}, u32[]{:S(2)}) collective-permute-start(f32[2,32,1024]{2,1,0:T(8,128)S(1)} %get-tuple-element.25), channel_id=1, source_target_pairs={{0,32},{1,33},{2,34},{3,35},{4,36},{5,37},{6,38},{7,39},{8,40},{9,... | collective-permute-start | bytes 786440 | tf_op jit(solution)/shard_map/ppermute | solution.py:33
  7.2 7.2 %collective-permute-start.5 = (bf16[32,1024]{1,0:T(8,128)(2,1)S(1)}, bf16[32,1024]{1,0:T(8,128)(2,1)S(1)}, u32[]{:S(2)}, u32[]{:S(2)}) collective-permute-start(bf16[32,1024]{1,0:T(8,128)(2,1)S(1)} %get-tuple-element.56), channel_id=1, source_target_pairs={{0,4},{1,5},{2,6},{3,7},{4,0},{5,1},{6,2},{7,3},{8,12},{9,13},{10,... | collective-permute-start | bytes 196616 | tf_op jit(solution)/shard_map/ppermute | solution.py:33
  12.4 7.1 %collective-permute-start.1 = (bf16[32,1024]{1,0:T(8,128)(2,1)S(1)}, bf16[32,1024]{1,0:T(8,128)(2,1)S(1)}, u32[]{:S(2)}, u32[]{:S(2)}) collective-permute-start(bf16[32,1024]{1,0:T(8,128)(2,1)S(1)} %get-tuple-element.58), channel_id=1, source_target_pairs={{0,4},{1,5},{2,6},{3,7},{4,0},{5,1},{6,2},{7,3},{8,12},{9,13},{10,... | collective-permute-start | bytes 196616 | tf_op jit(solution)/shard_map/ppermute | solution.py:33
  14.4 9.0 %collective-permute-start.6 = (bf16[64,1024]{1,0:T(8,128)(2,1)S(1)}, bf16[64,1024]{1,0:T(8,128)(2,1)S(1)}, u32[]{:S(2)}, u32[]{:S(2)}) collective-permute-start(bf16[64,1024]{1,0:T(8,128)(2,1)S(1)} %pad_maximum_fusion.3), channel_id=1, source_target_pairs={{0,1},{1,2},{2,3},{3,4},{4,5},{5,6},{6,7},{7,0},{8,9},{9,10},{10,1... | collective-permute-start | bytes 393224 | tf_op jit(solution)/shard_map/ppermute | solution.py:33
  19.5 6.6 %collective-permute-start.2 = (bf16[64,1024]{1,0:T(8,128)(2,1)S(1)}, bf16[64,1024]{1,0:T(8,128)(2,1)S(1)}, u32[]{:S(2)}, u32[]{:S(2)}) collective-permute-start(bf16[64,1024]{1,0:T(8,128)(2,1)S(1)} %pad_maximum_fusion.2), channel_id=1, source_target_pairs={{0,8},{1,9},{2,10},{3,11},{4,12},{5,13},{6,14},{7,15},{8,16},{9,17... | collective-permute-start | bytes 393224 | tf_op jit(solution)/shard_map/ppermute | solution.py:33
  22.3 8.4 %collective-permute-start.4 = (bf16[64,1024]{1,0:T(8,128)(2,1)S(1)}, bf16[64,1024]{1,0:T(8,128)(2,1)S(1)}, u32[]{:S(2)}, u32[]{:S(2)}) collective-permute-start(bf16[64,1024]{1,0:T(8,128)(2,1)S(1)} %pad_maximum_fusion.2), channel_id=1, source_target_pairs={{0,16},{1,17},{2,18},{3,19},{4,20},{5,21},{6,22},{7,23},{8,24},{9,... | collective-permute-start | bytes 393224 | tf_op jit(solution)/shard_map/ppermute | solution.py:33
  22.7 8.0 %collective-permute-start.3 = (bf16[64,1024]{1,0:T(8,128)(2,1)S(1)}, bf16[64,1024]{1,0:T(8,128)(2,1)S(1)}, u32[]{:S(2)}, u32[]{:S(2)}) collective-permute-start(bf16[64,1024]{1,0:T(8,128)(2,1)S(1)} %pad_maximum_fusion.2), channel_id=1, source_target_pairs={{0,24},{1,25},{2,26},{3,27},{4,28},{5,29},{6,30},{7,31},{8,0},{9,1... | collective-permute-start | bytes 393224 | tf_op jit(solution)/shard_map/ppermute | solution.py:33
  23.4 7.4 %collective-permute-start.7 = (bf16[64,1024]{1,0:T(8,128)(2,1)S(1)}, bf16[64,1024]{1,0:T(8,128)(2,1)S(1)}, u32[]{:S(2)}, u32[]{:S(2)}) collective-permute-start(bf16[64,1024]{1,0:T(8,128)(2,1)S(1)} %pad_maximum_fusion.3), channel_id=1, source_target_pairs={{0,7},{1,0},{2,1},{3,2},{4,3},{5,4},{6,5},{7,6},{8,15},{9,8},{10,9... | collective-permute-start | bytes 393224 | tf_op jit(solution)/shard_map/ppermute | solution.py:33
  24.3 6.5 %collective-permute-start.8 = (bf16[64,1024]{1,0:T(8,128)(2,1)S(1)}, bf16[64,1024]{1,0:T(8,128)(2,1)S(1)}, u32[]{:S(2)}, u32[]{:S(2)}) collective-permute-start(bf16[64,1024]{1,0:T(8,128)(2,1)S(1)} %collective-permute-done.6), channel_id=1, source_target_pairs={{0,1},{1,2},{2,3},{3,4},{4,5},{5,6},{6,7},{7,0},{8,9},{9,10},{10,1... | collective-permute-start | bytes 393224 | tf_op jit(solution)/shard_map/ppermute | solution.py:33
  30.8 8.4 %collective-permute-start.9 = (bf16[256,1024]{1,0:T(8,128)(2,1)S(1)}, bf16[256,1024]{1,0:T(8,128)(2,1)S(1)}, u32[]{:S(2)}, u32[]{:S(2)}) collective-permute-start(bf16[256,1024]{1,0:T(8,128)(2,1)S(1)} %constant_dynamic-update-slice_fusion.refs_0_), channel_id=1, source_target_pairs={{0,1},{1,2},{2,3},{3,4},{4,5},{5,6},{6,7},{7,0},{8,9},{9,10},{10,1... | collective-permute-start | bytes 1572872 | tf_op jit(solution)/shard_map/ppermute | solution.py:33
  31.6 9.2 %collective-permute-start.12 = (bf16[256,1024]{1,0:T(8,128)(2,1)S(1)}, bf16[256,1024]{1,0:T(8,128)(2,1)S(1)}, u32[]{:S(2)}, u32[]{:S(2)}) collective-permute-start(bf16[256,1024]{1,0:T(8,128)(2,1)S(1)} %pad_maximum_fusion.refs_4_), channel_id=1, source_target_pairs={{0,8},{1,9},{2,10},{3,11},{4,12},{5,13},{6,14},{7,15},{8,16},{9,17... | collective-permute-start | bytes 1572872 | tf_op jit(solution)/shard_map/ppermute | solution.py:33
  33.3 14.2 %collective-permute-start.10 = (bf16[256,1024]{1,0:T(8,128)(2,1)S(1)}, bf16[256,1024]{1,0:T(8,128)(2,1)S(1)}, u32[]{:S(2)}, u32[]{:S(2)}) collective-permute-start(bf16[256,1024]{1,0:T(8,128)(2,1)S(1)} %constant_dynamic-update-slice_fusion.refs_0_), channel_id=1, source_target_pairs={{0,7},{1,0},{2,1},{3,2},{4,3},{5,4},{6,5},{7,6},{8,15},{9,8},{10,9... | collective-permute-start | bytes 1572872 | tf_op jit(solution)/shard_map/ppermute | solution.py:33
  33.3 14.2 %collective-permute-start.13 = (bf16[256,1024]{1,0:T(8,128)(2,1)S(1)}, bf16[256,1024]{1,0:T(8,128)(2,1)S(1)}, u32[]{:S(2)}, u32[]{:S(2)}) collective-permute-start(bf16[256,1024]{1,0:T(8,128)(2,1)S(1)} %pad_maximum_fusion.refs_4_), channel_id=1, source_target_pairs={{0,24},{1,25},{2,26},{3,27},{4,28},{5,29},{6,30},{7,31},{8,0},{9,1... | collective-permute-start | bytes 1572872 | tf_op jit(solution)/shard_map/ppermute | solution.py:33
  39.2 11.9 %collective-permute-start.11 = (bf16[256,1024]{1,0:T(8,128)(2,1)S(1)}, bf16[256,1024]{1,0:T(8,128)(2,1)S(1)}, u32[]{:S(2)}, u32[]{:S(2)}) collective-permute-start(bf16[256,1024]{1,0:T(8,128)(2,1)S(1)} %collective-permute-done.9.refs_1_), channel_id=1, source_target_pairs={{0,1},{1,2},{2,3},{3,4},{4,5},{5,6},{6,7},{7,0},{8,9},{9,10},{10,1... | collective-permute-start | bytes 1572872 | tf_op jit(solution)/shard_map/ppermute | solution.py:33
  40.8 11.9 %collective-permute-start.14 = (bf16[256,1024]{1,0:T(8,128)(2,1)S(1)}, bf16[256,1024]{1,0:T(8,128)(2,1)S(1)}, u32[]{:S(2)}, u32[]{:S(2)}) collective-permute-start(bf16[256,1024]{1,0:T(8,128)(2,1)S(1)} %collective-permute-done.12.refs_5_), channel_id=1, source_target_pairs={{0,8},{1,9},{2,10},{3,11},{4,12},{5,13},{6,14},{7,15},{8,16},{9,17... | collective-permute-start | bytes 1572872 | tf_op jit(solution)/shard_map/ppermute | solution.py:33
  58.0 5.7 %collective-permute-start.15 = (bf16[128,1024]{1,0:T(8,128)(2,1)S(1)}, bf16[128,1024]{1,0:T(8,128)(2,1)S(1)}, u32[]{:S(2)}, u32[]{:S(2)}) collective-permute-start(bf16[128,1024]{1,0:T(8,128)(2,1)S(1)} %get-tuple-element.30), channel_id=1, source_target_pairs={{32,0},{33,1},{34,2},{35,3},{36,4},{37,5},{38,6},{39,7},{40,8},{41... | collective-permute-start | bytes 786440 | tf_op jit(solution)/shard_map/ppermute | solution.py:33
  67.6 5.0 %collective-permute-start.17 = (bf16[2,32,1024]{2,1,0:T(8,128)(2,1)S(1)}, bf16[2,32,1024]{2,1,0:T(8,128)(2,1)S(1)}, u32[]{:S(2)}, u32[]{:S(2)}) collective-permute-start(bf16[2,32,1024]{2,1,0:T(8,128)(2,1)S(1)} %broadcast_select_fusion), channel_id=1, source_target_pairs={{0,64},{1,65},{2,66},{3,67},{4,68},{5,69},{6,70},{7,71},{8,72},{9,... | collective-permute-start | bytes 393224 | tf_op jit(solution)/shard_map/ppermute | solution.py:33
  72.8 7.2 %collective-permute-start.22 = (bf16[32,1024]{1,0:T(8,128)(2,1)S(1)}, bf16[32,1024]{1,0:T(8,128)(2,1)S(1)}, u32[]{:S(2)}, u32[]{:S(2)}) collective-permute-start(bf16[32,1024]{1,0:T(8,128)(2,1)S(1)} %get-tuple-element.53), channel_id=1, source_target_pairs={{0,4},{1,5},{2,6},{3,7},{4,0},{5,1},{6,2},{7,3},{8,12},{9,13},{10,... | collective-permute-start | bytes 196616 | tf_op jit(solution)/shard_map/ppermute | solution.py:33
  76.5 7.8 %collective-permute-start.18 = (bf16[32,1024]{1,0:T(8,128)(2,1)S(1)}, bf16[32,1024]{1,0:T(8,128)(2,1)S(1)}, u32[]{:S(2)}, u32[]{:S(2)}) collective-permute-start(bf16[32,1024]{1,0:T(8,128)(2,1)S(1)} %get-tuple-element.55), channel_id=1, source_target_pairs={{0,4},{1,5},{2,6},{3,7},{4,0},{5,1},{6,2},{7,3},{8,12},{9,13},{10,... | collective-permute-start | bytes 196616 | tf_op jit(solution)/shard_map/ppermute | solution.py:33
  80.0 7.2 %collective-permute-start.23 = (bf16[64,1024]{1,0:T(8,128)(2,1)S(1)}, bf16[64,1024]{1,0:T(8,128)(2,1)S(1)}, u32[]{:S(2)}, u32[]{:S(2)}) collective-permute-start(bf16[64,1024]{1,0:T(8,128)(2,1)S(1)} %pad_maximum_fusion.5), channel_id=1, source_target_pairs={{0,1},{1,2},{2,3},{3,4},{4,5},{5,6},{6,7},{7,0},{8,9},{9,10},{10,1... | collective-permute-start | bytes 393224 | tf_op jit(solution)/shard_map/ppermute | solution.py:33
  84.3 5.7 %collective-permute-start.19 = (bf16[64,1024]{1,0:T(8,128)(2,1)S(1)}, bf16[64,1024]{1,0:T(8,128)(2,1)S(1)}, u32[]{:S(2)}, u32[]{:S(2)}) collective-permute-start(bf16[64,1024]{1,0:T(8,128)(2,1)S(1)} %pad_maximum_fusion.4), channel_id=1, source_target_pairs={{0,8},{1,9},{2,10},{3,11},{4,12},{5,13},{6,14},{7,15},{8,16},{9,17... | collective-permute-start | bytes 393224 | tf_op jit(solution)/shard_map/ppermute | solution.py:33
  84.4 10.3 %collective-permute-start.21 = (bf16[64,1024]{1,0:T(8,128)(2,1)S(1)}, bf16[64,1024]{1,0:T(8,128)(2,1)S(1)}, u32[]{:S(2)}, u32[]{:S(2)}) collective-permute-start(bf16[64,1024]{1,0:T(8,128)(2,1)S(1)} %pad_maximum_fusion.4), channel_id=1, source_target_pairs={{0,16},{1,17},{2,18},{3,19},{4,20},{5,21},{6,22},{7,23},{8,24},{9,... | collective-permute-start | bytes 393224 | tf_op jit(solution)/shard_map/ppermute | solution.py:33
  86.5 8.2 %collective-permute-start.20 = (bf16[64,1024]{1,0:T(8,128)(2,1)S(1)}, bf16[64,1024]{1,0:T(8,128)(2,1)S(1)}, u32[]{:S(2)}, u32[]{:S(2)}) collective-permute-start(bf16[64,1024]{1,0:T(8,128)(2,1)S(1)} %pad_maximum_fusion.4), channel_id=1, source_target_pairs={{0,24},{1,25},{2,26},{3,27},{4,28},{5,29},{6,30},{7,31},{8,0},{9,1... | collective-permute-start | bytes 393224 | tf_op jit(solution)/shard_map/ppermute | solution.py:33
  87.3 7.5 %collective-permute-start.24 = (bf16[64,1024]{1,0:T(8,128)(2,1)S(1)}, bf16[64,1024]{1,0:T(8,128)(2,1)S(1)}, u32[]{:S(2)}, u32[]{:S(2)}) collective-permute-start(bf16[64,1024]{1,0:T(8,128)(2,1)S(1)} %pad_maximum_fusion.5), channel_id=1, source_target_pairs={{0,7},{1,0},{2,1},{3,2},{4,3},{5,4},{6,5},{7,6},{8,15},{9,8},{10,9... | collective-permute-start | bytes 393224 | tf_op jit(solution)/shard_map/ppermute | solution.py:33
  87.3 7.4 %collective-permute-start.25 = (bf16[64,1024]{1,0:T(8,128)(2,1)S(1)}, bf16[64,1024]{1,0:T(8,128)(2,1)S(1)}, u32[]{:S(2)}, u32[]{:S(2)}) collective-permute-start(bf16[64,1024]{1,0:T(8,128)(2,1)S(1)} %collective-permute-done.23), channel_id=1, source_target_pairs={{0,1},{1,2},{2,3},{3,4},{4,5},{5,6},{6,7},{7,0},{8,9},{9,10},{10,1... | collective-permute-start | bytes 393224 | tf_op jit(solution)/shard_map/ppermute | solution.py:33
  94.8 8.1 %collective-permute-start.26 = (bf16[256,1024]{1,0:T(8,128)(2,1)S(1)}, bf16[256,1024]{1,0:T(8,128)(2,1)S(1)}, u32[]{:S(2)}, u32[]{:S(2)}) collective-permute-start(bf16[256,1024]{1,0:T(8,128)(2,1)S(1)} %constant_dynamic-update-slice_fusion.5.refs_0_), channel_id=1, source_target_pairs={{0,1},{1,2},{2,3},{3,4},{4,5},{5,6},{6,7},{7,0},{8,9},{9,10},{10,1... | collective-permute-start | bytes 1572872 | tf_op jit(solution)/shard_map/ppermute | solution.py:33
  95.4 9.9 %collective-permute-start.29 = (bf16[256,1024]{1,0:T(8,128)(2,1)S(1)}, bf16[256,1024]{1,0:T(8,128)(2,1)S(1)}, u32[]{:S(2)}, u32[]{:S(2)}) collective-permute-start(bf16[256,1024]{1,0:T(8,128)(2,1)S(1)} %pad_maximum_fusion.1.refs_4_), channel_id=1, source_target_pairs={{0,8},{1,9},{2,10},{3,11},{4,12},{5,13},{6,14},{7,15},{8,16},{9,17... | collective-permute-start | bytes 1572872 | tf_op jit(solution)/shard_map/ppermute | solution.py:33
  97.4 12.7 %collective-permute-start.27 = (bf16[256,1024]{1,0:T(8,128)(2,1)S(1)}, bf16[256,1024]{1,0:T(8,128)(2,1)S(1)}, u32[]{:S(2)}, u32[]{:S(2)}) collective-permute-start(bf16[256,1024]{1,0:T(8,128)(2,1)S(1)} %constant_dynamic-update-slice_fusion.5.refs_0_), channel_id=1, source_target_pairs={{0,7},{1,0},{2,1},{3,2},{4,3},{5,4},{6,5},{7,6},{8,15},{9,8},{10,9... | collective-permute-start | bytes 1572872 | tf_op jit(solution)/shard_map/ppermute | solution.py:33
  97.4 12.7 %collective-permute-start.30 = (bf16[256,1024]{1,0:T(8,128)(2,1)S(1)}, bf16[256,1024]{1,0:T(8,128)(2,1)S(1)}, u32[]{:S(2)}, u32[]{:S(2)}) collective-permute-start(bf16[256,1024]{1,0:T(8,128)(2,1)S(1)} %pad_maximum_fusion.1.refs_4_), channel_id=1, source_target_pairs={{0,24},{1,25},{2,26},{3,27},{4,28},{5,29},{6,30},{7,31},{8,0},{9,1... | collective-permute-start | bytes 1572872 | tf_op jit(solution)/shard_map/ppermute | solution.py:33
  102.9 12.4 %collective-permute-start.28 = (bf16[256,1024]{1,0:T(8,128)(2,1)S(1)}, bf16[256,1024]{1,0:T(8,128)(2,1)S(1)}, u32[]{:S(2)}, u32[]{:S(2)}) collective-permute-start(bf16[256,1024]{1,0:T(8,128)(2,1)S(1)} %collective-permute-done.26.refs_1_), channel_id=1, source_target_pairs={{0,1},{1,2},{2,3},{3,4},{4,5},{5,6},{6,7},{7,0},{8,9},{9,10},{10,1... | collective-permute-start | bytes 1572872 | tf_op jit(solution)/shard_map/ppermute | solution.py:33
  105.4 12.6 %collective-permute-start.31 = (bf16[256,1024]{1,0:T(8,128)(2,1)S(1)}, bf16[256,1024]{1,0:T(8,128)(2,1)S(1)}, u32[]{:S(2)}, u32[]{:S(2)}) collective-permute-start(bf16[256,1024]{1,0:T(8,128)(2,1)S(1)} %collective-permute-done.29.refs_5_), channel_id=1, source_target_pairs={{0,8},{1,9},{2,10},{3,11},{4,12},{5,13},{6,14},{7,15},{8,16},{9,17... | collective-permute-start | bytes 1572872 | tf_op jit(solution)/shard_map/ppermute | solution.py:33
  123.0 4.3 %collective-permute-start.32 = (bf16[128,1024]{1,0:T(8,128)(2,1)S(1)}, bf16[128,1024]{1,0:T(8,128)(2,1)S(1)}, u32[]{:S(2)}, u32[]{:S(2)}) collective-permute-start(bf16[128,1024]{1,0:T(8,128)(2,1)S(1)} %get-tuple-element.40), channel_id=1, source_target_pairs={{32,0},{33,1},{34,2},{35,3},{36,4},{37,5},{38,6},{39,7},{40,8},{41... | collective-permute-start | bytes 786440 | tf_op jit(solution)/shard_map/ppermute | solution.py:33
  (4 other events, 9.1 us)

commit v12 on v10

--- a/solution.py
+++ b/solution.py
@@ -47,8 +47,7 @@
     wide_b = jnp.concatenate([wide_b, send(wide_b, hop("z", NZ // 2))])
     ahead, behind = send(wide_a, hop("y", 1)), send(wide_a, hop("y", -1))
     wide_a = jnp.concatenate([wide_a, ahead, behind, send(wide_a, hop("y", 2))])
-    ahead, behind = send(wide_b, hop("z", 1)), send(wide_b, hop("z", -1))
-    wide_b = jnp.concatenate([wide_b, ahead, behind, send(ahead, hop("z", 1))])
+    wide_b = jnp.concatenate([wide_b] + [send(wide_b, hop("z", d)) for d in BACK[1:]])
     wide_a, wide_b = lax.optimization_barrier((wide_a, wide_b))
     parts = []
     for wide, axis in ((wide_a, "z"), (wide_b, "y")):

time: 137 us -> 137 us (level)
  starting transfers between devices: 61.8 us -> 72.9 us
  waiting for transfers between devices: 58.5 us -> 48.8 us
    ppermute x34, starting transfers between devices: 61.8 us -> 72.9 us  [send(): return lax.ppermute(block, AXES, route(move))]
    ppermute x34, waiting for transfers between devices: 58.5 us -> 48.8 us  [send(): return lax.ppermute(block, AXES, route(move))]
where the time goes in v12:
time: 137 us
  starting transfers between devices  72.9 us (53%)
  waiting for transfers between devices  48.8 us (36%)
  Pallas kernels  12 us (9%)
  local copies, waits for them, and re-layouts  2.05 us (1%)
    ppermute x34, starting transfers between devices, send(): return lax.ppermute(block, AXES, route(move))  72.9 us
    ppermute x34, waiting for transfers between devices, send(): return lax.ppermute(block, AXES, route(move))  48.8 us
    pallas_call x2, Pallas kernels, chain(): pl.pallas_call(chain_kernel, out_shape=[jax.ShapeDtypeStruct((128, M), jn...  10.2 us
  transfers between devices with their start and end apart: 34, of which 22 were waited for; matrix products, arithmetic and copies ran while one was open for 0% of the time, Pallas kernels for 0%

profile of v12, /device:TPU:1, one launch (start us, length us, event | category | flops | bytes accessed | tf_op | source)
XLA Modules:
  0.0 137.2 jit_solution(6485966873213752973)
XLA Ops:
  2.6 3.3 %collective-permute-start = (f32[2,32,1024]{2,1,0:T(8,128)S(1)}, f32[2,32,1024]{2,1,0:T(8,128)S(1)}, u32[]{:S(2)}, u32[]{:S(2)}) collective-permute-start(f32[2,32,1024]{2,1,0:T(8,128)S(1)} %get-tuple-element.21), channel_id=1, source_target_pairs={{0,32},{1,33},{2,34},{3,35},{4,36},{5,37},{6,38},{7,39},{8,40},{9,... | collective-permute-start | bytes 786440 | tf_op jit(solution)/shard_map/ppermute | solution.py:33
  7.2 5.3 %collective-permute-start.1 = (bf16[32,1024]{1,0:T(8,128)(2,1)S(1)}, bf16[32,1024]{1,0:T(8,128)(2,1)S(1)}, u32[]{:S(2)}, u32[]{:S(2)}) collective-permute-start(bf16[32,1024]{1,0:T(8,128)(2,1)S(1)} %get-tuple-element.52), channel_id=1, source_target_pairs={{0,4},{1,5},{2,6},{3,7},{4,0},{5,1},{6,2},{7,3},{8,12},{9,13},{10,... | collective-permute-start | bytes 196616 | tf_op jit(solution)/shard_map/ppermute | solution.py:33
  14.4 3.2 %collective-permute-start.4 = (bf16[64,1024]{1,0:T(8,128)(2,1)S(1)}, bf16[64,1024]{1,0:T(8,128)(2,1)S(1)}, u32[]{:S(2)}, u32[]{:S(2)}) collective-permute-start(bf16[64,1024]{1,0:T(8,128)(2,1)S(1)} %pad_maximum_fusion), channel_id=1, source_target_pairs={{0,16},{1,17},{2,18},{3,19},{4,20},{5,21},{6,22},{7,23},{8,24},{9,... | collective-permute-start | bytes 393224 | tf_op jit(solution)/shard_map/ppermute | solution.py:33
  18.0 2.3 %collective-permute-start.2 = (bf16[64,1024]{1,0:T(8,128)(2,1)S(1)}, bf16[64,1024]{1,0:T(8,128)(2,1)S(1)}, u32[]{:S(2)}, u32[]{:S(2)}) collective-permute-start(bf16[64,1024]{1,0:T(8,128)(2,1)S(1)} %pad_maximum_fusion), channel_id=1, source_target_pairs={{0,8},{1,9},{2,10},{3,11},{4,12},{5,13},{6,14},{7,15},{8,16},{9,17... | collective-permute-start | bytes 393224 | tf_op jit(solution)/shard_map/ppermute | solution.py:33
  20.3 4.0 %collective-permute-start.8 = (bf16[64,1024]{1,0:T(8,128)(2,1)S(1)}, bf16[64,1024]{1,0:T(8,128)(2,1)S(1)}, u32[]{:S(2)}, u32[]{:S(2)}) collective-permute-start(bf16[64,1024]{1,0:T(8,128)(2,1)S(1)} %pad_maximum_fusion.1), channel_id=1, source_target_pairs={{0,2},{1,3},{2,4},{3,5},{4,6},{5,7},{6,0},{7,1},{8,10},{9,11},{10,... | collective-permute-start | bytes 393224 | tf_op jit(solution)/shard_map/ppermute | solution.py:33
  25.7 2.9 %collective-permute-start.6 = (bf16[64,1024]{1,0:T(8,128)(2,1)S(1)}, bf16[64,1024]{1,0:T(8,128)(2,1)S(1)}, u32[]{:S(2)}, u32[]{:S(2)}) collective-permute-start(bf16[64,1024]{1,0:T(8,128)(2,1)S(1)} %pad_maximum_fusion.1), channel_id=1, source_target_pairs={{0,1},{1,2},{2,3},{3,4},{4,5},{5,6},{6,7},{7,0},{8,9},{9,10},{10,1... | collective-permute-start | bytes 393224 | tf_op jit(solution)/shard_map/ppermute | solution.py:33
  28.7 2.5 %collective-permute-done.6 = bf16[64,1024]{1,0:T(8,128)(2,1)S(1)} collective-permute-done((bf16[64,1024]{1,0:T(8,128)(2,1)S(1)}, bf16[64,1024]{1,0:T(8,128)(2,1)S(1)}, u32[]{:S(2)}, u32[]{:S(2)}) %collective-permute-start.6) | collective-permute-done | bytes 131104 | tf_op jit(solution)/shard_map/ppermute | solution.py:33
  31.4 2.7 %collective-permute-start.9 = (bf16[256,1024]{1,0:T(8,128)(2,1)S(1)}, bf16[256,1024]{1,0:T(8,128)(2,1)S(1)}, u32[]{:S(2)}, u32[]{:S(2)}) collective-permute-start(bf16[256,1024]{1,0:T(8,128)(2,1)S(1)} %constant_dynamic-update-slice_fusion.refs_0_), channel_id=1, source_target_pairs={{0,1},{1,2},{2,3},{3,4},{4,5},{5,6},{6,7},{7,0},{8,9},{9,10},{10,1... | collective-permute-start | bytes 1572872 | tf_op jit(solution)/shard_map/ppermute | solution.py:33
  34.1 3.1 %collective-permute-start.12 = (bf16[256,1024]{1,0:T(8,128)(2,1)S(1)}, bf16[256,1024]{1,0:T(8,128)(2,1)S(1)}, u32[]{:S(2)}, u32[]{:S(2)}) collective-permute-start(bf16[256,1024]{1,0:T(8,128)(2,1)S(1)} %constant_dynamic-update-slice_fusion.5.refs_4_), channel_id=1, source_target_pairs={{0,8},{1,9},{2,10},{3,11},{4,12},{5,13},{6,14},{7,15},{8,16},{9,17... | collective-permute-start | bytes 1572872 | tf_op jit(solution)/shard_map/ppermute | solution.py:33
  37.3 3.9 %collective-permute-done.9.refs_1_ = bf16[256,1024]{1,0:T(8,128)(2,1)S(1)} collective-permute-done((bf16[256,1024]{1,0:T(8,128)(2,1)S(1)}, bf16[256,1024]{1,0:T(8,128)(2,1)S(1)}, u32[]{:S(2)}, u32[]{:S(2)}) %collective-permute-start.9) | collective-permute-done | bytes 524320 | tf_op jit(solution)/shard_map/ppermute | solution.py:33
  41.2 3.4 %collective-permute-start.11 = (bf16[256,1024]{1,0:T(8,128)(2,1)S(1)}, bf16[256,1024]{1,0:T(8,128)(2,1)S(1)}, u32[]{:S(2)}, u32[]{:S(2)}) collective-permute-start(bf16[256,1024]{1,0:T(8,128)(2,1)S(1)} %collective-permute-done.9.refs_1_), channel_id=1, source_target_pairs={{0,1},{1,2},{2,3},{3,4},{4,5},{5,6},{6,7},{7,0},{8,9},{9,10},{10,1... | collective-permute-start | bytes 1572872 | tf_op jit(solution)/shard_map/ppermute | solution.py:33
  44.6 3.6 %collective-permute-start.14 = (bf16[256,1024]{1,0:T(8,128)(2,1)S(1)}, bf16[256,1024]{1,0:T(8,128)(2,1)S(1)}, u32[]{:S(2)}, u32[]{:S(2)}) collective-permute-start(bf16[256,1024]{1,0:T(8,128)(2,1)S(1)} %collective-permute-done.12.refs_5_), channel_id=1, source_target_pairs={{0,8},{1,9},{2,10},{3,11},{4,12},{5,13},{6,14},{7,15},{8,16},{9,17... | collective-permute-start | bytes 1572872 | tf_op jit(solution)/shard_map/ppermute | solution.py:33
  48.1 2.2 %collective-permute-done.10.refs_2_ = bf16[256,1024]{1,0:T(8,128)(2,1)S(1)} collective-permute-done((bf16[256,1024]{1,0:T(8,128)(2,1)S(1)}, bf16[256,1024]{1,0:T(8,128)(2,1)S(1)}, u32[]{:S(2)}, u32[]{:S(2)}) %collective-permute-start.10) | collective-permute-done | bytes 524320 | tf_op jit(solution)/shard_map/ppermute | solution.py:33
  51.5 3.1 %collective-permute-done.14.refs_7_ = bf16[256,1024]{1,0:T(8,128)(2,1)S(1)} collective-permute-done((bf16[256,1024]{1,0:T(8,128)(2,1)S(1)}, bf16[256,1024]{1,0:T(8,128)(2,1)S(1)}, u32[]{:S(2)}, u32[]{:S(2)}) %collective-permute-start.14) | collective-permute-done | bytes 524320 | tf_op jit(solution)/shard_map/ppermute | solution.py:33
  54.6 5.2 %chain.2 = (bf16[128,1024]{1,0:T(8,128)(2,1)S(1)}, bf16[1024,1024]{1,0:T(8,128)(2,1)S(1)}, bf16[1024,1024]{1,0:T(8,128)(2,1)S(1)}) custom-call(s32[4]{0:T(128)S(1)} %pad_add_fusion.where, f32[2,32,1024]{2,1,0:T(8,128)S(1)} %get-tuple-element.20.keep, f32[2,32,1024]{2,1,0:T(8,128)S(1)} %collective-permute-done.other, ...), custom_call_target="tpu_custom_call" | custom-call | tf_op jit(solution)/shard_map/chain/pallas_call | solution.py:148
  59.8 3.2 %collective-permute-start.15 = (bf16[128,1024]{1,0:T(8,128)(2,1)S(1)}, bf16[128,1024]{1,0:T(8,128)(2,1)S(1)}, u32[]{:S(2)}, u32[]{:S(2)}) collective-permute-start(bf16[128,1024]{1,0:T(8,128)(2,1)S(1)} %get-tuple-element.24), channel_id=1, source_target_pairs={{32,0},{33,1},{34,2},{35,3},{36,4},{37,5},{38,6},{39,7},{40,8},{41... | collective-permute-start | bytes 786440 | tf_op jit(solution)/shard_map/ppermute | solution.py:33
  66.0 2.1 %collective-permute-done.16 = bf16[2,32,1024]{2,1,0:T(8,128)(2,1)S(1)} collective-permute-done((bf16[2,32,1024]{2,1,0:T(8,128)(2,1)S(1)}, bf16[2,32,1024]{2,1,0:T(8,128)(2,1)S(1)}, u32[]{:S(2)}, u32[]{:S(2)}) %collective-permute-start.16) | collective-permute-done | bytes 131104 | tf_op jit(solution)/shard_map/ppermute | solution.py:33
  69.3 3.7 %collective-permute-done.17 = bf16[2,32,1024]{2,1,0:T(8,128)(2,1)S(1)} collective-permute-done((bf16[2,32,1024]{2,1,0:T(8,128)(2,1)S(1)}, bf16[2,32,1024]{2,1,0:T(8,128)(2,1)S(1)}, u32[]{:S(2)}, u32[]{:S(2)}) %collective-permute-start.17) | collective-permute-done | bytes 131104 | tf_op jit(solution)/shard_map/ppermute | solution.py:33
  73.3 4.5 %collective-permute-start.18 = (bf16[32,1024]{1,0:T(8,128)(2,1)S(1)}, bf16[32,1024]{1,0:T(8,128)(2,1)S(1)}, u32[]{:S(2)}, u32[]{:S(2)}) collective-permute-start(bf16[32,1024]{1,0:T(8,128)(2,1)S(1)} %get-tuple-element.48), channel_id=1, source_target_pairs={{0,4},{1,5},{2,6},{3,7},{4,0},{5,1},{6,2},{7,3},{8,12},{9,13},{10,... | collective-permute-start | bytes 196616 | tf_op jit(solution)/shard_map/ppermute | solution.py:33
  80.5 5.6 %collective-permute-start.21 = (bf16[64,1024]{1,0:T(8,128)(2,1)S(1)}, bf16[64,1024]{1,0:T(8,128)(2,1)S(1)}, u32[]{:S(2)}, u32[]{:S(2)}) collective-permute-start(bf16[64,1024]{1,0:T(8,128)(2,1)S(1)} %pad_maximum_fusion.2), channel_id=1, source_target_pairs={{0,16},{1,17},{2,18},{3,19},{4,20},{5,21},{6,22},{7,23},{8,24},{9,... | collective-permute-start | bytes 393224 | tf_op jit(solution)/shard_map/ppermute | solution.py:33
  86.1 2.7 %collective-permute-start.19 = (bf16[64,1024]{1,0:T(8,128)(2,1)S(1)}, bf16[64,1024]{1,0:T(8,128)(2,1)S(1)}, u32[]{:S(2)}, u32[]{:S(2)}) collective-permute-start(bf16[64,1024]{1,0:T(8,128)(2,1)S(1)} %pad_maximum_fusion.2), channel_id=1, source_target_pairs={{0,8},{1,9},{2,10},{3,11},{4,12},{5,13},{6,14},{7,15},{8,16},{9,17... | collective-permute-start | bytes 393224 | tf_op jit(solution)/shard_map/ppermute | solution.py:33
  89.6 3.2 %collective-permute-done.19 = bf16[64,1024]{1,0:T(8,128)(2,1)S(1)} collective-permute-done((bf16[64,1024]{1,0:T(8,128)(2,1)S(1)}, bf16[64,1024]{1,0:T(8,128)(2,1)S(1)}, u32[]{:S(2)}, u32[]{:S(2)}) %collective-permute-start.19) | collective-permute-done | bytes 131104 | tf_op jit(solution)/shard_map/ppermute | solution.py:33
  92.9 4.0 %collective-permute-done.23 = bf16[64,1024]{1,0:T(8,128)(2,1)S(1)} collective-permute-done((bf16[64,1024]{1,0:T(8,128)(2,1)S(1)}, bf16[64,1024]{1,0:T(8,128)(2,1)S(1)}, u32[]{:S(2)}, u32[]{:S(2)}) %collective-permute-start.23) | collective-permute-done | bytes 131104 | tf_op jit(solution)/shard_map/ppermute | solution.py:33
  98.8 2.6 %collective-permute-start.29 = (bf16[256,1024]{1,0:T(8,128)(2,1)S(1)}, bf16[256,1024]{1,0:T(8,128)(2,1)S(1)}, u32[]{:S(2)}, u32[]{:S(2)}) collective-permute-start(bf16[256,1024]{1,0:T(8,128)(2,1)S(1)} %constant_dynamic-update-slice_fusion.15.refs_4_), channel_id=1, source_target_pairs={{0,8},{1,9},{2,10},{3,11},{4,12},{5,13},{6,14},{7,15},{8,16},{9,17... | collective-permute-start | bytes 1572872 | tf_op jit(solution)/shard_map/ppermute | solution.py:33
  101.9 3.2 %collective-permute-done.26.refs_1_ = bf16[256,1024]{1,0:T(8,128)(2,1)S(1)} collective-permute-done((bf16[256,1024]{1,0:T(8,128)(2,1)S(1)}, bf16[256,1024]{1,0:T(8,128)(2,1)S(1)}, u32[]{:S(2)}, u32[]{:S(2)}) %collective-permute-start.26) | collective-permute-done | bytes 524320 | tf_op jit(solution)/shard_map/ppermute | solution.py:33
  105.1 3.0 %collective-permute-start.28 = (bf16[256,1024]{1,0:T(8,128)(2,1)S(1)}, bf16[256,1024]{1,0:T(8,128)(2,1)S(1)}, u32[]{:S(2)}, u32[]{:S(2)}) collective-permute-start(bf16[256,1024]{1,0:T(8,128)(2,1)S(1)} %collective-permute-done.26.refs_1_), channel_id=1, source_target_pairs={{0,1},{1,2},{2,3},{3,4},{4,5},{5,6},{6,7},{7,0},{8,9},{9,10},{10,1... | collective-permute-start | bytes 1572872 | tf_op jit(solution)/shard_map/ppermute | solution.py:33
  108.1 2.8 %collective-permute-start.31 = (bf16[256,1024]{1,0:T(8,128)(2,1)S(1)}, bf16[256,1024]{1,0:T(8,128)(2,1)S(1)}, u32[]{:S(2)}, u32[]{:S(2)}) collective-permute-start(bf16[256,1024]{1,0:T(8,128)(2,1)S(1)} %collective-permute-done.29.refs_5_), channel_id=1, source_target_pairs={{0,8},{1,9},{2,10},{3,11},{4,12},{5,13},{6,14},{7,15},{8,16},{9,17... | collective-permute-start | bytes 1572872 | tf_op jit(solution)/shard_map/ppermute | solution.py:33
  110.9 3.8 %collective-permute-done.27.refs_2_ = bf16[256,1024]{1,0:T(8,128)(2,1)S(1)} collective-permute-done((bf16[256,1024]{1,0:T(8,128)(2,1)S(1)}, bf16[256,1024]{1,0:T(8,128)(2,1)S(1)}, u32[]{:S(2)}, u32[]{:S(2)}) %collective-permute-start.27) | collective-permute-done | bytes 524320 | tf_op jit(solution)/shard_map/ppermute | solution.py:33
  117.8 3.2 %collective-permute-done.31.refs_7_ = bf16[256,1024]{1,0:T(8,128)(2,1)S(1)} collective-permute-done((bf16[256,1024]{1,0:T(8,128)(2,1)S(1)}, bf16[256,1024]{1,0:T(8,128)(2,1)S(1)}, u32[]{:S(2)}, u32[]{:S(2)}) %collective-permute-start.31) | collective-permute-done | bytes 524320 | tf_op jit(solution)/shard_map/ppermute | solution.py:33
  121.0 5.0 %chain.3 = (bf16[128,1024]{1,0:T(8,128)(2,1)S(1)}, bf16[1024,1024]{1,0:T(8,128)(2,1)S(1)}, bf16[1024,1024]{1,0:T(8,128)(2,1)S(1)}) custom-call(s32[4]{0:T(128)S(1)} %pad_add_fusion.where, f32[2,32,1024]{2,1,0:T(8,128)S(1)} %get-tuple-element.36.keep, f32[2,32,1024]{2,1,0:T(8,128)S(1)} %get-tuple-element.35.other, ...), custom_call_target="tpu_custom_call" | custom-call | tf_op jit(solution)/shard_map/chain/pallas_call | solution.py:148
  126.1 4.7 %collective-permute-start.32 = (bf16[128,1024]{1,0:T(8,128)(2,1)S(1)}, bf16[128,1024]{1,0:T(8,128)(2,1)S(1)}, u32[]{:S(2)}, u32[]{:S(2)}) collective-permute-start(bf16[128,1024]{1,0:T(8,128)(2,1)S(1)} %get-tuple-element.32), channel_id=1, source_target_pairs={{32,0},{33,1},{34,2},{35,3},{36,4},{37,5},{38,6},{39,7},{40,8},{41... | collective-permute-start | bytes 786440 | tf_op jit(solution)/shard_map/ppermute | solution.py:33
  133.7 2.6 %collective-permute-done.33 = f32[4,32,1024]{2,1,0:T(8,128)S(1)} collective-permute-done((f32[4,32,1024]{2,1,0:T(8,128)S(1)}, f32[4,32,1024]{2,1,0:T(8,128)S(1)}, u32[]{:S(2)}, u32[]{:S(2)}) %collective-permute-start.33) | collective-permute-done | bytes 524320 | tf_op jit(solution)/shard_map/ppermute | solution.py:33
  (76 shorter events, 26.2 us)
Async XLA Ops:
  2.6 4.5 %collective-permute-start = (f32[2,32,1024]{2,1,0:T(8,128)S(1)}, f32[2,32,1024]{2,1,0:T(8,128)S(1)}, u32[]{:S(2)}, u32[]{:S(2)}) collective-permute-start(f32[2,32,1024]{2,1,0:T(8,128)S(1)} %get-tuple-element.21), channel_id=1, source_target_pairs={{0,32},{1,33},{2,34},{3,35},{4,36},{5,37},{6,38},{7,39},{8,40},{9,... | collective-permute-start | bytes 786440 | tf_op jit(solution)/shard_map/ppermute | solution.py:33
  7.2 7.2 %collective-permute-start.1 = (bf16[32,1024]{1,0:T(8,128)(2,1)S(1)}, bf16[32,1024]{1,0:T(8,128)(2,1)S(1)}, u32[]{:S(2)}, u32[]{:S(2)}) collective-permute-start(bf16[32,1024]{1,0:T(8,128)(2,1)S(1)} %get-tuple-element.52), channel_id=1, source_target_pairs={{0,4},{1,5},{2,6},{3,7},{4,0},{5,1},{6,2},{7,3},{8,12},{9,13},{10,... | collective-permute-start | bytes 196616 | tf_op jit(solution)/shard_map/ppermute | solution.py:33
  12.4 7.9 %collective-permute-start.5 = (bf16[32,1024]{1,0:T(8,128)(2,1)S(1)}, bf16[32,1024]{1,0:T(8,128)(2,1)S(1)}, u32[]{:S(2)}, u32[]{:S(2)}) collective-permute-start(bf16[32,1024]{1,0:T(8,128)(2,1)S(1)} %get-tuple-element.49), channel_id=1, source_target_pairs={{0,4},{1,5},{2,6},{3,7},{4,0},{5,1},{6,2},{7,3},{8,12},{9,13},{10,... | collective-permute-start | bytes 196616 | tf_op jit(solution)/shard_map/ppermute | solution.py:33
  14.4 14.3 %collective-permute-start.4 = (bf16[64,1024]{1,0:T(8,128)(2,1)S(1)}, bf16[64,1024]{1,0:T(8,128)(2,1)S(1)}, u32[]{:S(2)}, u32[]{:S(2)}) collective-permute-start(bf16[64,1024]{1,0:T(8,128)(2,1)S(1)} %pad_maximum_fusion), channel_id=1, source_target_pairs={{0,16},{1,17},{2,18},{3,19},{4,20},{5,21},{6,22},{7,23},{8,24},{9,... | collective-permute-start | bytes 393224 | tf_op jit(solution)/shard_map/ppermute | solution.py:33
  17.6 11.1 %collective-permute-start.3 = (bf16[64,1024]{1,0:T(8,128)(2,1)S(1)}, bf16[64,1024]{1,0:T(8,128)(2,1)S(1)}, u32[]{:S(2)}, u32[]{:S(2)}) collective-permute-start(bf16[64,1024]{1,0:T(8,128)(2,1)S(1)} %pad_maximum_fusion), channel_id=1, source_target_pairs={{0,24},{1,25},{2,26},{3,27},{4,28},{5,29},{6,30},{7,31},{8,0},{9,1... | collective-permute-start | bytes 393224 | tf_op jit(solution)/shard_map/ppermute | solution.py:33
  18.0 7.7 %collective-permute-start.2 = (bf16[64,1024]{1,0:T(8,128)(2,1)S(1)}, bf16[64,1024]{1,0:T(8,128)(2,1)S(1)}, u32[]{:S(2)}, u32[]{:S(2)}) collective-permute-start(bf16[64,1024]{1,0:T(8,128)(2,1)S(1)} %pad_maximum_fusion), channel_id=1, source_target_pairs={{0,8},{1,9},{2,10},{3,11},{4,12},{5,13},{6,14},{7,15},{8,16},{9,17... | collective-permute-start | bytes 393224 | tf_op jit(solution)/shard_map/ppermute | solution.py:33
  20.3 11.1 %collective-permute-start.8 = (bf16[64,1024]{1,0:T(8,128)(2,1)S(1)}, bf16[64,1024]{1,0:T(8,128)(2,1)S(1)}, u32[]{:S(2)}, u32[]{:S(2)}) collective-permute-start(bf16[64,1024]{1,0:T(8,128)(2,1)S(1)} %pad_maximum_fusion.1), channel_id=1, source_target_pairs={{0,2},{1,3},{2,4},{3,5},{4,6},{5,7},{6,0},{7,1},{8,10},{9,11},{10,... | collective-permute-start | bytes 393224 | tf_op jit(solution)/shard_map/ppermute | solution.py:33
  24.4 7.0 %collective-permute-start.7 = (bf16[64,1024]{1,0:T(8,128)(2,1)S(1)}, bf16[64,1024]{1,0:T(8,128)(2,1)S(1)}, u32[]{:S(2)}, u32[]{:S(2)}) collective-permute-start(bf16[64,1024]{1,0:T(8,128)(2,1)S(1)} %pad_maximum_fusion.1), channel_id=1, source_target_pairs={{0,7},{1,0},{2,1},{3,2},{4,3},{5,4},{6,5},{7,6},{8,15},{9,8},{10,9... | collective-permute-start | bytes 393224 | tf_op jit(solution)/shard_map/ppermute | solution.py:33
  25.7 5.5 %collective-permute-start.6 = (bf16[64,1024]{1,0:T(8,128)(2,1)S(1)}, bf16[64,1024]{1,0:T(8,128)(2,1)S(1)}, u32[]{:S(2)}, u32[]{:S(2)}) collective-permute-start(bf16[64,1024]{1,0:T(8,128)(2,1)S(1)} %pad_maximum_fusion.1), channel_id=1, source_target_pairs={{0,1},{1,2},{2,3},{3,4},{4,5},{5,6},{6,7},{7,0},{8,9},{9,10},{10,1... | collective-permute-start | bytes 393224 | tf_op jit(solution)/shard_map/ppermute | solution.py:33
  31.4 9.7 %collective-permute-start.9 = (bf16[256,1024]{1,0:T(8,128)(2,1)S(1)}, bf16[256,1024]{1,0:T(8,128)(2,1)S(1)}, u32[]{:S(2)}, u32[]{:S(2)}) collective-permute-start(bf16[256,1024]{1,0:T(8,128)(2,1)S(1)} %constant_dynamic-update-slice_fusion.refs_0_), channel_id=1, source_target_pairs={{0,1},{1,2},{2,3},{3,4},{4,5},{5,6},{6,7},{7,0},{8,9},{9,10},{10,1... | collective-permute-start | bytes 1572872 | tf_op jit(solution)/shard_map/ppermute | solution.py:33
  34.1 10.5 %collective-permute-start.12 = (bf16[256,1024]{1,0:T(8,128)(2,1)S(1)}, bf16[256,1024]{1,0:T(8,128)(2,1)S(1)}, u32[]{:S(2)}, u32[]{:S(2)}) collective-permute-start(bf16[256,1024]{1,0:T(8,128)(2,1)S(1)} %constant_dynamic-update-slice_fusion.5.refs_4_), channel_id=1, source_target_pairs={{0,8},{1,9},{2,10},{3,11},{4,12},{5,13},{6,14},{7,15},{8,16},{9,17... | collective-permute-start | bytes 1572872 | tf_op jit(solution)/shard_map/ppermute | solution.py:33
  37.2 13.1 %collective-permute-start.10 = (bf16[256,1024]{1,0:T(8,128)(2,1)S(1)}, bf16[256,1024]{1,0:T(8,128)(2,1)S(1)}, u32[]{:S(2)}, u32[]{:S(2)}) collective-permute-start(bf16[256,1024]{1,0:T(8,128)(2,1)S(1)} %constant_dynamic-update-slice_fusion.refs_0_), channel_id=1, source_target_pairs={{0,7},{1,0},{2,1},{3,2},{4,3},{5,4},{6,5},{7,6},{8,15},{9,8},{10,9... | collective-permute-start | bytes 1572872 | tf_op jit(solution)/shard_map/ppermute | solution.py:33
  37.2 13.2 %collective-permute-start.13 = (bf16[256,1024]{1,0:T(8,128)(2,1)S(1)}, bf16[256,1024]{1,0:T(8,128)(2,1)S(1)}, u32[]{:S(2)}, u32[]{:S(2)}) collective-permute-start(bf16[256,1024]{1,0:T(8,128)(2,1)S(1)} %constant_dynamic-update-slice_fusion.5.refs_4_), channel_id=1, source_target_pairs={{0,24},{1,25},{2,26},{3,27},{4,28},{5,29},{6,30},{7,31},{8,0},{9,1... | collective-permute-start | bytes 1572872 | tf_op jit(solution)/shard_map/ppermute | solution.py:33
  41.2 10.3 %collective-permute-start.11 = (bf16[256,1024]{1,0:T(8,128)(2,1)S(1)}, bf16[256,1024]{1,0:T(8,128)(2,1)S(1)}, u32[]{:S(2)}, u32[]{:S(2)}) collective-permute-start(bf16[256,1024]{1,0:T(8,128)(2,1)S(1)} %collective-permute-done.9.refs_1_), channel_id=1, source_target_pairs={{0,1},{1,2},{2,3},{3,4},{4,5},{5,6},{6,7},{7,0},{8,9},{9,10},{10,1... | collective-permute-start | bytes 1572872 | tf_op jit(solution)/shard_map/ppermute | solution.py:33
  44.6 10.0 %collective-permute-start.14 = (bf16[256,1024]{1,0:T(8,128)(2,1)S(1)}, bf16[256,1024]{1,0:T(8,128)(2,1)S(1)}, u32[]{:S(2)}, u32[]{:S(2)}) collective-permute-start(bf16[256,1024]{1,0:T(8,128)(2,1)S(1)} %collective-permute-done.12.refs_5_), channel_id=1, source_target_pairs={{0,8},{1,9},{2,10},{3,11},{4,12},{5,13},{6,14},{7,15},{8,16},{9,17... | collective-permute-start | bytes 1572872 | tf_op jit(solution)/shard_map/ppermute | solution.py:33
  59.8 4.3 %collective-permute-start.15 = (bf16[128,1024]{1,0:T(8,128)(2,1)S(1)}, bf16[128,1024]{1,0:T(8,128)(2,1)S(1)}, u32[]{:S(2)}, u32[]{:S(2)}) collective-permute-start(bf16[128,1024]{1,0:T(8,128)(2,1)S(1)} %get-tuple-element.24), channel_id=1, source_target_pairs={{32,0},{33,1},{34,2},{35,3},{36,4},{37,5},{38,6},{39,7},{40,8},{41... | collective-permute-start | bytes 786440 | tf_op jit(solution)/shard_map/ppermute | solution.py:33
  68.0 5.0 %collective-permute-start.17 = (bf16[2,32,1024]{2,1,0:T(8,128)(2,1)S(1)}, bf16[2,32,1024]{2,1,0:T(8,128)(2,1)S(1)}, u32[]{:S(2)}, u32[]{:S(2)}) collective-permute-start(bf16[2,32,1024]{2,1,0:T(8,128)(2,1)S(1)} %broadcast_select_fusion), channel_id=1, source_target_pairs={{0,64},{1,65},{2,66},{3,67},{4,68},{5,69},{6,70},{7,71},{8,72},{9,... | collective-permute-start | bytes 393224 | tf_op jit(solution)/shard_map/ppermute | solution.py:33
  73.3 7.2 %collective-permute-start.18 = (bf16[32,1024]{1,0:T(8,128)(2,1)S(1)}, bf16[32,1024]{1,0:T(8,128)(2,1)S(1)}, u32[]{:S(2)}, u32[]{:S(2)}) collective-permute-start(bf16[32,1024]{1,0:T(8,128)(2,1)S(1)} %get-tuple-element.48), channel_id=1, source_target_pairs={{0,4},{1,5},{2,6},{3,7},{4,0},{5,1},{6,2},{7,3},{8,12},{9,13},{10,... | collective-permute-start | bytes 196616 | tf_op jit(solution)/shard_map/ppermute | solution.py:33
  77.8 11.0 %collective-permute-start.22 = (bf16[32,1024]{1,0:T(8,128)(2,1)S(1)}, bf16[32,1024]{1,0:T(8,128)(2,1)S(1)}, u32[]{:S(2)}, u32[]{:S(2)}) collective-permute-start(bf16[32,1024]{1,0:T(8,128)(2,1)S(1)} %get-tuple-element.45), channel_id=1, source_target_pairs={{0,4},{1,5},{2,6},{3,7},{4,0},{5,1},{6,2},{7,3},{8,12},{9,13},{10,... | collective-permute-start | bytes 196616 | tf_op jit(solution)/shard_map/ppermute | solution.py:33
  80.5 12.4 %collective-permute-start.21 = (bf16[64,1024]{1,0:T(8,128)(2,1)S(1)}, bf16[64,1024]{1,0:T(8,128)(2,1)S(1)}, u32[]{:S(2)}, u32[]{:S(2)}) collective-permute-start(bf16[64,1024]{1,0:T(8,128)(2,1)S(1)} %pad_maximum_fusion.2), channel_id=1, source_target_pairs={{0,16},{1,17},{2,18},{3,19},{4,20},{5,21},{6,22},{7,23},{8,24},{9,... | collective-permute-start | bytes 393224 | tf_op jit(solution)/shard_map/ppermute | solution.py:33
  86.1 6.7 %collective-permute-start.20 = (bf16[64,1024]{1,0:T(8,128)(2,1)S(1)}, bf16[64,1024]{1,0:T(8,128)(2,1)S(1)}, u32[]{:S(2)}, u32[]{:S(2)}) collective-permute-start(bf16[64,1024]{1,0:T(8,128)(2,1)S(1)} %pad_maximum_fusion.2), channel_id=1, source_target_pairs={{0,24},{1,25},{2,26},{3,27},{4,28},{5,29},{6,30},{7,31},{8,0},{9,1... | collective-permute-start | bytes 393224 | tf_op jit(solution)/shard_map/ppermute | solution.py:33
  86.1 6.7 %collective-permute-start.19 = (bf16[64,1024]{1,0:T(8,128)(2,1)S(1)}, bf16[64,1024]{1,0:T(8,128)(2,1)S(1)}, u32[]{:S(2)}, u32[]{:S(2)}) collective-permute-start(bf16[64,1024]{1,0:T(8,128)(2,1)S(1)} %pad_maximum_fusion.2), channel_id=1, source_target_pairs={{0,8},{1,9},{2,10},{3,11},{4,12},{5,13},{6,14},{7,15},{8,16},{9,17... | collective-permute-start | bytes 393224 | tf_op jit(solution)/shard_map/ppermute | solution.py:33
  88.8 8.2 %collective-permute-start.25 = (bf16[64,1024]{1,0:T(8,128)(2,1)S(1)}, bf16[64,1024]{1,0:T(8,128)(2,1)S(1)}, u32[]{:S(2)}, u32[]{:S(2)}) collective-permute-start(bf16[64,1024]{1,0:T(8,128)(2,1)S(1)} %pad_maximum_fusion.3), channel_id=1, source_target_pairs={{0,2},{1,3},{2,4},{3,5},{4,6},{5,7},{6,0},{7,1},{8,10},{9,11},{10,... | collective-permute-start | bytes 393224 | tf_op jit(solution)/shard_map/ppermute | solution.py:33
  89.6 7.3 %collective-permute-start.24 = (bf16[64,1024]{1,0:T(8,128)(2,1)S(1)}, bf16[64,1024]{1,0:T(8,128)(2,1)S(1)}, u32[]{:S(2)}, u32[]{:S(2)}) collective-permute-start(bf16[64,1024]{1,0:T(8,128)(2,1)S(1)} %pad_maximum_fusion.3), channel_id=1, source_target_pairs={{0,7},{1,0},{2,1},{3,2},{4,3},{5,4},{6,5},{7,6},{8,15},{9,8},{10,9... | collective-permute-start | bytes 393224 | tf_op jit(solution)/shard_map/ppermute | solution.py:33
  92.8 4.1 %collective-permute-start.23 = (bf16[64,1024]{1,0:T(8,128)(2,1)S(1)}, bf16[64,1024]{1,0:T(8,128)(2,1)S(1)}, u32[]{:S(2)}, u32[]{:S(2)}) collective-permute-start(bf16[64,1024]{1,0:T(8,128)(2,1)S(1)} %pad_maximum_fusion.3), channel_id=1, source_target_pairs={{0,1},{1,2},{2,3},{3,4},{4,5},{5,6},{6,7},{7,0},{8,9},{9,10},{10,1... | collective-permute-start | bytes 393224 | tf_op jit(solution)/shard_map/ppermute | solution.py:33
  97.0 8.1 %collective-permute-start.26 = (bf16[256,1024]{1,0:T(8,128)(2,1)S(1)}, bf16[256,1024]{1,0:T(8,128)(2,1)S(1)}, u32[]{:S(2)}, u32[]{:S(2)}) collective-permute-start(bf16[256,1024]{1,0:T(8,128)(2,1)S(1)} %constant_dynamic-update-slice_fusion.10.refs_0_), channel_id=1, source_target_pairs={{0,1},{1,2},{2,3},{3,4},{4,5},{5,6},{6,7},{7,0},{8,9},{9,10},{10,1... | collective-permute-start | bytes 1572872 | tf_op jit(solution)/shard_map/ppermute | solution.py:33
  98.8 9.2 %collective-permute-start.29 = (bf16[256,1024]{1,0:T(8,128)(2,1)S(1)}, bf16[256,1024]{1,0:T(8,128)(2,1)S(1)}, u32[]{:S(2)}, u32[]{:S(2)}) collective-permute-start(bf16[256,1024]{1,0:T(8,128)(2,1)S(1)} %constant_dynamic-update-slice_fusion.15.refs_4_), channel_id=1, source_target_pairs={{0,8},{1,9},{2,10},{3,11},{4,12},{5,13},{6,14},{7,15},{8,16},{9,17... | collective-permute-start | bytes 1572872 | tf_op jit(solution)/shard_map/ppermute | solution.py:33
  101.4 13.4 %collective-permute-start.27 = (bf16[256,1024]{1,0:T(8,128)(2,1)S(1)}, bf16[256,1024]{1,0:T(8,128)(2,1)S(1)}, u32[]{:S(2)}, u32[]{:S(2)}) collective-permute-start(bf16[256,1024]{1,0:T(8,128)(2,1)S(1)} %constant_dynamic-update-slice_fusion.10.refs_0_), channel_id=1, source_target_pairs={{0,7},{1,0},{2,1},{3,2},{4,3},{5,4},{6,5},{7,6},{8,15},{9,8},{10,9... | collective-permute-start | bytes 1572872 | tf_op jit(solution)/shard_map/ppermute | solution.py:33
  101.9 13.9 %collective-permute-start.30 = (bf16[256,1024]{1,0:T(8,128)(2,1)S(1)}, bf16[256,1024]{1,0:T(8,128)(2,1)S(1)}, u32[]{:S(2)}, u32[]{:S(2)}) collective-permute-start(bf16[256,1024]{1,0:T(8,128)(2,1)S(1)} %constant_dynamic-update-slice_fusion.15.refs_4_), channel_id=1, source_target_pairs={{0,24},{1,25},{2,26},{3,27},{4,28},{5,29},{6,30},{7,31},{8,0},{9,1... | collective-permute-start | bytes 1572872 | tf_op jit(solution)/shard_map/ppermute | solution.py:33
  105.1 12.7 %collective-permute-start.28 = (bf16[256,1024]{1,0:T(8,128)(2,1)S(1)}, bf16[256,1024]{1,0:T(8,128)(2,1)S(1)}, u32[]{:S(2)}, u32[]{:S(2)}) collective-permute-start(bf16[256,1024]{1,0:T(8,128)(2,1)S(1)} %collective-permute-done.26.refs_1_), channel_id=1, source_target_pairs={{0,1},{1,2},{2,3},{3,4},{4,5},{5,6},{6,7},{7,0},{8,9},{9,10},{10,1... | collective-permute-start | bytes 1572872 | tf_op jit(solution)/shard_map/ppermute | solution.py:33
  108.1 13.0 %collective-permute-start.31 = (bf16[256,1024]{1,0:T(8,128)(2,1)S(1)}, bf16[256,1024]{1,0:T(8,128)(2,1)S(1)}, u32[]{:S(2)}, u32[]{:S(2)}) collective-permute-start(bf16[256,1024]{1,0:T(8,128)(2,1)S(1)} %collective-permute-done.29.refs_5_), channel_id=1, source_target_pairs={{0,8},{1,9},{2,10},{3,11},{4,12},{5,13},{6,14},{7,15},{8,16},{9,17... | collective-permute-start | bytes 1572872 | tf_op jit(solution)/shard_map/ppermute | solution.py:33
  126.1 5.8 %collective-permute-start.32 = (bf16[128,1024]{1,0:T(8,128)(2,1)S(1)}, bf16[128,1024]{1,0:T(8,128)(2,1)S(1)}, u32[]{:S(2)}, u32[]{:S(2)}) collective-permute-start(bf16[128,1024]{1,0:T(8,128)(2,1)S(1)} %get-tuple-element.32), channel_id=1, source_target_pairs={{32,0},{33,1},{34,2},{35,3},{36,4},{37,5},{38,6},{39,7},{40,8},{41... | collective-permute-start | bytes 786440 | tf_op jit(solution)/shard_map/ppermute | solution.py:33
  (4 other events, 9.1 us)
